TPU v7x, 128 devices: a whole 4x4x4 slice. The times are simulated.
128 devices in a mesh: tm: 8 (over y, core), height: 8 (over z, x_hi), width: 2 (over x_lo).
Axes of the slice: x: 4 (x_hi: 2, x_lo: 2; x = x_hi * 2 + x_lo), y: 4, z: 4, core: 2. Of those that a mesh axis runs over, the one named last changes fastest.
Arguments:
- features: bfloat16 [16, 16, 128, 256], P('tm', ('height', 'width')), may hold values from -6 to 6
- conv_first: bfloat16 [3, 3, 3, 256, 256], replicated, may hold values from -0.078125 to 0.078125
- conv_second: bfloat16 [3, 3, 3, 256, 256], replicated, may hold values from -0.078125 to 0.078125
- up_kernel: bfloat16 [4, 4, 256, 256], replicated, may hold values from -0.1875 to 0.1875
- cotangent: bfloat16 [16, 32, 256, 256], P('tm', 'height', 'width'), may hold values from -6 to 6
Outputs:
- grad_features: bfloat16 [16, 16, 128, 256], P('tm', ('height', 'width'))
- grad_first: float32 [1769472], P(('tm', 'height', 'width'))
- grad_second: float32 [1769472], P(('tm', 'height', 'width'))
- grad_up: float32 [1048576], P(('tm', 'height', 'width'))
All inputs are finite; a program needn't handle non-finite values.
Results may differ from a plain program's by a relative error of at most 0.006.
Values may be sent and summed in bfloat16 or wider, within the bound.
No kernel may reach another device: no remote copies, remote signals or barrier semaphores. Data moves between devices by JAX's collectives and lax.ppermute only.
A program may use at most 128 MiB of HBM per device.

v0:
```python
import math

import jax
import jax.numpy as jnp
from jax import lax
from jax.sharding import PartitionSpec as P


def from_behind(value, axis, steps):
    count = lax.axis_size(axis)
    initial, last = (max(0, -steps), min(count, count - steps))
    return lax.ppermute(value, axis, [(source, source + steps) for source in range(initial, last)])


def with_halo(block, sides, width):
    for axis, dim in sides:
        count = lax.axis_size(axis)
        forward = [(i, i + 1) for i in range(count - 1)]
        backward = [(target, source) for source, target in forward]
        low = lax.ppermute(
            lax.slice_in_dim(block, block.shape[dim] - width, None, axis=dim), axis, forward
        )
        high = lax.ppermute(lax.slice_in_dim(block, 0, width, axis=dim), axis, backward)
        block = jnp.concatenate([low, block, high], axis=dim)
    return block


def silu_slope(values):
    sigma = jax.nn.sigmoid(values)
    return sigma * (1.0 + values * (1.0 - sigma))


def conv_taps(padded, kernel, frame_count, row_count, column_count):
    channels = padded.shape[-1]
    outputs = kernel.shape[-1]
    summed = jnp.zeros((frame_count * row_count * column_count, outputs), jnp.float32)
    for tap_t in range(3):
        for tap_h in range(3):
            patches = jnp.concatenate(
                [
                    padded[
                        tap_t : tap_t + frame_count,
                        tap_h : tap_h + row_count,
                        tap_w : tap_w + column_count,
                    ]
                    for tap_w in range(3)
                ],
                axis=-1,
            )
            summed = summed + jnp.dot(
                patches.reshape(-1, 3 * channels),
                kernel[tap_t, tap_h].reshape(3 * channels, outputs),
                preferred_element_type=jnp.float32,
            )
    return summed.reshape(frame_count, row_count, column_count, outputs)


def kernel_grads(padded, gradient, frame_count, row_count, column_count):
    channels = padded.shape[-1]
    flattened = gradient.reshape(-1, gradient.shape[-1])
    pieces = []
    for tap_t in range(3):
        for tap_h in range(3):
            patches = jnp.concatenate(
                [
                    padded[
                        tap_t : tap_t + frame_count,
                        tap_h : tap_h + row_count,
                        tap_w : tap_w + column_count,
                    ]
                    for tap_w in range(3)
                ],
                axis=-1,
            )
            pieces.append(
                lax.dot_general(
                    patches.reshape(-1, 3 * channels),
                    flattened,
                    (((0,), (0,)), ((), ())),
                    preferred_element_type=jnp.float32,
                )
            )
    return jnp.stack(pieces).reshape(-1)


def reverse_kernel(kernel):
    return jnp.transpose(jnp.flip(kernel, (0, 1, 2)), (0, 1, 2, 4, 3))


def upsample_back(padded_cot, activation, up_kernel, row_count, column_count):
    frame_count = activation.shape[0]
    channels = activation.shape[-1]
    parity_view = padded_cot.reshape(frame_count, row_count + 1, 2, column_count + 1, 2, channels)
    act_flat = activation.reshape(-1, channels)
    summed = jnp.zeros((act_flat.shape[0], channels), jnp.float32)
    pieces = []
    for tap_y in range(4):
        joined = jnp.concatenate(
            [
                parity_view[
                    :,
                    tap_y // 2 : tap_y // 2 + row_count,
                    tap_y % 2,
                    tap_x // 2 : tap_x // 2 + column_count,
                    tap_x % 2,
                ]
                for tap_x in range(4)
            ],
            axis=-1,
        )
        joined = joined.reshape(-1, 4 * channels)
        summed = summed + jnp.dot(
            joined,
            jnp.transpose(up_kernel[tap_y], (0, 2, 1)).reshape(4 * channels, channels),
            preferred_element_type=jnp.float32,
        )
        product = lax.dot_general(
            act_flat, joined, (((0,), (0,)), ((), ())), preferred_element_type=jnp.float32
        )
        pieces.append(jnp.transpose(product.reshape(channels, 4, channels), (1, 0, 2)))
    grad_act = summed.reshape(frame_count, row_count, column_count, channels)
    return (grad_act, jnp.stack(pieces).reshape(-1))


def pad_columns(values):
    return jnp.pad(values, ((0, 0), (0, 0), (1, 1), (0, 0)))


def shards(features, conv_first, conv_second, up_kernel, cotangent):
    frame_count, row_count, column_count, channels = features.shape
    earlier_in = from_behind(features, "tm", 1)
    extended = jnp.concatenate([earlier_in, features], axis=0)
    padded_in = pad_columns(with_halo(extended, ((("height", "width"), 1),), 1))
    first_pre = conv_taps(padded_in, conv_first, frame_count, row_count, column_count)
    first_act = jax.nn.silu(first_pre).astype(jnp.bfloat16)
    earlier_act = from_behind(first_act, "tm", 1)
    extended_act = jnp.concatenate([earlier_act, first_act], axis=0)
    padded_act = pad_columns(with_halo(extended_act, ((("height", "width"), 1),), 1))
    summed = features.astype(jnp.float32) + conv_taps(
        padded_act, conv_second, frame_count, row_count, column_count
    )
    up_act = jax.nn.silu(summed).astype(jnp.bfloat16)
    regrouped = lax.all_to_all(cotangent, "width", split_axis=1, concat_axis=2, tiled=True)
    padded_cot = pad_columns(with_halo(regrouped, ((("height", "width"), 1),), 1))
    grad_full, up_sum = upsample_back(padded_cot, up_act, up_kernel, row_count, column_count)
    grad_act = grad_full.astype(jnp.bfloat16)
    grad_act = lax.optimization_barrier(grad_act)
    up_share = lax.psum_scatter(up_sum, ("tm", "height", "width"), scatter_dimension=0, tiled=True)
    grad_summed = (grad_act.astype(jnp.float32) * silu_slope(summed)).astype(jnp.bfloat16)
    second_sum = kernel_grads(padded_act, grad_summed, frame_count, row_count, column_count)
    second_share = lax.psum_scatter(
        second_sum, ("tm", "height", "width"), scatter_dimension=0, tiled=True
    )
    later_grad = from_behind(grad_summed, "tm", -1)
    extended_grad = jnp.concatenate([grad_summed, later_grad], axis=0)
    padded_grad = pad_columns(with_halo(extended_grad, ((("height", "width"), 1),), 1))
    grad_inner = conv_taps(
        padded_grad, reverse_kernel(conv_second), frame_count, row_count, column_count
    )
    grad_hidden = (grad_inner * silu_slope(first_pre)).astype(jnp.bfloat16)
    first_sum = kernel_grads(padded_in, grad_hidden, frame_count, row_count, column_count)
    first_share = lax.psum_scatter(
        first_sum, ("tm", "height", "width"), scatter_dimension=0, tiled=True
    )
    later_hidden = from_behind(grad_hidden, "tm", -1)
    extended_hidden = jnp.concatenate([grad_hidden, later_hidden], axis=0)
    padded_hidden = pad_columns(with_halo(extended_hidden, ((("height", "width"), 1),), 1))
    grad_features = (
        grad_summed.astype(jnp.float32)
        + conv_taps(padded_hidden, reverse_kernel(conv_first), frame_count, row_count, column_count)
    ).astype(jnp.bfloat16)
    positions = (
        frame_count
        * lax.axis_size("tm")
        * row_count
        * lax.axis_size("height")
        * lax.axis_size("width")
        * column_count
    )
    factor = 1.0 / math.sqrt(positions)
    return (grad_features, first_share * factor, second_share * factor, up_share * factor)


def solution(mesh):
    in_specs = (
        P("tm", ("height", "width"), None, None),
        P(),
        P(),
        P(),
        P("tm", "height", "width", None),
    )
    out_specs = (
        P("tm", ("height", "width"), None, None),
        P(("tm", "height", "width")),
        P(("tm", "height", "width")),
        P(("tm", "height", "width")),
    )
    return jax.shard_map(shards, mesh=mesh, in_specs=in_specs, out_specs=out_specs, check_vma=False)
```

profile of v0, /device:TPU:1, one launch (start us, length us, event | category | flops | bytes accessed | tf_op | source)
XLA Modules:
  0.0 479.6 jit_solution(3470567419470990561)
XLA Ops:
  8.8 4.6 collective-permute-start.2
  15.3 4.2 all-to-all-start
  19.6 4.0 fusion.88
  23.6 4.0 copy.249
  27.6 3.4 fusion.89
  35.4 4.0 collective-permute-start.3
  43.6 4.7 collective-permute-start
  89.7 3.0 collective-permute-start.5
  102.6 4.2 collective-permute-start.6
  109.9 2.1 fusion.95
  150.8 2.3 collective-permute-start.8
  153.0 2.2 fusion.19
  155.3 2.2 fusion.18
  166.0 9.6 %copy.315 = f32[864,2,8,128]{3,1,2,0:T(2,128)} copy(f32[864,2,8,128]{3,2,1,0:T(8,128)} %bitcast.206) | data formatting | bytes 14155776
  178.5 5.3 %collective-permute-start.9 = (bf16[4,1,128,256]{2,3,0,1:T(8,128)(2,1)S(1)}, bf16[4,1,128,256]{2,3,0,1:T(8,128)(2,1)S(1)}, u32[]{:S(2)}, u32[]{:S(2)}) collective-permute-start(bf16[4,1,128,256]{2,3,0,1:T(8,128)(2,1)S(1)} %pad_maximum_fusion.42), channel_id=1, source_target_pairs={{0,1},{1,2},{2,3},{3,4},{4,5},{5,6},{6,7},{7,8},{8,9},{9,10},{10,1... | collective-permute-start | bytes 786440 | tf_op jit(solution)/shard_map/ppermute | solution.py:20
  184.0 4.1 copy.316
  221.7 9.6 %copy.314 = f32[864,2,8,128]{3,1,2,0:T(2,128)} copy(f32[864,2,8,128]{3,2,1,0:T(8,128)} %bitcast.204) | data formatting | bytes 14155776
  233.4 4.0 copy.261
  241.4 2.4 reverse_bitcast_fusion
  243.8 2.3 collective-permute-done.11
  246.9 5.8 %collective-permute-start.12 = (bf16[4,1,128,256]{2,3,0,1:T(8,128)(2,1)}, bf16[4,1,128,256]{2,3,0,1:T(8,128)(2,1)S(1)}, u32[]{:S(2)}, u32[]{:S(2)}) collective-permute-start(bf16[4,1,128,256]{2,3,0,1:T(8,128)(2,1)} %pad_maximum_fusion.43), channel_id=1, source_target_pairs={{0,1},{1,2},{2,3},{3,4},{4,5},{5,6},{6,7},{7,8},{8,9},{9,10},{10,1... | collective-permute-start | bytes 786440 | tf_op jit(solution)/shard_map/ppermute | solution.py:20
  255.7 4.6 collective-permute-done.12
  261.0 7.2 %collective-permute-done.13 = bf16[4,1,128,256]{2,3,0,1:T(8,128)(2,1)S(1)} collective-permute-done((bf16[4,1,128,256]{2,3,0,1:T(8,128)(2,1)}, bf16[4,1,128,256]{2,3,0,1:T(8,128)(2,1)S(1)}, u32[]{:S(2)}, u32[]{:S(2)}) %collective-permute-start.13) | collective-permute-done | bytes 262176 | tf_op jit(solution)/shard_map/ppermute | solution.py:23
  304.8 163.3 %all-reduce.11.cloned.1.call-done = (f32[1769472]{0:T(1024)}, f32[1769472]{0:T(1024)}, f32[1048576]{0:T(1024)}) async-done(((f32[1769472]{0:T(1024)}, f32[1769472]{0:T(1024)}, f32[1048576]{0:T(1024)}), (f32[1769472]{0:T(1024)}, f32[1769472]{0:T(1024)}, f32[1048576]{0:T(1024)})) %all-reduce.11.cloned.1.call-update) | async-done | bytes 18350096
  (506 shorter events, 200.2 us)
Async XLA Ops:
  8.8 24.3 %collective-permute-start.2 = (bf16[2,1,128,256]{2,3,0,1:T(8,128)(2,1)}, bf16[2,1,128,256]{2,3,0,1:T(8,128)(2,1)}, u32[]{:S(2)}, u32[]{:S(2)}) collective-permute-start(bf16[2,1,128,256]{2,3,0,1:T(8,128)(2,1)} %copy.222), channel_id=1, source_target_pairs={{0,16},{16,32},{32,48},{48,64},{64,80},{80,96},{96,112},{1,17},{17... | collective-permute-start | bytes 393224 | tf_op jit(solution)/shard_map/ppermute | solution.py:12
  15.3 25.0 %all-to-all-start = ((bf16[2,4,128,256]{3,2,0,1:T(8,128)(2,1)}), bf16[2,4,128,256]{3,2,0,1:T(8,128)(2,1)}, u32[]{:S(2)}, u32[]{:S(2)}) async-start(bf16[2,4,128,256]{3,2,0,1:T(8,128)(2,1)} %copy.197), calls=%async_computation | async-start | bytes 1048576 | tf_op jit(solution)/shard_map/all_to_all | solution.py:143
  19.5 448.6 %all-reduce.11.cloned.1.call-start = ((), (), s32[]{:S(2)}) async-start(), calls=%async_computation.1 | async-start | bytes 36700160
  34.1 14.1 %collective-permute-start.4 = (bf16[4,1,128,256]{2,3,0,1:T(8,128)(2,1)S(1)}, bf16[4,1,128,256]{2,3,0,1:T(8,128)(2,1)S(1)}, u32[]{:S(2)}, u32[]{:S(2)}) collective-permute-start(bf16[4,1,128,256]{2,3,0,1:T(8,128)(2,1)S(1)} %pad_maximum_fusion.40), channel_id=1, source_target_pairs={{1,0},{2,1},{3,2},{4,3},{5,4},{6,5},{7,6},{8,7},{9,8},{10,9},{11,1... | collective-permute-start | bytes 786440 | tf_op jit(solution)/shard_map/ppermute | solution.py:23
  35.4 12.9 %collective-permute-start.3 = (bf16[4,1,128,256]{2,3,0,1:T(8,128)(2,1)S(1)}, bf16[4,1,128,256]{2,3,0,1:T(8,128)(2,1)S(1)}, u32[]{:S(2)}, u32[]{:S(2)}) collective-permute-start(bf16[4,1,128,256]{2,3,0,1:T(8,128)(2,1)S(1)} %pad_maximum_fusion.40), channel_id=1, source_target_pairs={{0,1},{1,2},{2,3},{3,4},{4,5},{5,6},{6,7},{7,8},{8,9},{9,10},{10,1... | collective-permute-start | bytes 786440 | tf_op jit(solution)/shard_map/ppermute | solution.py:20
  40.3 25.5 %copy-start.41 = (bf16[2,1,128,256]{2,3,0,1:T(8,128)(2,1)}, bf16[2,1,128,256]{2,3,0,1:T(8,128)(2,1)S(1)}, u32[]{:S(2)}) copy-start(bf16[2,1,128,256]{2,3,0,1:T(8,128)(2,1)S(1)} %fusion.64) | copy-start | bytes 393220
  42.3 64.5 %collective-permute-start.1 = (bf16[2,1,256,256]{3,2,1,0:T(8,128)(2,1)}, bf16[2,1,256,256]{3,2,1,0:T(8,128)(2,1)}, u32[]{:S(2)}, u32[]{:S(2)}) collective-permute-start(bf16[2,1,256,256]{3,2,1,0:T(8,128)(2,1)} %get-tuple-element.152), channel_id=1, source_target_pairs={{1,0},{2,1},{3,2},{4,3},{5,4},{6,5},{7,6},{8,7},{9,8},{10,9},{11,1... | collective-permute-start | bytes 786440 | tf_op jit(solution)/shard_map/ppermute | solution.py:23
  43.6 63.3 %collective-permute-start = (bf16[2,1,256,256]{3,2,1,0:T(8,128)(2,1)}, bf16[2,1,256,256]{3,2,1,0:T(8,128)(2,1)}, u32[]{:S(2)}, u32[]{:S(2)}) collective-permute-start(bf16[2,1,256,256]{3,2,1,0:T(8,128)(2,1)} %get-tuple-element.151), channel_id=1, source_target_pairs={{0,1},{1,2},{2,3},{3,4},{4,5},{5,6},{6,7},{7,8},{8,9},{9,10},{10,1... | collective-permute-start | bytes 786440 | tf_op jit(solution)/shard_map/ppermute | solution.py:20
  51.6 20.1 %copy-start.43 = (bf16[2,1,128,256]{2,3,0,1:T(8,128)(2,1)}, bf16[2,1,128,256]{2,3,0,1:T(8,128)(2,1)S(1)}, u32[]{:S(2)}) copy-start(bf16[2,1,128,256]{2,3,0,1:T(8,128)(2,1)S(1)} %get-tuple-element.118) | copy-start | bytes 393220
  51.6 20.1 %copy-start.45 = (bf16[2,1,128,256]{2,3,0,1:T(8,128)(2,1)}, bf16[2,1,128,256]{2,3,0,1:T(8,128)(2,1)S(1)}, u32[]{:S(2)}) copy-start(bf16[2,1,128,256]{2,3,0,1:T(8,128)(2,1)S(1)} %get-tuple-element.119) | copy-start | bytes 393220
  51.6 20.1 %copy-start.47 = (bf16[2,1,128,256]{2,3,0,1:T(8,128)(2,1)}, bf16[2,1,128,256]{2,3,0,1:T(8,128)(2,1)S(1)}, u32[]{:S(2)}) copy-start(bf16[2,1,128,256]{2,3,0,1:T(8,128)(2,1)S(1)} %get-tuple-element.120) | copy-start | bytes 393220
  89.7 10.9 %collective-permute-start.5 = (bf16[2,1,128,256]{2,3,0,1:T(8,128)(2,1)S(1)}, bf16[2,1,128,256]{2,3,0,1:T(8,128)(2,1)S(1)}, u32[]{:S(2)}, u32[]{:S(2)}) collective-permute-start(bf16[2,1,128,256]{2,3,0,1:T(8,128)(2,1)S(1)} %multiply_convert_fusion.5), channel_id=1, source_target_pairs={{0,16},{16,32},{32,48},{48,64},{64,80},{80,96},{96,112},{1,17},{17... | collective-permute-start | bytes 393224 | tf_op jit(solution)/shard_map/ppermute | solution.py:12
  101.3 16.1 %collective-permute-start.7 = (bf16[4,1,128,256]{2,3,0,1:T(8,128)(2,1)}, bf16[4,1,128,256]{2,3,0,1:T(8,128)(2,1)S(1)}, u32[]{:S(2)}, u32[]{:S(2)}) collective-permute-start(bf16[4,1,128,256]{2,3,0,1:T(8,128)(2,1)} %pad_maximum_fusion.41), channel_id=1, source_target_pairs={{1,0},{2,1},{3,2},{4,3},{5,4},{6,5},{7,6},{8,7},{9,8},{10,9},{11,1... | collective-permute-start | bytes 786440 | tf_op jit(solution)/shard_map/ppermute | solution.py:23
  102.6 14.8 %collective-permute-start.6 = (bf16[4,1,128,256]{2,3,0,1:T(8,128)(2,1)}, bf16[4,1,128,256]{2,3,0,1:T(8,128)(2,1)S(1)}, u32[]{:S(2)}, u32[]{:S(2)}) collective-permute-start(bf16[4,1,128,256]{2,3,0,1:T(8,128)(2,1)} %pad_maximum_fusion.41), channel_id=1, source_target_pairs={{0,1},{1,2},{2,3},{3,4},{4,5},{5,6},{6,7},{7,8},{8,9},{9,10},{10,1... | collective-permute-start | bytes 786440 | tf_op jit(solution)/shard_map/ppermute | solution.py:20
  134.4 12.5 %copy-start.20 = (bf16[1,1,3,256,256]{4,3,2,1,0:T(8,128)(2,1)S(1)}, bf16[1,1,3,256,256]{4,3,2,1,0:T(8,128)(2,1)}, u32[]{:S(2)}) copy-start(bf16[1,1,3,256,256]{4,3,2,1,0:T(8,128)(2,1)} %get-tuple-element.46) | copy-start | bytes 1179652
  150.8 41.2 %copy-start.3 = (bf16[2,1,128,256]{2,3,0,1:T(8,128)(2,1)}, bf16[2,1,128,256]{2,3,0,1:T(8,128)(2,1)S(1)}, u32[]{:S(2)}) copy-start(bf16[2,1,128,256]{2,3,0,1:T(8,128)(2,1)S(1)} %get-tuple-element.154) | copy-start | bytes 393220
  150.8 26.3 %collective-permute-start.8 = (bf16[2,1,128,256]{2,3,0,1:T(8,128)(2,1)S(1)}, bf16[2,1,128,256]{2,3,0,1:T(8,128)(2,1)S(1)}, u32[]{:S(2)}, u32[]{:S(2)}) collective-permute-start(bf16[2,1,128,256]{2,3,0,1:T(8,128)(2,1)S(1)} %get-tuple-element.154), channel_id=1, source_target_pairs={{16,0},{32,16},{48,32},{64,48},{80,64},{96,80},{112,96},{17,1},{33... | collective-permute-start | bytes 393224 | tf_op jit(solution)/shard_map/ppermute | solution.py:12
  177.2 11.0 %collective-permute-start.10 = (bf16[4,1,128,256]{2,3,0,1:T(8,128)(2,1)S(1)}, bf16[4,1,128,256]{2,3,0,1:T(8,128)(2,1)S(1)}, u32[]{:S(2)}, u32[]{:S(2)}) collective-permute-start(bf16[4,1,128,256]{2,3,0,1:T(8,128)(2,1)S(1)} %pad_maximum_fusion.42), channel_id=1, source_target_pairs={{1,0},{2,1},{3,2},{4,3},{5,4},{6,5},{7,6},{8,7},{9,8},{10,9},{11,1... | collective-permute-start | bytes 786440 | tf_op jit(solution)/shard_map/ppermute | solution.py:23
  178.5 10.4 %collective-permute-start.9 = (bf16[4,1,128,256]{2,3,0,1:T(8,128)(2,1)S(1)}, bf16[4,1,128,256]{2,3,0,1:T(8,128)(2,1)S(1)}, u32[]{:S(2)}, u32[]{:S(2)}) collective-permute-start(bf16[4,1,128,256]{2,3,0,1:T(8,128)(2,1)S(1)} %pad_maximum_fusion.42), channel_id=1, source_target_pairs={{0,1},{1,2},{2,3},{3,4},{4,5},{5,6},{6,7},{7,8},{8,9},{9,10},{10,1... | collective-permute-start | bytes 786440 | tf_op jit(solution)/shard_map/ppermute | solution.py:20
  239.5 6.7 %collective-permute-start.11 = (bf16[2,1,128,256]{2,3,0,1:T(8,128)(2,1)S(1)}, bf16[2,1,128,256]{2,3,0,1:T(8,128)(2,1)S(1)}, u32[]{:S(2)}, u32[]{:S(2)}) collective-permute-start(bf16[2,1,128,256]{2,3,0,1:T(8,128)(2,1)S(1)} %multiply_convert_fusion.2), channel_id=1, source_target_pairs={{16,0},{32,16},{48,32},{64,48},{80,64},{96,80},{112,96},{17,1},{33... | collective-permute-start | bytes 393224 | tf_op jit(solution)/shard_map/ppermute | solution.py:12
  246.9 13.4 %collective-permute-start.12 = (bf16[4,1,128,256]{2,3,0,1:T(8,128)(2,1)}, bf16[4,1,128,256]{2,3,0,1:T(8,128)(2,1)S(1)}, u32[]{:S(2)}, u32[]{:S(2)}) collective-permute-start(bf16[4,1,128,256]{2,3,0,1:T(8,128)(2,1)} %pad_maximum_fusion.43), channel_id=1, source_target_pairs={{0,1},{1,2},{2,3},{3,4},{4,5},{5,6},{6,7},{7,8},{8,9},{9,10},{10,1... | collective-permute-start | bytes 786440 | tf_op jit(solution)/shard_map/ppermute | solution.py:20
  253.8 14.4 %collective-permute-start.13 = (bf16[4,1,128,256]{2,3,0,1:T(8,128)(2,1)}, bf16[4,1,128,256]{2,3,0,1:T(8,128)(2,1)S(1)}, u32[]{:S(2)}, u32[]{:S(2)}) collective-permute-start(bf16[4,1,128,256]{2,3,0,1:T(8,128)(2,1)} %pad_maximum_fusion.43), channel_id=1, source_target_pairs={{1,0},{2,1},{3,2},{4,3},{5,4},{6,5},{7,6},{8,7},{9,8},{10,9},{11,1... | collective-permute-start | bytes 786440 | tf_op jit(solution)/shard_map/ppermute | solution.py:23
  279.7 13.4 %copy-start.112 = (bf16[2,1,128,256]{2,3,0,1:T(8,128)(2,1)S(1)}, bf16[2,1,128,256]{2,3,0,1:T(8,128)(2,1)}, u32[]{:S(2)}) copy-start(bf16[2,1,128,256]{2,3,0,1:T(8,128)(2,1)} %get-tuple-element.63) | copy-start | bytes 393220
  281.7 15.1 %copy-start.24 = (bf16[1,1,3,256,256]{4,3,2,1,0:T(8,128)(2,1)S(1)}, bf16[1,1,3,256,256]{4,3,2,1,0:T(8,128)(2,1)}, u32[]{:S(2)}) copy-start(bf16[1,1,3,256,256]{4,3,2,1,0:T(8,128)(2,1)} %get-tuple-element.31) | copy-start | bytes 1179652
  (132 other events, 700.9 us)
Sparse Core Ops, SparseCore 0:
  231.5 236.5 all-reduce.10
where the time goes:
time: 489 us; the launch traced here: 480 us
  waiting for transfers between devices  178 us (36%)
  local copies, waits for them, and re-layouts  135 us (28%)
  matrix products  55.2 us (11%)
  other arithmetic  49 us (10%)
  starting transfers between devices  46.4 us (9%)
  between operations  16.4 us (3%)
    unnamed x2, waiting for transfers between devices  163 us
    unnamed x293, local copies, waits for them, and re-layouts  48.9 us
    concatenate x34, local copies, waits for them, and re-layouts, conv_taps(): jnp.concatenate([padded[tap_t:tap_t + frame_count, tap_h:tap_h + row_coun...  45.4 us
    concatenate x30, other arithmetic, conv_taps(): jnp.concatenate([padded[tap_t:tap_t + frame_count, tap_h:tap_h + row_coun...  30.7 us
    dot_general x36, matrix products, conv_taps(): jnp.dot(patches.reshape(-1, 3 * channels), kernel[tap_t, tap_h].reshape(3...  27.5 us
    dot_general x18, matrix products, kernel_grads(): lax.dot_general(patches.reshape(-1, 3 * channels), flattened, (((0,), (0,...  25.1 us
    ppermute x5, starting transfers between devices, with_halo(): lax.ppermute(lax.slice_in_dim(block, block.shape[dim] - width, None, axis...  23.9 us
    slice x16, local copies, waits for them, and re-layouts, conv_taps(): padded[tap_t:tap_t + frame_count, tap_h:tap_h + row_count, tap_w:tap_w +...  17.4 us
  transfers between devices with their start and end apart: 16, of which 5 were waited for; matrix products, arithmetic and copies ran while one was open for 32% of the time, Pallas kernels for 0%

commit v1 on v0

v1 whole, which is shorter than its diff:
```python
import functools
import math

import jax
import jax.numpy as jnp
from jax import lax
from jax.experimental import pallas as pl
from jax.experimental.pallas import tpu as pltpu
from jax.sharding import Mesh, PartitionSpec as P

F32 = jnp.float32
BF16 = jnp.bfloat16
VMEM_LIMIT = 48 * 1024 * 1024

FR = 4
ROWS = 16
WIN = 16
OWN = 8
EDGE = 4
CH = 256
TAPS = 27
SHARE = 54


def slope_of(values, sigma):
    return sigma * (1.0 + values * (1.0 - sigma))


def nt(lhs, rhs):
    return lax.dot_general(lhs, rhs, (((1,), (1,)), ((), ())), preferred_element_type=F32)


def nn(lhs, rhs):
    return jnp.dot(lhs, rhs, preferred_element_type=F32)


def fill_table(table, slot, block, forward):
    wide = block.astype(F32)
    before = pltpu.roll(wide, 1, axis=1).astype(BF16)
    after = pltpu.roll(wide, WIN - 1, axis=1).astype(BF16)
    table[slot, 1 : ROWS + 1, :, 0:CH] = before if forward else after
    table[slot, 1 : ROWS + 1, :, CH : 2 * CH] = block
    table[slot, 1 : ROWS + 1, :, 2 * CH : 3 * CH] = after if forward else before


def fill_own_table(table, slot, block):
    wide = block.astype(F32)
    for tap in range(3):
        moved = pltpu.roll(wide, WIN - (EDGE + 1 - tap), axis=1)
        table[slot, 1 : ROWS + 1, :, tap * CH : (tap + 1) * CH] = moved[:, :OWN].astype(BF16)


def clear_border(table):
    frames, _, columns, lanes = table.shape
    border = jnp.zeros((frames, columns, lanes), BF16)
    table[:, 0] = border
    table[:, ROWS + 1] = border


def own_columns(block):
    return pltpu.roll(block.astype(F32), WIN - EDGE, axis=1)[:, :OWN]


def first_kernel(halo, block, weights, mask, act, slope, table, total):
    step = pl.program_id(0)

    @pl.when(step == 0)
    def _():
        clear_border(table)
        for frame in range(2):
            fill_table(table, frame, halo[:, frame], True)
        for frame in range(FR):
            fill_table(table, 2 + frame, block[frame // 2, :, frame % 2], True)
        total[...] = jnp.zeros_like(total)

    for tap in range(3):
        lhs = table[pl.ds(step, FR), tap : tap + ROWS].reshape(FR * ROWS * WIN, 3 * CH)
        total[...] += nn(lhs, weights[0, tap].reshape(3 * CH, CH))

    @pl.when(step == 2)
    def _():
        inside = mask[...]
        for frame in range(FR):
            rows = ROWS * WIN
            values = total[frame * rows : (frame + 1) * rows].reshape(ROWS, WIN, CH)
            sigma = jax.nn.sigmoid(values)
            act[frame] = (values * sigma * inside).astype(BF16)
            slope[frame] = slope_of(values, sigma)


def second_kernel(halo, block, features, grad_act, weights, mask, grad_sum, up_act, table, total):
    step = pl.program_id(0)

    @pl.when(step == 0)
    def _():
        clear_border(table)
        for frame in range(2):
            fill_table(table, frame, halo[frame], True)
        for frame in range(FR):
            fill_table(table, 2 + frame, block[frame], True)
        total[...] = jnp.zeros_like(total)

    for tap in range(3):
        lhs = table[pl.ds(step, FR), tap : tap + ROWS].reshape(FR * ROWS * WIN, 3 * CH)
        total[...] += nn(lhs, weights[0, tap].reshape(3 * CH, CH))

    @pl.when(step == 2)
    def _():
        inside = mask[...]
        for frame in range(FR):
            rows = ROWS * WIN
            values = total[frame * rows : (frame + 1) * rows].reshape(ROWS, WIN, CH)
            values = values + features[frame // 2, :, frame % 2].astype(F32)
            sigma = jax.nn.sigmoid(values)
            up_act[frame] = (values * sigma).astype(BF16)
            grad = grad_act[frame].astype(F32) * slope_of(values, sigma) * inside
            grad_sum[frame] = grad.astype(BF16)


def hidden_kernel(block, later, slope, weights, mask, grad_hidden, table, total):
    step = pl.program_id(0)

    @pl.when(step == 0)
    def _():
        clear_border(table)
        for frame in range(FR):
            fill_table(table, frame, block[frame], False)
        for frame in range(2):
            fill_table(table, FR + frame, later[frame], False)
        total[...] = jnp.zeros_like(total)

    for tap in range(3):
        part = None
        for column in range(3):
            lhs = table[pl.ds(2 - step, FR), 2 - tap : 2 - tap + ROWS, :, column * CH : (column + 1) * CH]
            more = nt(lhs.reshape(FR * ROWS * WIN, CH), weights[0, tap, column])
            part = more if part is None else part + more
        total[...] += part

    @pl.when(step == 2)
    def _():
        inside = mask[...]
        for frame in range(FR):
            rows = ROWS * WIN
            values = total[frame * rows : (frame + 1) * rows].reshape(ROWS, WIN, CH)
            grad_hidden[frame] = (values * slope[frame] * inside).astype(BF16)


def features_kernel(core_ref, block, later, grad_sum, weights, grad_features, table, total):
    step = pl.program_id(0)
    core = core_ref[0]

    @pl.when(step == 0)
    def _():
        clear_border(table)
        for frame in range(FR):
            fill_own_table(table, frame, block[frame])
        for frame in range(2):
            fill_own_table(table, FR + frame, later[frame])
        total[...] = jnp.zeros_like(total)

    for tap in range(3):
        part = None
        for column in range(3):
            lhs = table[
                pl.ds(2 * core + 2 - step, 2), 2 - tap : 2 - tap + ROWS, :, column * CH : (column + 1) * CH
            ]
            more = nt(lhs.reshape(2 * ROWS * OWN, CH), weights[0, tap, column])
            part = more if part is None else part + more
        total[...] += part

    @pl.when(step == 2)
    def _():
        for frame in range(2):
            rows = ROWS * OWN
            values = total[frame * rows : (frame + 1) * rows].reshape(ROWS, OWN, CH)
            values = values + own_columns(grad_sum[2 * core + frame])
            grad_features[:, frame] = values.astype(BF16)


def cotangent_kernel(core_ref, mine, other, weights, grad_act, table):
    core = core_ref[0]
    border = jnp.zeros((FR, WIN, 4 * CH), BF16)
    table[:, 0, 0] = border
    table[:, ROWS, 1] = border
    for source, which in ((mine, core), (other, 1 - core)):
        for frame in range(2):
            slot = 2 * which + frame
            for parity in range(2):
                fine = source[:, frame, :, parity].reshape(ROWS, WIN, 2 * CH)
                even, odd = fine[:, :, :CH], fine[:, :, CH:]
                before = pltpu.roll(odd.astype(F32), 1, axis=1).astype(BF16)
                after = pltpu.roll(even.astype(F32), WIN - 1, axis=1).astype(BF16)
                low = 0 if parity == 0 else 1
                put = (slot, slice(low, low + ROWS), 1 - parity)
                table[put + (slice(None), slice(0, CH))] = before
                table[put + (slice(None), slice(CH, 2 * CH))] = even
                table[put + (slice(None), slice(2 * CH, 3 * CH))] = odd
                table[put + (slice(None), slice(3 * CH, 4 * CH))] = after
    for frame in range(FR):
        part = None
        for tap in range(4):
            for column in range(4):
                lhs = table[frame, tap // 2 : tap // 2 + ROWS, tap % 2, :, column * CH : (column + 1) * CH]
                more = nt(lhs.reshape(ROWS * WIN, CH), weights[tap, column])
                part = more if part is None else part + more
        grad_act[frame] = part.reshape(ROWS, WIN, CH).astype(BF16)


def up_grad_kernel(core_ref, act, mine, other, out, table, flipped):
    core = core_ref[0]
    border = jnp.zeros((FR, OWN, 4 * CH), BF16)
    table[:, 0, 0] = border
    table[:, ROWS, 1] = border
    for source, which in ((mine, core), (other, 1 - core)):
        for frame in range(2):
            slot = 2 * which + frame
            for parity in range(2):
                fine = source[:, frame, :, parity].reshape(ROWS, WIN, 2 * CH).astype(F32)
                even, odd = fine[:, :, :CH], fine[:, :, CH:]
                low = 0 if parity == 0 else 1
                put = (slot, slice(low, low + ROWS), 1 - parity)
                for column, (values, shift) in enumerate(((odd, -1), (even, 0), (odd, 0), (even, 1))):
                    moved = pltpu.roll(values, WIN - (EDGE + shift), axis=1)[:, :OWN].astype(BF16)
                    table[put + (slice(None), slice(column * CH, (column + 1) * CH))] = moved
    for frame in range(FR):
        rows = ROWS * OWN
        flipped[:, frame * rows : (frame + 1) * rows] = jnp.transpose(
            own_columns(act[frame]).reshape(rows, CH)
        ).astype(BF16)
    lanes = pl.ds(pl.multiple_of(core * 2 * CH, 2 * CH), 2 * CH)
    for tap in range(4):
        rhs = table[:, tap // 2 : tap // 2 + ROWS, tap % 2, :, lanes]
        result = nn(flipped[...], rhs.reshape(FR * ROWS * OWN, 2 * CH))
        for half in range(2):
            for piece in range(8):
                out[tap * 16 + half * 8 + piece] = result[
                    piece * 32 : (piece + 1) * 32, half * CH : (half + 1) * CH
                ].astype(BF16)


def kernel_grad_kernel(by_core, core_ref, act, block, later, out, table, flipped, sums):
    clear_border(table)
    for frame in range(FR):
        fill_own_table(table, frame, block[frame])
    for frame in range(2):
        fill_own_table(table, FR + frame, later[frame])
    for frame in range(FR):
        rows = ROWS * OWN
        values = act[frame // 2, :, frame % 2] if by_core else act[frame]
        flipped[:, frame * rows : (frame + 1) * rows] = jnp.transpose(
            own_columns(values).reshape(rows, CH)
        ).astype(BF16)
    sums[TAPS * CH :] = jnp.zeros((8, CH), F32)
    for tap_t in range(3):
        for tap_h in range(3):
            rhs = table[2 - tap_t : 2 - tap_t + FR, 2 - tap_h : 2 - tap_h + ROWS]
            result = nn(flipped[...], rhs.reshape(FR * ROWS * OWN, 3 * CH))
            for tap_w in range(3):
                at = (tap_t * 9 + tap_h * 3 + tap_w) * CH
                sums[at : at + CH] = result[:, tap_w * CH : (tap_w + 1) * CH]
    for core in range(2):

        @pl.when(core_ref[0] == core)
        def _(core=core):
            for group in range(4):
                for member in range(16):
                    at = 16 * SHARE * (2 * group + core) + SHARE * member
                    out[group * 16 + member] = sums[at : at + SHARE + 2].astype(BF16)


def whole(shape):
    zeros = (0,) * len(shape)
    return pl.BlockSpec(shape, lambda *_: zeros)


SMEM = pl.BlockSpec(memory_space=pltpu.SMEM)


def tap_weights():
    return pl.BlockSpec((1, 3, 3, CH, CH), lambda step: (step, 0, 0, 0, 0))


def call(kernel, grid, args, specs, outs, scratch, flops):
    shapes = [jax.ShapeDtypeStruct(shape, dtype) for shape, dtype in outs]
    moved = sum(math.prod(a.shape) * a.dtype.itemsize for a in args)
    moved += sum(math.prod(s.shape) * s.dtype.itemsize for s in shapes)
    single = len(shapes) == 1
    return pl.pallas_call(
        kernel,
        out_shape=shapes[0] if single else shapes,
        grid=grid,
        in_specs=specs,
        out_specs=whole(shapes[0].shape) if single else [whole(s.shape) for s in shapes],
        scratch_shapes=scratch,
        compiler_params=pltpu.CompilerParams(vmem_limit_bytes=VMEM_LIMIT),
        cost_estimate=pl.CostEstimate(flops=int(flops), bytes_accessed=moved, transcendentals=0),
    )(*args)


def shift(value, axis, step):
    count = lax.axis_size(axis)
    return lax.ppermute(value, axis, [(i, i + step) for i in range(count) if 0 <= i + step < count])


def shards(features, conv_first, conv_second, up_kernel, cotangent):
    core = lax.axis_index("core")
    height = lax.axis_index("height")
    width = lax.axis_index("width")
    core_arg = core.astype(jnp.int32).reshape(1)
    window = 8 * width + height
    columns = OWN * window - EDGE + jnp.arange(WIN)
    inside = ((columns >= 0) & (columns < 128)).astype(F32)
    mask = jnp.broadcast_to(inside[:, None], (WIN, CH))
    act_shape = (FR, ROWS, WIN, CH)
    table = pltpu.VMEM((FR + 2, ROWS + 2, WIN, 3 * CH), BF16)
    own_table = pltpu.VMEM((FR + 2, ROWS + 2, OWN, 3 * CH), BF16)
    total = pltpu.VMEM((FR * ROWS * WIN, CH), F32)
    tap_flops = 2 * FR * ROWS * WIN * CH * CH

    padded = jnp.pad(features[:, 0], ((0, 0), (EDGE, EDGE), (0, 0))).reshape(2, 17, OWN, CH)
    windows = jnp.concatenate([padded[:, :-1], padded[:, 1:]], axis=2)
    windows = windows.reshape(2, 2, 8, WIN, CH).transpose(2, 1, 0, 3, 4).reshape(1, 16, 2, WIN, CH)
    windows = jnp.broadcast_to(windows, (2, 16, 2, WIN, CH)).reshape(32, 2, WIN, CH)
    block = lax.all_to_all(windows, ("core", "height", "width"), 0, 0, tiled=True)
    block = block.reshape(2, ROWS, 2, WIN, CH)
    halo = shift(block[1], "y", 1)

    paired = cotangent.reshape(2, 4, 64, 2 * CH)
    edge = jnp.where(width == 0, paired[:, :, 64 - EDGE :], paired[:, :, :EDGE])
    edge = lax.ppermute(edge, "width", [(0, 1), (1, 0)])
    nothing = jnp.zeros_like(edge)
    low, high = jnp.where(width == 0, nothing, edge), jnp.where(width == 0, edge, nothing)
    paired = jnp.concatenate([low, paired, high], axis=2).reshape(2, 4, 9, OWN, 2 * CH)
    fine = jnp.concatenate([paired[:, :, :-1], paired[:, :, 1:]], axis=3).transpose(2, 0, 1, 3, 4)
    mine = lax.all_to_all(fine, "height", 0, 0, tiled=True).reshape(8, 2, 2, 2, WIN, 2 * CH)
    other = lax.ppermute(mine, "core", [(0, 1), (1, 0)])

    first_act, first_slope = call(
        first_kernel, (3,), (halo, block, conv_first, mask),
        [whole(halo.shape), whole(block.shape), tap_weights(), whole(mask.shape)],
        [(act_shape, BF16), (act_shape, F32)], [table, total], 27 * tap_flops,
    )
    earlier = shift(first_act[2:], "y", 1)
    grad_act = call(
        cotangent_kernel, (), (core_arg, mine, other, up_kernel),
        [SMEM, whole(mine.shape), whole(mine.shape), whole(up_kernel.shape)],
        [(act_shape, BF16)], [pltpu.VMEM((FR, ROWS + 1, 2, WIN, 4 * CH), BF16)], 16 * tap_flops,
    )
    grad_sum, up_act = call(
        second_kernel, (3,), (earlier, first_act, block, grad_act, conv_second, mask),
        [whole(earlier.shape), whole(act_shape), whole(block.shape), whole(act_shape), tap_weights(), whole(mask.shape)],
        [(act_shape, BF16), (act_shape, BF16)], [table, total], 27 * tap_flops,
    )
    later = shift(grad_sum[:2], "y", -1)
    up_part = call(
        up_grad_kernel, (), (core_arg, up_act, mine, other),
        [SMEM, whole(act_shape), whole(mine.shape), whole(mine.shape)],
        [((64, 32, CH), BF16)],
        [pltpu.VMEM((FR, ROWS + 1, 2, OWN, 4 * CH), BF16), pltpu.VMEM((CH, FR * ROWS * OWN), BF16)], 4 * tap_flops,
    )
    grad_hidden = call(
        hidden_kernel, (3,), (grad_sum, later, first_slope, conv_second, mask),
        [whole(act_shape), whole(later.shape), whole(act_shape), tap_weights(), whole(mask.shape)],
        [(act_shape, BF16)], [table, total], 27 * tap_flops,
    )
    later_hidden = shift(grad_hidden[:2], "y", -1)

    def kernel_grad(act, by_core, grad, after):
        return call(
            functools.partial(kernel_grad_kernel, by_core), (), (core_arg, act, grad, after),
            [SMEM, whole(act.shape), whole(act_shape), whole(after.shape)],
            [((64, SHARE + 2, CH), BF16)],
            [own_table, pltpu.VMEM((CH, FR * ROWS * OWN), BF16), pltpu.VMEM((TAPS * CH + 8, CH), F32)], 14 * tap_flops,
        )

    second_part = kernel_grad(first_act, False, grad_sum, later)
    first_part = kernel_grad(block, True, grad_hidden, later_hidden)
    rows_out = call(
        features_kernel, (3,), (core_arg, grad_hidden, later_hidden, grad_sum, conv_first),
        [SMEM, whole(act_shape), whole(later_hidden.shape), whole(act_shape), tap_weights()],
        [((ROWS, 2, OWN, CH), BF16)], [own_table, pltpu.VMEM((2 * ROWS * OWN, CH), F32)], 7 * tap_flops,
    )

    factor = 1.0 / math.sqrt(32768)

    def share_of(part, rows):
        received = lax.all_to_all(part, ("y", "height", "width"), 0, 0, tiled=True)
        return (jnp.sum(received[:, :rows].astype(F32), axis=0) * factor).reshape(-1)

    up_share = share_of(up_part, 32)
    second_share = share_of(second_part, SHARE)
    first_share = share_of(first_part, SHARE)
    returned = lax.all_to_all(rows_out, ("height", "width"), 0, 0, tiled=True)
    returned = returned.reshape(8, 2, 2, OWN, CH).transpose(2, 1, 0, 3, 4)
    grad_features = returned.reshape(2, 1, 128, CH)
    return (grad_features, first_share, second_share, up_share)


def solution(mesh):
    names = ("y", "core", "height", "width")
    split = Mesh(mesh.devices.reshape(4, 2, 8, 2), names)
    tm = ("y", "core")
    in_specs = (
        P(tm, ("height", "width"), None, None),
        P(),
        P(),
        P(),
        P(tm, "height", "width", None),
    )
    flat = P(names)
    out_specs = (P(tm, ("height", "width"), None, None), flat, flat, flat)
    return jax.shard_map(shards, mesh=split, in_specs=in_specs, out_specs=out_specs, check_vma=False)
```

time: 489 us -> 202 us (0.41)
  the two profiles are of different devices: /device:TPU:1 before, /device:TPU:0 now
where the time goes in v1:
time: 202 us; the launch traced here: 201 us
  waiting for transfers between devices  104 us (51%)
  starting transfers between devices  46.7 us (23%)
  Pallas kernels  32.5 us (16%)
  local copies, waits for them, and re-layouts  13.1 us (6%)
  other arithmetic  3.89 us (2%)
    all_to_all x3, waiting for transfers between devices, share_of(): received = lax.all_to_all(part, ('y', 'height', 'width'), 0, 0, tiled=True)  50.9 us
    pallas_call x8, Pallas kernels, call(): pl.pallas_call(kernel, out_shape=shapes[0] if single else shapes, grid=gr...  32.5 us
    ppermute x4, waiting for transfers between devices, shift(): lax.ppermute(value, axis, [(i, i + step) for i in range(count) if 0 <= i...  19.1 us
    all_to_all x3, starting transfers between devices, share_of(): received = lax.all_to_all(part, ('y', 'height', 'width'), 0, 0, tiled=True)  17.6 us
    all_to_all x1, waiting for transfers between devices, shards(): lax.all_to_all(fine, 'height', 0, 0, tiled=True)  15.9 us
    all_to_all x1, waiting for transfers between devices, shards(): lax.all_to_all(windows, ('core', 'height', 'width'), 0, 0, tiled=True)  11.6 us
    ppermute x4, starting transfers between devices, shift(): lax.ppermute(value, axis, [(i, i + step) for i in range(count) if 0 <= i...  10.5 us
    all_to_all x1, starting transfers between devices, shards(): lax.all_to_all(fine, 'height', 0, 0, tiled=True)  7.86 us
  transfers between devices with their start and end apart: 12, of which 10 were waited for; matrix products, arithmetic and copies ran while one was open for 3% of the time, Pallas kernels for 9%

profile of v1, /device:TPU:0, one launch (start us, length us, event | category | flops | bytes accessed | tf_op | source)
XLA Modules:
  0.0 201.0 jit_solution(16080347040808322188)
XLA Ops:
  7.4 7.9 %all-to-all-start.1 = ((bf16[8,2,4,16,512]{4,3,2,1,0:T(8,128)(2,1)}), bf16[8,2,4,16,512]{4,3,2,1,0:T(8,128)(2,1)S(1)}, u32[]{:S(2)}, u32[]{:S(2)}) async-start(bf16[8,2,4,16,512]{4,3,2,1,0:T(8,128)(2,1)} %copy.15), calls=%async_computation.1 | async-start | bytes 2097152 | tf_op jit(solution)/shard_map/all_to_all | solution.py:336
  15.4 15.9 %all-to-all-done.1 = bf16[8,2,4,16,512]{4,3,2,1,0:T(8,128)(2,1)S(1)} async-done(((bf16[8,2,4,16,512]{4,3,2,1,0:T(8,128)(2,1)}), bf16[8,2,4,16,512]{4,3,2,1,0:T(8,128)(2,1)S(1)}, u32[]{:S(2)}, u32[]{:S(2)}) %all-to-all-start.1) | async-done | bytes 1048608 | tf_op jit(solution)/shard_map/all_to_all | solution.py:336
  32.2 3.9 %all-to-all-start = ((bf16[32,2,16,256]{3,2,1,0:T(8,128)(2,1)}), bf16[32,2,16,256]{3,2,1,0:T(8,128)(2,1)S(1)}, u32[]{:S(2)}, u32[]{:S(2)}) async-start(bf16[32,2,16,256]{3,2,1,0:T(8,128)(2,1)} %bitcast.6), calls=%async_computation | async-start | bytes 1048576 | tf_op jit(solution)/shard_map/all_to_all | solution.py:325
  36.5 11.6 %all-to-all-done = bf16[32,2,16,256]{3,2,1,0:T(8,128)(2,1)S(1)} async-done(((bf16[32,2,16,256]{3,2,1,0:T(8,128)(2,1)}), bf16[32,2,16,256]{3,2,1,0:T(8,128)(2,1)S(1)}, u32[]{:S(2)}, u32[]{:S(2)}) %all-to-all-start) | async-done | bytes 524320 | tf_op jit(solution)/shard_map/all_to_all | solution.py:325
  48.1 3.5 %collective-permute-start = (bf16[16,2,16,256]{3,2,1,0:T(8,128)(2,1)S(1)}, bf16[16,2,16,256]{3,2,1,0:T(8,128)(2,1)S(1)}, u32[]{:S(2)}, u32[]{:S(2)}) collective-permute-start(bf16[16,2,16,256]{3,2,1,0:T(8,128)(2,1)S(1)} %slice.51), channel_id=1, source_target_pairs={{0,32},{32,64},{64,96},{1,33},{33,65},{65,97},{2,34},{34,66},{66,9... | collective-permute-start | bytes 786440 | tf_op jit(solution)/shard_map/ppermute | solution.py:303
  51.6 5.1 %collective-permute-done.halo = bf16[16,2,16,256]{3,2,1,0:T(8,128)(2,1)S(1)} collective-permute-done((bf16[16,2,16,256]{3,2,1,0:T(8,128)(2,1)S(1)}, bf16[16,2,16,256]{3,2,1,0:T(8,128)(2,1)S(1)}, u32[]{:S(2)}, u32[]{:S(2)}) %collective-permute-start) | collective-permute-done | bytes 262176 | tf_op jit(solution)/shard_map/ppermute | solution.py:303
  58.8 5.0 %shard_map.84 = (bf16[4,16,16,256]{3,2,1,0:T(8,128)(2,1)S(1)}, f32[4,16,16,256]{3,2,1,0:T(8,128)S(1)}) custom-call(bf16[16,2,16,256]{3,2,1,0:T(8,128)(2,1)S(1)} %collective-permute-done.halo, bf16[2,16,2,16,256]{4,3,2,1,0:T(8,128)(2,1)S(1)} %bitcast.27, bf16[3,3,3,256,256]{4,3,2,1,0:T(8,128)(2,1)S(1)} %copy-done, f32[16,256]{1,0:T(8,128)S(1)} %broadcast_in_dim.18.mask), custom_call_target="tpu_custom_call" | custom-call | flops 3623878656 | bytes 5914624 | tf_op jit(solution)/shard_map/pallas_call | solution.py:289
  65.6 4.4 %collective-permute-start.1 = (bf16[2,16,16,256]{3,2,1,0:T(8,128)(2,1)S(1)}, bf16[2,16,16,256]{3,2,1,0:T(8,128)(2,1)S(1)}, u32[]{:S(2)}, u32[]{:S(2)}) collective-permute-start(bf16[2,16,16,256]{3,2,1,0:T(8,128)(2,1)S(1)} %slice.40), channel_id=1, source_target_pairs={{0,32},{32,64},{64,96},{1,33},{33,65},{65,97},{2,34},{34,66},{66,9... | collective-permute-start | bytes 786440 | tf_op jit(solution)/shard_map/ppermute | solution.py:303
  72.0 3.4 %shard_map.85.grad_act = bf16[4,16,16,256]{3,2,1,0:T(8,128)(2,1)S(1)} custom-call(s32[1]{0:T(128)} %bitcast.core_ref, bf16[8,2,2,2,16,512]{5,4,3,2,1,0:T(8,128)(2,1)S(1)} %bitcast.25, bf16[8,2,2,2,16,512]{5,4,3,2,1,0:T(8,128)(2,1)S(1)} %collective-permute-done.3.other, bf16[4,4,256,256]{3,2,1,0:T(8,128)(2,1)S(1)} %copy-done.8), custom_call_target="tpu_custom_call" | custom-call | flops 2147483648 | bytes 4718596 | tf_op jit(solution)/shard_map/pallas_call | solution.py:289
  75.4 6.6 %shard_map.86 = (bf16[4,16,16,256]{3,2,1,0:T(8,128)(2,1)S(1)}, bf16[4,16,16,256]{3,2,1,0:T(8,128)(2,1)S(1)}) custom-call(bf16[2,16,16,256]{3,2,1,0:T(8,128)(2,1)S(1)} %collective-permute-done.1.halo, bf16[4,16,16,256]{3,2,1,0:T(8,128)(2,1)S(1)} %copy-done.5, bf16[2,16,2,16,256]{4,3,2,1,0:T(8,128)(2,1)S(1)} %bitcast.28, ...), custom_call_target="tpu_custom_call" | custom-call | flops 3623878656 | bytes 6438912 | tf_op jit(solution)/shard_map/pallas_call | solution.py:289
  83.3 7.0 %collective-permute-done.4.later = bf16[2,16,16,256]{3,2,1,0:T(8,128)(2,1)S(1)} collective-permute-done((bf16[2,16,16,256]{3,2,1,0:T(8,128)(2,1)S(1)}, bf16[2,16,16,256]{3,2,1,0:T(8,128)(2,1)S(1)}, u32[]{:S(2)}, u32[]{:S(2)}) %collective-permute-start.4) | collective-permute-done | bytes 262176 | tf_op jit(solution)/shard_map/ppermute | solution.py:303
  90.4 4.8 %shard_map.87.block = bf16[4,16,16,256]{3,2,1,0:T(8,128)(2,1)S(1)} custom-call(bf16[4,16,16,256]{3,2,1,0:T(8,128)(2,1)S(1)} %get-tuple-element.9.block.grad_sum, bf16[2,16,16,256]{3,2,1,0:T(8,128)(2,1)S(1)} %collective-permute-done.4.later, f32[4,16,16,256]{3,2,1,0:T(8,128)S(1)} %copy-done.12, bf16[3,3,3,256,256]{4,3,2,1,0:T(8,128)(2,1)S(1)} %copy-done.7, ...), custom_call_target="tpu_custom_call" | custom-call | flops 3623878656 | bytes 5914624 | tf_op jit(solution)/shard_map/pallas_call | solution.py:289
  96.5 7.0 %collective-permute-done.5.later = bf16[2,16,16,256]{3,2,1,0:T(8,128)(2,1)S(1)} collective-permute-done((bf16[2,16,16,256]{3,2,1,0:T(8,128)(2,1)S(1)}, bf16[2,16,16,256]{3,2,1,0:T(8,128)(2,1)S(1)}, u32[]{:S(2)}, u32[]{:S(2)}) %collective-permute-start.5) | collective-permute-done | bytes 262176 | tf_op jit(solution)/shard_map/ppermute | solution.py:303
  106.1 4.9 %all-to-all-start.2 = ((bf16[16,2,8,256]{3,2,1,0:T(8,128)(2,1)}), bf16[16,2,8,256]{3,2,1,0:T(8,128)(2,1)S(1)}, u32[]{:S(2)}, u32[]{:S(2)}) async-start(bf16[16,2,8,256]{3,2,1,0:T(8,128)(2,1)} %shard_map.88), calls=%async_computation.2 | async-start | bytes 262144 | tf_op jit(solution)/shard_map/all_to_all | solution.py:394
  112.2 2.7 %shard_map.91 = bf16[64,32,256]{2,1,0:T(8,128)(2,1)} custom-call(s32[1]{0:T(128)} %bitcast.core_ref, bf16[4,16,16,256]{3,2,1,0:T(8,128)(2,1)S(1)} %get-tuple-element.11.act, bf16[8,2,2,2,16,512]{5,4,3,2,1,0:T(8,128)(2,1)S(1)} %bitcast.26, bf16[8,2,2,2,16,512]{5,4,3,2,1,0:T(8,128)(2,1)S(1)} %copy-done.3), custom_call_target="tpu_custom_call" | custom-call | flops 536870912 | bytes 3670020 | tf_op jit(solution)/shard_map/pallas_call | solution.py:289
  114.9 4.0 %all-to-all-done.2 = bf16[16,2,8,256]{3,2,1,0:T(8,128)(2,1)S(1)} async-done(((bf16[16,2,8,256]{3,2,1,0:T(8,128)(2,1)}), bf16[16,2,8,256]{3,2,1,0:T(8,128)(2,1)S(1)}, u32[]{:S(2)}, u32[]{:S(2)}) %all-to-all-start.2) | async-done | bytes 131104 | tf_op jit(solution)/shard_map/all_to_all | solution.py:394
  118.9 7.4 %all-to-all-start.5 = ((bf16[64,32,256]{2,1,0:T(8,128)(2,1)}), bf16[64,32,256]{2,1,0:T(8,128)(2,1)}, u32[]{:S(2)}, u32[]{:S(2)}) async-start(bf16[64,32,256]{2,1,0:T(8,128)(2,1)} %shard_map.91), calls=%async_computation.5 | async-start | bytes 2097152 | tf_op jit(solution)/shard_map/all_to_all | solution.py:388
  126.3 3.7 %shard_map.90 = bf16[64,56,256]{2,1,0:T(8,128)(2,1)} custom-call(s32[1]{0:T(128)} %bitcast.core_ref, bf16[4,16,16,256]{3,2,1,0:T(8,128)(2,1)S(1)} %copy-done.6, bf16[4,16,16,256]{3,2,1,0:T(8,128)(2,1)S(1)} %get-tuple-element.9.block.grad_sum, bf16[2,16,16,256]{3,2,1,0:T(8,128)(2,1)S(1)} %copy-done.10), custom_call_target="tpu_custom_call" | custom-call | flops 1879048192 | bytes 3145732 | tf_op jit(solution)/shard_map/pallas_call | solution.py:289
  130.1 11.1 %all-to-all-done.5 = bf16[64,32,256]{2,1,0:T(8,128)(2,1)} async-done(((bf16[64,32,256]{2,1,0:T(8,128)(2,1)}), bf16[64,32,256]{2,1,0:T(8,128)(2,1)}, u32[]{:S(2)}, u32[]{:S(2)}) %all-to-all-start.5) | async-done | bytes 1048608 | tf_op jit(solution)/shard_map/all_to_all | solution.py:388
  141.2 5.5 %all-to-all-start.4 = ((bf16[64,56,256]{2,1,0:T(8,128)(2,1)}), bf16[64,56,256]{2,1,0:T(8,128)(2,1)}, u32[]{:S(2)}, u32[]{:S(2)}) async-start(bf16[64,56,256]{2,1,0:T(8,128)(2,1)} %shard_map.90), calls=%async_computation.4 | async-start | bytes 3670016 | tf_op jit(solution)/shard_map/all_to_all | solution.py:388
  146.7 3.7 %shard_map.89 = bf16[64,56,256]{2,1,0:T(8,128)(2,1)} custom-call(s32[1]{0:T(128)} %bitcast.core_ref, bf16[2,16,2,16,256]{4,3,2,1,0:T(8,128)(2,1)S(1)} %bitcast.29, bf16[4,16,16,256]{3,2,1,0:T(8,128)(2,1)S(1)} %shard_map.87.block, bf16[2,16,16,256]{3,2,1,0:T(8,128)(2,1)S(1)} %collective-permute-done.5.later), custom_call_target="tpu_custom_call" | custom-call | flops 1879048192 | bytes 3145732 | tf_op jit(solution)/shard_map/pallas_call | solution.py:289
  150.4 19.1 %all-to-all-done.4 = bf16[64,56,256]{2,1,0:T(8,128)(2,1)} async-done(((bf16[64,56,256]{2,1,0:T(8,128)(2,1)}), bf16[64,56,256]{2,1,0:T(8,128)(2,1)}, u32[]{:S(2)}, u32[]{:S(2)}) %all-to-all-start.4) | async-done | bytes 1835040 | tf_op jit(solution)/shard_map/all_to_all | solution.py:388
  169.5 4.7 %all-to-all-start.3 = ((bf16[64,56,256]{2,1,0:T(8,128)(2,1)}), bf16[64,56,256]{2,1,0:T(8,128)(2,1)S(1)}, u32[]{:S(2)}, u32[]{:S(2)}) async-start(bf16[64,56,256]{2,1,0:T(8,128)(2,1)} %shard_map.89), calls=%async_computation.3 | async-start | bytes 3670016 | tf_op jit(solution)/shard_map/all_to_all | solution.py:388
  179.4 20.7 %all-to-all-done.3 = bf16[64,56,256]{2,1,0:T(8,128)(2,1)S(1)} async-done(((bf16[64,56,256]{2,1,0:T(8,128)(2,1)}), bf16[64,56,256]{2,1,0:T(8,128)(2,1)S(1)}, u32[]{:S(2)}, u32[]{:S(2)}) %all-to-all-start.3) | async-done | bytes 1835040 | tf_op jit(solution)/shard_map/all_to_all | solution.py:388
  (64 shorter events, 26.5 us)
Async XLA Ops:
  1.9 4.0 %collective-permute-start.2 = (bf16[2,4,4,512]{3,2,1,0:T(4,128)(2,1)S(1)}, bf16[2,4,4,512]{3,2,1,0:T(4,128)(2,1)S(1)}, u32[]{:S(2)}, u32[]{:S(2)}) collective-permute-start(bf16[2,4,4,512]{3,2,1,0:T(4,128)(2,1)S(1)} %slice_select_fusion), channel_id=1, source_target_pairs={{0,1},{1,0},{2,3},{3,2},{4,5},{5,4},{6,7},{7,6},{8,9},{9,8},{10,11... | collective-permute-start | bytes 98312 | tf_op jit(solution)/shard_map/ppermute | solution.py:331
  6.3 9.0 %copy-start.13 = (bf16[2,1,128,256]{3,2,1,0:T(8,128)(2,1)S(1)}, bf16[2,1,128,256]{3,2,1,0:T(8,128)(2,1)}, u32[]{:S(2)}) copy-start(bf16[2,1,128,256]{3,2,1,0:T(8,128)(2,1)} %param.5) | copy-start | bytes 393220
  7.4 23.9 %all-to-all-start.1 = ((bf16[8,2,4,16,512]{4,3,2,1,0:T(8,128)(2,1)}), bf16[8,2,4,16,512]{4,3,2,1,0:T(8,128)(2,1)S(1)}, u32[]{:S(2)}, u32[]{:S(2)}) async-start(bf16[8,2,4,16,512]{4,3,2,1,0:T(8,128)(2,1)} %copy.15), calls=%async_computation.1 | async-start | bytes 2097152 | tf_op jit(solution)/shard_map/all_to_all | solution.py:336
  32.2 15.9 %all-to-all-start = ((bf16[32,2,16,256]{3,2,1,0:T(8,128)(2,1)}), bf16[32,2,16,256]{3,2,1,0:T(8,128)(2,1)S(1)}, u32[]{:S(2)}, u32[]{:S(2)}) async-start(bf16[32,2,16,256]{3,2,1,0:T(8,128)(2,1)} %bitcast.6), calls=%async_computation | async-start | bytes 1048576 | tf_op jit(solution)/shard_map/all_to_all | solution.py:325
  36.1 33.9 %collective-permute-start.3 = (bf16[8,2,2,2,16,512]{5,4,3,2,1,0:T(8,128)(2,1)S(1)}, bf16[8,2,2,2,16,512]{5,4,3,2,1,0:T(8,128)(2,1)S(1)}, u32[]{:S(2)}, u32[]{:S(2)}) collective-permute-start(bf16[8,2,2,2,16,512]{5,4,3,2,1,0:T(8,128)(2,1)S(1)} %bitcast.24), channel_id=1, source_target_pairs={{0,16},{16,0},{1,17},{17,1},{2,18},{18,2},{3,19},{19,3},{4,20},{20... | collective-permute-start | bytes 3145736 | tf_op jit(solution)/shard_map/ppermute | solution.py:337
  48.1 8.6 %collective-permute-start = (bf16[16,2,16,256]{3,2,1,0:T(8,128)(2,1)S(1)}, bf16[16,2,16,256]{3,2,1,0:T(8,128)(2,1)S(1)}, u32[]{:S(2)}, u32[]{:S(2)}) collective-permute-start(bf16[16,2,16,256]{3,2,1,0:T(8,128)(2,1)S(1)} %slice.51), channel_id=1, source_target_pairs={{0,32},{32,64},{64,96},{1,33},{33,65},{65,97},{2,34},{34,66},{66,9... | collective-permute-start | bytes 786440 | tf_op jit(solution)/shard_map/ppermute | solution.py:303
  56.8 2.0 copy-start
  65.6 9.8 %collective-permute-start.1 = (bf16[2,16,16,256]{3,2,1,0:T(8,128)(2,1)S(1)}, bf16[2,16,16,256]{3,2,1,0:T(8,128)(2,1)S(1)}, u32[]{:S(2)}, u32[]{:S(2)}) collective-permute-start(bf16[2,16,16,256]{3,2,1,0:T(8,128)(2,1)S(1)} %slice.40), channel_id=1, source_target_pairs={{0,32},{32,64},{64,96},{1,33},{33,65},{65,97},{2,34},{34,66},{66,9... | collective-permute-start | bytes 786440 | tf_op jit(solution)/shard_map/ppermute | solution.py:303
  70.0 5.4 %copy-start.2 = (bf16[8,2,2,2,16,512]{5,4,3,2,1,0:T(8,128)(2,1)}, bf16[8,2,2,2,16,512]{5,4,3,2,1,0:T(8,128)(2,1)S(1)}, u32[]{:S(2)}) copy-start(bf16[8,2,2,2,16,512]{5,4,3,2,1,0:T(8,128)(2,1)S(1)} %collective-permute-done.3.other) | copy-start | bytes 3145732
  70.0 2.0 copy-start.8
  72.0 3.4 %copy-start.5 = (bf16[4,16,16,256]{3,2,1,0:T(8,128)(2,1)S(1)}, bf16[4,16,16,256]{3,2,1,0:T(8,128)(2,1)}, u32[]{:S(2)}) copy-start(bf16[4,16,16,256]{3,2,1,0:T(8,128)(2,1)} %copy-done.4) | copy-start | bytes 1572868
  75.4 15.0 %copy-start.7 = (bf16[3,3,3,256,256]{4,3,2,1,0:T(8,128)(2,1)S(1)}, bf16[3,3,3,256,256]{4,3,2,1,0:T(8,128)(2,1)}, u32[]{:S(2)}) copy-start(bf16[3,3,3,256,256]{4,3,2,1,0:T(8,128)(2,1)} %weights.8) | copy-start | bytes 10616836
  75.4 15.0 %copy-start.12 = (f32[4,16,16,256]{3,2,1,0:T(8,128)S(1)}, f32[4,16,16,256]{3,2,1,0:T(8,128)}, u32[]{:S(2)}) copy-start(f32[4,16,16,256]{3,2,1,0:T(8,128)} %copy-done.11) | copy-start | bytes 3145732
  82.0 8.3 %collective-permute-start.4 = (bf16[2,16,16,256]{3,2,1,0:T(8,128)(2,1)S(1)}, bf16[2,16,16,256]{3,2,1,0:T(8,128)(2,1)S(1)}, u32[]{:S(2)}, u32[]{:S(2)}) collective-permute-start(bf16[2,16,16,256]{3,2,1,0:T(8,128)(2,1)S(1)} %slice.45), channel_id=1, source_target_pairs={{32,0},{64,32},{96,64},{33,1},{65,33},{97,65},{34,2},{66,34},{98,6... | collective-permute-start | bytes 786440 | tf_op jit(solution)/shard_map/ppermute | solution.py:303
  90.4 4.8 %copy-start.9 = (bf16[2,16,16,256]{3,2,1,0:T(8,128)(2,1)}, bf16[2,16,16,256]{3,2,1,0:T(8,128)(2,1)S(1)}, u32[]{:S(2)}) copy-start(bf16[2,16,16,256]{3,2,1,0:T(8,128)(2,1)S(1)} %collective-permute-done.4.later) | copy-start | bytes 786436
  90.4 13.1 %copy-start.1 = (bf16[3,3,3,256,256]{4,3,2,1,0:T(8,128)(2,1)S(1)}, bf16[3,3,3,256,256]{4,3,2,1,0:T(8,128)(2,1)}, u32[]{:S(2)}) copy-start(bf16[3,3,3,256,256]{4,3,2,1,0:T(8,128)(2,1)} %weights.9) | copy-start | bytes 10616836
  95.2 8.3 %collective-permute-start.5 = (bf16[2,16,16,256]{3,2,1,0:T(8,128)(2,1)S(1)}, bf16[2,16,16,256]{3,2,1,0:T(8,128)(2,1)S(1)}, u32[]{:S(2)}, u32[]{:S(2)}) collective-permute-start(bf16[2,16,16,256]{3,2,1,0:T(8,128)(2,1)S(1)} %slice.56), channel_id=1, source_target_pairs={{32,0},{64,32},{96,64},{33,1},{65,33},{97,65},{34,2},{66,34},{98,6... | collective-permute-start | bytes 786440 | tf_op jit(solution)/shard_map/ppermute | solution.py:303
  106.1 12.9 %all-to-all-start.2 = ((bf16[16,2,8,256]{3,2,1,0:T(8,128)(2,1)}), bf16[16,2,8,256]{3,2,1,0:T(8,128)(2,1)S(1)}, u32[]{:S(2)}, u32[]{:S(2)}) async-start(bf16[16,2,8,256]{3,2,1,0:T(8,128)(2,1)} %shard_map.88), calls=%async_computation.2 | async-start | bytes 262144 | tf_op jit(solution)/shard_map/all_to_all | solution.py:394
  111.0 1.2 copy-start.3
  114.9 11.4 %copy-start.6 = (bf16[4,16,16,256]{3,2,1,0:T(8,128)(2,1)S(1)}, bf16[4,16,16,256]{3,2,1,0:T(8,128)(2,1)}, u32[]{:S(2)}) copy-start(bf16[4,16,16,256]{3,2,1,0:T(8,128)(2,1)} %copy-done.4) | copy-start | bytes 1572868
  114.9 11.4 %copy-start.10 = (bf16[2,16,16,256]{3,2,1,0:T(8,128)(2,1)S(1)}, bf16[2,16,16,256]{3,2,1,0:T(8,128)(2,1)}, u32[]{:S(2)}) copy-start(bf16[2,16,16,256]{3,2,1,0:T(8,128)(2,1)} %copy-done.9) | copy-start | bytes 786436
  118.9 22.2 %all-to-all-start.5 = ((bf16[64,32,256]{2,1,0:T(8,128)(2,1)}), bf16[64,32,256]{2,1,0:T(8,128)(2,1)}, u32[]{:S(2)}, u32[]{:S(2)}) async-start(bf16[64,32,256]{2,1,0:T(8,128)(2,1)} %shard_map.91), calls=%async_computation.5 | async-start | bytes 2097152 | tf_op jit(solution)/shard_map/all_to_all | solution.py:388
  141.2 28.4 %all-to-all-start.4 = ((bf16[64,56,256]{2,1,0:T(8,128)(2,1)}), bf16[64,56,256]{2,1,0:T(8,128)(2,1)}, u32[]{:S(2)}, u32[]{:S(2)}) async-start(bf16[64,56,256]{2,1,0:T(8,128)(2,1)} %shard_map.90), calls=%async_computation.4 | async-start | bytes 3670016 | tf_op jit(solution)/shard_map/all_to_all | solution.py:388
  169.5 30.6 %all-to-all-start.3 = ((bf16[64,56,256]{2,1,0:T(8,128)(2,1)}), bf16[64,56,256]{2,1,0:T(8,128)(2,1)S(1)}, u32[]{:S(2)}, u32[]{:S(2)}) async-start(bf16[64,56,256]{2,1,0:T(8,128)(2,1)} %shard_map.89), calls=%async_computation.3 | async-start | bytes 3670016 | tf_op jit(solution)/shard_map/all_to_all | solution.py:388
  (2 other events, 1.8 us)

commit v2 on v1

--- a/solution.py
+++ b/solution.py
@@ -88,7 +88,7 @@
             slope[frame] = slope_of(values, sigma)
 
 
-def second_kernel(halo, block, features, grad_act, weights, mask, grad_sum, up_act, table, total):
+def second_kernel(halo, block, features, weights, summed, up_act, table, total):
     step = pl.program_id(0)
 
     @pl.when(step == 0)
@@ -106,15 +106,12 @@
 
     @pl.when(step == 2)
     def _():
-        inside = mask[...]
         for frame in range(FR):
             rows = ROWS * WIN
             values = total[frame * rows : (frame + 1) * rows].reshape(ROWS, WIN, CH)
             values = values + features[frame // 2, :, frame % 2].astype(F32)
-            sigma = jax.nn.sigmoid(values)
-            up_act[frame] = (values * sigma).astype(BF16)
-            grad = grad_act[frame].astype(F32) * slope_of(values, sigma) * inside
-            grad_sum[frame] = grad.astype(BF16)
+            summed[frame] = values
+            up_act[frame] = (values * jax.nn.sigmoid(values)).astype(BF16)
 
 
 def hidden_kernel(block, later, slope, weights, mask, grad_hidden, table, total):
@@ -178,7 +175,7 @@
             grad_features[:, frame] = values.astype(BF16)
 
 
-def cotangent_kernel(core_ref, mine, other, weights, grad_act, table):
+def cotangent_kernel(core_ref, mine, other, weights, summed, mask, grad_sum, table):
     core = core_ref[0]
     border = jnp.zeros((FR, WIN, 4 * CH), BF16)
     table[:, 0, 0] = border
@@ -204,7 +201,10 @@
                 lhs = table[frame, tap // 2 : tap // 2 + ROWS, tap % 2, :, column * CH : (column + 1) * CH]
                 more = nt(lhs.reshape(ROWS * WIN, CH), weights[tap, column])
                 part = more if part is None else part + more
-        grad_act[frame] = part.reshape(ROWS, WIN, CH).astype(BF16)
+        grad_act = part.reshape(ROWS, WIN, CH).astype(BF16).astype(F32)
+        values = summed[frame]
+        grad = grad_act * slope_of(values, jax.nn.sigmoid(values)) * mask[...]
+        grad_sum[frame] = grad.astype(BF16)
 
 
 def up_grad_kernel(core_ref, act, mine, other, out, table, flipped):
@@ -323,8 +323,6 @@
     windows = windows.reshape(2, 2, 8, WIN, CH).transpose(2, 1, 0, 3, 4).reshape(1, 16, 2, WIN, CH)
     windows = jnp.broadcast_to(windows, (2, 16, 2, WIN, CH)).reshape(32, 2, WIN, CH)
     block = lax.all_to_all(windows, ("core", "height", "width"), 0, 0, tiled=True)
-    block = block.reshape(2, ROWS, 2, WIN, CH)
-    halo = shift(block[1], "y", 1)
 
     paired = cotangent.reshape(2, 4, 64, 2 * CH)
     edge = jnp.where(width == 0, paired[:, :, 64 - EDGE :], paired[:, :, :EDGE])
@@ -333,25 +331,30 @@
     low, high = jnp.where(width == 0, nothing, edge), jnp.where(width == 0, edge, nothing)
     paired = jnp.concatenate([low, paired, high], axis=2).reshape(2, 4, 9, OWN, 2 * CH)
     fine = jnp.concatenate([paired[:, :, :-1], paired[:, :, 1:]], axis=3).transpose(2, 0, 1, 3, 4)
+    fine, block = lax.optimization_barrier((fine, block))
+    block = block.reshape(2, ROWS, 2, WIN, CH)
+    halo = shift(block[1], "y", 1)
     mine = lax.all_to_all(fine, "height", 0, 0, tiled=True).reshape(8, 2, 2, 2, WIN, 2 * CH)
-    other = lax.ppermute(mine, "core", [(0, 1), (1, 0)])
 
     first_act, first_slope = call(
         first_kernel, (3,), (halo, block, conv_first, mask),
         [whole(halo.shape), whole(block.shape), tap_weights(), whole(mask.shape)],
         [(act_shape, BF16), (act_shape, F32)], [table, total], 27 * tap_flops,
     )
+    mine, first_act = lax.optimization_barrier((mine, first_act))
     earlier = shift(first_act[2:], "y", 1)
-    grad_act = call(
-        cotangent_kernel, (), (core_arg, mine, other, up_kernel),
-        [SMEM, whole(mine.shape), whole(mine.shape), whole(up_kernel.shape)],
+    other = lax.ppermute(mine, "core", [(0, 1), (1, 0)])
+    summed, up_act = call(
+        second_kernel, (3,), (earlier, first_act, block, conv_second),
+        [whole(earlier.shape), whole(act_shape), whole(block.shape), tap_weights()],
+        [(act_shape, F32), (act_shape, BF16)], [table, total], 27 * tap_flops,
+    )
+    grad_sum = call(
+        cotangent_kernel, (), (core_arg, mine, other, up_kernel, summed, mask),
+        [SMEM, whole(mine.shape), whole(mine.shape), whole(up_kernel.shape), whole(act_shape), whole(mask.shape)],
         [(act_shape, BF16)], [pltpu.VMEM((FR, ROWS + 1, 2, WIN, 4 * CH), BF16)], 16 * tap_flops,
     )
-    grad_sum, up_act = call(
-        second_kernel, (3,), (earlier, first_act, block, grad_act, conv_second, mask),
-        [whole(earlier.shape), whole(act_shape), whole(block.shape), whole(act_shape), tap_weights(), whole(mask.shape)],
-        [(act_shape, BF16), (act_shape, BF16)], [table, total], 27 * tap_flops,
-    )
+    up_act, grad_sum = lax.optimization_barrier((up_act, grad_sum))
     later = shift(grad_sum[:2], "y", -1)
     up_part = call(
         up_grad_kernel, (), (core_arg, up_act, mine, other),
@@ -359,6 +362,8 @@
         [((64, 32, CH), BF16)],
         [pltpu.VMEM((FR, ROWS + 1, 2, OWN, 4 * CH), BF16), pltpu.VMEM((CH, FR * ROWS * OWN), BF16)], 4 * tap_flops,
     )
+    everyone = ("y", "height", "width")
+    up_received = lax.all_to_all(up_part, everyone, 0, 0, tiled=True)
     grad_hidden = call(
         hidden_kernel, (3,), (grad_sum, later, first_slope, conv_second, mask),
         [whole(act_shape), whole(later.shape), whole(act_shape), tap_weights(), whole(mask.shape)],
@@ -375,26 +380,32 @@
         )
 
     second_part = kernel_grad(first_act, False, grad_sum, later)
-    first_part = kernel_grad(block, True, grad_hidden, later_hidden)
+    second_part, up_received = lax.optimization_barrier((second_part, up_received))
+    second_received = lax.all_to_all(second_part, everyone, 0, 0, tiled=True)
     rows_out = call(
         features_kernel, (3,), (core_arg, grad_hidden, later_hidden, grad_sum, conv_first),
         [SMEM, whole(act_shape), whole(later_hidden.shape), whole(act_shape), tap_weights()],
         [((ROWS, 2, OWN, CH), BF16)], [own_table, pltpu.VMEM((2 * ROWS * OWN, CH), F32)], 7 * tap_flops,
     )
-
-    factor = 1.0 / math.sqrt(32768)
-
-    def share_of(part, rows):
-        received = lax.all_to_all(part, ("y", "height", "width"), 0, 0, tiled=True)
-        return (jnp.sum(received[:, :rows].astype(F32), axis=0) * factor).reshape(-1)
-
-    up_share = share_of(up_part, 32)
-    second_share = share_of(second_part, SHARE)
-    first_share = share_of(first_part, SHARE)
+    first_part = kernel_grad(block, True, grad_hidden, later_hidden)
+    first_part, rows_out, second_received = lax.optimization_barrier((first_part, rows_out, second_received))
+    first_received = lax.all_to_all(first_part, everyone, 0, 0, tiled=True)
+    rows_out, first_received = lax.optimization_barrier((rows_out, first_received))
     returned = lax.all_to_all(rows_out, ("height", "width"), 0, 0, tiled=True)
     returned = returned.reshape(8, 2, 2, OWN, CH).transpose(2, 1, 0, 3, 4)
     grad_features = returned.reshape(2, 1, 128, CH)
-    return (grad_features, first_share, second_share, up_share)
+
+    factor = 1.0 / math.sqrt(32768)
+
+    def share_of(received, rows):
+        return (jnp.sum(received[:, :rows].astype(F32), axis=0) * factor).reshape(-1)
+
+    return (
+        grad_features,
+        share_of(first_received, SHARE),
+        share_of(second_received, SHARE),
+        share_of(up_received, 32),
+    )
 
 
 def solution(mesh):

time: 202 us -> 197 us (0.975)
  waiting for transfers between devices: 104 us -> 87.3 us
  starting transfers between devices: 46.7 us -> 59 us
    all_to_all x3, waiting for transfers between devices: 50.9 us -> 22.5 us  [the longest x1 22.5 us: shards(): first_received = lax.all_to_all(first_part, everyone, 0, 0, tiled=True)]
    ppermute x4, waiting for transfers between devices: 19.1 us -> 46 us  [shift(): lax.ppermute(value, axis, [(i, i + step) for i in range(count) if 0 <= i...]
    all_to_all x1, waiting for transfers between devices: 15.9 us -> 0.34 us  [shards(): lax.all_to_all(fine, 'height', 0, 0, tiled=True)]
    all_to_all x3, starting transfers between devices: 17.6 us -> 32.1 us  [the longest x1 11.7 us: shards(): up_received = lax.all_to_all(up_part, everyone, 0, 0, tiled=True)]
    all_to_all x1, starting transfers between devices: 7.86 us -> 3.56 us  [shards(): lax.all_to_all(fine, 'height', 0, 0, tiled=True)]
    all_to_all x1, starting transfers between devices: 3.89 us -> 7.87 us  [shards(): lax.all_to_all(windows, ('core', 'height', 'width'), 0, 0, tiled=True)]
    all_to_all x1, waiting for transfers between devices: 4.01 us -> 7.02 us  [shards(): returned = lax.all_to_all(rows_out, ('height', 'width'), 0, 0, tiled=True)]
    ppermute x1, waiting for transfers between devices: 2.34 us -> 0.01 us  [shards(): edge = lax.ppermute(edge, 'width', [(0, 1), (1, 0)])]
  transfers between devices with their start and end apart: 12 -> 12, of which waited for: 10 -> 8; matrix products, arithmetic and copies ran while one was open for 3% -> 4% of each run, Pallas kernels for 9% -> 13%
where the time goes in v2:
time: 197 us; the launch traced here: 196 us
  waiting for transfers between devices  87.3 us (44%)
  starting transfers between devices  59 us (30%)
  Pallas kernels  32.1 us (16%)
  local copies, waits for them, and re-layouts  12.6 us (6%)
  other arithmetic  3.89 us (2%)
    ppermute x4, waiting for transfers between devices, shift(): lax.ppermute(value, axis, [(i, i + step) for i in range(count) if 0 <= i...  46 us
    pallas_call x8, Pallas kernels, call(): pl.pallas_call(kernel, out_shape=shapes[0] if single else shapes, grid=gr...  32.1 us
    all_to_all x1, waiting for transfers between devices, shards(): first_received = lax.all_to_all(first_part, everyone, 0, 0, tiled=True)  22.5 us
    all_to_all x1, starting transfers between devices, shards(): up_received = lax.all_to_all(up_part, everyone, 0, 0, tiled=True)  11.7 us
    all_to_all x1, waiting for transfers between devices, shards(): lax.all_to_all(windows, ('core', 'height', 'width'), 0, 0, tiled=True)  11.5 us
    ppermute x4, starting transfers between devices, shift(): lax.ppermute(value, axis, [(i, i + step) for i in range(count) if 0 <= i...  10.4 us
    all_to_all x1, starting transfers between devices, shards(): second_received = lax.all_to_all(second_part, everyone, 0, 0, tiled=True)  10.4 us
    all_to_all x1, starting transfers between devices, shards(): first_received = lax.all_to_all(first_part, everyone, 0, 0, tiled=True)  10 us
  transfers between devices with their start and end apart: 12, of which 8 were waited for; matrix products, arithmetic and copies ran while one was open for 4% of the time, Pallas kernels for 13%

profile of v2, /device:TPU:0, one launch (start us, length us, event | category | flops | bytes accessed | tf_op | source)
XLA Modules:
  0.0 196.0 jit_solution(7077080313695434371)
XLA Ops:
  5.5 7.9 %all-to-all-start = ((bf16[32,2,16,256]{3,2,1,0:T(8,128)(2,1)}), bf16[32,2,16,256]{3,2,1,0:T(8,128)(2,1)S(1)}, u32[]{:S(2)}, u32[]{:S(2)}) async-start(bf16[32,2,16,256]{3,2,1,0:T(8,128)(2,1)} %bitcast.8), calls=%async_computation | async-start | bytes 1048576 | tf_op jit(solution)/shard_map/all_to_all | solution.py:325
  13.8 11.5 %all-to-all-done = bf16[32,2,16,256]{3,2,1,0:T(8,128)(2,1)S(1)} async-done(((bf16[32,2,16,256]{3,2,1,0:T(8,128)(2,1)}), bf16[32,2,16,256]{3,2,1,0:T(8,128)(2,1)S(1)}, u32[]{:S(2)}, u32[]{:S(2)}) %all-to-all-start) | async-done | bytes 524320 | tf_op jit(solution)/shard_map/all_to_all | solution.py:325
  26.4 3.6 %all-to-all-start.1 = ((bf16[8,2,4,16,512]{4,3,2,1,0:T(8,128)(2,1)}), bf16[8,2,4,16,512]{4,3,2,1,0:T(8,128)(2,1)S(1)}, u32[]{:S(2)}, u32[]{:S(2)}) async-start(bf16[8,2,4,16,512]{4,3,2,1,0:T(8,128)(2,1)} %copy.15), calls=%async_computation.1 | async-start | bytes 2097152 | tf_op jit(solution)/shard_map/all_to_all | solution.py:337
  30.0 3.5 %collective-permute-start.1 = (bf16[16,2,16,256]{3,2,1,0:T(8,128)(2,1)S(1)}, bf16[16,2,16,256]{3,2,1,0:T(8,128)(2,1)S(1)}, u32[]{:S(2)}, u32[]{:S(2)}) collective-permute-start(bf16[16,2,16,256]{3,2,1,0:T(8,128)(2,1)S(1)} %slice.43), channel_id=1, source_target_pairs={{0,32},{32,64},{64,96},{1,33},{33,65},{65,97},{2,34},{34,66},{66,9... | collective-permute-start | bytes 786440 | tf_op jit(solution)/shard_map/ppermute | solution.py:303
  33.5 5.1 %collective-permute-done.1.halo = bf16[16,2,16,256]{3,2,1,0:T(8,128)(2,1)S(1)} collective-permute-done((bf16[16,2,16,256]{3,2,1,0:T(8,128)(2,1)S(1)}, bf16[16,2,16,256]{3,2,1,0:T(8,128)(2,1)S(1)}, u32[]{:S(2)}, u32[]{:S(2)}) %collective-permute-start.1) | collective-permute-done | bytes 262176 | tf_op jit(solution)/shard_map/ppermute | solution.py:303
  38.7 2.0 %copy-done = bf16[3,3,3,256,256]{4,3,2,1,0:T(8,128)(2,1)S(1)} copy-done((bf16[3,3,3,256,256]{4,3,2,1,0:T(8,128)(2,1)S(1)}, bf16[3,3,3,256,256]{4,3,2,1,0:T(8,128)(2,1)}, u32[]{:S(2)}) %copy-start) | copy-done | bytes 3538968
  40.7 5.0 %shard_map.84 = (bf16[4,16,16,256]{3,2,1,0:T(8,128)(2,1)S(1)}, f32[4,16,16,256]{3,2,1,0:T(8,128)S(1)}) custom-call(bf16[16,2,16,256]{3,2,1,0:T(8,128)(2,1)S(1)} %collective-permute-done.1.halo, bf16[2,16,2,16,256]{4,3,2,1,0:T(8,128)(2,1)S(1)} %bitcast.27, bf16[3,3,3,256,256]{4,3,2,1,0:T(8,128)(2,1)S(1)} %copy-done, f32[16,256]{1,0:T(8,128)S(1)} %broadcast_in_dim.19.mask), custom_call_target="tpu_custom_call" | custom-call | flops 3623878656 | bytes 5914624 | tf_op jit(solution)/shard_map/pallas_call | solution.py:289
  47.7 4.1 %collective-permute-start.2 = (bf16[2,16,16,256]{3,2,1,0:T(8,128)(2,1)}, bf16[2,16,16,256]{3,2,1,0:T(8,128)(2,1)S(1)}, u32[]{:S(2)}, u32[]{:S(2)}) collective-permute-start(bf16[2,16,16,256]{3,2,1,0:T(8,128)(2,1)} %slice.44), channel_id=1, source_target_pairs={{0,32},{32,64},{64,96},{1,33},{33,65},{65,97},{2,34},{34,66},{66,9... | collective-permute-start | bytes 786440 | tf_op jit(solution)/shard_map/ppermute | solution.py:303
  51.8 6.4 %collective-permute-done.2.halo = bf16[2,16,16,256]{3,2,1,0:T(8,128)(2,1)S(1)} collective-permute-done((bf16[2,16,16,256]{3,2,1,0:T(8,128)(2,1)}, bf16[2,16,16,256]{3,2,1,0:T(8,128)(2,1)S(1)}, u32[]{:S(2)}, u32[]{:S(2)}) %collective-permute-start.2) | collective-permute-done | bytes 262176 | tf_op jit(solution)/shard_map/ppermute | solution.py:303
  58.3 6.1 %shard_map.85 = (f32[4,16,16,256]{3,2,1,0:T(8,128)S(1)}, bf16[4,16,16,256]{3,2,1,0:T(8,128)(2,1)S(1)}) custom-call(bf16[2,16,16,256]{3,2,1,0:T(8,128)(2,1)S(1)} %collective-permute-done.2.halo, bf16[4,16,16,256]{3,2,1,0:T(8,128)(2,1)S(1)} %get-tuple-element.24.block.act, bf16[2,16,2,16,256]{4,3,2,1,0:T(8,128)(2,1)S(1)} %bitcast.28, ...), custom_call_target="tpu_custom_call" | custom-call | flops 3623878656 | bytes 6422528 | tf_op jit(solution)/shard_map/pallas_call | solution.py:289
  64.4 3.5 %shard_map.86.block.grad_sum = bf16[4,16,16,256]{3,2,1,0:T(8,128)(2,1)S(1)} custom-call(s32[1]{0:T(128)} %bitcast.core_ref, bf16[8,2,2,2,16,512]{5,4,3,2,1,0:T(8,128)(2,1)S(1)} %bitcast.25, bf16[8,2,2,2,16,512]{5,4,3,2,1,0:T(8,128)(2,1)S(1)} %collective-permute-done.3.other, bf16[4,4,256,256]{3,2,1,0:T(8,128)(2,1)S(1)} %copy-done.5, ...), custom_call_target="tpu_custom_call" | custom-call | flops 2147483648 | bytes 5783556 | tf_op jit(solution)/shard_map/pallas_call | solution.py:289
  67.9 2.7 %shard_map.91 = bf16[64,32,256]{2,1,0:T(8,128)(2,1)} custom-call(s32[1]{0:T(128)} %bitcast.core_ref, bf16[4,16,16,256]{3,2,1,0:T(8,128)(2,1)S(1)} %get-tuple-element.30.act, bf16[8,2,2,2,16,512]{5,4,3,2,1,0:T(8,128)(2,1)S(1)} %bitcast.26, bf16[8,2,2,2,16,512]{5,4,3,2,1,0:T(8,128)(2,1)S(1)} %collective-permute-done.3.other), custom_call_target="tpu_custom_call" | custom-call | flops 536870912 | bytes 3670020 | tf_op jit(solution)/shard_map/pallas_call | solution.py:289
  70.6 11.7 %all-to-all-start.2 = ((bf16[64,32,256]{2,1,0:T(8,128)(2,1)}), bf16[64,32,256]{2,1,0:T(8,128)(2,1)}, u32[]{:S(2)}, u32[]{:S(2)}) async-start(bf16[64,32,256]{2,1,0:T(8,128)(2,1)} %shard_map.91), calls=%async_computation.2 | async-start | bytes 2097152 | tf_op jit(solution)/shard_map/all_to_all | solution.py:366
  83.8 16.5 %collective-permute-done.4.later = bf16[2,16,16,256]{3,2,1,0:T(8,128)(2,1)S(1)} collective-permute-done((bf16[2,16,16,256]{3,2,1,0:T(8,128)(2,1)S(1)}, bf16[2,16,16,256]{3,2,1,0:T(8,128)(2,1)S(1)}, u32[]{:S(2)}, u32[]{:S(2)}) %collective-permute-start.4) | collective-permute-done | bytes 262176 | tf_op jit(solution)/shard_map/ppermute | solution.py:303
  100.3 3.7 %shard_map.90 = bf16[64,56,256]{2,1,0:T(8,128)(2,1)} custom-call(s32[1]{0:T(128)} %bitcast.core_ref, bf16[4,16,16,256]{3,2,1,0:T(8,128)(2,1)S(1)} %copy-done.3, bf16[4,16,16,256]{3,2,1,0:T(8,128)(2,1)S(1)} %shard_map.86.block.grad_sum, bf16[2,16,16,256]{3,2,1,0:T(8,128)(2,1)S(1)} %collective-permute-done.4.later), custom_call_target="tpu_custom_call" | custom-call | flops 1879048192 | bytes 3145732 | tf_op jit(solution)/shard_map/pallas_call | solution.py:289
  104.0 10.4 %all-to-all-start.3 = ((bf16[64,56,256]{2,1,0:T(8,128)(2,1)}), bf16[64,56,256]{2,1,0:T(8,128)(2,1)}, u32[]{:S(2)}, u32[]{:S(2)}) async-start(bf16[64,56,256]{2,1,0:T(8,128)(2,1)} %shard_map.90), calls=%async_computation.3 | async-start | bytes 3670016 | tf_op jit(solution)/shard_map/all_to_all | solution.py:384
  116.4 4.8 %shard_map.87.block = bf16[4,16,16,256]{3,2,1,0:T(8,128)(2,1)S(1)} custom-call(bf16[4,16,16,256]{3,2,1,0:T(8,128)(2,1)S(1)} %shard_map.86.block.grad_sum, bf16[2,16,16,256]{3,2,1,0:T(8,128)(2,1)S(1)} %collective-permute-done.4.later, f32[4,16,16,256]{3,2,1,0:T(8,128)S(1)} %copy-done.7, bf16[3,3,3,256,256]{4,3,2,1,0:T(8,128)(2,1)S(1)} %copy-done.4, ...), custom_call_target="tpu_custom_call" | custom-call | flops 3623878656 | bytes 5914624 | tf_op jit(solution)/shard_map/pallas_call | solution.py:289
  122.5 18.0 %collective-permute-done.5.later = bf16[2,16,16,256]{3,2,1,0:T(8,128)(2,1)S(1)} collective-permute-done((bf16[2,16,16,256]{3,2,1,0:T(8,128)(2,1)S(1)}, bf16[2,16,16,256]{3,2,1,0:T(8,128)(2,1)S(1)}, u32[]{:S(2)}, u32[]{:S(2)}) %collective-permute-start.5) | collective-permute-done | bytes 262176 | tf_op jit(solution)/shard_map/ppermute | solution.py:303
  140.5 2.6 %shard_map.89 = bf16[16,2,8,256]{3,2,1,0:T(8,128)(2,1)} custom-call(s32[1]{0:T(128)} %bitcast.core_ref, bf16[4,16,16,256]{3,2,1,0:T(8,128)(2,1)S(1)} %shard_map.87.block, bf16[2,16,16,256]{3,2,1,0:T(8,128)(2,1)S(1)} %collective-permute-done.5.later, bf16[4,16,16,256]{3,2,1,0:T(8,128)(2,1)S(1)} %shard_map.86.block.grad_sum, ...), custom_call_target="tpu_custom_call" | custom-call | flops 939524096 | bytes 4980740 | tf_op jit(solution)/shard_map/pallas_call | solution.py:289
  143.1 3.8 %shard_map.88 = bf16[64,56,256]{2,1,0:T(8,128)(2,1)} custom-call(s32[1]{0:T(128)} %bitcast.core_ref, bf16[2,16,2,16,256]{4,3,2,1,0:T(8,128)(2,1)S(1)} %bitcast.29, bf16[4,16,16,256]{3,2,1,0:T(8,128)(2,1)S(1)} %shard_map.87.block, bf16[2,16,16,256]{3,2,1,0:T(8,128)(2,1)S(1)} %collective-permute-done.5.later), custom_call_target="tpu_custom_call" | custom-call | flops 1879048192 | bytes 3145732 | tf_op jit(solution)/shard_map/pallas_call | solution.py:289
  146.9 10.0 %all-to-all-start.4 = ((bf16[64,56,256]{2,1,0:T(8,128)(2,1)}), bf16[64,56,256]{2,1,0:T(8,128)(2,1)S(1)}, u32[]{:S(2)}, u32[]{:S(2)}) async-start(bf16[64,56,256]{2,1,0:T(8,128)(2,1)} %shard_map.88), calls=%async_computation.4 | async-start | bytes 3670016 | tf_op jit(solution)/shard_map/all_to_all | solution.py:392
  161.4 22.5 %all-to-all-done.4 = bf16[64,56,256]{2,1,0:T(8,128)(2,1)S(1)} async-done(((bf16[64,56,256]{2,1,0:T(8,128)(2,1)}), bf16[64,56,256]{2,1,0:T(8,128)(2,1)S(1)}, u32[]{:S(2)}, u32[]{:S(2)}) %all-to-all-start.4) | async-done | bytes 1835040 | tf_op jit(solution)/shard_map/all_to_all | solution.py:392
  183.8 3.5 %all-to-all-start.5 = ((bf16[16,2,8,256]{3,2,1,0:T(8,128)(2,1)}), bf16[16,2,8,256]{3,2,1,0:T(8,128)(2,1)S(1)}, u32[]{:S(2)}, u32[]{:S(2)}) async-start(bf16[16,2,8,256]{3,2,1,0:T(8,128)(2,1)} %shard_map.89), calls=%async_computation.5 | async-start | bytes 262144 | tf_op jit(solution)/shard_map/all_to_all | solution.py:394
  188.3 7.0 %all-to-all-done.5 = bf16[16,2,8,256]{3,2,1,0:T(8,128)(2,1)S(1)} async-done(((bf16[16,2,8,256]{3,2,1,0:T(8,128)(2,1)}), bf16[16,2,8,256]{3,2,1,0:T(8,128)(2,1)S(1)}, u32[]{:S(2)}, u32[]{:S(2)}) %all-to-all-start.5) | async-done | bytes 131104 | tf_op jit(solution)/shard_map/all_to_all | solution.py:394
  (52 shorter events, 19.3 us)
Async XLA Ops:
  1.9 11.4 %collective-permute-start = (bf16[2,4,4,512]{3,2,1,0:T(4,128)(2,1)S(1)}, bf16[2,4,4,512]{3,2,1,0:T(4,128)(2,1)S(1)}, u32[]{:S(2)}, u32[]{:S(2)}) collective-permute-start(bf16[2,4,4,512]{3,2,1,0:T(4,128)(2,1)S(1)} %slice_select_fusion), channel_id=1, source_target_pairs={{0,1},{1,0},{2,3},{3,2},{4,5},{5,4},{6,7},{7,6},{8,9},{9,8},{10,11... | collective-permute-start | bytes 98312 | tf_op jit(solution)/shard_map/ppermute | solution.py:329
  5.5 19.8 %all-to-all-start = ((bf16[32,2,16,256]{3,2,1,0:T(8,128)(2,1)}), bf16[32,2,16,256]{3,2,1,0:T(8,128)(2,1)S(1)}, u32[]{:S(2)}, u32[]{:S(2)}) async-start(bf16[32,2,16,256]{3,2,1,0:T(8,128)(2,1)} %bitcast.8), calls=%async_computation | async-start | bytes 1048576 | tf_op jit(solution)/shard_map/all_to_all | solution.py:325
  26.4 20.6 %all-to-all-start.1 = ((bf16[8,2,4,16,512]{4,3,2,1,0:T(8,128)(2,1)}), bf16[8,2,4,16,512]{4,3,2,1,0:T(8,128)(2,1)S(1)}, u32[]{:S(2)}, u32[]{:S(2)}) async-start(bf16[8,2,4,16,512]{4,3,2,1,0:T(8,128)(2,1)} %copy.15), calls=%async_computation.1 | async-start | bytes 2097152 | tf_op jit(solution)/shard_map/all_to_all | solution.py:337
  30.0 8.6 %collective-permute-start.1 = (bf16[16,2,16,256]{3,2,1,0:T(8,128)(2,1)S(1)}, bf16[16,2,16,256]{3,2,1,0:T(8,128)(2,1)S(1)}, u32[]{:S(2)}, u32[]{:S(2)}) collective-permute-start(bf16[16,2,16,256]{3,2,1,0:T(8,128)(2,1)S(1)} %slice.43), channel_id=1, source_target_pairs={{0,32},{32,64},{64,96},{1,33},{33,65},{65,97},{2,34},{34,66},{66,9... | collective-permute-start | bytes 786440 | tf_op jit(solution)/shard_map/ppermute | solution.py:303
  38.7 2.0 %copy-start = (bf16[3,3,3,256,256]{4,3,2,1,0:T(8,128)(2,1)S(1)}, bf16[3,3,3,256,256]{4,3,2,1,0:T(8,128)(2,1)}, u32[]{:S(2)}) copy-start(bf16[3,3,3,256,256]{4,3,2,1,0:T(8,128)(2,1)} %weights.9) | copy-start | bytes 10616836
  45.6 1.0 copy-start.6
  46.6 17.7 %copy-start.2 = (bf16[4,16,16,256]{3,2,1,0:T(8,128)(2,1)}, bf16[4,16,16,256]{3,2,1,0:T(8,128)(2,1)S(1)}, u32[]{:S(2)}) copy-start(bf16[4,16,16,256]{3,2,1,0:T(8,128)(2,1)S(1)} %get-tuple-element.24.block.act) | copy-start | bytes 1572868
  47.0 17.4 %collective-permute-start.3 = (bf16[8,2,2,2,16,512]{5,4,3,2,1,0:T(8,128)(2,1)S(1)}, bf16[8,2,2,2,16,512]{5,4,3,2,1,0:T(8,128)(2,1)S(1)}, u32[]{:S(2)}, u32[]{:S(2)}) collective-permute-start(bf16[8,2,2,2,16,512]{5,4,3,2,1,0:T(8,128)(2,1)S(1)} %bitcast.24), channel_id=1, source_target_pairs={{0,16},{16,0},{1,17},{17,1},{2,18},{18,2},{3,19},{19,3},{4,20},{20... | collective-permute-start | bytes 3145736 | tf_op jit(solution)/shard_map/ppermute | solution.py:346
  47.7 10.6 %collective-permute-start.2 = (bf16[2,16,16,256]{3,2,1,0:T(8,128)(2,1)}, bf16[2,16,16,256]{3,2,1,0:T(8,128)(2,1)S(1)}, u32[]{:S(2)}, u32[]{:S(2)}) collective-permute-start(bf16[2,16,16,256]{3,2,1,0:T(8,128)(2,1)} %slice.44), channel_id=1, source_target_pairs={{0,32},{32,64},{64,96},{1,33},{33,65},{65,97},{2,34},{34,66},{66,9... | collective-permute-start | bytes 786440 | tf_op jit(solution)/shard_map/ppermute | solution.py:303
  51.8 12.6 %copy-start.5 = (bf16[4,4,256,256]{3,2,1,0:T(8,128)(2,1)S(1)}, bf16[4,4,256,256]{3,2,1,0:T(8,128)(2,1)}, u32[]{:S(2)}) copy-start(bf16[4,4,256,256]{3,2,1,0:T(8,128)(2,1)} %weights.7) | copy-start | bytes 6291460
  70.6 29.7 %copy-start.3 = (bf16[4,16,16,256]{3,2,1,0:T(8,128)(2,1)S(1)}, bf16[4,16,16,256]{3,2,1,0:T(8,128)(2,1)}, u32[]{:S(2)}) copy-start(bf16[4,16,16,256]{3,2,1,0:T(8,128)(2,1)} %copy-done.2) | copy-start | bytes 1572868
  70.6 33.4 %all-to-all-start.2 = ((bf16[64,32,256]{2,1,0:T(8,128)(2,1)}), bf16[64,32,256]{2,1,0:T(8,128)(2,1)}, u32[]{:S(2)}, u32[]{:S(2)}) async-start(bf16[64,32,256]{2,1,0:T(8,128)(2,1)} %shard_map.91), calls=%async_computation.2 | async-start | bytes 2097152 | tf_op jit(solution)/shard_map/all_to_all | solution.py:366
  82.4 17.9 %collective-permute-start.4 = (bf16[2,16,16,256]{3,2,1,0:T(8,128)(2,1)S(1)}, bf16[2,16,16,256]{3,2,1,0:T(8,128)(2,1)S(1)}, u32[]{:S(2)}, u32[]{:S(2)}) collective-permute-start(bf16[2,16,16,256]{3,2,1,0:T(8,128)(2,1)S(1)} %slice.45), channel_id=1, source_target_pairs={{32,0},{64,32},{96,64},{33,1},{65,33},{97,65},{34,2},{66,34},{98,6... | collective-permute-start | bytes 786440 | tf_op jit(solution)/shard_map/ppermute | solution.py:303
  104.0 10.4 %copy-start.7 = (f32[4,16,16,256]{3,2,1,0:T(8,128)S(1)}, f32[4,16,16,256]{3,2,1,0:T(8,128)}, u32[]{:S(2)}) copy-start(f32[4,16,16,256]{3,2,1,0:T(8,128)} %copy-done.6) | copy-start | bytes 3145732
  104.0 42.8 %all-to-all-start.3 = ((bf16[64,56,256]{2,1,0:T(8,128)(2,1)}), bf16[64,56,256]{2,1,0:T(8,128)(2,1)}, u32[]{:S(2)}, u32[]{:S(2)}) async-start(bf16[64,56,256]{2,1,0:T(8,128)(2,1)} %shard_map.90), calls=%async_computation.3 | async-start | bytes 3670016 | tf_op jit(solution)/shard_map/all_to_all | solution.py:384
  114.4 2.0 %copy-start.4 = (bf16[3,3,3,256,256]{4,3,2,1,0:T(8,128)(2,1)S(1)}, bf16[3,3,3,256,256]{4,3,2,1,0:T(8,128)(2,1)}, u32[]{:S(2)}) copy-start(bf16[3,3,3,256,256]{4,3,2,1,0:T(8,128)(2,1)} %weights.8) | copy-start | bytes 10616836
  116.4 24.1 %copy-start.1 = (bf16[3,3,3,256,256]{4,3,2,1,0:T(8,128)(2,1)S(1)}, bf16[3,3,3,256,256]{4,3,2,1,0:T(8,128)(2,1)}, u32[]{:S(2)}) copy-start(bf16[3,3,3,256,256]{4,3,2,1,0:T(8,128)(2,1)} %weights.9) | copy-start | bytes 10616836
  121.2 19.3 %collective-permute-start.5 = (bf16[2,16,16,256]{3,2,1,0:T(8,128)(2,1)S(1)}, bf16[2,16,16,256]{3,2,1,0:T(8,128)(2,1)S(1)}, u32[]{:S(2)}, u32[]{:S(2)}) collective-permute-start(bf16[2,16,16,256]{3,2,1,0:T(8,128)(2,1)S(1)} %slice.55), channel_id=1, source_target_pairs={{32,0},{64,32},{96,64},{33,1},{65,33},{97,65},{34,2},{66,34},{98,6... | collective-permute-start | bytes 786440 | tf_op jit(solution)/shard_map/ppermute | solution.py:303
  146.9 37.0 %all-to-all-start.4 = ((bf16[64,56,256]{2,1,0:T(8,128)(2,1)}), bf16[64,56,256]{2,1,0:T(8,128)(2,1)S(1)}, u32[]{:S(2)}, u32[]{:S(2)}) async-start(bf16[64,56,256]{2,1,0:T(8,128)(2,1)} %shard_map.88), calls=%async_computation.4 | async-start | bytes 3670016 | tf_op jit(solution)/shard_map/all_to_all | solution.py:392
  183.8 11.5 %all-to-all-start.5 = ((bf16[16,2,8,256]{3,2,1,0:T(8,128)(2,1)}), bf16[16,2,8,256]{3,2,1,0:T(8,128)(2,1)S(1)}, u32[]{:S(2)}, u32[]{:S(2)}) async-start(bf16[16,2,8,256]{3,2,1,0:T(8,128)(2,1)} %shard_map.89), calls=%async_computation.5 | async-start | bytes 262144 | tf_op jit(solution)/shard_map/all_to_all | solution.py:394

commit v3 on v2

--- a/solution.py
+++ b/solution.py
@@ -1,4 +1,3 @@
-import functools
 import math
 
 import jax
@@ -20,6 +19,10 @@
 CH = 256
 TAPS = 27
 SHARE = 54
+PIECE = 56
+UP_ROWS = 32
+GRAD_ROWS = UP_ROWS + 2 * OWN
+SENT_ROWS = GRAD_ROWS + 2 * PIECE
 
 
 def slope_of(values, sigma):
@@ -239,7 +242,7 @@
                 ].astype(BF16)
 
 
-def kernel_grad_kernel(by_core, core_ref, act, block, later, out, table, flipped, sums):
+def tap_sums(act_of, block, later, table, flipped, sums):
     clear_border(table)
     for frame in range(FR):
         fill_own_table(table, frame, block[frame])
@@ -247,9 +250,8 @@
         fill_own_table(table, FR + frame, later[frame])
     for frame in range(FR):
         rows = ROWS * OWN
-        values = act[frame // 2, :, frame % 2] if by_core else act[frame]
         flipped[:, frame * rows : (frame + 1) * rows] = jnp.transpose(
-            own_columns(values).reshape(rows, CH)
+            own_columns(act_of(frame)).reshape(rows, CH)
         ).astype(BF16)
     sums[TAPS * CH :] = jnp.zeros((8, CH), F32)
     for tap_t in range(3):
@@ -259,14 +261,39 @@
             for tap_w in range(3):
                 at = (tap_t * 9 + tap_h * 3 + tap_w) * CH
                 sums[at : at + CH] = result[:, tap_w * CH : (tap_w + 1) * CH]
+
+
+def second_grad_kernel(place, act, block, later, out, table, flipped, sums):
+    tap_sums(lambda frame: act[frame], block, later, table, flipped, sums)
     for core in range(2):
 
-        @pl.when(core_ref[0] == core)
+        @pl.when(place[0] == core)
         def _(core=core):
             for group in range(4):
                 for member in range(16):
                     at = 16 * SHARE * (2 * group + core) + SHARE * member
-                    out[group * 16 + member] = sums[at : at + SHARE + 2].astype(BF16)
+                    out[group * 16 + member] = sums[at : at + PIECE].astype(BF16)
+
+
+def first_grad_kernel(place, act, block, later, second, up, rows_out, out, table, flipped, sums):
+    tap_sums(lambda frame: act[frame // 2, :, frame % 2], block, later, table, flipped, sums)
+    for group in range(4):
+        here = (place[1] == group).astype(F32)
+        for member in range(16):
+            chunk = group * 16 + member
+            out[chunk, :UP_ROWS] = up[chunk]
+            rows = rows_out[member].astype(F32) * here
+            out[chunk, UP_ROWS:GRAD_ROWS] = rows.reshape(2 * OWN, CH).astype(BF16)
+    for core in range(2):
+
+        @pl.when(place[0] == core)
+        def _(core=core):
+            for group in range(4):
+                for member in range(16):
+                    chunk = group * 16 + member
+                    at = 16 * SHARE * (2 * group + core) + SHARE * member
+                    both = jnp.concatenate([second[chunk].astype(F32), sums[at : at + PIECE]], axis=0)
+                    out[chunk, GRAD_ROWS:] = both.astype(BF16)
 
 
 def whole(shape):
@@ -308,6 +335,7 @@
     height = lax.axis_index("height")
     width = lax.axis_index("width")
     core_arg = core.astype(jnp.int32).reshape(1)
+    place = jnp.stack([core, lax.axis_index("y")]).astype(jnp.int32)
     window = 8 * width + height
     columns = OWN * window - EDGE + jnp.arange(WIN)
     inside = ((columns >= 0) & (columns < 128)).astype(F32)
@@ -362,8 +390,6 @@
         [((64, 32, CH), BF16)],
         [pltpu.VMEM((FR, ROWS + 1, 2, OWN, 4 * CH), BF16), pltpu.VMEM((CH, FR * ROWS * OWN), BF16)], 4 * tap_flops,
     )
-    everyone = ("y", "height", "width")
-    up_received = lax.all_to_all(up_part, everyone, 0, 0, tiled=True)
     grad_hidden = call(
         hidden_kernel, (3,), (grad_sum, later, first_slope, conv_second, mask),
         [whole(act_shape), whole(later.shape), whole(act_shape), tap_weights(), whole(mask.shape)],
@@ -371,41 +397,34 @@
     )
     later_hidden = shift(grad_hidden[:2], "y", -1)
 
-    def kernel_grad(act, by_core, grad, after):
-        return call(
-            functools.partial(kernel_grad_kernel, by_core), (), (core_arg, act, grad, after),
-            [SMEM, whole(act.shape), whole(act_shape), whole(after.shape)],
-            [((64, SHARE + 2, CH), BF16)],
-            [own_table, pltpu.VMEM((CH, FR * ROWS * OWN), BF16), pltpu.VMEM((TAPS * CH + 8, CH), F32)], 14 * tap_flops,
-        )
-
-    second_part = kernel_grad(first_act, False, grad_sum, later)
-    second_part, up_received = lax.optimization_barrier((second_part, up_received))
-    second_received = lax.all_to_all(second_part, everyone, 0, 0, tiled=True)
+    grad_scratch = [own_table, pltpu.VMEM((CH, FR * ROWS * OWN), BF16), pltpu.VMEM((TAPS * CH + 8, CH), F32)]
+    tied_act, grad_hidden = lax.optimization_barrier((first_act, grad_hidden))
+    second_part = call(
+        second_grad_kernel, (), (place, tied_act, grad_sum, later),
+        [SMEM, whole(act_shape), whole(act_shape), whole(later.shape)],
+        [((64, PIECE, CH), BF16)], grad_scratch, 14 * tap_flops,
+    )
     rows_out = call(
         features_kernel, (3,), (core_arg, grad_hidden, later_hidden, grad_sum, conv_first),
         [SMEM, whole(act_shape), whole(later_hidden.shape), whole(act_shape), tap_weights()],
         [((ROWS, 2, OWN, CH), BF16)], [own_table, pltpu.VMEM((2 * ROWS * OWN, CH), F32)], 7 * tap_flops,
     )
-    first_part = kernel_grad(block, True, grad_hidden, later_hidden)
-    first_part, rows_out, second_received = lax.optimization_barrier((first_part, rows_out, second_received))
-    first_received = lax.all_to_all(first_part, everyone, 0, 0, tiled=True)
-    rows_out, first_received = lax.optimization_barrier((rows_out, first_received))
-    returned = lax.all_to_all(rows_out, ("height", "width"), 0, 0, tiled=True)
+    parts = call(
+        first_grad_kernel, (), (place, block, grad_hidden, later_hidden, second_part, up_part, rows_out),
+        [SMEM, whole(block.shape), whole(act_shape), whole(later_hidden.shape), whole(second_part.shape),
+         whole(up_part.shape), whole(rows_out.shape)],
+        [((64, SENT_ROWS, CH), BF16)], grad_scratch, 14 * tap_flops,
+    )
+    received = lax.all_to_all(parts, ("y", "height", "width"), 0, 0, tiled=True)
+    returned = lax.dynamic_slice_in_dim(received, 16 * lax.axis_index("y"), 16, 0)[:, UP_ROWS:GRAD_ROWS]
     returned = returned.reshape(8, 2, 2, OWN, CH).transpose(2, 1, 0, 3, 4)
     grad_features = returned.reshape(2, 1, 128, CH)
-
     factor = 1.0 / math.sqrt(32768)
-
-    def share_of(received, rows):
-        return (jnp.sum(received[:, :rows].astype(F32), axis=0) * factor).reshape(-1)
-
-    return (
-        grad_features,
-        share_of(first_received, SHARE),
-        share_of(second_received, SHARE),
-        share_of(up_received, 32),
-    )
+    summed_parts = jnp.sum(received.astype(F32), axis=0) * factor
+    up_share = summed_parts[:UP_ROWS].reshape(-1)
+    second_share = summed_parts[GRAD_ROWS : GRAD_ROWS + SHARE].reshape(-1)
+    first_share = summed_parts[GRAD_ROWS + PIECE : GRAD_ROWS + PIECE + SHARE].reshape(-1)
+    return (grad_features, first_share, second_share, up_share)
 
 
 def solution(mesh):

time: 197 us -> 188 us (0.954)
  starting transfers between devices: 59 us -> 34.2 us
  waiting for transfers between devices: 87.3 us -> 100 us
  local copies, waits for them, and re-layouts: 12.6 us -> 16.3 us
    all_to_all x4 -> x1, waiting for transfers between devices: 29.5 us -> 64.7 us  [shards(): received = lax.all_to_all(parts, ('y', 'height', 'width'), 0, 0, tiled=True)]
    all_to_all x4 -> x1, starting transfers between devices: 35.6 us -> 10.6 us  [shards(): received = lax.all_to_all(parts, ('y', 'height', 'width'), 0, 0, tiled=True)]
    ppermute x4, waiting for transfers between devices: 46 us -> 23.6 us  [shift(): lax.ppermute(value, axis, [(i, i + step) for i in range(count) if 0 <= i...]
    unnamed x17 -> x22, local copies, waits for them, and re-layouts: 5.62 us -> 7.68 us
  transfers between devices with their start and end apart: 12 -> 9, of which waited for: 8 -> 7; matrix products, arithmetic and copies ran while one was open for 4% -> 2% of each run, Pallas kernels for 13% -> 8%
where the time goes in v3:
time: 188 us; the launch traced here: 187 us
  waiting for transfers between devices  100 us (53%)
  starting transfers between devices  34.2 us (18%)
  Pallas kernels  31.6 us (17%)
  local copies, waits for them, and re-layouts  16.3 us (9%)
  other arithmetic  3.74 us (2%)
    all_to_all x1, waiting for transfers between devices, shards(): received = lax.all_to_all(parts, ('y', 'height', 'width'), 0, 0, tiled=True)  64.7 us
    pallas_call x8, Pallas kernels, call(): pl.pallas_call(kernel, out_shape=shapes[0] if single else shapes, grid=gr...  31.6 us
    ppermute x4, waiting for transfers between devices, shift(): lax.ppermute(value, axis, [(i, i + step) for i in range(count) if 0 <= i...  23.6 us
    all_to_all x1, waiting for transfers between devices, shards(): lax.all_to_all(windows, ('core', 'height', 'width'), 0, 0, tiled=True)  11.5 us
    all_to_all x1, starting transfers between devices, shards(): received = lax.all_to_all(parts, ('y', 'height', 'width'), 0, 0, tiled=True)  10.6 us
    ppermute x4, starting transfers between devices, shift(): lax.ppermute(value, axis, [(i, i + step) for i in range(count) if 0 <= i...  10.6 us
    all_to_all x1, starting transfers between devices, shards(): lax.all_to_all(windows, ('core', 'height', 'width'), 0, 0, tiled=True)  7.87 us
    unnamed x22, local copies, waits for them, and re-layouts  7.68 us
  transfers between devices with their start and end apart: 9, of which 7 were waited for; matrix products, arithmetic and copies ran while one was open for 2% of the time, Pallas kernels for 8%

profile of v3, /device:TPU:0, one launch (start us, length us, event | category | flops | bytes accessed | tf_op | source)
XLA Modules:
  0.0 186.9 jit_solution(9371645003237448779)
XLA Ops:
  1.9 1.7 collective-permute-start
  5.4 7.9 %all-to-all-start = ((bf16[32,2,16,256]{3,2,1,0:T(8,128)(2,1)}), bf16[32,2,16,256]{3,2,1,0:T(8,128)(2,1)S(1)}, u32[]{:S(2)}, u32[]{:S(2)}) async-start(bf16[32,2,16,256]{3,2,1,0:T(8,128)(2,1)} %bitcast.9), calls=%async_computation | async-start | bytes 1048576 | tf_op jit(solution)/shard_map/all_to_all | solution.py:353
  13.8 11.5 %all-to-all-done = bf16[32,2,16,256]{3,2,1,0:T(8,128)(2,1)S(1)} async-done(((bf16[32,2,16,256]{3,2,1,0:T(8,128)(2,1)}), bf16[32,2,16,256]{3,2,1,0:T(8,128)(2,1)S(1)}, u32[]{:S(2)}, u32[]{:S(2)}) %all-to-all-start) | async-done | bytes 524320 | tf_op jit(solution)/shard_map/all_to_all | solution.py:353
  26.4 3.6 %all-to-all-start.1 = ((bf16[8,2,4,16,512]{4,3,2,1,0:T(8,128)(2,1)}), bf16[8,2,4,16,512]{4,3,2,1,0:T(8,128)(2,1)S(1)}, u32[]{:S(2)}, u32[]{:S(2)}) async-start(bf16[8,2,4,16,512]{4,3,2,1,0:T(8,128)(2,1)} %copy.15), calls=%async_computation.1 | async-start | bytes 2097152 | tf_op jit(solution)/shard_map/all_to_all | solution.py:365
  29.9 3.5 %collective-permute-start.1 = (bf16[16,2,16,256]{3,2,1,0:T(8,128)(2,1)S(1)}, bf16[16,2,16,256]{3,2,1,0:T(8,128)(2,1)S(1)}, u32[]{:S(2)}, u32[]{:S(2)}) collective-permute-start(bf16[16,2,16,256]{3,2,1,0:T(8,128)(2,1)S(1)} %slice.49), channel_id=1, source_target_pairs={{0,32},{32,64},{64,96},{1,33},{33,65},{65,97},{2,34},{34,66},{66,9... | collective-permute-start | bytes 786440 | tf_op jit(solution)/shard_map/ppermute | solution.py:330
  33.5 5.1 %collective-permute-done.1.halo = bf16[16,2,16,256]{3,2,1,0:T(8,128)(2,1)S(1)} collective-permute-done((bf16[16,2,16,256]{3,2,1,0:T(8,128)(2,1)S(1)}, bf16[16,2,16,256]{3,2,1,0:T(8,128)(2,1)S(1)}, u32[]{:S(2)}, u32[]{:S(2)}) %collective-permute-start.1) | collective-permute-done | bytes 262176 | tf_op jit(solution)/shard_map/ppermute | solution.py:330
  38.6 2.0 %copy-done = bf16[3,3,3,256,256]{4,3,2,1,0:T(8,128)(2,1)S(1)} copy-done((bf16[3,3,3,256,256]{4,3,2,1,0:T(8,128)(2,1)S(1)}, bf16[3,3,3,256,256]{4,3,2,1,0:T(8,128)(2,1)}, u32[]{:S(2)}) %copy-start) | copy-done | bytes 3538968
  40.6 5.0 %shard_map.84 = (bf16[4,16,16,256]{3,2,1,0:T(8,128)(2,1)S(1)}, f32[4,16,16,256]{3,2,1,0:T(8,128)S(1)}) custom-call(bf16[16,2,16,256]{3,2,1,0:T(8,128)(2,1)S(1)} %collective-permute-done.1.halo, bf16[2,16,2,16,256]{4,3,2,1,0:T(8,128)(2,1)S(1)} %bitcast.28, bf16[3,3,3,256,256]{4,3,2,1,0:T(8,128)(2,1)S(1)} %copy-done, f32[16,256]{1,0:T(8,128)S(1)} %broadcast_in_dim.19.mask), custom_call_target="tpu_custom_call" | custom-call | flops 3623878656 | bytes 5914624 | tf_op jit(solution)/shard_map/pallas_call | solution.py:316
  47.6 4.2 %collective-permute-start.2 = (bf16[2,16,16,256]{3,2,1,0:T(8,128)(2,1)}, bf16[2,16,16,256]{3,2,1,0:T(8,128)(2,1)S(1)}, u32[]{:S(2)}, u32[]{:S(2)}) collective-permute-start(bf16[2,16,16,256]{3,2,1,0:T(8,128)(2,1)} %slice.50), channel_id=1, source_target_pairs={{0,32},{32,64},{64,96},{1,33},{33,65},{65,97},{2,34},{34,66},{66,9... | collective-permute-start | bytes 786440 | tf_op jit(solution)/shard_map/ppermute | solution.py:330
  51.8 6.4 %collective-permute-done.2.halo = bf16[2,16,16,256]{3,2,1,0:T(8,128)(2,1)S(1)} collective-permute-done((bf16[2,16,16,256]{3,2,1,0:T(8,128)(2,1)}, bf16[2,16,16,256]{3,2,1,0:T(8,128)(2,1)S(1)}, u32[]{:S(2)}, u32[]{:S(2)}) %collective-permute-start.2) | collective-permute-done | bytes 262176 | tf_op jit(solution)/shard_map/ppermute | solution.py:330
  58.3 6.1 %shard_map.85 = (f32[4,16,16,256]{3,2,1,0:T(8,128)S(1)}, bf16[4,16,16,256]{3,2,1,0:T(8,128)(2,1)S(1)}) custom-call(bf16[2,16,16,256]{3,2,1,0:T(8,128)(2,1)S(1)} %collective-permute-done.2.halo, bf16[4,16,16,256]{3,2,1,0:T(8,128)(2,1)S(1)} %get-tuple-element.26.block.act, bf16[2,16,2,16,256]{4,3,2,1,0:T(8,128)(2,1)S(1)} %bitcast.29, ...), custom_call_target="tpu_custom_call" | custom-call | flops 3623878656 | bytes 6422528 | tf_op jit(solution)/shard_map/pallas_call | solution.py:316
  65.2 3.5 %shard_map.86.block.grad_sum = bf16[4,16,16,256]{3,2,1,0:T(8,128)(2,1)S(1)} custom-call(s32[1]{0:T(128)} %bitcast.core_ref, bf16[8,2,2,2,16,512]{5,4,3,2,1,0:T(8,128)(2,1)S(1)} %bitcast.26, bf16[8,2,2,2,16,512]{5,4,3,2,1,0:T(8,128)(2,1)S(1)} %collective-permute-done.3.other, bf16[4,4,256,256]{3,2,1,0:T(8,128)(2,1)S(1)} %copy-done.7, ...), custom_call_target="tpu_custom_call" | custom-call | flops 2147483648 | bytes 5783556 | tf_op jit(solution)/shard_map/pallas_call | solution.py:316
  70.7 9.3 %collective-permute-done.4.later = bf16[2,16,16,256]{3,2,1,0:T(8,128)(2,1)S(1)} collective-permute-done((bf16[2,16,16,256]{3,2,1,0:T(8,128)(2,1)}, bf16[2,16,16,256]{3,2,1,0:T(8,128)(2,1)S(1)}, u32[]{:S(2)}, u32[]{:S(2)}) %collective-permute-start.4) | collective-permute-done | bytes 262176 | tf_op jit(solution)/shard_map/ppermute | solution.py:330
  80.0 2.0 %copy-done.6 = bf16[3,3,3,256,256]{4,3,2,1,0:T(8,128)(2,1)S(1)} copy-done((bf16[3,3,3,256,256]{4,3,2,1,0:T(8,128)(2,1)S(1)}, bf16[3,3,3,256,256]{4,3,2,1,0:T(8,128)(2,1)}, u32[]{:S(2)}) %copy-start.6) | copy-done | bytes 3538968
  83.2 4.8 %shard_map.87.block = bf16[4,16,16,256]{3,2,1,0:T(8,128)(2,1)S(1)} custom-call(bf16[4,16,16,256]{3,2,1,0:T(8,128)(2,1)S(1)} %shard_map.86.block.grad_sum, bf16[2,16,16,256]{3,2,1,0:T(8,128)(2,1)S(1)} %collective-permute-done.4.later, f32[4,16,16,256]{3,2,1,0:T(8,128)S(1)} %copy-done.9, bf16[3,3,3,256,256]{4,3,2,1,0:T(8,128)(2,1)S(1)} %copy-done.6, ...), custom_call_target="tpu_custom_call" | custom-call | flops 3623878656 | bytes 5914624 | tf_op jit(solution)/shard_map/pallas_call | solution.py:316
  88.0 1.6 collective-permute-start.5
  89.7 1.7 shard_map.89.up
  91.5 3.0 %shard_map.88.second = bf16[64,56,256]{2,1,0:T(8,128)(2,1)S(1)} custom-call(s32[2]{0:T(128)S(1)} %pad_add_fusion.place, bf16[4,16,16,256]{3,2,1,0:T(8,128)(2,1)S(1)} %copy-done.5, bf16[4,16,16,256]{3,2,1,0:T(8,128)(2,1)S(1)} %shard_map.86.block.grad_sum, bf16[2,16,16,256]{3,2,1,0:T(8,128)(2,1)S(1)} %collective-permute-done.4.later), custom_call_target="tpu_custom_call" | custom-call | flops 1879048192 | bytes 3145736 | tf_op jit(solution)/shard_map/pallas_call | solution.py:316
  94.5 2.8 %collective-permute-done.5.later = bf16[2,16,16,256]{3,2,1,0:T(8,128)(2,1)S(1)} collective-permute-done((bf16[2,16,16,256]{3,2,1,0:T(8,128)(2,1)S(1)}, bf16[2,16,16,256]{3,2,1,0:T(8,128)(2,1)S(1)}, u32[]{:S(2)}, u32[]{:S(2)}) %collective-permute-start.5) | collective-permute-done | bytes 262176 | tf_op jit(solution)/shard_map/ppermute | solution.py:330
  97.4 1.9 %shard_map.90.rows_out = bf16[16,2,8,256]{3,2,1,0:T(8,128)(2,1)S(1)} custom-call(s32[1]{0:T(128)} %bitcast.core_ref, bf16[4,16,16,256]{3,2,1,0:T(8,128)(2,1)S(1)} %shard_map.87.block, bf16[2,16,16,256]{3,2,1,0:T(8,128)(2,1)S(1)} %collective-permute-done.5.later, bf16[4,16,16,256]{3,2,1,0:T(8,128)(2,1)S(1)} %shard_map.86.block.grad_sum, ...), custom_call_target="tpu_custom_call" | custom-call | flops 939524096 | bytes 4980740 | tf_op jit(solution)/shard_map/pallas_call | solution.py:316
  99.3 5.6 %shard_map.91 = bf16[64,160,256]{2,1,0:T(8,128)(2,1)} custom-call(s32[2]{0:T(128)S(1)} %pad_add_fusion.place, bf16[2,16,2,16,256]{4,3,2,1,0:T(8,128)(2,1)S(1)} %bitcast.30, bf16[4,16,16,256]{3,2,1,0:T(8,128)(2,1)S(1)} %shard_map.87.block, bf16[2,16,16,256]{3,2,1,0:T(8,128)(2,1)S(1)} %collective-permute-done.5.later, ...), custom_call_target="tpu_custom_call" | custom-call | flops 1879048192 | bytes 9568264 | tf_op jit(solution)/shard_map/pallas_call | solution.py:316
  104.8 10.6 %all-to-all-start.2 = ((bf16[64,160,256]{2,1,0:T(8,128)(2,1)}), bf16[64,160,256]{2,1,0:T(8,128)(2,1)}, u32[]{:S(2)}, u32[]{:S(2)}) async-start(bf16[64,160,256]{2,1,0:T(8,128)(2,1)} %shard_map.91), calls=%async_computation.2 | async-start | bytes 10485760 | tf_op jit(solution)/shard_map/all_to_all | solution.py:418
  115.4 64.7 %all-to-all-done.2 = bf16[64,160,256]{2,1,0:T(8,128)(2,1)} async-done(((bf16[64,160,256]{2,1,0:T(8,128)(2,1)}), bf16[64,160,256]{2,1,0:T(8,128)(2,1)}, u32[]{:S(2)}, u32[]{:S(2)}) %all-to-all-start.2) | async-done | bytes 5242912 | tf_op jit(solution)/shard_map/all_to_all | solution.py:418
  180.1 3.3 %convert_reduce_fusion = f32[160,256]{1,0:T(8,128)S(1)} fusion(bf16[64,160,256]{2,1,0:T(8,128)(2,1)} %all-to-all-done.2), kind=kLoop, calls=%fused_computation | loop fusion | flops 5201920 | bytes 5406720 | tf_op jit(solution)/shard_map/reduce_sum | solution.py:423
  (50 shorter events, 14.3 us)
Async XLA Ops:
  1.9 11.4 %collective-permute-start = (bf16[2,4,4,512]{3,2,1,0:T(4,128)(2,1)S(1)}, bf16[2,4,4,512]{3,2,1,0:T(4,128)(2,1)S(1)}, u32[]{:S(2)}, u32[]{:S(2)}) collective-permute-start(bf16[2,4,4,512]{3,2,1,0:T(4,128)(2,1)S(1)} %slice_select_fusion), channel_id=1, source_target_pairs={{0,1},{1,0},{2,3},{3,2},{4,5},{5,4},{6,7},{7,6},{8,9},{9,8},{10,11... | collective-permute-start | bytes 98312 | tf_op jit(solution)/shard_map/ppermute | solution.py:357
  5.4 19.8 %all-to-all-start = ((bf16[32,2,16,256]{3,2,1,0:T(8,128)(2,1)}), bf16[32,2,16,256]{3,2,1,0:T(8,128)(2,1)S(1)}, u32[]{:S(2)}, u32[]{:S(2)}) async-start(bf16[32,2,16,256]{3,2,1,0:T(8,128)(2,1)} %bitcast.9), calls=%async_computation | async-start | bytes 1048576 | tf_op jit(solution)/shard_map/all_to_all | solution.py:353
  26.4 20.6 %all-to-all-start.1 = ((bf16[8,2,4,16,512]{4,3,2,1,0:T(8,128)(2,1)}), bf16[8,2,4,16,512]{4,3,2,1,0:T(8,128)(2,1)S(1)}, u32[]{:S(2)}, u32[]{:S(2)}) async-start(bf16[8,2,4,16,512]{4,3,2,1,0:T(8,128)(2,1)} %copy.15), calls=%async_computation.1 | async-start | bytes 2097152 | tf_op jit(solution)/shard_map/all_to_all | solution.py:365
  29.9 8.6 %collective-permute-start.1 = (bf16[16,2,16,256]{3,2,1,0:T(8,128)(2,1)S(1)}, bf16[16,2,16,256]{3,2,1,0:T(8,128)(2,1)S(1)}, u32[]{:S(2)}, u32[]{:S(2)}) collective-permute-start(bf16[16,2,16,256]{3,2,1,0:T(8,128)(2,1)S(1)} %slice.49), channel_id=1, source_target_pairs={{0,32},{32,64},{64,96},{1,33},{33,65},{65,97},{2,34},{34,66},{66,9... | collective-permute-start | bytes 786440 | tf_op jit(solution)/shard_map/ppermute | solution.py:330
  38.6 2.0 %copy-start = (bf16[3,3,3,256,256]{4,3,2,1,0:T(8,128)(2,1)S(1)}, bf16[3,3,3,256,256]{4,3,2,1,0:T(8,128)(2,1)}, u32[]{:S(2)}) copy-start(bf16[3,3,3,256,256]{4,3,2,1,0:T(8,128)(2,1)} %weights.9) | copy-start | bytes 10616836
  45.6 1.0 copy-start.8
  46.6 17.8 %copy-start.4 = (bf16[4,16,16,256]{3,2,1,0:T(8,128)(2,1)}, bf16[4,16,16,256]{3,2,1,0:T(8,128)(2,1)S(1)}, u32[]{:S(2)}) copy-start(bf16[4,16,16,256]{3,2,1,0:T(8,128)(2,1)S(1)} %get-tuple-element.26.block.act) | copy-start | bytes 1572868
  46.9 18.3 %collective-permute-start.3 = (bf16[8,2,2,2,16,512]{5,4,3,2,1,0:T(8,128)(2,1)S(1)}, bf16[8,2,2,2,16,512]{5,4,3,2,1,0:T(8,128)(2,1)S(1)}, u32[]{:S(2)}, u32[]{:S(2)}) collective-permute-start(bf16[8,2,2,2,16,512]{5,4,3,2,1,0:T(8,128)(2,1)S(1)} %bitcast.25), channel_id=1, source_target_pairs={{0,16},{16,0},{1,17},{17,1},{2,18},{18,2},{3,19},{19,3},{4,20},{20... | collective-permute-start | bytes 3145736 | tf_op jit(solution)/shard_map/ppermute | solution.py:374
  47.6 10.6 %collective-permute-start.2 = (bf16[2,16,16,256]{3,2,1,0:T(8,128)(2,1)}, bf16[2,16,16,256]{3,2,1,0:T(8,128)(2,1)S(1)}, u32[]{:S(2)}, u32[]{:S(2)}) collective-permute-start(bf16[2,16,16,256]{3,2,1,0:T(8,128)(2,1)} %slice.50), channel_id=1, source_target_pairs={{0,32},{32,64},{64,96},{1,33},{33,65},{65,97},{2,34},{34,66},{66,9... | collective-permute-start | bytes 786440 | tf_op jit(solution)/shard_map/ppermute | solution.py:330
  51.8 13.4 %copy-start.7 = (bf16[4,4,256,256]{3,2,1,0:T(8,128)(2,1)S(1)}, bf16[4,4,256,256]{3,2,1,0:T(8,128)(2,1)}, u32[]{:S(2)}) copy-start(bf16[4,4,256,256]{3,2,1,0:T(8,128)(2,1)} %weights.7) | copy-start | bytes 6291460
  64.4 0.8 copy-start.2
  69.4 10.6 %collective-permute-start.4 = (bf16[2,16,16,256]{3,2,1,0:T(8,128)(2,1)}, bf16[2,16,16,256]{3,2,1,0:T(8,128)(2,1)S(1)}, u32[]{:S(2)}, u32[]{:S(2)}) collective-permute-start(bf16[2,16,16,256]{3,2,1,0:T(8,128)(2,1)} %slice.51), channel_id=1, source_target_pairs={{32,0},{64,32},{96,64},{33,1},{65,33},{97,65},{34,2},{66,34},{98,6... | collective-permute-start | bytes 786440 | tf_op jit(solution)/shard_map/ppermute | solution.py:330
  80.0 2.0 %copy-start.6 = (bf16[3,3,3,256,256]{4,3,2,1,0:T(8,128)(2,1)S(1)}, bf16[3,3,3,256,256]{4,3,2,1,0:T(8,128)(2,1)}, u32[]{:S(2)}) copy-start(bf16[3,3,3,256,256]{4,3,2,1,0:T(8,128)(2,1)} %weights.8) | copy-start | bytes 10616836
  82.0 1.2 copy-start.9
  83.2 6.5 %copy-start.3 = (bf16[4,16,16,256]{3,2,1,0:T(8,128)(2,1)S(1)}, bf16[4,16,16,256]{3,2,1,0:T(8,128)(2,1)}, u32[]{:S(2)}) copy-start(bf16[4,16,16,256]{3,2,1,0:T(8,128)(2,1)} %copy-done.2) | copy-start | bytes 1572868
  88.0 3.5 %copy-start.5 = (bf16[4,16,16,256]{3,2,1,0:T(8,128)(2,1)S(1)}, bf16[4,16,16,256]{3,2,1,0:T(8,128)(2,1)}, u32[]{:S(2)}) copy-start(bf16[4,16,16,256]{3,2,1,0:T(8,128)(2,1)} %copy-done.4) | copy-start | bytes 1572868
  88.0 9.3 %collective-permute-start.5 = (bf16[2,16,16,256]{3,2,1,0:T(8,128)(2,1)S(1)}, bf16[2,16,16,256]{3,2,1,0:T(8,128)(2,1)S(1)}, u32[]{:S(2)}, u32[]{:S(2)}) collective-permute-start(bf16[2,16,16,256]{3,2,1,0:T(8,128)(2,1)S(1)} %slice.63), channel_id=1, source_target_pairs={{32,0},{64,32},{96,64},{33,1},{65,33},{97,65},{34,2},{66,34},{98,6... | collective-permute-start | bytes 786440 | tf_op jit(solution)/shard_map/ppermute | solution.py:330
  91.5 5.9 %copy-start.1 = (bf16[3,3,3,256,256]{4,3,2,1,0:T(8,128)(2,1)S(1)}, bf16[3,3,3,256,256]{4,3,2,1,0:T(8,128)(2,1)}, u32[]{:S(2)}) copy-start(bf16[3,3,3,256,256]{4,3,2,1,0:T(8,128)(2,1)} %weights.9) | copy-start | bytes 10616836
  104.8 75.3 %all-to-all-start.2 = ((bf16[64,160,256]{2,1,0:T(8,128)(2,1)}), bf16[64,160,256]{2,1,0:T(8,128)(2,1)}, u32[]{:S(2)}, u32[]{:S(2)}) async-start(bf16[64,160,256]{2,1,0:T(8,128)(2,1)} %shard_map.91), calls=%async_computation.2 | async-start | bytes 10485760 | tf_op jit(solution)/shard_map/all_to_all | solution.py:418

commit v4 on v3

--- a/solution.py
+++ b/solution.py
@@ -1,3 +1,4 @@
+import functools
 import math
 
 import jax
@@ -22,7 +23,6 @@
 PIECE = 56
 UP_ROWS = 32
 GRAD_ROWS = UP_ROWS + 2 * OWN
-SENT_ROWS = GRAD_ROWS + 2 * PIECE
 
 
 def slope_of(values, sigma):
@@ -263,8 +263,11 @@
                 sums[at : at + CH] = result[:, tap_w * CH : (tap_w + 1) * CH]
 
 
-def second_grad_kernel(place, act, block, later, out, table, flipped, sums):
-    tap_sums(lambda frame: act[frame], block, later, table, flipped, sums)
+def kernel_grad_kernel(by_core, place, act, block, later, out, table, flipped, sums):
+    def act_of(frame):
+        return act[frame // 2, :, frame % 2] if by_core else act[frame]
+
+    tap_sums(act_of, block, later, table, flipped, sums)
     for core in range(2):
 
         @pl.when(place[0] == core)
@@ -273,27 +276,6 @@
                 for member in range(16):
                     at = 16 * SHARE * (2 * group + core) + SHARE * member
                     out[group * 16 + member] = sums[at : at + PIECE].astype(BF16)
-
-
-def first_grad_kernel(place, act, block, later, second, up, rows_out, out, table, flipped, sums):
-    tap_sums(lambda frame: act[frame // 2, :, frame % 2], block, later, table, flipped, sums)
-    for group in range(4):
-        here = (place[1] == group).astype(F32)
-        for member in range(16):
-            chunk = group * 16 + member
-            out[chunk, :UP_ROWS] = up[chunk]
-            rows = rows_out[member].astype(F32) * here
-            out[chunk, UP_ROWS:GRAD_ROWS] = rows.reshape(2 * OWN, CH).astype(BF16)
-    for core in range(2):
-
-        @pl.when(place[0] == core)
-        def _(core=core):
-            for group in range(4):
-                for member in range(16):
-                    chunk = group * 16 + member
-                    at = 16 * SHARE * (2 * group + core) + SHARE * member
-                    both = jnp.concatenate([second[chunk].astype(F32), sums[at : at + PIECE]], axis=0)
-                    out[chunk, GRAD_ROWS:] = both.astype(BF16)
 
 
 def whole(shape):
@@ -335,7 +317,6 @@
     height = lax.axis_index("height")
     width = lax.axis_index("width")
     core_arg = core.astype(jnp.int32).reshape(1)
-    place = jnp.stack([core, lax.axis_index("y")]).astype(jnp.int32)
     window = 8 * width + height
     columns = OWN * window - EDGE + jnp.arange(WIN)
     inside = ((columns >= 0) & (columns < 128)).astype(F32)
@@ -398,26 +379,38 @@
     later_hidden = shift(grad_hidden[:2], "y", -1)
 
     grad_scratch = [own_table, pltpu.VMEM((CH, FR * ROWS * OWN), BF16), pltpu.VMEM((TAPS * CH + 8, CH), F32)]
+
+    def kernel_grad(act, by_core, grad, after):
+        return call(
+            functools.partial(kernel_grad_kernel, by_core), (), (core_arg, act, grad, after),
+            [SMEM, whole(act.shape), whole(act_shape), whole(after.shape)],
+            [((64, PIECE, CH), BF16)], grad_scratch, 14 * tap_flops,
+        ).reshape(4, 16 * PIECE, CH)
+
+    up_sum = lax.psum_scatter(up_part.reshape(4, 16 * UP_ROWS, CH), "y", scatter_dimension=0, tiled=True)
     tied_act, grad_hidden = lax.optimization_barrier((first_act, grad_hidden))
-    second_part = call(
-        second_grad_kernel, (), (place, tied_act, grad_sum, later),
-        [SMEM, whole(act_shape), whole(act_shape), whole(later.shape)],
-        [((64, PIECE, CH), BF16)], grad_scratch, 14 * tap_flops,
-    )
+    second_part = kernel_grad(tied_act, False, grad_sum, later)
+    second_sum = lax.psum_scatter(second_part, "y", scatter_dimension=0, tiled=True)
+    first_part = kernel_grad(block, True, grad_hidden, later_hidden)
+    first_sum = lax.all_to_all(first_part, "y", 0, 0, tiled=True)
+    tied_hidden, first_part = lax.optimization_barrier((grad_hidden, first_part))
     rows_out = call(
-        features_kernel, (3,), (core_arg, grad_hidden, later_hidden, grad_sum, conv_first),
+        features_kernel, (3,), (core_arg, tied_hidden, later_hidden, grad_sum, conv_first),
         [SMEM, whole(act_shape), whole(later_hidden.shape), whole(act_shape), tap_weights()],
         [((ROWS, 2, OWN, CH), BF16)], [own_table, pltpu.VMEM((2 * ROWS * OWN, CH), F32)], 7 * tap_flops,
     )
-    parts = call(
-        first_grad_kernel, (), (place, block, grad_hidden, later_hidden, second_part, up_part, rows_out),
-        [SMEM, whole(block.shape), whole(act_shape), whole(later_hidden.shape), whole(second_part.shape),
-         whole(up_part.shape), whole(rows_out.shape)],
-        [((64, SENT_ROWS, CH), BF16)], grad_scratch, 14 * tap_flops,
-    )
-    received = lax.all_to_all(parts, ("y", "height", "width"), 0, 0, tiled=True)
-    returned = lax.dynamic_slice_in_dim(received, 16 * lax.axis_index("y"), 16, 0)[:, UP_ROWS:GRAD_ROWS]
-    returned = returned.reshape(8, 2, 2, OWN, CH).transpose(2, 1, 0, 3, 4)
+    first_sum = jnp.sum(first_sum.astype(F32), axis=0).astype(BF16)
+    parts = jnp.concatenate(
+        [
+            up_sum.reshape(16, UP_ROWS, CH),
+            rows_out.reshape(16, 2 * OWN, CH),
+            second_sum.reshape(16, PIECE, CH),
+            first_sum.reshape(16, PIECE, CH),
+        ],
+        axis=1,
+    )
+    received = lax.all_to_all(parts, ("height", "width"), 0, 0, tiled=True)
+    returned = received[:, UP_ROWS:GRAD_ROWS].reshape(8, 2, 2, OWN, CH).transpose(2, 1, 0, 3, 4)
     grad_features = returned.reshape(2, 1, 128, CH)
     factor = 1.0 / math.sqrt(32768)
     summed_parts = jnp.sum(received.astype(F32), axis=0) * factor

time: 188 us -> 192 us (1.021)
  waiting for transfers between devices: 100 us -> 69.2 us
  blocking collectives: 0 us -> 26.1 us
  between operations: 0.96 us -> 14.5 us
  starting transfers between devices: 34.2 us -> 28.3 us
  local copies, waits for them, and re-layouts: 16.3 us -> 18.9 us
    all_to_all x1, waiting for transfers between devices: 64.7 us -> 28.9 us  [shards(): first_sum = lax.all_to_all(first_part, 'y', 0, 0, tiled=True)]
    all_to_all x0 -> x1, blocking collectives: none -> 26.1 us  [shards(): received = lax.all_to_all(parts, ('height', 'width'), 0, 0, tiled=True)]
    all_to_all x1, starting transfers between devices: 10.6 us -> 4.66 us  [shards(): first_sum = lax.all_to_all(first_part, 'y', 0, 0, tiled=True)]
    ppermute x4, waiting for transfers between devices: 23.6 us -> 28.4 us  [shift(): lax.ppermute(value, axis, [(i, i + step) for i in range(count) if 0 <= i...]
    unnamed x22 -> x36, local copies, waits for them, and re-layouts: 7.68 us -> 11.9 us
    reduce_sum x1, other arithmetic: 3.27 us -> 0.18 us  [shards(): summed_parts = jnp.sum(received.astype(F32), axis=0) * factor]
    reduce_sum x0 -> x1, other arithmetic: none -> 2.04 us  [shards(): first_sum = jnp.sum(first_sum.astype(F32), axis=0).astype(BF16)]
  transfers between devices with their start and end apart: 9 -> 11, of which waited for: 7 -> 7; matrix products, arithmetic and copies ran while one was open for 2% -> 3% of each run, Pallas kernels for 8% -> 13%
where the time goes in v4:
time: 192 us; the launch traced here: 191 us
  waiting for transfers between devices  69.2 us (36%)
  Pallas kernels  30.3 us (16%)
  starting transfers between devices  28.3 us (15%)
  blocking collectives  26.1 us (14%)
  local copies, waits for them, and re-layouts  18.9 us (10%)
  between operations  14.5 us (8%)
  other arithmetic  3.82 us (2%)
    pallas_call x8, Pallas kernels, call(): pl.pallas_call(kernel, out_shape=shapes[0] if single else shapes, grid=gr...  30.3 us
    all_to_all x1, waiting for transfers between devices, shards(): first_sum = lax.all_to_all(first_part, 'y', 0, 0, tiled=True)  28.9 us
    ppermute x4, waiting for transfers between devices, shift(): lax.ppermute(value, axis, [(i, i + step) for i in range(count) if 0 <= i...  28.4 us
    all_to_all x1, blocking collectives, shards(): received = lax.all_to_all(parts, ('height', 'width'), 0, 0, tiled=True)  26.1 us
    unnamed x36, local copies, waits for them, and re-layouts  11.9 us
    all_to_all x1, waiting for transfers between devices, shards(): lax.all_to_all(windows, ('core', 'height', 'width'), 0, 0, tiled=True)  11.5 us
    ppermute x4, starting transfers between devices, shift(): lax.ppermute(value, axis, [(i, i + step) for i in range(count) if 0 <= i...  10.4 us
    all_to_all x1, starting transfers between devices, shards(): lax.all_to_all(windows, ('core', 'height', 'width'), 0, 0, tiled=True)  7.87 us
  transfers between devices with their start and end apart: 11, of which 7 were waited for; matrix products, arithmetic and copies ran while one was open for 3% of the time, Pallas kernels for 13%

profile of v4, /device:TPU:0, one launch (start us, length us, event | category | flops | bytes accessed | tf_op | source)
XLA Modules:
  0.0 191.0 jit_solution(9006980374015673028)
XLA Ops:
  8.4 1.7 collective-permute-start
  12.0 7.9 %all-to-all-start = ((bf16[32,2,16,256]{3,2,1,0:T(8,128)(2,1)}), bf16[32,2,16,256]{3,2,1,0:T(8,128)(2,1)S(1)}, u32[]{:S(2)}, u32[]{:S(2)}) async-start(bf16[32,2,16,256]{3,2,1,0:T(8,128)(2,1)} %bitcast.8), calls=%async_computation | async-start | bytes 1048576 | tf_op jit(solution)/shard_map/all_to_all | solution.py:334
  20.3 11.5 %all-to-all-done = bf16[32,2,16,256]{3,2,1,0:T(8,128)(2,1)S(1)} async-done(((bf16[32,2,16,256]{3,2,1,0:T(8,128)(2,1)}), bf16[32,2,16,256]{3,2,1,0:T(8,128)(2,1)S(1)}, u32[]{:S(2)}, u32[]{:S(2)}) %all-to-all-start) | async-done | bytes 524320 | tf_op jit(solution)/shard_map/all_to_all | solution.py:334
  32.9 3.6 %all-to-all-start.1 = ((bf16[8,2,4,16,512]{4,3,2,1,0:T(8,128)(2,1)}), bf16[8,2,4,16,512]{4,3,2,1,0:T(8,128)(2,1)S(1)}, u32[]{:S(2)}, u32[]{:S(2)}) async-start(bf16[8,2,4,16,512]{4,3,2,1,0:T(8,128)(2,1)} %copy.17), calls=%async_computation.1 | async-start | bytes 2097152 | tf_op jit(solution)/shard_map/all_to_all | solution.py:346
  36.5 3.5 %collective-permute-start.1 = (bf16[16,2,16,256]{3,2,1,0:T(8,128)(2,1)S(1)}, bf16[16,2,16,256]{3,2,1,0:T(8,128)(2,1)S(1)}, u32[]{:S(2)}, u32[]{:S(2)}) collective-permute-start(bf16[16,2,16,256]{3,2,1,0:T(8,128)(2,1)S(1)} %slice.49), channel_id=1, source_target_pairs={{0,32},{32,64},{64,96},{1,33},{33,65},{65,97},{2,34},{34,66},{66,9... | collective-permute-start | bytes 786440 | tf_op jit(solution)/shard_map/ppermute | solution.py:312
  40.0 5.1 %collective-permute-done.1.halo = bf16[16,2,16,256]{3,2,1,0:T(8,128)(2,1)S(1)} collective-permute-done((bf16[16,2,16,256]{3,2,1,0:T(8,128)(2,1)S(1)}, bf16[16,2,16,256]{3,2,1,0:T(8,128)(2,1)S(1)}, u32[]{:S(2)}, u32[]{:S(2)}) %collective-permute-start.1) | collective-permute-done | bytes 262176 | tf_op jit(solution)/shard_map/ppermute | solution.py:312
  45.2 2.0 %copy-done = bf16[3,3,3,256,256]{4,3,2,1,0:T(8,128)(2,1)S(1)} copy-done((bf16[3,3,3,256,256]{4,3,2,1,0:T(8,128)(2,1)S(1)}, bf16[3,3,3,256,256]{4,3,2,1,0:T(8,128)(2,1)}, u32[]{:S(2)}) %copy-start) | copy-done | bytes 3538968
  47.2 5.0 %shard_map.84 = (bf16[4,16,16,256]{3,2,1,0:T(8,128)(2,1)S(1)}, f32[4,16,16,256]{3,2,1,0:T(8,128)S(1)}) custom-call(bf16[16,2,16,256]{3,2,1,0:T(8,128)(2,1)S(1)} %collective-permute-done.1.halo, bf16[2,16,2,16,256]{4,3,2,1,0:T(8,128)(2,1)S(1)} %bitcast.37, bf16[3,3,3,256,256]{4,3,2,1,0:T(8,128)(2,1)S(1)} %copy-done, f32[16,256]{1,0:T(8,128)S(1)} %broadcast_in_dim.19.mask), custom_call_target="tpu_custom_call" | custom-call | flops 3623878656 | bytes 5914624 | tf_op jit(solution)/shard_map/pallas_call | solution.py:298
  54.2 4.2 %collective-permute-start.2 = (bf16[2,16,16,256]{3,2,1,0:T(8,128)(2,1)}, bf16[2,16,16,256]{3,2,1,0:T(8,128)(2,1)S(1)}, u32[]{:S(2)}, u32[]{:S(2)}) collective-permute-start(bf16[2,16,16,256]{3,2,1,0:T(8,128)(2,1)} %slice.50), channel_id=1, source_target_pairs={{0,32},{32,64},{64,96},{1,33},{33,65},{65,97},{2,34},{34,66},{66,9... | collective-permute-start | bytes 786440 | tf_op jit(solution)/shard_map/ppermute | solution.py:312
  58.4 6.4 %collective-permute-done.2.halo = bf16[2,16,16,256]{3,2,1,0:T(8,128)(2,1)S(1)} collective-permute-done((bf16[2,16,16,256]{3,2,1,0:T(8,128)(2,1)}, bf16[2,16,16,256]{3,2,1,0:T(8,128)(2,1)S(1)}, u32[]{:S(2)}, u32[]{:S(2)}) %collective-permute-start.2) | collective-permute-done | bytes 262176 | tf_op jit(solution)/shard_map/ppermute | solution.py:312
  64.8 6.1 %shard_map.85 = (f32[4,16,16,256]{3,2,1,0:T(8,128)S(1)}, bf16[4,16,16,256]{3,2,1,0:T(8,128)(2,1)S(1)}) custom-call(bf16[2,16,16,256]{3,2,1,0:T(8,128)(2,1)S(1)} %collective-permute-done.2.halo, bf16[4,16,16,256]{3,2,1,0:T(8,128)(2,1)S(1)} %get-tuple-element.29.block.act, bf16[2,16,2,16,256]{4,3,2,1,0:T(8,128)(2,1)S(1)} %bitcast.38, ...), custom_call_target="tpu_custom_call" | custom-call | flops 3623878656 | bytes 6422528 | tf_op jit(solution)/shard_map/pallas_call | solution.py:298
  70.9 3.5 %shard_map.86.block.grad_sum = bf16[4,16,16,256]{3,2,1,0:T(8,128)(2,1)S(1)} custom-call(s32[1]{0:T(128)} %bitcast.core_ref.place, bf16[8,2,2,2,16,512]{5,4,3,2,1,0:T(8,128)(2,1)S(1)} %bitcast.34, bf16[8,2,2,2,16,512]{5,4,3,2,1,0:T(8,128)(2,1)S(1)} %collective-permute-done.3.other, bf16[4,4,256,256]{3,2,1,0:T(8,128)(2,1)S(1)} %copy-done.14, ...), custom_call_target="tpu_custom_call" | custom-call | flops 2147483648 | bytes 5783556 | tf_op jit(solution)/shard_map/pallas_call | solution.py:298
  74.5 2.7 %shard_map.87 = bf16[64,32,256]{2,1,0:T(8,128)(2,1)} custom-call(s32[1]{0:T(128)} %bitcast.core_ref.place, bf16[4,16,16,256]{3,2,1,0:T(8,128)(2,1)S(1)} %get-tuple-element.24.act, bf16[8,2,2,2,16,512]{5,4,3,2,1,0:T(8,128)(2,1)S(1)} %bitcast.35, bf16[8,2,2,2,16,512]{5,4,3,2,1,0:T(8,128)(2,1)S(1)} %collective-permute-done.3.other), custom_call_target="tpu_custom_call" | custom-call | flops 536870912 | bytes 3670020 | tf_op jit(solution)/shard_map/pallas_call | solution.py:298
  78.8 8.9 %collective-permute-done.4.later = bf16[2,16,16,256]{3,2,1,0:T(8,128)(2,1)S(1)} collective-permute-done((bf16[2,16,16,256]{3,2,1,0:T(8,128)(2,1)S(1)}, bf16[2,16,16,256]{3,2,1,0:T(8,128)(2,1)S(1)}, u32[]{:S(2)}, u32[]{:S(2)}) %collective-permute-start.4) | collective-permute-done | bytes 262176 | tf_op jit(solution)/shard_map/ppermute | solution.py:312
  87.7 2.1 %copy-done.13 = bf16[3,3,3,256,256]{4,3,2,1,0:T(8,128)(2,1)S(1)} copy-done((bf16[3,3,3,256,256]{4,3,2,1,0:T(8,128)(2,1)S(1)}, bf16[3,3,3,256,256]{4,3,2,1,0:T(8,128)(2,1)}, u32[]{:S(2)}) %copy-start.13) | copy-done | bytes 3538968
  91.0 4.8 %shard_map.88.block = bf16[4,16,16,256]{3,2,1,0:T(8,128)(2,1)S(1)} custom-call(bf16[4,16,16,256]{3,2,1,0:T(8,128)(2,1)S(1)} %shard_map.86.block.grad_sum, bf16[2,16,16,256]{3,2,1,0:T(8,128)(2,1)S(1)} %collective-permute-done.4.later, f32[4,16,16,256]{3,2,1,0:T(8,128)S(1)} %copy-done.16, bf16[3,3,3,256,256]{4,3,2,1,0:T(8,128)(2,1)S(1)} %copy-done.13, ...), custom_call_target="tpu_custom_call" | custom-call | flops 3623878656 | bytes 5914624 | tf_op jit(solution)/shard_map/pallas_call | solution.py:298
  95.8 3.7 %shard_map.91 = bf16[64,56,256]{2,1,0:T(8,128)(2,1)} custom-call(s32[1]{0:T(128)} %bitcast.core_ref.place, bf16[4,16,16,256]{3,2,1,0:T(8,128)(2,1)S(1)} %copy-done.12, bf16[4,16,16,256]{3,2,1,0:T(8,128)(2,1)S(1)} %shard_map.86.block.grad_sum, bf16[2,16,16,256]{3,2,1,0:T(8,128)(2,1)S(1)} %collective-permute-done.4.later), custom_call_target="tpu_custom_call" | custom-call | flops 1879048192 | bytes 3145732 | tf_op jit(solution)/shard_map/pallas_call | solution.py:298
  100.9 8.0 %collective-permute-done.5.later = bf16[2,16,16,256]{3,2,1,0:T(8,128)(2,1)S(1)} collective-permute-done((bf16[2,16,16,256]{3,2,1,0:T(8,128)(2,1)S(1)}, bf16[2,16,16,256]{3,2,1,0:T(8,128)(2,1)S(1)}, u32[]{:S(2)}, u32[]{:S(2)}) %collective-permute-start.5) | collective-permute-done | bytes 262176 | tf_op jit(solution)/shard_map/ppermute | solution.py:312
  108.9 2.5 %shard_map.89 = bf16[64,56,256]{2,1,0:T(8,128)(2,1)S(1)} custom-call(s32[1]{0:T(128)} %bitcast.core_ref.place, bf16[2,16,2,16,256]{4,3,2,1,0:T(8,128)(2,1)S(1)} %bitcast.39, bf16[4,16,16,256]{3,2,1,0:T(8,128)(2,1)S(1)} %shard_map.88.block, bf16[2,16,16,256]{3,2,1,0:T(8,128)(2,1)S(1)} %collective-permute-done.5.later), custom_call_target="tpu_custom_call" | custom-call | flops 1879048192 | bytes 3145732 | tf_op jit(solution)/shard_map/pallas_call | solution.py:298
  112.7 4.7 %all-to-all-start.2 = ((bf16[4,896,256]{2,1,0:T(8,128)(2,1)}), bf16[4,896,256]{2,1,0:T(8,128)(2,1)}, u32[]{:S(2)}, u32[]{:S(2)}) async-start(bf16[4,896,256]{2,1,0:T(8,128)(2,1)} %bitcast.36), calls=%async_computation.4 | async-start | bytes 3670016 | tf_op jit(solution)/shard_map/all_to_all | solution.py:395
  120.4 1.9 %shard_map.90 = bf16[16,2,8,256]{3,2,1,0:T(8,128)(2,1)S(1)} custom-call(s32[1]{0:T(128)} %bitcast.core_ref.place, bf16[4,16,16,256]{3,2,1,0:T(8,128)(2,1)S(1)} %copy-done.6, bf16[2,16,16,256]{3,2,1,0:T(8,128)(2,1)S(1)} %copy-done.10, bf16[4,16,16,256]{3,2,1,0:T(8,128)(2,1)S(1)} %copy-done.4, bf16[3,3,3,256,256]{4,3,2,1,0:T(8,128)(2,1)S(1)} %copy-done.1), custom_call_target="tpu_custom_call" | custom-call | flops 939524096 | bytes 4980740 | tf_op jit(solution)/shard_map/pallas_call | solution.py:298
  123.0 28.9 %all-to-all-done.2 = bf16[4,896,256]{2,1,0:T(8,128)(2,1)} async-done(((bf16[4,896,256]{2,1,0:T(8,128)(2,1)}), bf16[4,896,256]{2,1,0:T(8,128)(2,1)}, u32[]{:S(2)}, u32[]{:S(2)}) %all-to-all-start.2) | async-done | bytes 1835040 | tf_op jit(solution)/shard_map/all_to_all | solution.py:395
  151.9 2.0 %reduce_sum.21 = bf16[896,256]{1,0:T(8,128)(2,1)S(1)} reduce(bf16[4,896,256]{2,1,0:T(8,128)(2,1)} %all-to-all-done.2, bf16[]{:T(256)} %constant.9.clone.1), dimensions={0}, to_apply=%region_2.3 | reduce | flops 688128 | bytes 2293762 | tf_op jit(solution)/shard_map/reduce_sum | solution.py:402
  155.3 26.1 %all_to_all.20 = bf16[16,160,256]{2,1,0:T(8,128)(2,1)S(1)} all-to-all(bf16[16,160,256]{2,1,0:T(8,128)(2,1)S(1)} %pad_maximum_fusion), channel_id=1, replica_groups=mesh['y'=4,'core'=2,'height'=8,'width'=2] {'height','width'}, dimensions={0} | all-to-all | bytes 2621440 | tf_op jit(solution)/shard_map/all_to_all | solution.py:412
  (72 shorter events, 19.8 us)
Async XLA Ops:
  8.4 11.4 %collective-permute-start = (bf16[2,4,4,512]{3,2,1,0:T(4,128)(2,1)S(1)}, bf16[2,4,4,512]{3,2,1,0:T(4,128)(2,1)S(1)}, u32[]{:S(2)}, u32[]{:S(2)}) collective-permute-start(bf16[2,4,4,512]{3,2,1,0:T(4,128)(2,1)S(1)} %slice_select_fusion), channel_id=1, source_target_pairs={{0,1},{1,0},{2,3},{3,2},{4,5},{5,4},{6,7},{7,6},{8,9},{9,8},{10,11... | collective-permute-start | bytes 98312 | tf_op jit(solution)/shard_map/ppermute | solution.py:338
  12.0 19.8 %all-to-all-start = ((bf16[32,2,16,256]{3,2,1,0:T(8,128)(2,1)}), bf16[32,2,16,256]{3,2,1,0:T(8,128)(2,1)S(1)}, u32[]{:S(2)}, u32[]{:S(2)}) async-start(bf16[32,2,16,256]{3,2,1,0:T(8,128)(2,1)} %bitcast.8), calls=%async_computation | async-start | bytes 1048576 | tf_op jit(solution)/shard_map/all_to_all | solution.py:334
  32.9 20.6 %all-to-all-start.1 = ((bf16[8,2,4,16,512]{4,3,2,1,0:T(8,128)(2,1)}), bf16[8,2,4,16,512]{4,3,2,1,0:T(8,128)(2,1)S(1)}, u32[]{:S(2)}, u32[]{:S(2)}) async-start(bf16[8,2,4,16,512]{4,3,2,1,0:T(8,128)(2,1)} %copy.17), calls=%async_computation.1 | async-start | bytes 2097152 | tf_op jit(solution)/shard_map/all_to_all | solution.py:346
  36.4 117.6 %reduce-scatter.3.cloned.1.call-start = ((), (), s32[]{:S(2)}) async-start(), calls=%async_computation.6 | async-start | bytes 1310720 | tf_op jit(solution)/shard_map/reduce_scatter | solution.py:390
  36.5 8.6 %collective-permute-start.1 = (bf16[16,2,16,256]{3,2,1,0:T(8,128)(2,1)S(1)}, bf16[16,2,16,256]{3,2,1,0:T(8,128)(2,1)S(1)}, u32[]{:S(2)}, u32[]{:S(2)}) collective-permute-start(bf16[16,2,16,256]{3,2,1,0:T(8,128)(2,1)S(1)} %slice.49), channel_id=1, source_target_pairs={{0,32},{32,64},{64,96},{1,33},{33,65},{65,97},{2,34},{34,66},{66,9... | collective-permute-start | bytes 786440 | tf_op jit(solution)/shard_map/ppermute | solution.py:312
  45.2 2.0 %copy-start = (bf16[3,3,3,256,256]{4,3,2,1,0:T(8,128)(2,1)S(1)}, bf16[3,3,3,256,256]{4,3,2,1,0:T(8,128)(2,1)}, u32[]{:S(2)}) copy-start(bf16[3,3,3,256,256]{4,3,2,1,0:T(8,128)(2,1)} %weights.9) | copy-start | bytes 10616836
  53.2 17.7 %copy-start.11 = (bf16[4,16,16,256]{3,2,1,0:T(8,128)(2,1)}, bf16[4,16,16,256]{3,2,1,0:T(8,128)(2,1)S(1)}, u32[]{:S(2)}) copy-start(bf16[4,16,16,256]{3,2,1,0:T(8,128)(2,1)S(1)} %get-tuple-element.29.block.act) | copy-start | bytes 1572868
  53.4 17.5 %collective-permute-start.3 = (bf16[8,2,2,2,16,512]{5,4,3,2,1,0:T(8,128)(2,1)S(1)}, bf16[8,2,2,2,16,512]{5,4,3,2,1,0:T(8,128)(2,1)S(1)}, u32[]{:S(2)}, u32[]{:S(2)}) collective-permute-start(bf16[8,2,2,2,16,512]{5,4,3,2,1,0:T(8,128)(2,1)S(1)} %bitcast.33), channel_id=1, source_target_pairs={{0,16},{16,0},{1,17},{17,1},{2,18},{18,2},{3,19},{19,3},{4,20},{20... | collective-permute-start | bytes 3145736 | tf_op jit(solution)/shard_map/ppermute | solution.py:355
  54.2 10.6 %collective-permute-start.2 = (bf16[2,16,16,256]{3,2,1,0:T(8,128)(2,1)}, bf16[2,16,16,256]{3,2,1,0:T(8,128)(2,1)S(1)}, u32[]{:S(2)}, u32[]{:S(2)}) collective-permute-start(bf16[2,16,16,256]{3,2,1,0:T(8,128)(2,1)} %slice.50), channel_id=1, source_target_pairs={{0,32},{32,64},{64,96},{1,33},{33,65},{65,97},{2,34},{34,66},{66,9... | collective-permute-start | bytes 786440 | tf_op jit(solution)/shard_map/ppermute | solution.py:312
  58.3 12.6 %copy-start.14 = (bf16[4,4,256,256]{3,2,1,0:T(8,128)(2,1)S(1)}, bf16[4,4,256,256]{3,2,1,0:T(8,128)(2,1)}, u32[]{:S(2)}) copy-start(bf16[4,4,256,256]{3,2,1,0:T(8,128)(2,1)} %weights.7) | copy-start | bytes 6291460
  74.5 21.3 %copy-start.3 = (bf16[4,16,16,256]{3,2,1,0:T(8,128)(2,1)}, bf16[4,16,16,256]{3,2,1,0:T(8,128)(2,1)S(1)}, u32[]{:S(2)}) copy-start(bf16[4,16,16,256]{3,2,1,0:T(8,128)(2,1)S(1)} %shard_map.86.block.grad_sum) | copy-start | bytes 1572868
  77.2 76.8 %reduce-scatter.5.cloned.1.call-start = ((), (), s32[]{:S(2)}) async-start(), calls=%async_computation.7 | async-start | bytes 2293760 | tf_op jit(solution)/shard_map/reduce_scatter | solution.py:393
  77.3 10.4 %collective-permute-start.4 = (bf16[2,16,16,256]{3,2,1,0:T(8,128)(2,1)S(1)}, bf16[2,16,16,256]{3,2,1,0:T(8,128)(2,1)S(1)}, u32[]{:S(2)}, u32[]{:S(2)}) collective-permute-start(bf16[2,16,16,256]{3,2,1,0:T(8,128)(2,1)S(1)} %slice.51), channel_id=1, source_target_pairs={{32,0},{64,32},{96,64},{33,1},{65,33},{97,65},{34,2},{66,34},{98,6... | collective-permute-start | bytes 786440 | tf_op jit(solution)/shard_map/ppermute | solution.py:312
  87.7 2.1 %copy-start.13 = (bf16[3,3,3,256,256]{4,3,2,1,0:T(8,128)(2,1)S(1)}, bf16[3,3,3,256,256]{4,3,2,1,0:T(8,128)(2,1)}, u32[]{:S(2)}) copy-start(bf16[3,3,3,256,256]{4,3,2,1,0:T(8,128)(2,1)} %weights.8) | copy-start | bytes 10616836
  89.8 1.2 copy-start.16
  91.0 4.8 %copy-start.12 = (bf16[4,16,16,256]{3,2,1,0:T(8,128)(2,1)S(1)}, bf16[4,16,16,256]{3,2,1,0:T(8,128)(2,1)}, u32[]{:S(2)}) copy-start(bf16[4,16,16,256]{3,2,1,0:T(8,128)(2,1)} %copy-done.11) | copy-start | bytes 1572868
  95.8 13.1 %copy-start.5 = (bf16[4,16,16,256]{3,2,1,0:T(8,128)(2,1)}, bf16[4,16,16,256]{3,2,1,0:T(8,128)(2,1)S(1)}, u32[]{:S(2)}) copy-start(bf16[4,16,16,256]{3,2,1,0:T(8,128)(2,1)S(1)} %shard_map.88.block) | copy-start | bytes 1572868
  99.6 9.3 %collective-permute-start.5 = (bf16[2,16,16,256]{3,2,1,0:T(8,128)(2,1)S(1)}, bf16[2,16,16,256]{3,2,1,0:T(8,128)(2,1)S(1)}, u32[]{:S(2)}, u32[]{:S(2)}) collective-permute-start(bf16[2,16,16,256]{3,2,1,0:T(8,128)(2,1)S(1)} %slice.63), channel_id=1, source_target_pairs={{32,0},{64,32},{96,64},{33,1},{65,33},{97,65},{34,2},{66,34},{98,6... | collective-permute-start | bytes 786440 | tf_op jit(solution)/shard_map/ppermute | solution.py:312
  108.9 2.5 %copy-start.9 = (bf16[2,16,16,256]{3,2,1,0:T(8,128)(2,1)}, bf16[2,16,16,256]{3,2,1,0:T(8,128)(2,1)S(1)}, u32[]{:S(2)}) copy-start(bf16[2,16,16,256]{3,2,1,0:T(8,128)(2,1)S(1)} %collective-permute-done.5.later) | copy-start | bytes 786436
  111.4 1.3 copy-start.2
  112.7 4.7 %copy-start.1 = (bf16[3,3,3,256,256]{4,3,2,1,0:T(8,128)(2,1)S(1)}, bf16[3,3,3,256,256]{4,3,2,1,0:T(8,128)(2,1)}, u32[]{:S(2)}) copy-start(bf16[3,3,3,256,256]{4,3,2,1,0:T(8,128)(2,1)} %weights.9) | copy-start | bytes 10616836
  112.7 39.2 %all-to-all-start.2 = ((bf16[4,896,256]{2,1,0:T(8,128)(2,1)}), bf16[4,896,256]{2,1,0:T(8,128)(2,1)}, u32[]{:S(2)}, u32[]{:S(2)}) async-start(bf16[4,896,256]{2,1,0:T(8,128)(2,1)} %bitcast.36), calls=%async_computation.4 | async-start | bytes 3670016 | tf_op jit(solution)/shard_map/all_to_all | solution.py:395
  117.4 1.0 copy-start.4
  151.9 2.1 %copy-start.8 = (bf16[16,2,8,256]{3,2,1,0:T(8,128)(2,1)S(1)}, bf16[16,2,8,256]{3,2,1,0:T(8,128)(2,1)}, u32[]{:S(2)}) copy-start(bf16[16,2,8,256]{3,2,1,0:T(8,128)(2,1)} %copy-done.7) | copy-start | bytes 393220
  (4 other events, 3.6 us)
Sparse Core Ops, SparseCore 0:
  77.3 25.7 reduce-scatter.2
  105.7 38.4 reduce-scatter.4

commit v5 on v2

--- a/solution.py
+++ b/solution.py
@@ -1,4 +1,3 @@
-import functools
 import math
 
 import jax
@@ -20,6 +19,8 @@
 CH = 256
 TAPS = 27
 SHARE = 54
+PIECE = 56
+UP_ROWS = 32
 
 
 def slope_of(values, sigma):
@@ -239,7 +240,7 @@
                 ].astype(BF16)
 
 
-def kernel_grad_kernel(by_core, core_ref, act, block, later, out, table, flipped, sums):
+def tap_sums(act_of, block, later, table, flipped, sums):
     clear_border(table)
     for frame in range(FR):
         fill_own_table(table, frame, block[frame])
@@ -247,9 +248,8 @@
         fill_own_table(table, FR + frame, later[frame])
     for frame in range(FR):
         rows = ROWS * OWN
-        values = act[frame // 2, :, frame % 2] if by_core else act[frame]
         flipped[:, frame * rows : (frame + 1) * rows] = jnp.transpose(
-            own_columns(values).reshape(rows, CH)
+            own_columns(act_of(frame)).reshape(rows, CH)
         ).astype(BF16)
     sums[TAPS * CH :] = jnp.zeros((8, CH), F32)
     for tap_t in range(3):
@@ -259,14 +259,29 @@
             for tap_w in range(3):
                 at = (tap_t * 9 + tap_h * 3 + tap_w) * CH
                 sums[at : at + CH] = result[:, tap_w * CH : (tap_w + 1) * CH]
-    for core in range(2):
-
-        @pl.when(core_ref[0] == core)
-        def _(core=core):
-            for group in range(4):
-                for member in range(16):
-                    at = 16 * SHARE * (2 * group + core) + SHARE * member
-                    out[group * 16 + member] = sums[at : at + SHARE + 2].astype(BF16)
+
+
+def piece_of(sums, owner, member):
+    at = SHARE * member
+    start = pl.multiple_of(16 * SHARE * owner + at // 8 * 8, 8)
+    return sums[pl.ds(start, PIECE + 8)][at % 8 : at % 8 + PIECE]
+
+
+def second_grad_kernel(place, act, block, later, up, out, table, flipped, sums):
+    tap_sums(lambda frame: act[frame], block, later, table, flipped, sums)
+    for group in range(4):
+        for member in range(16):
+            chunk = member // 4 * 16 + group * 4 + member % 4
+            out[chunk, :UP_ROWS] = up[group * 16 + member]
+            out[chunk, UP_ROWS:] = piece_of(sums, 2 * group + place[0], member).astype(BF16)
+
+
+def first_grad_kernel(place, act, block, later, own, next_one, next_two, next_three, table, flipped, sums):
+    tap_sums(lambda frame: act[frame // 2, :, frame % 2], block, later, table, flipped, sums)
+    for step, out in enumerate((own, next_one, next_two, next_three)):
+        group = lax.rem(place[1] + step, 4)
+        for member in range(16):
+            out[member] = piece_of(sums, 2 * group + place[0], member).astype(BF16)
 
 
 def whole(shape):
@@ -305,9 +320,10 @@
 
 def shards(features, conv_first, conv_second, up_kernel, cotangent):
     core = lax.axis_index("core")
-    height = lax.axis_index("height")
+    height = 2 * lax.axis_index("z") + lax.axis_index("x_hi")
     width = lax.axis_index("width")
     core_arg = core.astype(jnp.int32).reshape(1)
+    place = jnp.stack([core, lax.axis_index("y")]).astype(jnp.int32)
     window = 8 * width + height
     columns = OWN * window - EDGE + jnp.arange(WIN)
     inside = ((columns >= 0) & (columns < 128)).astype(F32)
@@ -322,7 +338,7 @@
     windows = jnp.concatenate([padded[:, :-1], padded[:, 1:]], axis=2)
     windows = windows.reshape(2, 2, 8, WIN, CH).transpose(2, 1, 0, 3, 4).reshape(1, 16, 2, WIN, CH)
     windows = jnp.broadcast_to(windows, (2, 16, 2, WIN, CH)).reshape(32, 2, WIN, CH)
-    block = lax.all_to_all(windows, ("core", "height", "width"), 0, 0, tiled=True)
+    block = lax.all_to_all(windows, ("core", "z", "x_hi", "width"), 0, 0, tiled=True)
 
     paired = cotangent.reshape(2, 4, 64, 2 * CH)
     edge = jnp.where(width == 0, paired[:, :, 64 - EDGE :], paired[:, :, :EDGE])
@@ -334,7 +350,7 @@
     fine, block = lax.optimization_barrier((fine, block))
     block = block.reshape(2, ROWS, 2, WIN, CH)
     halo = shift(block[1], "y", 1)
-    mine = lax.all_to_all(fine, "height", 0, 0, tiled=True).reshape(8, 2, 2, 2, WIN, 2 * CH)
+    mine = lax.all_to_all(fine, ("z", "x_hi"), 0, 0, tiled=True).reshape(8, 2, 2, 2, WIN, 2 * CH)
 
     first_act, first_slope = call(
         first_kernel, (3,), (halo, block, conv_first, mask),
@@ -354,71 +370,73 @@
         [SMEM, whole(mine.shape), whole(mine.shape), whole(up_kernel.shape), whole(act_shape), whole(mask.shape)],
         [(act_shape, BF16)], [pltpu.VMEM((FR, ROWS + 1, 2, WIN, 4 * CH), BF16)], 16 * tap_flops,
     )
-    up_act, grad_sum = lax.optimization_barrier((up_act, grad_sum))
     later = shift(grad_sum[:2], "y", -1)
+    up_act, later = lax.optimization_barrier((up_act, later))
     up_part = call(
         up_grad_kernel, (), (core_arg, up_act, mine, other),
         [SMEM, whole(act_shape), whole(mine.shape), whole(mine.shape)],
         [((64, 32, CH), BF16)],
         [pltpu.VMEM((FR, ROWS + 1, 2, OWN, 4 * CH), BF16), pltpu.VMEM((CH, FR * ROWS * OWN), BF16)], 4 * tap_flops,
     )
-    everyone = ("y", "height", "width")
-    up_received = lax.all_to_all(up_part, everyone, 0, 0, tiled=True)
+    grad_scratch = [own_table, pltpu.VMEM((CH, FR * ROWS * OWN), BF16), pltpu.VMEM((TAPS * CH + 8, CH), F32)]
+    early = call(
+        second_grad_kernel, (), (place, first_act, grad_sum, later, up_part),
+        [SMEM, whole(act_shape), whole(act_shape), whole(later.shape), whole(up_part.shape)],
+        [((64, UP_ROWS + PIECE, CH), BF16)], grad_scratch, 14 * tap_flops,
+    )
+    early = lax.all_to_all(early, "z", 0, 0, tiled=True)
+
     grad_hidden = call(
         hidden_kernel, (3,), (grad_sum, later, first_slope, conv_second, mask),
         [whole(act_shape), whole(later.shape), whole(act_shape), tap_weights(), whole(mask.shape)],
         [(act_shape, BF16)], [table, total], 27 * tap_flops,
     )
     later_hidden = shift(grad_hidden[:2], "y", -1)
-
-    def kernel_grad(act, by_core, grad, after):
-        return call(
-            functools.partial(kernel_grad_kernel, by_core), (), (core_arg, act, grad, after),
-            [SMEM, whole(act.shape), whole(act_shape), whole(after.shape)],
-            [((64, SHARE + 2, CH), BF16)],
-            [own_table, pltpu.VMEM((CH, FR * ROWS * OWN), BF16), pltpu.VMEM((TAPS * CH + 8, CH), F32)], 14 * tap_flops,
-        )
-
-    second_part = kernel_grad(first_act, False, grad_sum, later)
-    second_part, up_received = lax.optimization_barrier((second_part, up_received))
-    second_received = lax.all_to_all(second_part, everyone, 0, 0, tiled=True)
+    blocks = call(
+        first_grad_kernel, (), (place, block, grad_hidden, later_hidden),
+        [SMEM, whole(block.shape), whole(act_shape), whole(later_hidden.shape)],
+        [((16, PIECE, CH), BF16)] * 4, grad_scratch, 14 * tap_flops,
+    )
+    arrived = [blocks[0]]
+    for step in (2, 1, 3):
+        arrived.append(lax.ppermute(blocks[step], "y", [(i, (i + step) % 4) for i in range(4)]))
+    tied_hidden, _ = lax.optimization_barrier((grad_hidden, blocks[0]))
     rows_out = call(
-        features_kernel, (3,), (core_arg, grad_hidden, later_hidden, grad_sum, conv_first),
+        features_kernel, (3,), (core_arg, tied_hidden, later_hidden, grad_sum, conv_first),
         [SMEM, whole(act_shape), whole(later_hidden.shape), whole(act_shape), tap_weights()],
         [((ROWS, 2, OWN, CH), BF16)], [own_table, pltpu.VMEM((2 * ROWS * OWN, CH), F32)], 7 * tap_flops,
     )
-    first_part = kernel_grad(block, True, grad_hidden, later_hidden)
-    first_part, rows_out, second_received = lax.optimization_barrier((first_part, rows_out, second_received))
-    first_received = lax.all_to_all(first_part, everyone, 0, 0, tiled=True)
-    rows_out, first_received = lax.optimization_barrier((rows_out, first_received))
-    returned = lax.all_to_all(rows_out, ("height", "width"), 0, 0, tiled=True)
-    returned = returned.reshape(8, 2, 2, OWN, CH).transpose(2, 1, 0, 3, 4)
-    grad_features = returned.reshape(2, 1, 128, CH)
+
+    early = jnp.sum(early.reshape(4, 16, UP_ROWS + PIECE, CH).astype(F32), axis=0).astype(BF16)
+    early = lax.all_to_all(early, ("y", "x_hi", "width"), 0, 0, tiled=True)
+    first_sum = sum(value.astype(F32) for value in arrived).astype(BF16)
+    late = jnp.concatenate([rows_out.reshape(16, 2 * OWN, CH), first_sum], axis=1)
+    late, early = lax.optimization_barrier((late, early))
+    late = lax.all_to_all(late, ("z", "x_hi", "width"), 0, 0, tiled=True)
 
     factor = 1.0 / math.sqrt(32768)
-
-    def share_of(received, rows):
-        return (jnp.sum(received[:, :rows].astype(F32), axis=0) * factor).reshape(-1)
-
+    early = jnp.sum(early.astype(F32), axis=0) * factor
+    returned = late[:, : 2 * OWN].reshape(8, 2, 2, OWN, CH).transpose(2, 1, 0, 3, 4)
+    first_share = jnp.sum(late[:, 2 * OWN : 2 * OWN + SHARE].astype(F32), axis=0) * factor
     return (
-        grad_features,
-        share_of(first_received, SHARE),
-        share_of(second_received, SHARE),
-        share_of(up_received, 32),
+        returned.reshape(2, 1, 128, CH),
+        first_share.reshape(-1),
+        early[UP_ROWS : UP_ROWS + SHARE].reshape(-1),
+        early[:UP_ROWS].reshape(-1),
     )
 
 
 def solution(mesh):
-    names = ("y", "core", "height", "width")
-    split = Mesh(mesh.devices.reshape(4, 2, 8, 2), names)
-    tm = ("y", "core")
+    names = ("y", "core", "z", "x_hi", "width")
+    split = Mesh(mesh.devices.reshape(4, 2, 4, 2, 2), names)
+    tm, height = ("y", "core"), ("z", "x_hi")
     in_specs = (
-        P(tm, ("height", "width"), None, None),
+        P(tm, (*height, "width"), None, None),
         P(),
         P(),
         P(),
-        P(tm, "height", "width", None),
+        P(tm, height, "width", None),
     )
     flat = P(names)
-    out_specs = (P(tm, ("height", "width"), None, None), flat, flat, flat)
+    out_specs = (P(tm, (*height, "width"), None, None), flat, flat, flat)
     return jax.shard_map(shards, mesh=split, in_specs=in_specs, out_specs=out_specs, check_vma=False)

time: 197 us -> 165 us (0.84)
  waiting for transfers between devices: 87.3 us -> 61 us
  starting transfers between devices: 59 us -> 43.9 us
  local copies, waits for them, and re-layouts: 12.6 us -> 19 us
  other arithmetic: 3.89 us -> 7.64 us
    all_to_all x6 -> x5, starting transfers between devices: 47 us -> 26.8 us  [the longest x1 7.87 us: shards(): lax.all_to_all(windows, ('core', 'z', 'x_hi', 'width'), 0, 0, tiled=True)]
    ppermute x4, waiting for transfers between devices: 46 us -> 28.4 us  [shift(): lax.ppermute(value, axis, [(i, i + step) for i in range(count) if 0 <= i...]
    all_to_all x6 -> x5, waiting for transfers between devices: 41.4 us -> 32.6 us  [the longest x1 11.5 us: shards(): lax.all_to_all(windows, ('core', 'z', 'x_hi', 'width'), 0, 0, tiled=True)]
    unnamed x17 -> x38, local copies, waits for them, and re-layouts: 5.62 us -> 11.3 us
    ppermute x0 -> x3, starting transfers between devices: none -> 5.05 us  [shards(): lax.ppermute(blocks[step], 'y', [(i, (i + step) % 4) for i in range(4)])]
  transfers between devices with their start and end apart: 12 -> 14, of which waited for: 8 -> 9; matrix products, arithmetic and copies ran while one was open for 4% -> 7% of each run, Pallas kernels for 13% -> 13%
where the time goes in v5:
time: 165 us; the launch traced here: 164 us
  waiting for transfers between devices  61 us (37%)
  starting transfers between devices  43.9 us (27%)
  Pallas kernels  31.6 us (19%)
  local copies, waits for them, and re-layouts  19 us (12%)
  other arithmetic  7.64 us (5%)
    pallas_call x8, Pallas kernels, call(): pl.pallas_call(kernel, out_shape=shapes[0] if single else shapes, grid=gr...  31.6 us
    ppermute x4, waiting for transfers between devices, shift(): lax.ppermute(value, axis, [(i, i + step) for i in range(count) if 0 <= i...  28.4 us
    all_to_all x1, waiting for transfers between devices, shards(): lax.all_to_all(windows, ('core', 'z', 'x_hi', 'width'), 0, 0, tiled=True)  11.5 us
    unnamed x38, local copies, waits for them, and re-layouts  11.3 us
    ppermute x4, starting transfers between devices, shift(): lax.ppermute(value, axis, [(i, i + step) for i in range(count) if 0 <= i...  10.4 us
    all_to_all x1, waiting for transfers between devices, shards(): early = lax.all_to_all(early, 'z', 0, 0, tiled=True)  8.52 us
    all_to_all x1, waiting for transfers between devices, shards(): late = lax.all_to_all(late, ('z', 'x_hi', 'width'), 0, 0, tiled=True)  7.94 us
    all_to_all x1, starting transfers between devices, shards(): lax.all_to_all(windows, ('core', 'z', 'x_hi', 'width'), 0, 0, tiled=True)  7.87 us
  transfers between devices with their start and end apart: 14, of which 9 were waited for; matrix products, arithmetic and copies ran while one was open for 7% of the time, Pallas kernels for 13%

profile of v5, /device:TPU:0, one launch (start us, length us, event | category | flops | bytes accessed | tf_op | source)
XLA Modules:
  0.0 164.3 jit_solution(14686878292044087747)
XLA Ops:
  5.4 7.9 %all-to-all-start = ((bf16[32,2,16,256]{3,2,1,0:T(8,128)(2,1)}), bf16[32,2,16,256]{3,2,1,0:T(8,128)(2,1)S(1)}, u32[]{:S(2)}, u32[]{:S(2)}) async-start(bf16[32,2,16,256]{3,2,1,0:T(8,128)(2,1)} %bitcast.8), calls=%async_computation | async-start | bytes 1048576 | tf_op jit(solution)/shard_map/all_to_all | solution.py:341
  13.8 11.5 %all-to-all-done = bf16[32,2,16,256]{3,2,1,0:T(8,128)(2,1)S(1)} async-done(((bf16[32,2,16,256]{3,2,1,0:T(8,128)(2,1)}), bf16[32,2,16,256]{3,2,1,0:T(8,128)(2,1)S(1)}, u32[]{:S(2)}, u32[]{:S(2)}) %all-to-all-start) | async-done | bytes 524320 | tf_op jit(solution)/shard_map/all_to_all | solution.py:341
  26.4 3.6 %all-to-all-start.1 = ((bf16[8,2,4,16,512]{4,3,2,1,0:T(8,128)(2,1)}), bf16[8,2,4,16,512]{4,3,2,1,0:T(8,128)(2,1)S(1)}, u32[]{:S(2)}, u32[]{:S(2)}) async-start(bf16[8,2,4,16,512]{4,3,2,1,0:T(8,128)(2,1)} %copy.18), calls=%async_computation.1 | async-start | bytes 2097152 | tf_op jit(solution)/shard_map/all_to_all | solution.py:353
  30.0 3.5 %collective-permute-start.1 = (bf16[16,2,16,256]{3,2,1,0:T(8,128)(2,1)S(1)}, bf16[16,2,16,256]{3,2,1,0:T(8,128)(2,1)S(1)}, u32[]{:S(2)}, u32[]{:S(2)}) collective-permute-start(bf16[16,2,16,256]{3,2,1,0:T(8,128)(2,1)S(1)} %slice.49), channel_id=1, source_target_pairs={{0,32},{32,64},{64,96},{1,33},{33,65},{65,97},{2,34},{34,66},{66,9... | collective-permute-start | bytes 786440 | tf_op jit(solution)/shard_map/ppermute | solution.py:318
  33.5 5.1 %collective-permute-done.1.halo = bf16[16,2,16,256]{3,2,1,0:T(8,128)(2,1)S(1)} collective-permute-done((bf16[16,2,16,256]{3,2,1,0:T(8,128)(2,1)S(1)}, bf16[16,2,16,256]{3,2,1,0:T(8,128)(2,1)S(1)}, u32[]{:S(2)}, u32[]{:S(2)}) %collective-permute-start.1) | collective-permute-done | bytes 262176 | tf_op jit(solution)/shard_map/ppermute | solution.py:318
  38.6 2.0 %copy-done = bf16[3,3,3,256,256]{4,3,2,1,0:T(8,128)(2,1)S(1)} copy-done((bf16[3,3,3,256,256]{4,3,2,1,0:T(8,128)(2,1)S(1)}, bf16[3,3,3,256,256]{4,3,2,1,0:T(8,128)(2,1)}, u32[]{:S(2)}) %copy-start) | copy-done | bytes 3538968
  40.6 5.0 %shard_map.84 = (bf16[4,16,16,256]{3,2,1,0:T(8,128)(2,1)S(1)}, f32[4,16,16,256]{3,2,1,0:T(8,128)S(1)}) custom-call(bf16[16,2,16,256]{3,2,1,0:T(8,128)(2,1)S(1)} %collective-permute-done.1.halo, bf16[2,16,2,16,256]{4,3,2,1,0:T(8,128)(2,1)S(1)} %bitcast.30, bf16[3,3,3,256,256]{4,3,2,1,0:T(8,128)(2,1)S(1)} %copy-done, f32[16,256]{1,0:T(8,128)S(1)} %broadcast_in_dim.19.mask), custom_call_target="tpu_custom_call" | custom-call | flops 3623878656 | bytes 5914624 | tf_op jit(solution)/shard_map/pallas_call | solution.py:304
  47.6 4.2 %collective-permute-start.3 = (bf16[2,16,16,256]{3,2,1,0:T(8,128)(2,1)}, bf16[2,16,16,256]{3,2,1,0:T(8,128)(2,1)S(1)}, u32[]{:S(2)}, u32[]{:S(2)}) collective-permute-start(bf16[2,16,16,256]{3,2,1,0:T(8,128)(2,1)} %slice.50), channel_id=1, source_target_pairs={{0,32},{32,64},{64,96},{1,33},{33,65},{65,97},{2,34},{34,66},{66,9... | collective-permute-start | bytes 786440 | tf_op jit(solution)/shard_map/ppermute | solution.py:318
  51.8 6.4 %collective-permute-done.3.halo = bf16[2,16,16,256]{3,2,1,0:T(8,128)(2,1)S(1)} collective-permute-done((bf16[2,16,16,256]{3,2,1,0:T(8,128)(2,1)}, bf16[2,16,16,256]{3,2,1,0:T(8,128)(2,1)S(1)}, u32[]{:S(2)}, u32[]{:S(2)}) %collective-permute-start.3) | collective-permute-done | bytes 262176 | tf_op jit(solution)/shard_map/ppermute | solution.py:318
  58.3 6.1 %shard_map.85 = (f32[4,16,16,256]{3,2,1,0:T(8,128)S(1)}, bf16[4,16,16,256]{3,2,1,0:T(8,128)(2,1)S(1)}) custom-call(bf16[2,16,16,256]{3,2,1,0:T(8,128)(2,1)S(1)} %collective-permute-done.3.halo, bf16[4,16,16,256]{3,2,1,0:T(8,128)(2,1)S(1)} %get-tuple-element.25.block.act, bf16[2,16,2,16,256]{4,3,2,1,0:T(8,128)(2,1)S(1)} %bitcast.31, ...), custom_call_target="tpu_custom_call" | custom-call | flops 3623878656 | bytes 6422528 | tf_op jit(solution)/shard_map/pallas_call | solution.py:304
  65.2 3.5 %shard_map.86.block.grad_sum = bf16[4,16,16,256]{3,2,1,0:T(8,128)(2,1)S(1)} custom-call(s32[1]{0:T(128)} %bitcast.core_ref, bf16[8,2,2,2,16,512]{5,4,3,2,1,0:T(8,128)(2,1)S(1)} %bitcast.28, bf16[8,2,2,2,16,512]{5,4,3,2,1,0:T(8,128)(2,1)S(1)} %collective-permute-done.2.other, bf16[4,4,256,256]{3,2,1,0:T(8,128)(2,1)S(1)} %copy-done.15, ...), custom_call_target="tpu_custom_call" | custom-call | flops 2147483648 | bytes 5783556 | tf_op jit(solution)/shard_map/pallas_call | solution.py:304
  71.0 9.0 %collective-permute-done.4.later = bf16[2,16,16,256]{3,2,1,0:T(8,128)(2,1)S(1)} collective-permute-done((bf16[2,16,16,256]{3,2,1,0:T(8,128)(2,1)}, bf16[2,16,16,256]{3,2,1,0:T(8,128)(2,1)S(1)}, u32[]{:S(2)}, u32[]{:S(2)}) %collective-permute-start.4) | collective-permute-done | bytes 262176 | tf_op jit(solution)/shard_map/ppermute | solution.py:318
  82.9 4.7 %shard_map.91 = bf16[64,88,256]{2,1,0:T(8,128)(2,1)} custom-call(s32[2]{0:T(128)S(1)} %pad_add_fusion.place, bf16[4,16,16,256]{3,2,1,0:T(8,128)(2,1)S(1)} %copy-done.13, bf16[4,16,16,256]{3,2,1,0:T(8,128)(2,1)S(1)} %shard_map.86.block.grad_sum, bf16[2,16,16,256]{3,2,1,0:T(8,128)(2,1)S(1)} %collective-permute-done.4.later, bf16[64,32,256]{2,1,0:T(8,128)(2,1)S(1)} %shard_map.90.up), custom_call_target="tpu_custom_call" | custom-call | flops 1879048192 | bytes 5242888 | tf_op jit(solution)/shard_map/pallas_call | solution.py:304
  87.5 4.7 %all-to-all-start.2 = ((bf16[64,88,256]{2,1,0:T(8,128)(2,1)}), bf16[64,88,256]{2,1,0:T(8,128)(2,1)}, u32[]{:S(2)}, u32[]{:S(2)}) async-start(bf16[64,88,256]{2,1,0:T(8,128)(2,1)} %shard_map.91), calls=%async_computation.2 | async-start | bytes 5767168 | tf_op jit(solution)/shard_map/all_to_all | solution.py:387
  94.3 4.8 %shard_map.87.block = bf16[4,16,16,256]{3,2,1,0:T(8,128)(2,1)S(1)} custom-call(bf16[4,16,16,256]{3,2,1,0:T(8,128)(2,1)S(1)} %shard_map.86.block.grad_sum, bf16[2,16,16,256]{3,2,1,0:T(8,128)(2,1)S(1)} %collective-permute-done.4.later, f32[4,16,16,256]{3,2,1,0:T(8,128)S(1)} %copy-done.17, bf16[3,3,3,256,256]{4,3,2,1,0:T(8,128)(2,1)S(1)} %copy-done.14, ...), custom_call_target="tpu_custom_call" | custom-call | flops 3623878656 | bytes 5914624 | tf_op jit(solution)/shard_map/pallas_call | solution.py:304
  100.4 7.9 %collective-permute-done.5.later = bf16[2,16,16,256]{3,2,1,0:T(8,128)(2,1)S(1)} collective-permute-done((bf16[2,16,16,256]{3,2,1,0:T(8,128)(2,1)S(1)}, bf16[2,16,16,256]{3,2,1,0:T(8,128)(2,1)S(1)}, u32[]{:S(2)}, u32[]{:S(2)}) %collective-permute-start.5) | collective-permute-done | bytes 262176 | tf_op jit(solution)/shard_map/ppermute | solution.py:318
  108.3 4.0 %shard_map.88 = (bf16[16,56,256]{2,1,0:T(8,128)(2,1)S(1)}, bf16[16,56,256]{2,1,0:T(8,128)(2,1)}, bf16[16,56,256]{2,1,0:T(8,128)(2,1)}, bf16[16,56,256]{2,1,0:T(8,128)(2,1)}) custom-call(s32[2]{0:T(128)S(1)} %pad_add_fusion.place, bf16[2,16,2,16,256]{4,3,2,1,0:T(8,128)(2,1)S(1)} %bitcast.32, bf16[4,16,16,256]{3,2,1,0:T(8,128)(2,1)S(1)} %shard_map.87.block, ...), custom_call_target="tpu_custom_call" | custom-call | flops 1879048192 | bytes 3145736 | tf_op jit(solution)/shard_map/pallas_call | solution.py:304
  115.1 3.0 %collective-permute-start.6 = (bf16[16,56,256]{2,1,0:T(8,128)(2,1)}, bf16[16,56,256]{2,1,0:T(8,128)(2,1)}, u32[]{:S(2)}, u32[]{:S(2)}) collective-permute-start(bf16[16,56,256]{2,1,0:T(8,128)(2,1)} %get-tuple-element.32), channel_id=1, source_target_pairs={{0,64},{32,96},{64,0},{96,32},{1,65},{33,97},{65,1},{97,33},{2,66}... | collective-permute-start | bytes 1376264 | tf_op jit(solution)/shard_map/ppermute | solution.py:402
  118.1 8.5 %all-to-all-done.2 = bf16[64,88,256]{2,1,0:T(8,128)(2,1)} async-done(((bf16[64,88,256]{2,1,0:T(8,128)(2,1)}), bf16[64,88,256]{2,1,0:T(8,128)(2,1)}, u32[]{:S(2)}, u32[]{:S(2)}) %all-to-all-start.2) | async-done | bytes 2883616 | tf_op jit(solution)/shard_map/all_to_all | solution.py:387
  126.6 3.5 %reduce_sum.30 = bf16[16,88,256]{2,1,0:T(8,128)(2,1)} reduce(bf16[4,16,88,256]{3,2,1,0:T(8,128)(2,1)} %bitcast.13, bf16[]{:T(256)} %constant.30.clone.1), dimensions={0}, to_apply=%region_0.1 | reduce | flops 1081344 | bytes 3604482 | tf_op jit(solution)/shard_map/reduce_sum | solution.py:410
  130.1 7.0 %all-to-all-start.3 = ((bf16[16,88,256]{2,1,0:T(8,128)(2,1)}), bf16[16,88,256]{2,1,0:T(8,128)(2,1)}, u32[]{:S(2)}, u32[]{:S(2)}) async-start(bf16[16,88,256]{2,1,0:T(8,128)(2,1)} %reduce_sum.30), calls=%async_computation.3 | async-start | bytes 1441792 | tf_op jit(solution)/shard_map/all_to_all | solution.py:411
  144.5 4.3 %all-to-all-done.3 = bf16[16,88,256]{2,1,0:T(8,128)(2,1)} async-done(((bf16[16,88,256]{2,1,0:T(8,128)(2,1)}), bf16[16,88,256]{2,1,0:T(8,128)(2,1)}, u32[]{:S(2)}, u32[]{:S(2)}) %all-to-all-start.3) | async-done | bytes 720928 | tf_op jit(solution)/shard_map/all_to_all | solution.py:411
  148.8 3.6 %all-to-all-start.4 = ((bf16[16,72,256]{2,1,0:T(8,128)(2,1)}), bf16[16,72,256]{2,1,0:T(8,128)(2,1)S(1)}, u32[]{:S(2)}, u32[]{:S(2)}) async-start(bf16[16,72,256]{2,1,0:T(8,128)(2,1)} %pad_maximum_fusion), calls=%async_computation.4 | async-start | bytes 1179648 | tf_op jit(solution)/shard_map/all_to_all | solution.py:415
  155.0 7.9 %all-to-all-done.4 = bf16[16,72,256]{2,1,0:T(8,128)(2,1)S(1)} async-done(((bf16[16,72,256]{2,1,0:T(8,128)(2,1)}), bf16[16,72,256]{2,1,0:T(8,128)(2,1)S(1)}, u32[]{:S(2)}, u32[]{:S(2)}) %all-to-all-start.4) | async-done | bytes 589856 | tf_op jit(solution)/shard_map/all_to_all | solution.py:415
  (81 shorter events, 31.6 us)
Async XLA Ops:
  1.9 11.4 %collective-permute-start = (bf16[2,4,4,512]{3,2,1,0:T(4,128)(2,1)S(1)}, bf16[2,4,4,512]{3,2,1,0:T(4,128)(2,1)S(1)}, u32[]{:S(2)}, u32[]{:S(2)}) collective-permute-start(bf16[2,4,4,512]{3,2,1,0:T(4,128)(2,1)S(1)} %slice_select_fusion), channel_id=1, source_target_pairs={{0,1},{1,0},{2,3},{3,2},{4,5},{5,4},{6,7},{7,6},{8,9},{9,8},{10,11... | collective-permute-start | bytes 98312 | tf_op jit(solution)/shard_map/ppermute | solution.py:345
  5.4 19.8 %all-to-all-start = ((bf16[32,2,16,256]{3,2,1,0:T(8,128)(2,1)}), bf16[32,2,16,256]{3,2,1,0:T(8,128)(2,1)S(1)}, u32[]{:S(2)}, u32[]{:S(2)}) async-start(bf16[32,2,16,256]{3,2,1,0:T(8,128)(2,1)} %bitcast.8), calls=%async_computation | async-start | bytes 1048576 | tf_op jit(solution)/shard_map/all_to_all | solution.py:341
  26.4 20.6 %all-to-all-start.1 = ((bf16[8,2,4,16,512]{4,3,2,1,0:T(8,128)(2,1)}), bf16[8,2,4,16,512]{4,3,2,1,0:T(8,128)(2,1)S(1)}, u32[]{:S(2)}, u32[]{:S(2)}) async-start(bf16[8,2,4,16,512]{4,3,2,1,0:T(8,128)(2,1)} %copy.18), calls=%async_computation.1 | async-start | bytes 2097152 | tf_op jit(solution)/shard_map/all_to_all | solution.py:353
  30.0 8.6 %collective-permute-start.1 = (bf16[16,2,16,256]{3,2,1,0:T(8,128)(2,1)S(1)}, bf16[16,2,16,256]{3,2,1,0:T(8,128)(2,1)S(1)}, u32[]{:S(2)}, u32[]{:S(2)}) collective-permute-start(bf16[16,2,16,256]{3,2,1,0:T(8,128)(2,1)S(1)} %slice.49), channel_id=1, source_target_pairs={{0,32},{32,64},{64,96},{1,33},{33,65},{65,97},{2,34},{34,66},{66,9... | collective-permute-start | bytes 786440 | tf_op jit(solution)/shard_map/ppermute | solution.py:318
  38.6 2.0 %copy-start = (bf16[3,3,3,256,256]{4,3,2,1,0:T(8,128)(2,1)S(1)}, bf16[3,3,3,256,256]{4,3,2,1,0:T(8,128)(2,1)}, u32[]{:S(2)}) copy-start(bf16[3,3,3,256,256]{4,3,2,1,0:T(8,128)(2,1)} %weights.9) | copy-start | bytes 10616836
  46.6 17.8 %copy-start.12 = (bf16[4,16,16,256]{3,2,1,0:T(8,128)(2,1)}, bf16[4,16,16,256]{3,2,1,0:T(8,128)(2,1)S(1)}, u32[]{:S(2)}) copy-start(bf16[4,16,16,256]{3,2,1,0:T(8,128)(2,1)S(1)} %get-tuple-element.25.block.act) | copy-start | bytes 1572868
  46.9 18.3 %collective-permute-start.2 = (bf16[8,2,2,2,16,512]{5,4,3,2,1,0:T(8,128)(2,1)S(1)}, bf16[8,2,2,2,16,512]{5,4,3,2,1,0:T(8,128)(2,1)S(1)}, u32[]{:S(2)}, u32[]{:S(2)}) collective-permute-start(bf16[8,2,2,2,16,512]{5,4,3,2,1,0:T(8,128)(2,1)S(1)} %bitcast.27), channel_id=1, source_target_pairs={{0,16},{16,0},{1,17},{17,1},{2,18},{18,2},{3,19},{19,3},{4,20},{20... | collective-permute-start | bytes 3145736 | tf_op jit(solution)/shard_map/ppermute | solution.py:362
  47.6 10.6 %collective-permute-start.3 = (bf16[2,16,16,256]{3,2,1,0:T(8,128)(2,1)}, bf16[2,16,16,256]{3,2,1,0:T(8,128)(2,1)S(1)}, u32[]{:S(2)}, u32[]{:S(2)}) collective-permute-start(bf16[2,16,16,256]{3,2,1,0:T(8,128)(2,1)} %slice.50), channel_id=1, source_target_pairs={{0,32},{32,64},{64,96},{1,33},{33,65},{65,97},{2,34},{34,66},{66,9... | collective-permute-start | bytes 786440 | tf_op jit(solution)/shard_map/ppermute | solution.py:318
  51.8 13.4 %copy-start.15 = (bf16[4,4,256,256]{3,2,1,0:T(8,128)(2,1)S(1)}, bf16[4,4,256,256]{3,2,1,0:T(8,128)(2,1)}, u32[]{:S(2)}) copy-start(bf16[4,4,256,256]{3,2,1,0:T(8,128)(2,1)} %weights.7) | copy-start | bytes 6291460
  68.7 23.6 %copy-start.2 = (bf16[4,16,16,256]{3,2,1,0:T(8,128)(2,1)}, bf16[4,16,16,256]{3,2,1,0:T(8,128)(2,1)S(1)}, u32[]{:S(2)}) copy-start(bf16[4,16,16,256]{3,2,1,0:T(8,128)(2,1)S(1)} %shard_map.86.block.grad_sum) | copy-start | bytes 1572868
  69.5 10.6 %collective-permute-start.4 = (bf16[2,16,16,256]{3,2,1,0:T(8,128)(2,1)}, bf16[2,16,16,256]{3,2,1,0:T(8,128)(2,1)S(1)}, u32[]{:S(2)}, u32[]{:S(2)}) collective-permute-start(bf16[2,16,16,256]{3,2,1,0:T(8,128)(2,1)} %slice.63), channel_id=1, source_target_pairs={{32,0},{64,32},{96,64},{33,1},{65,33},{97,65},{34,2},{66,34},{98,6... | collective-permute-start | bytes 786440 | tf_op jit(solution)/shard_map/ppermute | solution.py:318
  87.5 4.8 %copy-start.17 = (f32[4,16,16,256]{3,2,1,0:T(8,128)S(1)}, f32[4,16,16,256]{3,2,1,0:T(8,128)}, u32[]{:S(2)}) copy-start(f32[4,16,16,256]{3,2,1,0:T(8,128)} %copy-done.16) | copy-start | bytes 3145732
  87.5 39.1 %all-to-all-start.2 = ((bf16[64,88,256]{2,1,0:T(8,128)(2,1)}), bf16[64,88,256]{2,1,0:T(8,128)(2,1)}, u32[]{:S(2)}, u32[]{:S(2)}) async-start(bf16[64,88,256]{2,1,0:T(8,128)(2,1)} %shard_map.91), calls=%async_computation.2 | async-start | bytes 5767168 | tf_op jit(solution)/shard_map/all_to_all | solution.py:387
  92.3 2.0 %copy-start.14 = (bf16[3,3,3,256,256]{4,3,2,1,0:T(8,128)(2,1)S(1)}, bf16[3,3,3,256,256]{4,3,2,1,0:T(8,128)(2,1)}, u32[]{:S(2)}) copy-start(bf16[3,3,3,256,256]{4,3,2,1,0:T(8,128)(2,1)} %weights.8) | copy-start | bytes 10616836
  99.1 13.2 %copy-start.4 = (bf16[4,16,16,256]{3,2,1,0:T(8,128)(2,1)}, bf16[4,16,16,256]{3,2,1,0:T(8,128)(2,1)S(1)}, u32[]{:S(2)}) copy-start(bf16[4,16,16,256]{3,2,1,0:T(8,128)(2,1)S(1)} %shard_map.87.block) | copy-start | bytes 1572868
  99.1 9.2 %collective-permute-start.5 = (bf16[2,16,16,256]{3,2,1,0:T(8,128)(2,1)S(1)}, bf16[2,16,16,256]{3,2,1,0:T(8,128)(2,1)S(1)}, u32[]{:S(2)}, u32[]{:S(2)}) collective-permute-start(bf16[2,16,16,256]{3,2,1,0:T(8,128)(2,1)S(1)} %slice.64), channel_id=1, source_target_pairs={{32,0},{64,32},{96,64},{33,1},{65,33},{97,65},{34,2},{66,34},{98,6... | collective-permute-start | bytes 786440 | tf_op jit(solution)/shard_map/ppermute | solution.py:318
  108.3 4.0 %copy-start.10 = (bf16[2,16,16,256]{3,2,1,0:T(8,128)(2,1)}, bf16[2,16,16,256]{3,2,1,0:T(8,128)(2,1)S(1)}, u32[]{:S(2)}) copy-start(bf16[2,16,16,256]{3,2,1,0:T(8,128)(2,1)S(1)} %collective-permute-done.5.later) | copy-start | bytes 786436
  113.0 29.1 %collective-permute-start.8 = (bf16[16,56,256]{2,1,0:T(8,128)(2,1)}, bf16[16,56,256]{2,1,0:T(8,128)(2,1)}, u32[]{:S(2)}, u32[]{:S(2)}) collective-permute-start(bf16[16,56,256]{2,1,0:T(8,128)(2,1)} %get-tuple-element.34), channel_id=1, source_target_pairs={{0,96},{32,0},{64,32},{96,64},{1,97},{33,1},{65,33},{97,65},{2,98}... | collective-permute-start | bytes 1376264 | tf_op jit(solution)/shard_map/ppermute | solution.py:402
  114.1 28.0 %collective-permute-start.7 = (bf16[16,56,256]{2,1,0:T(8,128)(2,1)}, bf16[16,56,256]{2,1,0:T(8,128)(2,1)}, u32[]{:S(2)}, u32[]{:S(2)}) collective-permute-start(bf16[16,56,256]{2,1,0:T(8,128)(2,1)} %get-tuple-element.33), channel_id=1, source_target_pairs={{0,32},{32,64},{64,96},{96,0},{1,33},{33,65},{65,97},{97,1},{2,34}... | collective-permute-start | bytes 1376264 | tf_op jit(solution)/shard_map/ppermute | solution.py:402
  115.1 27.1 %collective-permute-start.6 = (bf16[16,56,256]{2,1,0:T(8,128)(2,1)}, bf16[16,56,256]{2,1,0:T(8,128)(2,1)}, u32[]{:S(2)}, u32[]{:S(2)}) collective-permute-start(bf16[16,56,256]{2,1,0:T(8,128)(2,1)} %get-tuple-element.32), channel_id=1, source_target_pairs={{0,64},{32,96},{64,0},{96,32},{1,65},{33,97},{65,1},{97,33},{2,66}... | collective-permute-start | bytes 1376264 | tf_op jit(solution)/shard_map/ppermute | solution.py:402
  126.6 10.5 %copy-start.1 = (bf16[3,3,3,256,256]{4,3,2,1,0:T(8,128)(2,1)S(1)}, bf16[3,3,3,256,256]{4,3,2,1,0:T(8,128)(2,1)}, u32[]{:S(2)}) copy-start(bf16[3,3,3,256,256]{4,3,2,1,0:T(8,128)(2,1)} %weights.9) | copy-start | bytes 10616836
  130.1 18.8 %all-to-all-start.3 = ((bf16[16,88,256]{2,1,0:T(8,128)(2,1)}), bf16[16,88,256]{2,1,0:T(8,128)(2,1)}, u32[]{:S(2)}, u32[]{:S(2)}) async-start(bf16[16,88,256]{2,1,0:T(8,128)(2,1)} %reduce_sum.30), calls=%async_computation.3 | async-start | bytes 1441792 | tf_op jit(solution)/shard_map/all_to_all | solution.py:411
  140.1 2.0 %copy-start.9 = (bf16[16,56,256]{2,1,0:T(8,128)(2,1)S(1)}, bf16[16,56,256]{2,1,0:T(8,128)(2,1)}, u32[]{:S(2)}) copy-start(bf16[16,56,256]{2,1,0:T(8,128)(2,1)} %copy-done.8) | copy-start | bytes 1376260
  148.8 14.0 %all-to-all-start.4 = ((bf16[16,72,256]{2,1,0:T(8,128)(2,1)}), bf16[16,72,256]{2,1,0:T(8,128)(2,1)S(1)}, u32[]{:S(2)}, u32[]{:S(2)}) async-start(bf16[16,72,256]{2,1,0:T(8,128)(2,1)} %pad_maximum_fusion), calls=%async_computation.4 | async-start | bytes 1179648 | tf_op jit(solution)/shard_map/all_to_all | solution.py:415
  (8 other events, 8.4 us)

commit v6 on v5

--- a/solution.py
+++ b/solution.py
@@ -62,121 +62,108 @@
     return pltpu.roll(block.astype(F32), WIN - EDGE, axis=1)[:, :OWN]
 
 
-def first_kernel(halo, block, weights, mask, act, slope, table, total):
-    step = pl.program_id(0)
-
-    @pl.when(step == 0)
-    def _():
-        clear_border(table)
-        for frame in range(2):
-            fill_table(table, frame, halo[:, frame], True)
-        for frame in range(FR):
-            fill_table(table, 2 + frame, block[frame // 2, :, frame % 2], True)
-        total[...] = jnp.zeros_like(total)
-
-    for tap in range(3):
-        lhs = table[pl.ds(step, FR), tap : tap + ROWS].reshape(FR * ROWS * WIN, 3 * CH)
-        total[...] += nn(lhs, weights[0, tap].reshape(3 * CH, CH))
-
-    @pl.when(step == 2)
-    def _():
-        inside = mask[...]
-        for frame in range(FR):
-            rows = ROWS * WIN
-            values = total[frame * rows : (frame + 1) * rows].reshape(ROWS, WIN, CH)
-            sigma = jax.nn.sigmoid(values)
-            act[frame] = (values * sigma * inside).astype(BF16)
-            slope[frame] = slope_of(values, sigma)
-
-
-def second_kernel(halo, block, features, weights, summed, up_act, table, total):
-    step = pl.program_id(0)
-
-    @pl.when(step == 0)
-    def _():
-        clear_border(table)
-        for frame in range(2):
-            fill_table(table, frame, halo[frame], True)
-        for frame in range(FR):
-            fill_table(table, 2 + frame, block[frame], True)
-        total[...] = jnp.zeros_like(total)
-
-    for tap in range(3):
-        lhs = table[pl.ds(step, FR), tap : tap + ROWS].reshape(FR * ROWS * WIN, 3 * CH)
-        total[...] += nn(lhs, weights[0, tap].reshape(3 * CH, CH))
-
-    @pl.when(step == 2)
-    def _():
-        for frame in range(FR):
-            rows = ROWS * WIN
-            values = total[frame * rows : (frame + 1) * rows].reshape(ROWS, WIN, CH)
-            values = values + features[frame // 2, :, frame % 2].astype(F32)
-            summed[frame] = values
-            up_act[frame] = (values * jax.nn.sigmoid(values)).astype(BF16)
-
-
-def hidden_kernel(block, later, slope, weights, mask, grad_hidden, table, total):
-    step = pl.program_id(0)
-
-    @pl.when(step == 0)
-    def _():
-        clear_border(table)
-        for frame in range(FR):
-            fill_table(table, frame, block[frame], False)
-        for frame in range(2):
-            fill_table(table, FR + frame, later[frame], False)
-        total[...] = jnp.zeros_like(total)
-
-    for tap in range(3):
-        part = None
-        for column in range(3):
-            lhs = table[pl.ds(2 - step, FR), 2 - tap : 2 - tap + ROWS, :, column * CH : (column + 1) * CH]
-            more = nt(lhs.reshape(FR * ROWS * WIN, CH), weights[0, tap, column])
-            part = more if part is None else part + more
-        total[...] += part
-
-    @pl.when(step == 2)
-    def _():
-        inside = mask[...]
-        for frame in range(FR):
-            rows = ROWS * WIN
-            values = total[frame * rows : (frame + 1) * rows].reshape(ROWS, WIN, CH)
-            grad_hidden[frame] = (values * slope[frame] * inside).astype(BF16)
-
-
-def features_kernel(core_ref, block, later, grad_sum, weights, grad_features, table, total):
-    step = pl.program_id(0)
+def fetch(weights, held, arrived):
+    copies = [pltpu.make_async_copy(weights.at[tap], held.at[tap], arrived.at[tap]) for tap in range(3)]
+    for copy in copies:
+        copy.start()
+    return copies
+
+
+def forward_taps(table, held, copies, total):
+    for tap_t in range(3):
+        copies[tap_t].wait()
+        for tap_h in range(3):
+            lhs = table[tap_t : tap_t + FR, tap_h : tap_h + ROWS].reshape(FR * ROWS * WIN, 3 * CH)
+            part = nn(lhs, held[tap_t, tap_h].reshape(3 * CH, CH))
+            if tap_t + tap_h == 0:
+                total[...] = part
+            else:
+                total[...] += part
+
+
+def backward_taps(table, start, frames, columns, held, copies, total):
+    for tap_t in range(3):
+        copies[tap_t].wait()
+        for tap_h in range(3):
+            part = None
+            for tap_w in range(3):
+                lanes = slice(tap_w * CH, (tap_w + 1) * CH)
+                lhs = table[pl.ds(start + 2 - tap_t, frames), 2 - tap_h : 2 - tap_h + ROWS, :, lanes]
+                more = nt(lhs.reshape(frames * ROWS * columns, CH), held[tap_t, tap_h, tap_w])
+                part = more if part is None else part + more
+            if tap_t + tap_h == 0:
+                total[...] = part
+            else:
+                total[...] += part
+
+
+def frame_of(total, frame, columns):
+    rows = ROWS * columns
+    return total[frame * rows : (frame + 1) * rows].reshape(ROWS, columns, CH)
+
+
+def first_kernel(halo, block, weights, mask, act, tail, slope, table, total, held, arrived):
+    copies = fetch(weights, held, arrived)
+    clear_border(table)
+    for frame in range(2):
+        fill_table(table, frame, halo[:, frame], True)
+    for frame in range(FR):
+        fill_table(table, 2 + frame, block[frame // 2, :, frame % 2], True)
+    forward_taps(table, held, copies, total)
+    for frame in range(FR):
+        values = frame_of(total, frame, WIN)
+        sigma = jax.nn.sigmoid(values)
+        result = (values * sigma * mask[...]).astype(BF16)
+        act[frame] = result
+        if frame >= 2:
+            tail[frame - 2] = result
+        slope[frame] = slope_of(values, sigma)
+
+
+def second_kernel(halo, block, features, weights, summed, up_act, table, total, held, arrived):
+    copies = fetch(weights, held, arrived)
+    clear_border(table)
+    for frame in range(2):
+        fill_table(table, frame, halo[frame], True)
+    for frame in range(FR):
+        fill_table(table, 2 + frame, block[frame], True)
+    forward_taps(table, held, copies, total)
+    for frame in range(FR):
+        values = frame_of(total, frame, WIN) + features[frame // 2, :, frame % 2].astype(F32)
+        summed[frame] = values
+        up_act[frame] = (values * jax.nn.sigmoid(values)).astype(BF16)
+
+
+def hidden_kernel(block, later, slope, weights, mask, grad_hidden, head, table, total, held, arrived):
+    copies = fetch(weights, held, arrived)
+    clear_border(table)
+    for frame in range(FR):
+        fill_table(table, frame, block[frame], False)
+    for frame in range(2):
+        fill_table(table, FR + frame, later[frame], False)
+    backward_taps(table, 0, FR, WIN, held, copies, total)
+    for frame in range(FR):
+        result = (frame_of(total, frame, WIN) * slope[frame] * mask[...]).astype(BF16)
+        grad_hidden[frame] = result
+        if frame < 2:
+            head[frame] = result
+
+
+def features_kernel(core_ref, block, later, grad_sum, weights, grad_features, table, total, held, arrived):
+    copies = fetch(weights, held, arrived)
     core = core_ref[0]
-
-    @pl.when(step == 0)
-    def _():
-        clear_border(table)
-        for frame in range(FR):
-            fill_own_table(table, frame, block[frame])
-        for frame in range(2):
-            fill_own_table(table, FR + frame, later[frame])
-        total[...] = jnp.zeros_like(total)
-
-    for tap in range(3):
-        part = None
-        for column in range(3):
-            lhs = table[
-                pl.ds(2 * core + 2 - step, 2), 2 - tap : 2 - tap + ROWS, :, column * CH : (column + 1) * CH
-            ]
-            more = nt(lhs.reshape(2 * ROWS * OWN, CH), weights[0, tap, column])
-            part = more if part is None else part + more
-        total[...] += part
-
-    @pl.when(step == 2)
-    def _():
-        for frame in range(2):
-            rows = ROWS * OWN
-            values = total[frame * rows : (frame + 1) * rows].reshape(ROWS, OWN, CH)
-            values = values + own_columns(grad_sum[2 * core + frame])
-            grad_features[:, frame] = values.astype(BF16)
-
-
-def cotangent_kernel(core_ref, mine, other, weights, summed, mask, grad_sum, table):
+    clear_border(table)
+    for frame in range(FR):
+        fill_own_table(table, frame, block[frame])
+    for frame in range(2):
+        fill_own_table(table, FR + frame, later[frame])
+    backward_taps(table, 2 * core, 2, OWN, held, copies, total)
+    for frame in range(2):
+        values = frame_of(total, frame, OWN) + own_columns(grad_sum[2 * core + frame])
+        grad_features[:, frame] = values.astype(BF16)
+
+
+def cotangent_kernel(core_ref, mine, other, weights, summed, mask, grad_sum, head, table):
     core = core_ref[0]
     border = jnp.zeros((FR, WIN, 4 * CH), BF16)
     table[:, 0, 0] = border
@@ -206,6 +193,8 @@
         values = summed[frame]
         grad = grad_act * slope_of(values, jax.nn.sigmoid(values)) * mask[...]
         grad_sum[frame] = grad.astype(BF16)
+        if frame < 2:
+            head[frame] = grad.astype(BF16)
 
 
 def up_grad_kernel(core_ref, act, mine, other, out, table, flipped):
@@ -269,9 +258,10 @@
 
 def second_grad_kernel(place, act, block, later, up, out, table, flipped, sums):
     tap_sums(lambda frame: act[frame], block, later, table, flipped, sums)
-    for group in range(4):
+    for step in range(4):
+        group = lax.rem(place[1] + step, 4)
         for member in range(16):
-            chunk = member // 4 * 16 + group * 4 + member % 4
+            chunk = member * 4 + step
             out[chunk, :UP_ROWS] = up[group * 16 + member]
             out[chunk, UP_ROWS:] = piece_of(sums, 2 * group + place[0], member).astype(BF16)
 
@@ -292,8 +282,8 @@
 SMEM = pl.BlockSpec(memory_space=pltpu.SMEM)
 
 
-def tap_weights():
-    return pl.BlockSpec((1, 3, 3, CH, CH), lambda step: (step, 0, 0, 0, 0))
+HBM = pl.BlockSpec(memory_space=pltpu.HBM)
+WEIGHTS = [pltpu.VMEM((3, 3, 3, CH, CH), BF16), pltpu.SemaphoreType.DMA((3,))]
 
 
 def call(kernel, grid, args, specs, outs, scratch, flops):
@@ -318,6 +308,10 @@
     return lax.ppermute(value, axis, [(i, i + step) for i in range(count) if 0 <= i + step < count])
 
 
+def over_y(value, step):
+    return lax.ppermute(value, "y", [(i, (i + step) % 4) for i in range(4)])
+
+
 def shards(features, conv_first, conv_second, up_kernel, cotangent):
     core = lax.axis_index("core")
     height = 2 * lax.axis_index("z") + lax.axis_index("x_hi")
@@ -329,6 +323,7 @@
     inside = ((columns >= 0) & (columns < 128)).astype(F32)
     mask = jnp.broadcast_to(inside[:, None], (WIN, CH))
     act_shape = (FR, ROWS, WIN, CH)
+    two_frames = (2, ROWS, WIN, CH)
     table = pltpu.VMEM((FR + 2, ROWS + 2, WIN, 3 * CH), BF16)
     own_table = pltpu.VMEM((FR + 2, ROWS + 2, OWN, 3 * CH), BF16)
     total = pltpu.VMEM((FR * ROWS * WIN, CH), F32)
@@ -352,26 +347,26 @@
     halo = shift(block[1], "y", 1)
     mine = lax.all_to_all(fine, ("z", "x_hi"), 0, 0, tiled=True).reshape(8, 2, 2, 2, WIN, 2 * CH)
 
-    first_act, first_slope = call(
-        first_kernel, (3,), (halo, block, conv_first, mask),
-        [whole(halo.shape), whole(block.shape), tap_weights(), whole(mask.shape)],
-        [(act_shape, BF16), (act_shape, F32)], [table, total], 27 * tap_flops,
-    )
-    mine, first_act = lax.optimization_barrier((mine, first_act))
-    earlier = shift(first_act[2:], "y", 1)
+    first_act, first_tail, first_slope = call(
+        first_kernel, (), (halo, block, conv_first, mask),
+        [whole(halo.shape), whole(block.shape), HBM, whole(mask.shape)],
+        [(act_shape, BF16), (two_frames, BF16), (act_shape, F32)], [table, total, *WEIGHTS], 27 * tap_flops,
+    )
+    mine, first_tail = lax.optimization_barrier((mine, first_tail))
+    earlier = shift(first_tail, "y", 1)
     other = lax.ppermute(mine, "core", [(0, 1), (1, 0)])
     summed, up_act = call(
-        second_kernel, (3,), (earlier, first_act, block, conv_second),
-        [whole(earlier.shape), whole(act_shape), whole(block.shape), tap_weights()],
-        [(act_shape, F32), (act_shape, BF16)], [table, total], 27 * tap_flops,
-    )
-    grad_sum = call(
+        second_kernel, (), (earlier, first_act, block, conv_second),
+        [whole(earlier.shape), whole(act_shape), whole(block.shape), HBM],
+        [(act_shape, F32), (act_shape, BF16)], [table, total, *WEIGHTS], 27 * tap_flops,
+    )
+    grad_sum, sum_head = call(
         cotangent_kernel, (), (core_arg, mine, other, up_kernel, summed, mask),
         [SMEM, whole(mine.shape), whole(mine.shape), whole(up_kernel.shape), whole(act_shape), whole(mask.shape)],
-        [(act_shape, BF16)], [pltpu.VMEM((FR, ROWS + 1, 2, WIN, 4 * CH), BF16)], 16 * tap_flops,
-    )
-    later = shift(grad_sum[:2], "y", -1)
-    up_act, later = lax.optimization_barrier((up_act, later))
+        [(act_shape, BF16), (two_frames, BF16)], [pltpu.VMEM((FR, ROWS + 1, 2, WIN, 4 * CH), BF16)], 16 * tap_flops,
+    )
+    later = shift(sum_head, "y", -1)
+    up_act, grad_sum = lax.optimization_barrier((up_act, grad_sum))
     up_part = call(
         up_grad_kernel, (), (core_arg, up_act, mine, other),
         [SMEM, whole(act_shape), whole(mine.shape), whole(mine.shape)],
@@ -384,14 +379,14 @@
         [SMEM, whole(act_shape), whole(act_shape), whole(later.shape), whole(up_part.shape)],
         [((64, UP_ROWS + PIECE, CH), BF16)], grad_scratch, 14 * tap_flops,
     )
-    early = lax.all_to_all(early, "z", 0, 0, tiled=True)
-
-    grad_hidden = call(
-        hidden_kernel, (3,), (grad_sum, later, first_slope, conv_second, mask),
-        [whole(act_shape), whole(later.shape), whole(act_shape), tap_weights(), whole(mask.shape)],
-        [(act_shape, BF16)], [table, total], 27 * tap_flops,
-    )
-    later_hidden = shift(grad_hidden[:2], "y", -1)
+    early = lax.all_to_all(early, ("z", "x_hi", "width"), 0, 0, tiled=True)
+
+    grad_hidden, hidden_head = call(
+        hidden_kernel, (), (grad_sum, later, first_slope, conv_second, mask),
+        [whole(act_shape), whole(later.shape), whole(act_shape), HBM, whole(mask.shape)],
+        [(act_shape, BF16), (two_frames, BF16)], [table, total, *WEIGHTS], 27 * tap_flops,
+    )
+    later_hidden = shift(hidden_head, "y", -1)
     blocks = call(
         first_grad_kernel, (), (place, block, grad_hidden, later_hidden),
         [SMEM, whole(block.shape), whole(act_shape), whole(later_hidden.shape)],
@@ -399,23 +394,25 @@
     )
     arrived = [blocks[0]]
     for step in (2, 1, 3):
-        arrived.append(lax.ppermute(blocks[step], "y", [(i, (i + step) % 4) for i in range(4)]))
+        arrived.append(over_y(blocks[step], step))
     tied_hidden, _ = lax.optimization_barrier((grad_hidden, blocks[0]))
     rows_out = call(
-        features_kernel, (3,), (core_arg, tied_hidden, later_hidden, grad_sum, conv_first),
-        [SMEM, whole(act_shape), whole(later_hidden.shape), whole(act_shape), tap_weights()],
-        [((ROWS, 2, OWN, CH), BF16)], [own_table, pltpu.VMEM((2 * ROWS * OWN, CH), F32)], 7 * tap_flops,
-    )
-
-    early = jnp.sum(early.reshape(4, 16, UP_ROWS + PIECE, CH).astype(F32), axis=0).astype(BF16)
-    early = lax.all_to_all(early, ("y", "x_hi", "width"), 0, 0, tiled=True)
+        features_kernel, (), (core_arg, tied_hidden, later_hidden, grad_sum, conv_first),
+        [SMEM, whole(act_shape), whole(later_hidden.shape), whole(act_shape), HBM],
+        [((ROWS, 2, OWN, CH), BF16)], [own_table, pltpu.VMEM((2 * ROWS * OWN, CH), F32), *WEIGHTS], 7 * tap_flops,
+    )
+
+    tied_rows, early = lax.optimization_barrier((rows_out, early))
+    early = jnp.sum(early.reshape(16, 4, UP_ROWS + PIECE, CH).astype(F32), axis=0)
+    early_total = early[0]
+    for step in (2, 1, 3):
+        early_total += over_y(early[step].astype(BF16), step).astype(F32)
     first_sum = sum(value.astype(F32) for value in arrived).astype(BF16)
-    late = jnp.concatenate([rows_out.reshape(16, 2 * OWN, CH), first_sum], axis=1)
-    late, early = lax.optimization_barrier((late, early))
+    late = jnp.concatenate([tied_rows.reshape(16, 2 * OWN, CH), first_sum], axis=1)
     late = lax.all_to_all(late, ("z", "x_hi", "width"), 0, 0, tiled=True)
 
     factor = 1.0 / math.sqrt(32768)
-    early = jnp.sum(early.astype(F32), axis=0) * factor
+    early = early_total * factor
     returned = late[:, : 2 * OWN].reshape(8, 2, 2, OWN, CH).transpose(2, 1, 0, 3, 4)
     first_share = jnp.sum(late[:, 2 * OWN : 2 * OWN + SHARE].astype(F32), axis=0) * factor
     return (

time: 165 us -> 163 us (0.988)
  Pallas kernels: 31.6 us -> 39 us
  waiting for transfers between devices: 61 us -> 56.7 us
  other arithmetic: 7.64 us -> 3.94 us
  local copies, waits for them, and re-layouts: 19 us -> 15.6 us
  starting transfers between devices: 43.9 us -> 45.8 us
    ppermute x3 -> x6, waiting for transfers between devices: 0.01 us -> 19.5 us  [over_y(): return lax.ppermute(value, 'y', [(i, (i + step) % 4) for i in range(4)])]
    all_to_all x2 -> x1, waiting for transfers between devices: 12.8 us -> 0.01 us  [shards(): early = lax.all_to_all(early, ('z', 'x_hi', 'width'), 0, 0, tiled=True)]
    all_to_all x1, waiting for transfers between devices: 7.94 us -> 0.01 us  [shards(): late = lax.all_to_all(late, ('z', 'x_hi', 'width'), 0, 0, tiled=True)]
    pallas_call x8, Pallas kernels: 31.6 us -> 39 us  [call(): pl.pallas_call(kernel, out_shape=shapes[0] if single else shapes, grid=gr...]
    all_to_all x2 -> x1, starting transfers between devices: 11.8 us -> 7.41 us  [shards(): early = lax.all_to_all(early, ('z', 'x_hi', 'width'), 0, 0, tiled=True)]
    all_to_all x1, starting transfers between devices: 3.58 us -> 6.6 us  [shards(): late = lax.all_to_all(late, ('z', 'x_hi', 'width'), 0, 0, tiled=True)]
    ppermute x3 -> x6, starting transfers between devices: 5.05 us -> 8.05 us  [over_y(): return lax.ppermute(value, 'y', [(i, (i + step) % 4) for i in range(4)])]
    ppermute x4, waiting for transfers between devices: 28.4 us -> 25.7 us  [shift(): lax.ppermute(value, axis, [(i, i + step) for i in range(count) if 0 <= i...]
  transfers between devices with their start and end apart: 14 -> 16, of which waited for: 9 -> 11; matrix products, arithmetic and copies ran while one was open for 7% -> 4% of each run, Pallas kernels for 13% -> 19%
where the time goes in v6:
time: 163 us; the launch traced here: 162 us
  waiting for transfers between devices  56.7 us (35%)
  starting transfers between devices  45.8 us (28%)
  Pallas kernels  39 us (24%)
  local copies, waits for them, and re-layouts  15.6 us (10%)
  other arithmetic  3.94 us (2%)
    pallas_call x8, Pallas kernels, call(): pl.pallas_call(kernel, out_shape=shapes[0] if single else shapes, grid=gr...  39 us
    ppermute x4, waiting for transfers between devices, shift(): lax.ppermute(value, axis, [(i, i + step) for i in range(count) if 0 <= i...  25.7 us
    ppermute x6, waiting for transfers between devices, over_y(): return lax.ppermute(value, 'y', [(i, (i + step) % 4) for i in range(4)])  19.5 us
    all_to_all x1, waiting for transfers between devices, shards(): lax.all_to_all(windows, ('core', 'z', 'x_hi', 'width'), 0, 0, tiled=True)  11.5 us
    ppermute x4, starting transfers between devices, shift(): lax.ppermute(value, axis, [(i, i + step) for i in range(count) if 0 <= i...  10.7 us
    unnamed x24, local copies, waits for them, and re-layouts  9.31 us
    ppermute x6, starting transfers between devices, over_y(): return lax.ppermute(value, 'y', [(i, (i + step) % 4) for i in range(4)])  8.05 us
    all_to_all x1, starting transfers between devices, shards(): lax.all_to_all(windows, ('core', 'z', 'x_hi', 'width'), 0, 0, tiled=True)  7.87 us
  transfers between devices with their start and end apart: 16, of which 11 were waited for; matrix products, arithmetic and copies ran while one was open for 4% of the time, Pallas kernels for 19%

profile of v6, /device:TPU:0, one launch (start us, length us, event | category | flops | bytes accessed | tf_op | source)
XLA Modules:
  0.0 162.0 jit_solution(971276996419872368)
XLA Ops:
  5.4 7.9 %all-to-all-start = ((bf16[32,2,16,256]{3,2,1,0:T(8,128)(2,1)}), bf16[32,2,16,256]{3,2,1,0:T(8,128)(2,1)S(1)}, u32[]{:S(2)}, u32[]{:S(2)}) async-start(bf16[32,2,16,256]{3,2,1,0:T(8,128)(2,1)} %bitcast.8), calls=%async_computation | async-start | bytes 1048576 | tf_op jit(solution)/shard_map/all_to_all | solution.py:336
  13.8 11.5 %all-to-all-done = bf16[32,2,16,256]{3,2,1,0:T(8,128)(2,1)S(1)} async-done(((bf16[32,2,16,256]{3,2,1,0:T(8,128)(2,1)}), bf16[32,2,16,256]{3,2,1,0:T(8,128)(2,1)S(1)}, u32[]{:S(2)}, u32[]{:S(2)}) %all-to-all-start) | async-done | bytes 524320 | tf_op jit(solution)/shard_map/all_to_all | solution.py:336
  26.4 3.6 %all-to-all-start.1 = ((bf16[8,2,4,16,512]{4,3,2,1,0:T(8,128)(2,1)}), bf16[8,2,4,16,512]{4,3,2,1,0:T(8,128)(2,1)S(1)}, u32[]{:S(2)}, u32[]{:S(2)}) async-start(bf16[8,2,4,16,512]{4,3,2,1,0:T(8,128)(2,1)} %copy.15), calls=%async_computation.1 | async-start | bytes 2097152 | tf_op jit(solution)/shard_map/all_to_all | solution.py:348
  30.0 3.5 %collective-permute-start.1 = (bf16[16,2,16,256]{3,2,1,0:T(8,128)(2,1)S(1)}, bf16[16,2,16,256]{3,2,1,0:T(8,128)(2,1)S(1)}, u32[]{:S(2)}, u32[]{:S(2)}) collective-permute-start(bf16[16,2,16,256]{3,2,1,0:T(8,128)(2,1)S(1)} %slice.55), channel_id=1, source_target_pairs={{0,32},{32,64},{64,96},{1,33},{33,65},{65,97},{2,34},{34,66},{66,9... | collective-permute-start | bytes 786440 | tf_op jit(solution)/shard_map/ppermute | solution.py:308
  33.5 5.1 %collective-permute-done.1.halo = bf16[16,2,16,256]{3,2,1,0:T(8,128)(2,1)S(1)} collective-permute-done((bf16[16,2,16,256]{3,2,1,0:T(8,128)(2,1)S(1)}, bf16[16,2,16,256]{3,2,1,0:T(8,128)(2,1)S(1)}, u32[]{:S(2)}, u32[]{:S(2)}) %collective-permute-start.1) | collective-permute-done | bytes 262176 | tf_op jit(solution)/shard_map/ppermute | solution.py:308
  38.6 2.0 %copy-done = bf16[3,3,3,256,256]{4,3,2,1,0:T(8,128)(2,1)S(1)} copy-done((bf16[3,3,3,256,256]{4,3,2,1,0:T(8,128)(2,1)S(1)}, bf16[3,3,3,256,256]{4,3,2,1,0:T(8,128)(2,1)}, u32[]{:S(2)}) %copy-start) | copy-done | bytes 3538968
  40.6 7.6 %shard_map.84 = (bf16[4,16,16,256]{3,2,1,0:T(8,128)(2,1)S(1)}, bf16[2,16,16,256]{3,2,1,0:T(8,128)(2,1)S(1)}, f32[4,16,16,256]{3,2,1,0:T(8,128)S(1)}) custom-call(bf16[16,2,16,256]{3,2,1,0:T(8,128)(2,1)S(1)} %collective-permute-done.1.halo, bf16[2,16,2,16,256]{4,3,2,1,0:T(8,128)(2,1)S(1)} %bitcast.47, bf16[3,3,3,256,256]{4,3,2,1,0:T(8,128)(2,1)S(1)} %copy-done, ...), custom_call_target="tpu_custom_call" | custom-call | flops 3623878656 | bytes 6176768 | tf_op jit(solution)/shard_map/pallas_call | solution.py:294
  50.1 4.6 %collective-permute-start.2 = (bf16[2,16,16,256]{3,2,1,0:T(8,128)(2,1)S(1)}, bf16[2,16,16,256]{3,2,1,0:T(8,128)(2,1)S(1)}, u32[]{:S(2)}, u32[]{:S(2)}) collective-permute-start(bf16[2,16,16,256]{3,2,1,0:T(8,128)(2,1)S(1)} %get-tuple-element.29), channel_id=1, source_target_pairs={{0,32},{32,64},{64,96},{1,33},{33,65},{65,97},{2,34},{34,66},{66,9... | collective-permute-start | bytes 786440 | tf_op jit(solution)/shard_map/ppermute | solution.py:308
  54.6 6.0 %collective-permute-done.2.halo = bf16[2,16,16,256]{3,2,1,0:T(8,128)(2,1)S(1)} collective-permute-done((bf16[2,16,16,256]{3,2,1,0:T(8,128)(2,1)S(1)}, bf16[2,16,16,256]{3,2,1,0:T(8,128)(2,1)S(1)}, u32[]{:S(2)}, u32[]{:S(2)}) %collective-permute-start.2) | collective-permute-done | bytes 262176 | tf_op jit(solution)/shard_map/ppermute | solution.py:308
  61.7 7.9 %shard_map.85 = (f32[4,16,16,256]{3,2,1,0:T(8,128)S(1)}, bf16[4,16,16,256]{3,2,1,0:T(8,128)(2,1)S(1)}) custom-call(bf16[2,16,16,256]{3,2,1,0:T(8,128)(2,1)S(1)} %collective-permute-done.2.halo, bf16[4,16,16,256]{3,2,1,0:T(8,128)(2,1)S(1)} %copy-done.7, bf16[2,16,2,16,256]{4,3,2,1,0:T(8,128)(2,1)S(1)} %bitcast.48, bf16[3,3,3,256,256]{4,3,2,1,0:T(8,128)(2,1)} %weights.8), custom_call_target="tpu_custom_call" | custom-call | flops 3623878656 | bytes 6422528 | tf_op jit(solution)/shard_map/pallas_call | solution.py:294
  70.4 3.5 %shard_map.86 = (bf16[4,16,16,256]{3,2,1,0:T(8,128)(2,1)S(1)}, bf16[2,16,16,256]{3,2,1,0:T(8,128)(2,1)}) custom-call(s32[1]{0:T(128)} %bitcast.core_ref, bf16[8,2,2,2,16,512]{5,4,3,2,1,0:T(8,128)(2,1)S(1)} %bitcast.45, bf16[8,2,2,2,16,512]{5,4,3,2,1,0:T(8,128)(2,1)S(1)} %collective-permute-done.3.other, bf16[4,4,256,256]{3,2,1,0:T(8,128)(2,1)S(1)} %copy-done.5, ...), custom_call_target="tpu_custom_call" | custom-call | flops 2147483648 | bytes 6045700 | tf_op jit(solution)/shard_map/pallas_call | solution.py:294
  78.1 6.6 %collective-permute-done.4.later = bf16[2,16,16,256]{3,2,1,0:T(8,128)(2,1)S(1)} collective-permute-done((bf16[2,16,16,256]{3,2,1,0:T(8,128)(2,1)}, bf16[2,16,16,256]{3,2,1,0:T(8,128)(2,1)S(1)}, u32[]{:S(2)}, u32[]{:S(2)}) %collective-permute-start.4) | collective-permute-done | bytes 262176 | tf_op jit(solution)/shard_map/ppermute | solution.py:308
  84.7 4.7 %shard_map.91 = bf16[64,88,256]{2,1,0:T(8,128)(2,1)} custom-call(s32[2]{0:T(128)S(1)} %pad_add_fusion.place, bf16[4,16,16,256]{3,2,1,0:T(8,128)(2,1)S(1)} %copy-done.8, bf16[4,16,16,256]{3,2,1,0:T(8,128)(2,1)S(1)} %get-tuple-element.35.block.grad_sum, bf16[2,16,16,256]{3,2,1,0:T(8,128)(2,1)S(1)} %collective-permute-done.4.later, ...), custom_call_target="tpu_custom_call" | custom-call | flops 1879048192 | bytes 5242888 | tf_op jit(solution)/shard_map/pallas_call | solution.py:294
  89.4 7.4 %all-to-all-start.2 = ((bf16[64,88,256]{2,1,0:T(8,128)(2,1)}), bf16[64,88,256]{2,1,0:T(8,128)(2,1)}, u32[]{:S(2)}, u32[]{:S(2)}) async-start(bf16[64,88,256]{2,1,0:T(8,128)(2,1)} %shard_map.91), calls=%async_computation.2 | async-start | bytes 5767168 | tf_op jit(solution)/shard_map/all_to_all | solution.py:382
  96.8 2.0 %copy-done.4 = bf16[3,3,3,256,256]{4,3,2,1,0:T(8,128)(2,1)S(1)} copy-done((bf16[3,3,3,256,256]{4,3,2,1,0:T(8,128)(2,1)S(1)}, bf16[3,3,3,256,256]{4,3,2,1,0:T(8,128)(2,1)}, u32[]{:S(2)}) %copy-start.4) | copy-done | bytes 3538968
  98.8 7.6 %shard_map.87 = (bf16[4,16,16,256]{3,2,1,0:T(8,128)(2,1)S(1)}, bf16[2,16,16,256]{3,2,1,0:T(8,128)(2,1)S(1)}) custom-call(bf16[4,16,16,256]{3,2,1,0:T(8,128)(2,1)S(1)} %get-tuple-element.35.block.grad_sum, bf16[2,16,16,256]{3,2,1,0:T(8,128)(2,1)S(1)} %collective-permute-done.4.later, f32[4,16,16,256]{3,2,1,0:T(8,128)S(1)} %copy-done.10, ...), custom_call_target="tpu_custom_call" | custom-call | flops 3623878656 | bytes 6176768 | tf_op jit(solution)/shard_map/pallas_call | solution.py:294
  107.7 8.0 %collective-permute-done.5.later = bf16[2,16,16,256]{3,2,1,0:T(8,128)(2,1)S(1)} collective-permute-done((bf16[2,16,16,256]{3,2,1,0:T(8,128)(2,1)S(1)}, bf16[2,16,16,256]{3,2,1,0:T(8,128)(2,1)S(1)}, u32[]{:S(2)}, u32[]{:S(2)}) %collective-permute-start.5) | collective-permute-done | bytes 262176 | tf_op jit(solution)/shard_map/ppermute | solution.py:308
  115.7 3.0 %shard_map.88 = (bf16[16,56,256]{2,1,0:T(8,128)(2,1)S(1)}, bf16[16,56,256]{2,1,0:T(8,128)(2,1)S(1)}, bf16[16,56,256]{2,1,0:T(8,128)(2,1)S(1)}, bf16[16,56,256]{2,1,0:T(8,128)(2,1)S(1)}) custom-call(s32[2]{0:T(128)S(1)} %pad_add_fusion.place, bf16[2,16,2,16,256]{4,3,2,1,0:T(8,128)(2,1)S(1)} %bitcast.49, bf16[4,16,16,256]{3,2,1,0:T(8,128)(2,1)S(1)} %get-tuple-element.41.block, ...), custom_call_target="tpu_custom_call" | custom-call | flops 1879048192 | bytes 3145736 | tf_op jit(solution)/shard_map/pallas_call | solution.py:294
  120.9 2.8 %collective-permute-start.6 = (bf16[16,56,256]{2,1,0:T(8,128)(2,1)S(1)}, bf16[16,56,256]{2,1,0:T(8,128)(2,1)S(1)}, u32[]{:S(2)}, u32[]{:S(2)}) collective-permute-start(bf16[16,56,256]{2,1,0:T(8,128)(2,1)S(1)} %get-tuple-element.44), channel_id=1, source_target_pairs={{0,64},{32,96},{64,0},{96,32},{1,65},{33,97},{65,1},{97,33},{2,66}... | collective-permute-start | bytes 1376264 | tf_op jit(solution)/shard_map/ppermute | solution.py:312
  123.6 3.0 %shard_map.89 = bf16[16,2,8,256]{3,2,1,0:T(8,128)(2,1)S(1)} custom-call(s32[1]{0:T(128)} %bitcast.core_ref, bf16[4,16,16,256]{3,2,1,0:T(8,128)(2,1)S(1)} %get-tuple-element.41.block, bf16[2,16,16,256]{3,2,1,0:T(8,128)(2,1)S(1)} %collective-permute-done.5.later, bf16[4,16,16,256]{3,2,1,0:T(8,128)(2,1)S(1)} %get-tuple-element.35.block.grad_sum, ...), custom_call_target="tpu_custom_call" | custom-call | flops 939524096 | bytes 4980740 | tf_op jit(solution)/shard_map/pallas_call | solution.py:294
  126.6 5.7 %collective-permute-done.8 = bf16[16,56,256]{2,1,0:T(8,128)(2,1)S(1)} collective-permute-done((bf16[16,56,256]{2,1,0:T(8,128)(2,1)S(1)}, bf16[16,56,256]{2,1,0:T(8,128)(2,1)S(1)}, u32[]{:S(2)}, u32[]{:S(2)}) %collective-permute-start.8) | collective-permute-done | bytes 458784 | tf_op jit(solution)/shard_map/ppermute | solution.py:312
  133.4 8.2 %collective-permute-done.6 = bf16[16,56,256]{2,1,0:T(8,128)(2,1)S(1)} collective-permute-done((bf16[16,56,256]{2,1,0:T(8,128)(2,1)S(1)}, bf16[16,56,256]{2,1,0:T(8,128)(2,1)S(1)}, u32[]{:S(2)}, u32[]{:S(2)}) %collective-permute-start.6) | collective-permute-done | bytes 458784 | tf_op jit(solution)/shard_map/ppermute | solution.py:312
  142.7 6.6 %all-to-all-start.3 = ((bf16[16,72,256]{2,1,0:T(8,128)(2,1)}), bf16[16,72,256]{2,1,0:T(8,128)(2,1)S(1)}, u32[]{:S(2)}, u32[]{:S(2)}) async-start(bf16[16,72,256]{2,1,0:T(8,128)(2,1)} %pad_maximum_fusion), calls=%async_computation.3 | async-start | bytes 1179648 | tf_op jit(solution)/shard_map/all_to_all | solution.py:412
  149.3 2.2 %convert_reduce_fusion = f32[4,88,256]{2,1,0:T(8,128)S(1)} fusion(bf16[16,4,88,256]{3,2,1,0:T(8,128)(2,1)} %bitcast.23), kind=kLoop, calls=%fused_computation | loop fusion | flops 2793472 | bytes 3244032 | tf_op jit(solution)/shard_map/reduce_sum | solution.py:406
  (69 shorter events, 30.1 us)
Async XLA Ops:
  1.9 11.4 %collective-permute-start = (bf16[2,4,4,512]{3,2,1,0:T(4,128)(2,1)S(1)}, bf16[2,4,4,512]{3,2,1,0:T(4,128)(2,1)S(1)}, u32[]{:S(2)}, u32[]{:S(2)}) collective-permute-start(bf16[2,4,4,512]{3,2,1,0:T(4,128)(2,1)S(1)} %slice_select_fusion), channel_id=1, source_target_pairs={{0,1},{1,0},{2,3},{3,2},{4,5},{5,4},{6,7},{7,6},{8,9},{9,8},{10,11... | collective-permute-start | bytes 98312 | tf_op jit(solution)/shard_map/ppermute | solution.py:340
  5.4 19.8 %all-to-all-start = ((bf16[32,2,16,256]{3,2,1,0:T(8,128)(2,1)}), bf16[32,2,16,256]{3,2,1,0:T(8,128)(2,1)S(1)}, u32[]{:S(2)}, u32[]{:S(2)}) async-start(bf16[32,2,16,256]{3,2,1,0:T(8,128)(2,1)} %bitcast.8), calls=%async_computation | async-start | bytes 1048576 | tf_op jit(solution)/shard_map/all_to_all | solution.py:336
  26.4 23.7 %all-to-all-start.1 = ((bf16[8,2,4,16,512]{4,3,2,1,0:T(8,128)(2,1)}), bf16[8,2,4,16,512]{4,3,2,1,0:T(8,128)(2,1)S(1)}, u32[]{:S(2)}, u32[]{:S(2)}) async-start(bf16[8,2,4,16,512]{4,3,2,1,0:T(8,128)(2,1)} %copy.15), calls=%async_computation.1 | async-start | bytes 2097152 | tf_op jit(solution)/shard_map/all_to_all | solution.py:348
  30.0 8.6 %collective-permute-start.1 = (bf16[16,2,16,256]{3,2,1,0:T(8,128)(2,1)S(1)}, bf16[16,2,16,256]{3,2,1,0:T(8,128)(2,1)S(1)}, u32[]{:S(2)}, u32[]{:S(2)}) collective-permute-start(bf16[16,2,16,256]{3,2,1,0:T(8,128)(2,1)S(1)} %slice.55), channel_id=1, source_target_pairs={{0,32},{32,64},{64,96},{1,33},{33,65},{65,97},{2,34},{34,66},{66,9... | collective-permute-start | bytes 786440 | tf_op jit(solution)/shard_map/ppermute | solution.py:308
  38.6 2.0 %copy-start = (bf16[3,3,3,256,256]{4,3,2,1,0:T(8,128)(2,1)S(1)}, bf16[3,3,3,256,256]{4,3,2,1,0:T(8,128)(2,1)}, u32[]{:S(2)}) copy-start(bf16[3,3,3,256,256]{4,3,2,1,0:T(8,128)(2,1)} %weights.9) | copy-start | bytes 10616836
  50.1 20.3 %collective-permute-start.3 = (bf16[8,2,2,2,16,512]{5,4,3,2,1,0:T(8,128)(2,1)S(1)}, bf16[8,2,2,2,16,512]{5,4,3,2,1,0:T(8,128)(2,1)S(1)}, u32[]{:S(2)}, u32[]{:S(2)}) collective-permute-start(bf16[8,2,2,2,16,512]{5,4,3,2,1,0:T(8,128)(2,1)S(1)} %bitcast.44), channel_id=1, source_target_pairs={{0,16},{16,0},{1,17},{17,1},{2,18},{18,2},{3,19},{19,3},{4,20},{20... | collective-permute-start | bytes 3145736 | tf_op jit(solution)/shard_map/ppermute | solution.py:357
  50.1 10.6 %collective-permute-start.2 = (bf16[2,16,16,256]{3,2,1,0:T(8,128)(2,1)S(1)}, bf16[2,16,16,256]{3,2,1,0:T(8,128)(2,1)S(1)}, u32[]{:S(2)}, u32[]{:S(2)}) collective-permute-start(bf16[2,16,16,256]{3,2,1,0:T(8,128)(2,1)S(1)} %get-tuple-element.29), channel_id=1, source_target_pairs={{0,32},{32,64},{64,96},{1,33},{33,65},{65,97},{2,34},{34,66},{66,9... | collective-permute-start | bytes 786440 | tf_op jit(solution)/shard_map/ppermute | solution.py:308
  60.7 1.0 copy-start.7
  61.7 8.7 %copy-start.5 = (bf16[4,4,256,256]{3,2,1,0:T(8,128)(2,1)S(1)}, bf16[4,4,256,256]{3,2,1,0:T(8,128)(2,1)}, u32[]{:S(2)}) copy-start(bf16[4,4,256,256]{3,2,1,0:T(8,128)(2,1)} %weights.7) | copy-start | bytes 6291460
  73.9 10.8 %collective-permute-start.4 = (bf16[2,16,16,256]{3,2,1,0:T(8,128)(2,1)}, bf16[2,16,16,256]{3,2,1,0:T(8,128)(2,1)S(1)}, u32[]{:S(2)}, u32[]{:S(2)}) collective-permute-start(bf16[2,16,16,256]{3,2,1,0:T(8,128)(2,1)} %get-tuple-element.36), channel_id=1, source_target_pairs={{32,0},{64,32},{96,64},{33,1},{65,33},{97,65},{34,2},{66,34},{98,6... | collective-permute-start | bytes 786440 | tf_op jit(solution)/shard_map/ppermute | solution.py:308
  75.3 1.0 copy-start.3
  76.3 8.4 %copy-start.8 = (bf16[4,16,16,256]{3,2,1,0:T(8,128)(2,1)S(1)}, bf16[4,16,16,256]{3,2,1,0:T(8,128)(2,1)}, u32[]{:S(2)}) copy-start(bf16[4,16,16,256]{3,2,1,0:T(8,128)(2,1)} %copy-done.6) | copy-start | bytes 1572868
  89.4 7.4 %copy-start.10 = (f32[4,16,16,256]{3,2,1,0:T(8,128)S(1)}, f32[4,16,16,256]{3,2,1,0:T(8,128)}, u32[]{:S(2)}) copy-start(f32[4,16,16,256]{3,2,1,0:T(8,128)} %copy-done.9) | copy-start | bytes 3145732
  89.4 52.5 %all-to-all-start.2 = ((bf16[64,88,256]{2,1,0:T(8,128)(2,1)}), bf16[64,88,256]{2,1,0:T(8,128)(2,1)}, u32[]{:S(2)}, u32[]{:S(2)}) async-start(bf16[64,88,256]{2,1,0:T(8,128)(2,1)} %shard_map.91), calls=%async_computation.2 | async-start | bytes 5767168 | tf_op jit(solution)/shard_map/all_to_all | solution.py:382
  96.8 2.0 %copy-start.4 = (bf16[3,3,3,256,256]{4,3,2,1,0:T(8,128)(2,1)S(1)}, bf16[3,3,3,256,256]{4,3,2,1,0:T(8,128)(2,1)}, u32[]{:S(2)}) copy-start(bf16[3,3,3,256,256]{4,3,2,1,0:T(8,128)(2,1)} %weights.8) | copy-start | bytes 10616836
  106.4 9.3 %collective-permute-start.5 = (bf16[2,16,16,256]{3,2,1,0:T(8,128)(2,1)S(1)}, bf16[2,16,16,256]{3,2,1,0:T(8,128)(2,1)S(1)}, u32[]{:S(2)}, u32[]{:S(2)}) collective-permute-start(bf16[2,16,16,256]{3,2,1,0:T(8,128)(2,1)S(1)} %get-tuple-element.39), channel_id=1, source_target_pairs={{32,0},{64,32},{96,64},{33,1},{65,33},{97,65},{34,2},{66,34},{98,6... | collective-permute-start | bytes 786440 | tf_op jit(solution)/shard_map/ppermute | solution.py:308
  115.7 7.9 %copy-start.1 = (bf16[3,3,3,256,256]{4,3,2,1,0:T(8,128)(2,1)S(1)}, bf16[3,3,3,256,256]{4,3,2,1,0:T(8,128)(2,1)}, u32[]{:S(2)}) copy-start(bf16[3,3,3,256,256]{4,3,2,1,0:T(8,128)(2,1)} %weights.9) | copy-start | bytes 10616836
  118.8 13.5 %collective-permute-start.8 = (bf16[16,56,256]{2,1,0:T(8,128)(2,1)S(1)}, bf16[16,56,256]{2,1,0:T(8,128)(2,1)S(1)}, u32[]{:S(2)}, u32[]{:S(2)}) collective-permute-start(bf16[16,56,256]{2,1,0:T(8,128)(2,1)S(1)} %get-tuple-element.46), channel_id=1, source_target_pairs={{0,96},{32,0},{64,32},{96,64},{1,97},{33,1},{65,33},{97,65},{2,98}... | collective-permute-start | bytes 1376264 | tf_op jit(solution)/shard_map/ppermute | solution.py:312
  119.7 13.8 %collective-permute-start.7 = (bf16[16,56,256]{2,1,0:T(8,128)(2,1)S(1)}, bf16[16,56,256]{2,1,0:T(8,128)(2,1)S(1)}, u32[]{:S(2)}, u32[]{:S(2)}) collective-permute-start(bf16[16,56,256]{2,1,0:T(8,128)(2,1)S(1)} %get-tuple-element.45), channel_id=1, source_target_pairs={{0,32},{32,64},{64,96},{96,0},{1,33},{33,65},{65,97},{97,1},{2,34}... | collective-permute-start | bytes 1376264 | tf_op jit(solution)/shard_map/ppermute | solution.py:312
  120.9 20.7 %collective-permute-start.6 = (bf16[16,56,256]{2,1,0:T(8,128)(2,1)S(1)}, bf16[16,56,256]{2,1,0:T(8,128)(2,1)S(1)}, u32[]{:S(2)}, u32[]{:S(2)}) collective-permute-start(bf16[16,56,256]{2,1,0:T(8,128)(2,1)S(1)} %get-tuple-element.44), channel_id=1, source_target_pairs={{0,64},{32,96},{64,0},{96,32},{1,65},{33,97},{65,1},{97,33},{2,66}... | collective-permute-start | bytes 1376264 | tf_op jit(solution)/shard_map/ppermute | solution.py:312
  142.7 17.9 %all-to-all-start.3 = ((bf16[16,72,256]{2,1,0:T(8,128)(2,1)}), bf16[16,72,256]{2,1,0:T(8,128)(2,1)S(1)}, u32[]{:S(2)}, u32[]{:S(2)}) async-start(bf16[16,72,256]{2,1,0:T(8,128)(2,1)} %pad_maximum_fusion), calls=%async_computation.3 | async-start | bytes 1179648 | tf_op jit(solution)/shard_map/all_to_all | solution.py:412
  151.6 4.1 %collective-permute-start.11 = (bf16[88,256]{1,0:T(8,128)(2,1)S(1)}, bf16[88,256]{1,0:T(8,128)(2,1)S(1)}, u32[]{:S(2)}, u32[]{:S(2)}) collective-permute-start(bf16[88,256]{1,0:T(8,128)(2,1)S(1)} %get-tuple-element.51), channel_id=1, source_target_pairs={{0,96},{32,0},{64,32},{96,64},{1,97},{33,1},{65,33},{97,65},{2,98}... | collective-permute-start | bytes 135176 | tf_op jit(solution)/shard_map/ppermute | solution.py:312
  152.2 5.3 %collective-permute-start.10 = (bf16[88,256]{1,0:T(8,128)(2,1)S(1)}, bf16[88,256]{1,0:T(8,128)(2,1)S(1)}, u32[]{:S(2)}, u32[]{:S(2)}) collective-permute-start(bf16[88,256]{1,0:T(8,128)(2,1)S(1)} %get-tuple-element.52), channel_id=1, source_target_pairs={{0,32},{32,64},{64,96},{96,0},{1,33},{33,65},{65,97},{97,1},{2,34}... | collective-permute-start | bytes 135176 | tf_op jit(solution)/shard_map/ppermute | solution.py:312
  153.7 5.6 %collective-permute-start.9 = (bf16[88,256]{1,0:T(8,128)(2,1)S(1)}, bf16[88,256]{1,0:T(8,128)(2,1)S(1)}, u32[]{:S(2)}, u32[]{:S(2)}) collective-permute-start(bf16[88,256]{1,0:T(8,128)(2,1)S(1)} %get-tuple-element.50), channel_id=1, source_target_pairs={{0,64},{32,96},{64,0},{96,32},{1,65},{33,97},{65,1},{97,33},{2,66}... | collective-permute-start | bytes 135176 | tf_op jit(solution)/shard_map/ppermute | solution.py:312
  (3 other events, 2.6 us)

commit v7 on v5

--- a/solution.py
+++ b/solution.py
@@ -62,63 +62,72 @@
     return pltpu.roll(block.astype(F32), WIN - EDGE, axis=1)[:, :OWN]
 
 
-def first_kernel(halo, block, weights, mask, act, slope, table, total):
+def forward_taps(table, frames, weights, total):
     step = pl.program_id(0)
-
-    @pl.when(step == 0)
+    for tap in range(3):
+        lhs = table[pl.ds(step, frames), tap : tap + ROWS].reshape(frames * ROWS * WIN, 3 * CH)
+        total[...] += nn(lhs, weights[0, tap].reshape(3 * CH, CH))
+
+
+def backward_taps(table, start, frames, columns, weights, total):
+    step = pl.program_id(0)
+    for tap_h in range(3):
+        part = None
+        for tap_w in range(3):
+            lanes = slice(tap_w * CH, (tap_w + 1) * CH)
+            lhs = table[pl.ds(start + 2 - step, frames), 2 - tap_h : 2 - tap_h + ROWS, :, lanes]
+            more = nt(lhs.reshape(frames * ROWS * columns, CH), weights[0, tap_h, tap_w])
+            part = more if part is None else part + more
+        total[...] += part
+
+
+def frame_of(total, frame, columns):
+    rows = ROWS * columns
+    return total[frame * rows : (frame + 1) * rows].reshape(ROWS, columns, CH)
+
+
+def first_kernel(block, weights, mask, act, slope, table, total):
+    @pl.when(pl.program_id(0) == 0)
     def _():
         clear_border(table)
-        for frame in range(2):
-            fill_table(table, frame, halo[:, frame], True)
+        for core in range(2):
+            for frame in range(FR):
+                slot = 2 * core + frame if frame < 2 else 2 + 2 * core + frame
+                fill_table(table, slot, block[core, :, frame], True)
+        total[...] = jnp.zeros_like(total)
+
+    forward_taps(table, FR + 2, weights, total)
+
+    @pl.when(pl.program_id(0) == 2)
+    def _():
+        for frame in range(FR + 2):
+            values = frame_of(total, frame, WIN)
+            sigma = jax.nn.sigmoid(values)
+            act[frame] = (values * sigma * mask[...]).astype(BF16)
+            if frame >= 2:
+                slope[frame - 2] = slope_of(values, sigma)
+
+
+def second_kernel(act, features, weights, summed, up_act, table, total):
+    @pl.when(pl.program_id(0) == 0)
+    def _():
+        clear_border(table)
+        for frame in range(FR + 2):
+            fill_table(table, frame, act[frame], True)
+        total[...] = jnp.zeros_like(total)
+
+    forward_taps(table, FR, weights, total)
+
+    @pl.when(pl.program_id(0) == 2)
+    def _():
         for frame in range(FR):
-            fill_table(table, 2 + frame, block[frame // 2, :, frame % 2], True)
-        total[...] = jnp.zeros_like(total)
-
-    for tap in range(3):
-        lhs = table[pl.ds(step, FR), tap : tap + ROWS].reshape(FR * ROWS * WIN, 3 * CH)
-        total[...] += nn(lhs, weights[0, tap].reshape(3 * CH, CH))
-
-    @pl.when(step == 2)
-    def _():
-        inside = mask[...]
-        for frame in range(FR):
-            rows = ROWS * WIN
-            values = total[frame * rows : (frame + 1) * rows].reshape(ROWS, WIN, CH)
-            sigma = jax.nn.sigmoid(values)
-            act[frame] = (values * sigma * inside).astype(BF16)
-            slope[frame] = slope_of(values, sigma)
-
-
-def second_kernel(halo, block, features, weights, summed, up_act, table, total):
-    step = pl.program_id(0)
-
-    @pl.when(step == 0)
-    def _():
-        clear_border(table)
-        for frame in range(2):
-            fill_table(table, frame, halo[frame], True)
-        for frame in range(FR):
-            fill_table(table, 2 + frame, block[frame], True)
-        total[...] = jnp.zeros_like(total)
-
-    for tap in range(3):
-        lhs = table[pl.ds(step, FR), tap : tap + ROWS].reshape(FR * ROWS * WIN, 3 * CH)
-        total[...] += nn(lhs, weights[0, tap].reshape(3 * CH, CH))
-
-    @pl.when(step == 2)
-    def _():
-        for frame in range(FR):
-            rows = ROWS * WIN
-            values = total[frame * rows : (frame + 1) * rows].reshape(ROWS, WIN, CH)
-            values = values + features[frame // 2, :, frame % 2].astype(F32)
+            values = frame_of(total, frame, WIN) + features[frame // 2, :, 2 + frame % 2].astype(F32)
             summed[frame] = values
             up_act[frame] = (values * jax.nn.sigmoid(values)).astype(BF16)
 
 
-def hidden_kernel(block, later, slope, weights, mask, grad_hidden, table, total):
-    step = pl.program_id(0)
-
-    @pl.when(step == 0)
+def hidden_kernel(block, later, slope, weights, mask, grad_hidden, head, table, total):
+    @pl.when(pl.program_id(0) == 0)
     def _():
         clear_border(table)
         for frame in range(FR):
@@ -127,28 +136,21 @@
             fill_table(table, FR + frame, later[frame], False)
         total[...] = jnp.zeros_like(total)
 
-    for tap in range(3):
-        part = None
-        for column in range(3):
-            lhs = table[pl.ds(2 - step, FR), 2 - tap : 2 - tap + ROWS, :, column * CH : (column + 1) * CH]
-            more = nt(lhs.reshape(FR * ROWS * WIN, CH), weights[0, tap, column])
-            part = more if part is None else part + more
-        total[...] += part
-
-    @pl.when(step == 2)
-    def _():
-        inside = mask[...]
+    backward_taps(table, 0, FR, WIN, weights, total)
+
+    @pl.when(pl.program_id(0) == 2)
+    def _():
         for frame in range(FR):
-            rows = ROWS * WIN
-            values = total[frame * rows : (frame + 1) * rows].reshape(ROWS, WIN, CH)
-            grad_hidden[frame] = (values * slope[frame] * inside).astype(BF16)
+            result = (frame_of(total, frame, WIN) * slope[frame] * mask[...]).astype(BF16)
+            grad_hidden[frame] = result
+            if frame < 2:
+                head[frame] = result
 
 
 def features_kernel(core_ref, block, later, grad_sum, weights, grad_features, table, total):
-    step = pl.program_id(0)
     core = core_ref[0]
 
-    @pl.when(step == 0)
+    @pl.when(pl.program_id(0) == 0)
     def _():
         clear_border(table)
         for frame in range(FR):
@@ -157,26 +159,16 @@
             fill_own_table(table, FR + frame, later[frame])
         total[...] = jnp.zeros_like(total)
 
-    for tap in range(3):
-        part = None
-        for column in range(3):
-            lhs = table[
-                pl.ds(2 * core + 2 - step, 2), 2 - tap : 2 - tap + ROWS, :, column * CH : (column + 1) * CH
-            ]
-            more = nt(lhs.reshape(2 * ROWS * OWN, CH), weights[0, tap, column])
-            part = more if part is None else part + more
-        total[...] += part
-
-    @pl.when(step == 2)
+    backward_taps(table, 2 * core, 2, OWN, weights, total)
+
+    @pl.when(pl.program_id(0) == 2)
     def _():
         for frame in range(2):
-            rows = ROWS * OWN
-            values = total[frame * rows : (frame + 1) * rows].reshape(ROWS, OWN, CH)
-            values = values + own_columns(grad_sum[2 * core + frame])
+            values = frame_of(total, frame, OWN) + own_columns(grad_sum[2 * core + frame])
             grad_features[:, frame] = values.astype(BF16)
 
 
-def cotangent_kernel(core_ref, mine, other, weights, summed, mask, grad_sum, table):
+def cotangent_kernel(core_ref, mine, other, weights, summed, mask, grad_sum, head, table):
     core = core_ref[0]
     border = jnp.zeros((FR, WIN, 4 * CH), BF16)
     table[:, 0, 0] = border
@@ -206,6 +198,8 @@
         values = summed[frame]
         grad = grad_act * slope_of(values, jax.nn.sigmoid(values)) * mask[...]
         grad_sum[frame] = grad.astype(BF16)
+        if frame < 2:
+            head[frame] = grad.astype(BF16)
 
 
 def up_grad_kernel(core_ref, act, mine, other, out, table, flipped):
@@ -268,16 +262,17 @@
 
 
 def second_grad_kernel(place, act, block, later, up, out, table, flipped, sums):
-    tap_sums(lambda frame: act[frame], block, later, table, flipped, sums)
-    for group in range(4):
+    tap_sums(lambda frame: act[2 + frame], block, later, table, flipped, sums)
+    for step in range(4):
+        group = lax.rem(place[1] + step, 4)
         for member in range(16):
-            chunk = member // 4 * 16 + group * 4 + member % 4
+            chunk = member * 4 + step
             out[chunk, :UP_ROWS] = up[group * 16 + member]
             out[chunk, UP_ROWS:] = piece_of(sums, 2 * group + place[0], member).astype(BF16)
 
 
 def first_grad_kernel(place, act, block, later, own, next_one, next_two, next_three, table, flipped, sums):
-    tap_sums(lambda frame: act[frame // 2, :, frame % 2], block, later, table, flipped, sums)
+    tap_sums(lambda frame: act[frame // 2, :, 2 + frame % 2], block, later, table, flipped, sums)
     for step, out in enumerate((own, next_one, next_two, next_three)):
         group = lax.rem(place[1] + step, 4)
         for member in range(16):
@@ -318,6 +313,10 @@
     return lax.ppermute(value, axis, [(i, i + step) for i in range(count) if 0 <= i + step < count])
 
 
+def over_y(value, step):
+    return lax.ppermute(value, "y", [(i, (i + step) % 4) for i in range(4)])
+
+
 def shards(features, conv_first, conv_second, up_kernel, cotangent):
     core = lax.axis_index("core")
     height = 2 * lax.axis_index("z") + lax.axis_index("x_hi")
@@ -329,18 +328,23 @@
     inside = ((columns >= 0) & (columns < 128)).astype(F32)
     mask = jnp.broadcast_to(inside[:, None], (WIN, CH))
     act_shape = (FR, ROWS, WIN, CH)
+    two_frames = (2, ROWS, WIN, CH)
+    six_frames = (FR + 2, ROWS, WIN, CH)
     table = pltpu.VMEM((FR + 2, ROWS + 2, WIN, 3 * CH), BF16)
     own_table = pltpu.VMEM((FR + 2, ROWS + 2, OWN, 3 * CH), BF16)
     total = pltpu.VMEM((FR * ROWS * WIN, CH), F32)
     tap_flops = 2 * FR * ROWS * WIN * CH * CH
 
-    padded = jnp.pad(features[:, 0], ((0, 0), (EDGE, EDGE), (0, 0))).reshape(2, 17, OWN, CH)
+    frames = features[:, 0]
+    frames = jnp.concatenate([shift(frames, "y", 1), frames], axis=0)
+    padded = jnp.pad(frames, ((0, 0), (EDGE, EDGE), (0, 0))).reshape(4, 17, OWN, CH)
     windows = jnp.concatenate([padded[:, :-1], padded[:, 1:]], axis=2)
-    windows = windows.reshape(2, 2, 8, WIN, CH).transpose(2, 1, 0, 3, 4).reshape(1, 16, 2, WIN, CH)
-    windows = jnp.broadcast_to(windows, (2, 16, 2, WIN, CH)).reshape(32, 2, WIN, CH)
+    windows = windows.reshape(4, 2, 8, WIN, CH).transpose(2, 1, 0, 3, 4).reshape(1, 16, 4, WIN, CH)
+    windows = jnp.broadcast_to(windows, (2, 16, 4, WIN, CH)).reshape(32, 4, WIN, CH)
     block = lax.all_to_all(windows, ("core", "z", "x_hi", "width"), 0, 0, tiled=True)
 
-    paired = cotangent.reshape(2, 4, 64, 2 * CH)
+    paired, _ = lax.optimization_barrier((cotangent, windows))
+    paired = paired.reshape(2, 4, 64, 2 * CH)
     edge = jnp.where(width == 0, paired[:, :, 64 - EDGE :], paired[:, :, :EDGE])
     edge = lax.ppermute(edge, "width", [(0, 1), (1, 0)])
     nothing = jnp.zeros_like(edge)
@@ -348,30 +352,30 @@
     paired = jnp.concatenate([low, paired, high], axis=2).reshape(2, 4, 9, OWN, 2 * CH)
     fine = jnp.concatenate([paired[:, :, :-1], paired[:, :, 1:]], axis=3).transpose(2, 0, 1, 3, 4)
     fine, block = lax.optimization_barrier((fine, block))
-    block = block.reshape(2, ROWS, 2, WIN, CH)
-    halo = shift(block[1], "y", 1)
+    block = block.reshape(2, ROWS, 4, WIN, CH)
     mine = lax.all_to_all(fine, ("z", "x_hi"), 0, 0, tiled=True).reshape(8, 2, 2, 2, WIN, 2 * CH)
 
     first_act, first_slope = call(
-        first_kernel, (3,), (halo, block, conv_first, mask),
-        [whole(halo.shape), whole(block.shape), tap_weights(), whole(mask.shape)],
-        [(act_shape, BF16), (act_shape, F32)], [table, total], 27 * tap_flops,
-    )
-    mine, first_act = lax.optimization_barrier((mine, first_act))
-    earlier = shift(first_act[2:], "y", 1)
+        first_kernel, (3,), (block, conv_first, mask),
+        [whole(block.shape), tap_weights(), whole(mask.shape)],
+        [(six_frames, BF16), (act_shape, F32)],
+        [pltpu.VMEM((FR + 4, ROWS + 2, WIN, 3 * CH), BF16), pltpu.VMEM(((FR + 2) * ROWS * WIN, CH), F32)],
+        40 * tap_flops,
+    )
+    mine, first_slope = lax.optimization_barrier((mine, first_slope))
     other = lax.ppermute(mine, "core", [(0, 1), (1, 0)])
     summed, up_act = call(
-        second_kernel, (3,), (earlier, first_act, block, conv_second),
-        [whole(earlier.shape), whole(act_shape), whole(block.shape), tap_weights()],
+        second_kernel, (3,), (first_act, block, conv_second),
+        [whole(six_frames), whole(block.shape), tap_weights()],
         [(act_shape, F32), (act_shape, BF16)], [table, total], 27 * tap_flops,
     )
-    grad_sum = call(
+    grad_sum, sum_head = call(
         cotangent_kernel, (), (core_arg, mine, other, up_kernel, summed, mask),
         [SMEM, whole(mine.shape), whole(mine.shape), whole(up_kernel.shape), whole(act_shape), whole(mask.shape)],
-        [(act_shape, BF16)], [pltpu.VMEM((FR, ROWS + 1, 2, WIN, 4 * CH), BF16)], 16 * tap_flops,
-    )
-    later = shift(grad_sum[:2], "y", -1)
-    up_act, later = lax.optimization_barrier((up_act, later))
+        [(act_shape, BF16), (two_frames, BF16)], [pltpu.VMEM((FR, ROWS + 1, 2, WIN, 4 * CH), BF16)], 16 * tap_flops,
+    )
+    later = shift(sum_head, "y", -1)
+    up_act, grad_sum = lax.optimization_barrier((up_act, grad_sum))
     up_part = call(
         up_grad_kernel, (), (core_arg, up_act, mine, other),
         [SMEM, whole(act_shape), whole(mine.shape), whole(mine.shape)],
@@ -381,17 +385,17 @@
     grad_scratch = [own_table, pltpu.VMEM((CH, FR * ROWS * OWN), BF16), pltpu.VMEM((TAPS * CH + 8, CH), F32)]
     early = call(
         second_grad_kernel, (), (place, first_act, grad_sum, later, up_part),
-        [SMEM, whole(act_shape), whole(act_shape), whole(later.shape), whole(up_part.shape)],
+        [SMEM, whole(six_frames), whole(act_shape), whole(later.shape), whole(up_part.shape)],
         [((64, UP_ROWS + PIECE, CH), BF16)], grad_scratch, 14 * tap_flops,
     )
-    early = lax.all_to_all(early, "z", 0, 0, tiled=True)
-
-    grad_hidden = call(
+    early = lax.all_to_all(early, ("z", "x_hi", "width"), 0, 0, tiled=True)
+
+    grad_hidden, hidden_head = call(
         hidden_kernel, (3,), (grad_sum, later, first_slope, conv_second, mask),
         [whole(act_shape), whole(later.shape), whole(act_shape), tap_weights(), whole(mask.shape)],
-        [(act_shape, BF16)], [table, total], 27 * tap_flops,
-    )
-    later_hidden = shift(grad_hidden[:2], "y", -1)
+        [(act_shape, BF16), (two_frames, BF16)], [table, total], 27 * tap_flops,
+    )
+    later_hidden = shift(hidden_head, "y", -1)
     blocks = call(
         first_grad_kernel, (), (place, block, grad_hidden, later_hidden),
         [SMEM, whole(block.shape), whole(act_shape), whole(later_hidden.shape)],
@@ -399,7 +403,7 @@
     )
     arrived = [blocks[0]]
     for step in (2, 1, 3):
-        arrived.append(lax.ppermute(blocks[step], "y", [(i, (i + step) % 4) for i in range(4)]))
+        arrived.append(over_y(blocks[step], step))
     tied_hidden, _ = lax.optimization_barrier((grad_hidden, blocks[0]))
     rows_out = call(
         features_kernel, (3,), (core_arg, tied_hidden, later_hidden, grad_sum, conv_first),
@@ -407,15 +411,17 @@
         [((ROWS, 2, OWN, CH), BF16)], [own_table, pltpu.VMEM((2 * ROWS * OWN, CH), F32)], 7 * tap_flops,
     )
 
-    early = jnp.sum(early.reshape(4, 16, UP_ROWS + PIECE, CH).astype(F32), axis=0).astype(BF16)
-    early = lax.all_to_all(early, ("y", "x_hi", "width"), 0, 0, tiled=True)
+    tied_rows, early = lax.optimization_barrier((rows_out, early))
+    early = jnp.sum(early.reshape(16, 4, UP_ROWS + PIECE, CH).astype(F32), axis=0)
+    early_total = early[0]
+    for step in (2, 1, 3):
+        early_total += over_y(early[step].astype(BF16), step).astype(F32)
     first_sum = sum(value.astype(F32) for value in arrived).astype(BF16)
-    late = jnp.concatenate([rows_out.reshape(16, 2 * OWN, CH), first_sum], axis=1)
-    late, early = lax.optimization_barrier((late, early))
+    late = jnp.concatenate([tied_rows.reshape(16, 2 * OWN, CH), first_sum], axis=1)
     late = lax.all_to_all(late, ("z", "x_hi", "width"), 0, 0, tiled=True)
 
     factor = 1.0 / math.sqrt(32768)
-    early = jnp.sum(early.astype(F32), axis=0) * factor
+    early = early_total * factor
     returned = late[:, : 2 * OWN].reshape(8, 2, 2, OWN, CH).transpose(2, 1, 0, 3, 4)
     first_share = jnp.sum(late[:, 2 * OWN : 2 * OWN + SHARE].astype(F32), axis=0) * factor
     return (

time: 165 us -> 157 us (0.952)
  local copies, waits for them, and re-layouts: 19 us -> 14.1 us
  starting transfers between devices: 43.9 us -> 39.3 us
  Pallas kernels: 31.6 us -> 34.3 us
  other arithmetic: 7.64 us -> 4.95 us
    ppermute x3 -> x6, waiting for transfers between devices: 0.01 us -> 21.9 us  [over_y(): return lax.ppermute(value, 'y', [(i, (i + step) % 4) for i in range(4)])]
    all_to_all x2 -> x1, waiting for transfers between devices: 12.8 us -> 0.01 us  [shards(): early = lax.all_to_all(early, ('z', 'x_hi', 'width'), 0, 0, tiled=True)]
    ppermute x1, waiting for transfers between devices: 0.01 us -> 12.7 us  [shards(): edge = lax.ppermute(edge, 'width', [(0, 1), (1, 0)])]
    ppermute x4 -> x3, waiting for transfers between devices: 28.4 us -> 18.8 us  [shift(): lax.ppermute(value, axis, [(i, i + step) for i in range(count) if 0 <= i...]
    all_to_all x1, waiting for transfers between devices: 11.5 us -> 2.47 us  [shards(): lax.all_to_all(windows, ('core', 'z', 'x_hi', 'width'), 0, 0, tiled=True)]
    all_to_all x1, waiting for transfers between devices: 7.94 us -> 0.01 us  [shards(): late = lax.all_to_all(late, ('z', 'x_hi', 'width'), 0, 0, tiled=True)]
    all_to_all x2 -> x1, starting transfers between devices: 11.8 us -> 4.6 us  [shards(): early = lax.all_to_all(early, ('z', 'x_hi', 'width'), 0, 0, tiled=True)]
    all_to_all x1, waiting for transfers between devices: 0.31 us -> 6.7 us  [shards(): lax.all_to_all(fine, ('z', 'x_hi'), 0, 0, tiled=True)]
  transfers between devices with their start and end apart: 14 -> 15, of which waited for: 9 -> 12; matrix products, arithmetic and copies ran while one was open for 7% -> 3% of each run, Pallas kernels for 13% -> 17%
where the time goes in v7:
time: 157 us; the launch traced here: 156 us
  waiting for transfers between devices  62.6 us (40%)
  starting transfers between devices  39.3 us (25%)
  Pallas kernels  34.3 us (22%)
  local copies, waits for them, and re-layouts  14.1 us (9%)
  other arithmetic  4.95 us (3%)
    pallas_call x8, Pallas kernels, call(): pl.pallas_call(kernel, out_shape=shapes[0] if single else shapes, grid=gr...  34.3 us
    ppermute x6, waiting for transfers between devices, over_y(): return lax.ppermute(value, 'y', [(i, (i + step) % 4) for i in range(4)])  21.9 us
    ppermute x3, waiting for transfers between devices, shift(): lax.ppermute(value, axis, [(i, i + step) for i in range(count) if 0 <= i...  18.8 us
    ppermute x1, waiting for transfers between devices, shards(): edge = lax.ppermute(edge, 'width', [(0, 1), (1, 0)])  12.7 us
    unnamed x30, local copies, waits for them, and re-layouts  9.55 us
    all_to_all x1, starting transfers between devices, shards(): lax.all_to_all(windows, ('core', 'z', 'x_hi', 'width'), 0, 0, tiled=True)  8.16 us
    ppermute x6, starting transfers between devices, over_y(): return lax.ppermute(value, 'y', [(i, (i + step) % 4) for i in range(4)])  7.94 us
    all_to_all x1, waiting for transfers between devices, shards(): lax.all_to_all(fine, ('z', 'x_hi'), 0, 0, tiled=True)  6.7 us
  transfers between devices with their start and end apart: 15, of which 12 were waited for; matrix products, arithmetic and copies ran while one was open for 3% of the time, Pallas kernels for 17%

profile of v7, /device:TPU:0, one launch (start us, length us, event | category | flops | bytes accessed | tf_op | source)
XLA Modules:
  0.0 156.2 jit_solution(10965653113796467139)
XLA Ops:
  0.6 3.6 %collective-permute-start = (bf16[2,128,256]{2,1,0:T(8,128)(2,1)}, bf16[2,128,256]{2,1,0:T(8,128)(2,1)S(1)}, u32[]{:S(2)}, u32[]{:S(2)}) collective-permute-start(bf16[2,128,256]{2,1,0:T(8,128)(2,1)} %bitcast.55), channel_id=1, source_target_pairs={{0,32},{32,64},{64,96},{1,33},{33,65},{65,97},{2,34},{34,66},{66,9... | collective-permute-start | bytes 393224 | tf_op jit(solution)/shard_map/ppermute | solution.py:313
  4.2 3.0 %collective-permute-done = bf16[2,128,256]{2,1,0:T(8,128)(2,1)S(1)} collective-permute-done((bf16[2,128,256]{2,1,0:T(8,128)(2,1)}, bf16[2,128,256]{2,1,0:T(8,128)(2,1)S(1)}, u32[]{:S(2)}, u32[]{:S(2)}) %collective-permute-start) | collective-permute-done | bytes 131104 | tf_op jit(solution)/shard_map/ppermute | solution.py:313
  9.5 8.2 %all-to-all-start = ((bf16[32,4,16,256]{3,2,1,0:T(8,128)(2,1)}), bf16[32,4,16,256]{3,2,1,0:T(8,128)(2,1)S(1)}, u32[]{:S(2)}, u32[]{:S(2)}) async-start(bf16[32,4,16,256]{3,2,1,0:T(8,128)(2,1)} %bitcast.6), calls=%async_computation | async-start | bytes 2097152 | tf_op jit(solution)/shard_map/all_to_all | solution.py:344
  19.8 12.7 %collective-permute-done.1 = bf16[2,4,4,512]{3,2,1,0:T(4,128)(2,1)S(1)} collective-permute-done((bf16[2,4,4,512]{3,2,1,0:T(4,128)(2,1)S(1)}, bf16[2,4,4,512]{3,2,1,0:T(4,128)(2,1)S(1)}, u32[]{:S(2)}, u32[]{:S(2)}) %collective-permute-start.1) | collective-permute-done | bytes 32800 | tf_op jit(solution)/shard_map/ppermute | solution.py:349
  32.9 2.5 %all-to-all-done = bf16[32,4,16,256]{3,2,1,0:T(8,128)(2,1)S(1)} async-done(((bf16[32,4,16,256]{3,2,1,0:T(8,128)(2,1)}), bf16[32,4,16,256]{3,2,1,0:T(8,128)(2,1)S(1)}, u32[]{:S(2)}, u32[]{:S(2)}) %all-to-all-start) | async-done | bytes 1048608 | tf_op jit(solution)/shard_map/all_to_all | solution.py:344
  36.5 3.9 %all-to-all-start.1 = ((bf16[8,2,4,16,512]{4,3,2,1,0:T(8,128)(2,1)}), bf16[8,2,4,16,512]{4,3,2,1,0:T(8,128)(2,1)S(1)}, u32[]{:S(2)}, u32[]{:S(2)}) async-start(bf16[8,2,4,16,512]{4,3,2,1,0:T(8,128)(2,1)} %copy.16), calls=%async_computation.1 | async-start | bytes 2097152 | tf_op jit(solution)/shard_map/all_to_all | solution.py:356
  40.5 8.4 %shard_map.84 = (bf16[6,16,16,256]{3,2,1,0:T(8,128)(2,1)S(1)}, f32[4,16,16,256]{3,2,1,0:T(8,128)S(1)}) custom-call(bf16[2,16,4,16,256]{4,3,2,1,0:T(8,128)(2,1)S(1)} %bitcast.47, bf16[3,3,3,256,256]{4,3,2,1,0:T(8,128)(2,1)} %weights.9, f32[16,256]{1,0:T(8,128)S(1)} %broadcast_in_dim.19.mask), custom_call_target="tpu_custom_call" | custom-call | flops 5368709120 | bytes 6438912 | tf_op jit(solution)/shard_map/pallas_call | solution.py:299
  50.7 6.7 %all-to-all-done.1 = bf16[8,2,4,16,512]{4,3,2,1,0:T(8,128)(2,1)S(1)} async-done(((bf16[8,2,4,16,512]{4,3,2,1,0:T(8,128)(2,1)}), bf16[8,2,4,16,512]{4,3,2,1,0:T(8,128)(2,1)S(1)}, u32[]{:S(2)}, u32[]{:S(2)}) %all-to-all-start.1) | async-done | bytes 1048608 | tf_op jit(solution)/shard_map/all_to_all | solution.py:356
  58.6 6.2 %shard_map.85 = (f32[4,16,16,256]{3,2,1,0:T(8,128)S(1)}, bf16[4,16,16,256]{3,2,1,0:T(8,128)(2,1)S(1)}) custom-call(bf16[6,16,16,256]{3,2,1,0:T(8,128)(2,1)S(1)} %copy-done.9, bf16[2,16,4,16,256]{4,3,2,1,0:T(8,128)(2,1)S(1)} %bitcast.48, bf16[3,3,3,256,256]{4,3,2,1,0:T(8,128)(2,1)} %weights.8), custom_call_target="tpu_custom_call" | custom-call | flops 3623878656 | bytes 6946816 | tf_op jit(solution)/shard_map/pallas_call | solution.py:299
  65.6 3.5 %shard_map.86 = (bf16[4,16,16,256]{3,2,1,0:T(8,128)(2,1)S(1)}, bf16[2,16,16,256]{3,2,1,0:T(8,128)(2,1)}) custom-call(s32[1]{0:T(128)} %bitcast.core_ref, bf16[8,2,2,2,16,512]{5,4,3,2,1,0:T(8,128)(2,1)S(1)} %bitcast.45, bf16[8,2,2,2,16,512]{5,4,3,2,1,0:T(8,128)(2,1)S(1)} %collective-permute-done.2.other, bf16[4,4,256,256]{3,2,1,0:T(8,128)(2,1)S(1)} %copy-done.7, ...), custom_call_target="tpu_custom_call" | custom-call | flops 2147483648 | bytes 6045700 | tf_op jit(solution)/shard_map/pallas_call | solution.py:299
  74.3 7.1 %collective-permute-done.3.later = bf16[2,16,16,256]{3,2,1,0:T(8,128)(2,1)S(1)} collective-permute-done((bf16[2,16,16,256]{3,2,1,0:T(8,128)(2,1)}, bf16[2,16,16,256]{3,2,1,0:T(8,128)(2,1)S(1)}, u32[]{:S(2)}, u32[]{:S(2)}) %collective-permute-start.3) | collective-permute-done | bytes 262176 | tf_op jit(solution)/shard_map/ppermute | solution.py:313
  81.4 4.7 %shard_map.91 = bf16[64,88,256]{2,1,0:T(8,128)(2,1)} custom-call(s32[2]{0:T(128)S(1)} %pad_add_fusion.place, bf16[6,16,16,256]{3,2,1,0:T(8,128)(2,1)S(1)} %copy-done.10, bf16[4,16,16,256]{3,2,1,0:T(8,128)(2,1)S(1)} %copy-done.2, bf16[2,16,16,256]{3,2,1,0:T(8,128)(2,1)S(1)} %collective-permute-done.3.later, bf16[64,32,256]{2,1,0:T(8,128)(2,1)S(1)} %shard_map.90.up), custom_call_target="tpu_custom_call" | custom-call | flops 1879048192 | bytes 5505032 | tf_op jit(solution)/shard_map/pallas_call | solution.py:299
  86.0 4.6 %all-to-all-start.2 = ((bf16[64,88,256]{2,1,0:T(8,128)(2,1)}), bf16[64,88,256]{2,1,0:T(8,128)(2,1)}, u32[]{:S(2)}, u32[]{:S(2)}) async-start(bf16[64,88,256]{2,1,0:T(8,128)(2,1)} %shard_map.91), calls=%async_computation.2 | async-start | bytes 5767168 | tf_op jit(solution)/shard_map/all_to_all | solution.py:391
  90.7 2.0 %copy-done.6 = bf16[3,3,3,256,256]{4,3,2,1,0:T(8,128)(2,1)S(1)} copy-done((bf16[3,3,3,256,256]{4,3,2,1,0:T(8,128)(2,1)S(1)}, bf16[3,3,3,256,256]{4,3,2,1,0:T(8,128)(2,1)}, u32[]{:S(2)}) %copy-start.6) | copy-done | bytes 3538968
  93.9 4.8 %shard_map.87 = (bf16[4,16,16,256]{3,2,1,0:T(8,128)(2,1)S(1)}, bf16[2,16,16,256]{3,2,1,0:T(8,128)(2,1)S(1)}) custom-call(bf16[4,16,16,256]{3,2,1,0:T(8,128)(2,1)S(1)} %copy-done.3, bf16[2,16,16,256]{3,2,1,0:T(8,128)(2,1)S(1)} %collective-permute-done.3.later, f32[4,16,16,256]{3,2,1,0:T(8,128)S(1)} %copy-done.12, bf16[3,3,3,256,256]{4,3,2,1,0:T(8,128)(2,1)S(1)} %copy-done.6, ...), custom_call_target="tpu_custom_call" | custom-call | flops 3623878656 | bytes 6176768 | tf_op jit(solution)/shard_map/pallas_call | solution.py:299
  100.0 8.7 %collective-permute-done.4.later = bf16[2,16,16,256]{3,2,1,0:T(8,128)(2,1)S(1)} collective-permute-done((bf16[2,16,16,256]{3,2,1,0:T(8,128)(2,1)S(1)}, bf16[2,16,16,256]{3,2,1,0:T(8,128)(2,1)S(1)}, u32[]{:S(2)}, u32[]{:S(2)}) %collective-permute-start.4) | collective-permute-done | bytes 262176 | tf_op jit(solution)/shard_map/ppermute | solution.py:313
  108.7 3.0 %shard_map.88 = (bf16[16,56,256]{2,1,0:T(8,128)(2,1)S(1)}, bf16[16,56,256]{2,1,0:T(8,128)(2,1)S(1)}, bf16[16,56,256]{2,1,0:T(8,128)(2,1)S(1)}, bf16[16,56,256]{2,1,0:T(8,128)(2,1)S(1)}) custom-call(s32[2]{0:T(128)S(1)} %pad_add_fusion.place, bf16[2,16,4,16,256]{4,3,2,1,0:T(8,128)(2,1)S(1)} %bitcast.49, bf16[4,16,16,256]{3,2,1,0:T(8,128)(2,1)S(1)} %get-tuple-element.41.block, ...), custom_call_target="tpu_custom_call" | custom-call | flops 1879048192 | bytes 3670024 | tf_op jit(solution)/shard_map/pallas_call | solution.py:299
  113.9 3.1 %collective-permute-start.5 = (bf16[16,56,256]{2,1,0:T(8,128)(2,1)S(1)}, bf16[16,56,256]{2,1,0:T(8,128)(2,1)S(1)}, u32[]{:S(2)}, u32[]{:S(2)}) collective-permute-start(bf16[16,56,256]{2,1,0:T(8,128)(2,1)S(1)} %get-tuple-element.44), channel_id=1, source_target_pairs={{0,64},{32,96},{64,0},{96,32},{1,65},{33,97},{65,1},{97,33},{2,66}... | collective-permute-start | bytes 1376264 | tf_op jit(solution)/shard_map/ppermute | solution.py:317
  119.0 6.3 %collective-permute-done.7 = bf16[16,56,256]{2,1,0:T(8,128)(2,1)S(1)} collective-permute-done((bf16[16,56,256]{2,1,0:T(8,128)(2,1)S(1)}, bf16[16,56,256]{2,1,0:T(8,128)(2,1)S(1)}, u32[]{:S(2)}, u32[]{:S(2)}) %collective-permute-start.7) | collective-permute-done | bytes 458784 | tf_op jit(solution)/shard_map/ppermute | solution.py:317
  126.8 9.1 %collective-permute-done.5 = bf16[16,56,256]{2,1,0:T(8,128)(2,1)S(1)} collective-permute-done((bf16[16,56,256]{2,1,0:T(8,128)(2,1)S(1)}, bf16[16,56,256]{2,1,0:T(8,128)(2,1)S(1)}, u32[]{:S(2)}, u32[]{:S(2)}) %collective-permute-start.5) | collective-permute-done | bytes 458784 | tf_op jit(solution)/shard_map/ppermute | solution.py:317
  137.0 6.5 %all-to-all-start.3 = ((bf16[16,72,256]{2,1,0:T(8,128)(2,1)}), bf16[16,72,256]{2,1,0:T(8,128)(2,1)S(1)}, u32[]{:S(2)}, u32[]{:S(2)}) async-start(bf16[16,72,256]{2,1,0:T(8,128)(2,1)} %pad_maximum_fusion), calls=%async_computation.3 | async-start | bytes 1179648 | tf_op jit(solution)/shard_map/all_to_all | solution.py:421
  143.5 2.2 %convert_reduce_fusion = f32[4,88,256]{2,1,0:T(8,128)S(1)} fusion(bf16[16,4,88,256]{3,2,1,0:T(8,128)(2,1)} %bitcast.23), kind=kLoop, calls=%fused_computation | loop fusion | flops 2793472 | bytes 3244032 | tf_op jit(solution)/shard_map/reduce_sum | solution.py:415
  145.9 2.0 %collective-permute-start.9 = (bf16[88,256]{1,0:T(8,128)(2,1)S(1)}, bf16[88,256]{1,0:T(8,128)(2,1)S(1)}, u32[]{:S(2)}, u32[]{:S(2)}) collective-permute-start(bf16[88,256]{1,0:T(8,128)(2,1)S(1)} %get-tuple-element.54), channel_id=1, source_target_pairs={{0,32},{32,64},{64,96},{96,0},{1,33},{33,65},{65,97},{97,1},{2,34}... | collective-permute-start | bytes 135176 | tf_op jit(solution)/shard_map/ppermute | solution.py:317
  151.3 2.2 %collective-permute-done.8 = bf16[88,256]{1,0:T(8,128)(2,1)S(1)} collective-permute-done((bf16[88,256]{1,0:T(8,128)(2,1)S(1)}, bf16[88,256]{1,0:T(8,128)(2,1)S(1)}, u32[]{:S(2)}, u32[]{:S(2)}) %collective-permute-start.8) | collective-permute-done | bytes 45088 | tf_op jit(solution)/shard_map/ppermute | solution.py:317
  (72 shorter events, 30.1 us)
Async XLA Ops:
  0.6 6.6 %collective-permute-start = (bf16[2,128,256]{2,1,0:T(8,128)(2,1)}, bf16[2,128,256]{2,1,0:T(8,128)(2,1)S(1)}, u32[]{:S(2)}, u32[]{:S(2)}) collective-permute-start(bf16[2,128,256]{2,1,0:T(8,128)(2,1)} %bitcast.55), channel_id=1, source_target_pairs={{0,32},{32,64},{64,96},{1,33},{33,65},{65,97},{2,34},{34,66},{66,9... | collective-permute-start | bytes 393224 | tf_op jit(solution)/shard_map/ppermute | solution.py:313
  8.4 9.3 %copy-start.13 = (bf16[2,4,128,256]{3,2,1,0:T(8,128)(2,1)S(1)}, bf16[2,4,128,256]{3,2,1,0:T(8,128)(2,1)}, u32[]{:S(2)}) copy-start(bf16[2,4,128,256]{3,2,1,0:T(8,128)(2,1)} %param.9) | copy-start | bytes 1572868
  9.5 25.9 %all-to-all-start = ((bf16[32,4,16,256]{3,2,1,0:T(8,128)(2,1)}), bf16[32,4,16,256]{3,2,1,0:T(8,128)(2,1)S(1)}, u32[]{:S(2)}, u32[]{:S(2)}) async-start(bf16[32,4,16,256]{3,2,1,0:T(8,128)(2,1)} %bitcast.6), calls=%async_computation | async-start | bytes 2097152 | tf_op jit(solution)/shard_map/all_to_all | solution.py:344
  17.9 14.6 %collective-permute-start.1 = (bf16[2,4,4,512]{3,2,1,0:T(4,128)(2,1)S(1)}, bf16[2,4,4,512]{3,2,1,0:T(4,128)(2,1)S(1)}, u32[]{:S(2)}, u32[]{:S(2)}) collective-permute-start(bf16[2,4,4,512]{3,2,1,0:T(4,128)(2,1)S(1)} %slice_select_fusion), channel_id=1, source_target_pairs={{0,1},{1,0},{2,3},{3,2},{4,5},{5,4},{6,7},{7,6},{8,9},{9,8},{10,11... | collective-permute-start | bytes 98312 | tf_op jit(solution)/shard_map/ppermute | solution.py:349
  36.5 21.0 %all-to-all-start.1 = ((bf16[8,2,4,16,512]{4,3,2,1,0:T(8,128)(2,1)}), bf16[8,2,4,16,512]{4,3,2,1,0:T(8,128)(2,1)S(1)}, u32[]{:S(2)}, u32[]{:S(2)}) async-start(bf16[8,2,4,16,512]{4,3,2,1,0:T(8,128)(2,1)} %copy.16), calls=%async_computation.1 | async-start | bytes 2097152 | tf_op jit(solution)/shard_map/all_to_all | solution.py:356
  57.4 8.2 %collective-permute-start.2 = (bf16[8,2,2,2,16,512]{5,4,3,2,1,0:T(8,128)(2,1)S(1)}, bf16[8,2,2,2,16,512]{5,4,3,2,1,0:T(8,128)(2,1)S(1)}, u32[]{:S(2)}, u32[]{:S(2)}) collective-permute-start(bf16[8,2,2,2,16,512]{5,4,3,2,1,0:T(8,128)(2,1)S(1)} %bitcast.44), channel_id=1, source_target_pairs={{0,16},{16,0},{1,17},{17,1},{2,18},{18,2},{3,19},{19,3},{4,20},{20... | collective-permute-start | bytes 3145736 | tf_op jit(solution)/shard_map/ppermute | solution.py:366
  57.4 1.1 copy-start.9
  58.6 7.1 %copy-start.7 = (bf16[4,4,256,256]{3,2,1,0:T(8,128)(2,1)S(1)}, bf16[4,4,256,256]{3,2,1,0:T(8,128)(2,1)}, u32[]{:S(2)}) copy-start(bf16[4,4,256,256]{3,2,1,0:T(8,128)(2,1)} %weights.7) | copy-start | bytes 6291460
  69.9 11.4 %collective-permute-start.3 = (bf16[2,16,16,256]{3,2,1,0:T(8,128)(2,1)}, bf16[2,16,16,256]{3,2,1,0:T(8,128)(2,1)S(1)}, u32[]{:S(2)}, u32[]{:S(2)}) collective-permute-start(bf16[2,16,16,256]{3,2,1,0:T(8,128)(2,1)} %get-tuple-element.36), channel_id=1, source_target_pairs={{32,0},{64,32},{96,64},{33,1},{65,33},{97,65},{34,2},{66,34},{98,6... | collective-permute-start | bytes 786440 | tf_op jit(solution)/shard_map/ppermute | solution.py:313
  71.4 10.0 %copy-start.2 = (bf16[4,16,16,256]{3,2,1,0:T(8,128)(2,1)S(1)}, bf16[4,16,16,256]{3,2,1,0:T(8,128)(2,1)}, u32[]{:S(2)}) copy-start(bf16[4,16,16,256]{3,2,1,0:T(8,128)(2,1)} %copy-done.1) | copy-start | bytes 1572868
  72.6 8.8 %copy-start.10 = (bf16[6,16,16,256]{3,2,1,0:T(8,128)(2,1)S(1)}, bf16[6,16,16,256]{3,2,1,0:T(8,128)(2,1)}, u32[]{:S(2)}) copy-start(bf16[6,16,16,256]{3,2,1,0:T(8,128)(2,1)} %copy-done.8) | copy-start | bytes 2359300
  86.0 4.6 %copy-start.3 = (bf16[4,16,16,256]{3,2,1,0:T(8,128)(2,1)S(1)}, bf16[4,16,16,256]{3,2,1,0:T(8,128)(2,1)}, u32[]{:S(2)}) copy-start(bf16[4,16,16,256]{3,2,1,0:T(8,128)(2,1)} %copy-done.1) | copy-start | bytes 1572868
  86.0 50.1 %all-to-all-start.2 = ((bf16[64,88,256]{2,1,0:T(8,128)(2,1)}), bf16[64,88,256]{2,1,0:T(8,128)(2,1)}, u32[]{:S(2)}, u32[]{:S(2)}) async-start(bf16[64,88,256]{2,1,0:T(8,128)(2,1)} %shard_map.91), calls=%async_computation.2 | async-start | bytes 5767168 | tf_op jit(solution)/shard_map/all_to_all | solution.py:391
  90.7 2.0 %copy-start.6 = (bf16[3,3,3,256,256]{4,3,2,1,0:T(8,128)(2,1)S(1)}, bf16[3,3,3,256,256]{4,3,2,1,0:T(8,128)(2,1)}, u32[]{:S(2)}) copy-start(bf16[3,3,3,256,256]{4,3,2,1,0:T(8,128)(2,1)} %weights.8) | copy-start | bytes 10616836
  92.7 1.2 copy-start.12
  98.7 10.0 %collective-permute-start.4 = (bf16[2,16,16,256]{3,2,1,0:T(8,128)(2,1)S(1)}, bf16[2,16,16,256]{3,2,1,0:T(8,128)(2,1)S(1)}, u32[]{:S(2)}, u32[]{:S(2)}) collective-permute-start(bf16[2,16,16,256]{3,2,1,0:T(8,128)(2,1)S(1)} %get-tuple-element.39), channel_id=1, source_target_pairs={{32,0},{64,32},{96,64},{33,1},{65,33},{97,65},{34,2},{66,34},{98,6... | collective-permute-start | bytes 786440 | tf_op jit(solution)/shard_map/ppermute | solution.py:313
  108.7 8.3 %copy-start = (bf16[3,3,3,256,256]{4,3,2,1,0:T(8,128)(2,1)S(1)}, bf16[3,3,3,256,256]{4,3,2,1,0:T(8,128)(2,1)}, u32[]{:S(2)}) copy-start(bf16[3,3,3,256,256]{4,3,2,1,0:T(8,128)(2,1)} %weights.9) | copy-start | bytes 10616836
  111.8 13.5 %collective-permute-start.7 = (bf16[16,56,256]{2,1,0:T(8,128)(2,1)S(1)}, bf16[16,56,256]{2,1,0:T(8,128)(2,1)S(1)}, u32[]{:S(2)}, u32[]{:S(2)}) collective-permute-start(bf16[16,56,256]{2,1,0:T(8,128)(2,1)S(1)} %get-tuple-element.46), channel_id=1, source_target_pairs={{0,96},{32,0},{64,32},{96,64},{1,97},{33,1},{65,33},{97,65},{2,98}... | collective-permute-start | bytes 1376264 | tf_op jit(solution)/shard_map/ppermute | solution.py:317
  113.1 13.8 %collective-permute-start.6 = (bf16[16,56,256]{2,1,0:T(8,128)(2,1)S(1)}, bf16[16,56,256]{2,1,0:T(8,128)(2,1)S(1)}, u32[]{:S(2)}, u32[]{:S(2)}) collective-permute-start(bf16[16,56,256]{2,1,0:T(8,128)(2,1)S(1)} %get-tuple-element.45), channel_id=1, source_target_pairs={{0,32},{32,64},{64,96},{96,0},{1,33},{33,65},{65,97},{97,1},{2,34}... | collective-permute-start | bytes 1376264 | tf_op jit(solution)/shard_map/ppermute | solution.py:317
  113.9 22.0 %collective-permute-start.5 = (bf16[16,56,256]{2,1,0:T(8,128)(2,1)S(1)}, bf16[16,56,256]{2,1,0:T(8,128)(2,1)S(1)}, u32[]{:S(2)}, u32[]{:S(2)}) collective-permute-start(bf16[16,56,256]{2,1,0:T(8,128)(2,1)S(1)} %get-tuple-element.44), channel_id=1, source_target_pairs={{0,64},{32,96},{64,0},{96,32},{1,65},{33,97},{65,1},{97,33},{2,66}... | collective-permute-start | bytes 1376264 | tf_op jit(solution)/shard_map/ppermute | solution.py:317
  137.0 17.8 %all-to-all-start.3 = ((bf16[16,72,256]{2,1,0:T(8,128)(2,1)}), bf16[16,72,256]{2,1,0:T(8,128)(2,1)S(1)}, u32[]{:S(2)}, u32[]{:S(2)}) async-start(bf16[16,72,256]{2,1,0:T(8,128)(2,1)} %pad_maximum_fusion), calls=%async_computation.3 | async-start | bytes 1179648 | tf_op jit(solution)/shard_map/all_to_all | solution.py:421
  145.8 4.1 %collective-permute-start.10 = (bf16[88,256]{1,0:T(8,128)(2,1)S(1)}, bf16[88,256]{1,0:T(8,128)(2,1)S(1)}, u32[]{:S(2)}, u32[]{:S(2)}) collective-permute-start(bf16[88,256]{1,0:T(8,128)(2,1)S(1)} %get-tuple-element.53), channel_id=1, source_target_pairs={{0,96},{32,0},{64,32},{96,64},{1,97},{33,1},{65,33},{97,65},{2,98}... | collective-permute-start | bytes 135176 | tf_op jit(solution)/shard_map/ppermute | solution.py:317
  145.9 5.3 %collective-permute-start.9 = (bf16[88,256]{1,0:T(8,128)(2,1)S(1)}, bf16[88,256]{1,0:T(8,128)(2,1)S(1)}, u32[]{:S(2)}, u32[]{:S(2)}) collective-permute-start(bf16[88,256]{1,0:T(8,128)(2,1)S(1)} %get-tuple-element.54), channel_id=1, source_target_pairs={{0,32},{32,64},{64,96},{96,0},{1,33},{33,65},{65,97},{97,1},{2,34}... | collective-permute-start | bytes 135176 | tf_op jit(solution)/shard_map/ppermute | solution.py:317
  147.9 5.6 %collective-permute-start.8 = (bf16[88,256]{1,0:T(8,128)(2,1)S(1)}, bf16[88,256]{1,0:T(8,128)(2,1)S(1)}, u32[]{:S(2)}, u32[]{:S(2)}) collective-permute-start(bf16[88,256]{1,0:T(8,128)(2,1)S(1)} %get-tuple-element.52), channel_id=1, source_target_pairs={{0,64},{32,96},{64,0},{96,32},{1,65},{33,97},{65,1},{97,33},{2,66}... | collective-permute-start | bytes 135176 | tf_op jit(solution)/shard_map/ppermute | solution.py:317
  (5 other events, 4.6 us)

commit v8 on v7

--- a/solution.py
+++ b/solution.py
@@ -234,22 +234,22 @@
                 ].astype(BF16)
 
 
-def tap_sums(act_of, block, later, table, flipped, sums):
+def tap_sums(act_of, block, table, flipped, sums):
     clear_border(table)
+    column = lax.broadcasted_iota(jnp.int32, (ROWS, WIN, CH), 1)
+    own = (column >= EDGE) & (column < EDGE + OWN)
     for frame in range(FR):
-        fill_own_table(table, frame, block[frame])
-    for frame in range(2):
-        fill_own_table(table, FR + frame, later[frame])
-    for frame in range(FR):
-        rows = ROWS * OWN
-        flipped[:, frame * rows : (frame + 1) * rows] = jnp.transpose(
-            own_columns(act_of(frame)).reshape(rows, CH)
-        ).astype(BF16)
+        fill_table(table, frame, jnp.where(own, block[frame].astype(F32), 0.0).astype(BF16), False)
+    rows = ROWS * WIN
+    for frame in range(FR + 2):
+        values = act_of(frame).astype(F32).reshape(rows, CH)
+        flipped[:, frame * rows : (frame + 1) * rows] = jnp.transpose(values).astype(BF16)
     sums[TAPS * CH :] = jnp.zeros((8, CH), F32)
     for tap_t in range(3):
+        lhs = flipped[:, tap_t * rows : (tap_t + FR) * rows]
         for tap_h in range(3):
-            rhs = table[2 - tap_t : 2 - tap_t + FR, 2 - tap_h : 2 - tap_h + ROWS]
-            result = nn(flipped[...], rhs.reshape(FR * ROWS * OWN, 3 * CH))
+            rhs = table[:, 2 - tap_h : 2 - tap_h + ROWS]
+            result = nn(lhs, rhs.reshape(FR * rows, 3 * CH))
             for tap_w in range(3):
                 at = (tap_t * 9 + tap_h * 3 + tap_w) * CH
                 sums[at : at + CH] = result[:, tap_w * CH : (tap_w + 1) * CH]
@@ -261,8 +261,8 @@
     return sums[pl.ds(start, PIECE + 8)][at % 8 : at % 8 + PIECE]
 
 
-def second_grad_kernel(place, act, block, later, up, out, table, flipped, sums):
-    tap_sums(lambda frame: act[2 + frame], block, later, table, flipped, sums)
+def second_grad_kernel(place, act, block, up, out, table, flipped, sums):
+    tap_sums(lambda frame: act[frame], block, table, flipped, sums)
     for step in range(4):
         group = lax.rem(place[1] + step, 4)
         for member in range(16):
@@ -271,8 +271,11 @@
             out[chunk, UP_ROWS:] = piece_of(sums, 2 * group + place[0], member).astype(BF16)
 
 
-def first_grad_kernel(place, act, block, later, own, next_one, next_two, next_three, table, flipped, sums):
-    tap_sums(lambda frame: act[frame // 2, :, 2 + frame % 2], block, later, table, flipped, sums)
+def first_grad_kernel(place, act, block, own, next_one, next_two, next_three, table, flipped, sums):
+    def frame_at(frame):
+        return act[1, :, frame] if frame < 2 else act[(frame - 2) // 2, :, 2 + frame % 2]
+
+    tap_sums(frame_at, block, table, flipped, sums)
     for step, out in enumerate((own, next_one, next_two, next_three)):
         group = lax.rem(place[1] + step, 4)
         for member in range(16):
@@ -335,18 +338,18 @@
     total = pltpu.VMEM((FR * ROWS * WIN, CH), F32)
     tap_flops = 2 * FR * ROWS * WIN * CH * CH
 
+    paired = cotangent.reshape(2, 4, 64, 2 * CH)
+    edge = jnp.where(width == 0, paired[:, :, 64 - EDGE :], paired[:, :, :EDGE])
+    edge = lax.ppermute(edge, "width", [(0, 1), (1, 0)])
     frames = features[:, 0]
-    frames = jnp.concatenate([shift(frames, "y", 1), frames], axis=0)
+    before, edge = lax.optimization_barrier((shift(frames, "y", 1), edge))
+    frames = jnp.concatenate([before, frames], axis=0)
     padded = jnp.pad(frames, ((0, 0), (EDGE, EDGE), (0, 0))).reshape(4, 17, OWN, CH)
     windows = jnp.concatenate([padded[:, :-1], padded[:, 1:]], axis=2)
     windows = windows.reshape(4, 2, 8, WIN, CH).transpose(2, 1, 0, 3, 4).reshape(1, 16, 4, WIN, CH)
     windows = jnp.broadcast_to(windows, (2, 16, 4, WIN, CH)).reshape(32, 4, WIN, CH)
     block = lax.all_to_all(windows, ("core", "z", "x_hi", "width"), 0, 0, tiled=True)
 
-    paired, _ = lax.optimization_barrier((cotangent, windows))
-    paired = paired.reshape(2, 4, 64, 2 * CH)
-    edge = jnp.where(width == 0, paired[:, :, 64 - EDGE :], paired[:, :, :EDGE])
-    edge = lax.ppermute(edge, "width", [(0, 1), (1, 0)])
     nothing = jnp.zeros_like(edge)
     low, high = jnp.where(width == 0, nothing, edge), jnp.where(width == 0, edge, nothing)
     paired = jnp.concatenate([low, paired, high], axis=2).reshape(2, 4, 9, OWN, 2 * CH)
@@ -382,12 +385,14 @@
         [((64, 32, CH), BF16)],
         [pltpu.VMEM((FR, ROWS + 1, 2, OWN, 4 * CH), BF16), pltpu.VMEM((CH, FR * ROWS * OWN), BF16)], 4 * tap_flops,
     )
-    grad_scratch = [own_table, pltpu.VMEM((CH, FR * ROWS * OWN), BF16), pltpu.VMEM((TAPS * CH + 8, CH), F32)]
+    grad_table = pltpu.VMEM((FR, ROWS + 2, WIN, 3 * CH), BF16)
+    grad_scratch = [grad_table, pltpu.VMEM((CH, (FR + 2) * ROWS * WIN), BF16), pltpu.VMEM((TAPS * CH + 8, CH), F32)]
     early = call(
-        second_grad_kernel, (), (place, first_act, grad_sum, later, up_part),
-        [SMEM, whole(six_frames), whole(act_shape), whole(later.shape), whole(up_part.shape)],
-        [((64, UP_ROWS + PIECE, CH), BF16)], grad_scratch, 14 * tap_flops,
-    )
+        second_grad_kernel, (), (place, first_act, grad_sum, up_part),
+        [SMEM, whole(six_frames), whole(act_shape), whole(up_part.shape)],
+        [((64, UP_ROWS + PIECE, CH), BF16)], grad_scratch, 27 * tap_flops,
+    )
+    early, later = lax.optimization_barrier((early, later))
     early = lax.all_to_all(early, ("z", "x_hi", "width"), 0, 0, tiled=True)
 
     grad_hidden, hidden_head = call(
@@ -397,9 +402,9 @@
     )
     later_hidden = shift(hidden_head, "y", -1)
     blocks = call(
-        first_grad_kernel, (), (place, block, grad_hidden, later_hidden),
-        [SMEM, whole(block.shape), whole(act_shape), whole(later_hidden.shape)],
-        [((16, PIECE, CH), BF16)] * 4, grad_scratch, 14 * tap_flops,
+        first_grad_kernel, (), (place, block, grad_hidden),
+        [SMEM, whole(block.shape), whole(act_shape)],
+        [((16, PIECE, CH), BF16)] * 4, grad_scratch, 27 * tap_flops,
     )
     arrived = [blocks[0]]
     for step in (2, 1, 3):

time: 157 us -> 151 us (0.962)
  waiting for transfers between devices: 62.6 us -> 53.8 us
  Pallas kernels: 34.3 us -> 37.8 us
  local copies, waits for them, and re-layouts: 14.1 us -> 11.3 us
  starting transfers between devices: 39.3 us -> 41.1 us
    ppermute x6, waiting for transfers between devices: 21.9 us -> 3.55 us  [over_y(): return lax.ppermute(value, 'y', [(i, (i + step) % 4) for i in range(4)])]
    all_to_all x1, waiting for transfers between devices: 2.47 us -> 17.3 us  [shards(): lax.all_to_all(windows, ('core', 'z', 'x_hi', 'width'), 0, 0, tiled=True)]
    ppermute x1, waiting for transfers between devices: 12.7 us -> 2.42 us  [shards(): edge = lax.ppermute(edge, 'width', [(0, 1), (1, 0)])]
    unnamed x30 -> x22, local copies, waits for them, and re-layouts: 9.55 us -> 5.69 us
    ppermute x6, starting transfers between devices: 7.94 us -> 11.7 us  [over_y(): return lax.ppermute(value, 'y', [(i, (i + step) % 4) for i in range(4)])]
    pallas_call x8, Pallas kernels: 34.3 us -> 37.8 us  [call(): pl.pallas_call(kernel, out_shape=shapes[0] if single else shapes, grid=gr...]
    ppermute x3, waiting for transfers between devices: 18.8 us -> 22.2 us  [shift(): lax.ppermute(value, axis, [(i, i + step) for i in range(count) if 0 <= i...]
    all_to_all x1, waiting for transfers between devices: 0.01 us -> 1.97 us  [shards(): early = lax.all_to_all(early, ('z', 'x_hi', 'width'), 0, 0, tiled=True)]
  transfers between devices with their start and end apart: 15 -> 15, of which waited for: 12 -> 7; matrix products, arithmetic and copies ran while one was open for 3% -> 4% of each run, Pallas kernels for 17% -> 23%
where the time goes in v8:
time: 151 us; the launch traced here: 150 us
  waiting for transfers between devices  53.8 us (36%)
  starting transfers between devices  41.1 us (27%)
  Pallas kernels  37.8 us (25%)
  local copies, waits for them, and re-layouts  11.3 us (7%)
  other arithmetic  4.93 us (3%)
    pallas_call x8, Pallas kernels, call(): pl.pallas_call(kernel, out_shape=shapes[0] if single else shapes, grid=gr...  37.8 us
    ppermute x3, waiting for transfers between devices, shift(): lax.ppermute(value, axis, [(i, i + step) for i in range(count) if 0 <= i...  22.2 us
    all_to_all x1, waiting for transfers between devices, shards(): lax.all_to_all(windows, ('core', 'z', 'x_hi', 'width'), 0, 0, tiled=True)  17.3 us
    ppermute x6, starting transfers between devices, over_y(): return lax.ppermute(value, 'y', [(i, (i + step) % 4) for i in range(4)])  11.7 us
    all_to_all x1, starting transfers between devices, shards(): lax.all_to_all(windows, ('core', 'z', 'x_hi', 'width'), 0, 0, tiled=True)  8.16 us
    ppermute x3, starting transfers between devices, shift(): lax.ppermute(value, axis, [(i, i + step) for i in range(count) if 0 <= i...  6.68 us
    all_to_all x1, waiting for transfers between devices, shards(): lax.all_to_all(fine, ('z', 'x_hi'), 0, 0, tiled=True)  6.28 us
    unnamed x22, local copies, waits for them, and re-layouts  5.69 us
  transfers between devices with their start and end apart: 15, of which 7 were waited for; matrix products, arithmetic and copies ran while one was open for 4% of the time, Pallas kernels for 23%

profile of v8, /device:TPU:0, one launch (start us, length us, event | category | flops | bytes accessed | tf_op | source)
XLA Modules:
  0.0 149.9 jit_solution(12110807687365744597)
XLA Ops:
  0.6 3.6 %collective-permute-start = (bf16[2,128,256]{2,1,0:T(8,128)(2,1)}, bf16[2,128,256]{2,1,0:T(8,128)(2,1)S(1)}, u32[]{:S(2)}, u32[]{:S(2)}) collective-permute-start(bf16[2,128,256]{2,1,0:T(8,128)(2,1)} %bitcast.55), channel_id=1, source_target_pairs={{0,32},{32,64},{64,96},{1,33},{33,65},{65,97},{2,34},{34,66},{66,9... | collective-permute-start | bytes 393224 | tf_op jit(solution)/shard_map/ppermute | solution.py:316
  7.0 2.4 %collective-permute-done.1 = bf16[2,4,4,512]{3,2,1,0:T(4,128)(2,1)S(1)} collective-permute-done((bf16[2,4,4,512]{3,2,1,0:T(4,128)(2,1)S(1)}, bf16[2,4,4,512]{3,2,1,0:T(4,128)(2,1)S(1)}, u32[]{:S(2)}, u32[]{:S(2)}) %collective-permute-start.1) | collective-permute-done | bytes 32800 | tf_op jit(solution)/shard_map/ppermute | solution.py:343
  11.7 8.2 %all-to-all-start = ((bf16[32,4,16,256]{3,2,1,0:T(8,128)(2,1)}), bf16[32,4,16,256]{3,2,1,0:T(8,128)(2,1)S(1)}, u32[]{:S(2)}, u32[]{:S(2)}) async-start(bf16[32,4,16,256]{3,2,1,0:T(8,128)(2,1)} %bitcast.8), calls=%async_computation | async-start | bytes 2097152 | tf_op jit(solution)/shard_map/all_to_all | solution.py:351
  20.3 17.3 %all-to-all-done = bf16[32,4,16,256]{3,2,1,0:T(8,128)(2,1)S(1)} async-done(((bf16[32,4,16,256]{3,2,1,0:T(8,128)(2,1)}), bf16[32,4,16,256]{3,2,1,0:T(8,128)(2,1)S(1)}, u32[]{:S(2)}, u32[]{:S(2)}) %all-to-all-start) | async-done | bytes 1048608 | tf_op jit(solution)/shard_map/all_to_all | solution.py:351
  38.7 3.6 %all-to-all-start.1 = ((bf16[8,2,4,16,512]{4,3,2,1,0:T(8,128)(2,1)}), bf16[8,2,4,16,512]{4,3,2,1,0:T(8,128)(2,1)S(1)}, u32[]{:S(2)}, u32[]{:S(2)}) async-start(bf16[8,2,4,16,512]{4,3,2,1,0:T(8,128)(2,1)} %copy.16), calls=%async_computation.1 | async-start | bytes 2097152 | tf_op jit(solution)/shard_map/all_to_all | solution.py:359
  42.4 8.4 %shard_map.84 = (bf16[6,16,16,256]{3,2,1,0:T(8,128)(2,1)S(1)}, f32[4,16,16,256]{3,2,1,0:T(8,128)S(1)}) custom-call(bf16[2,16,4,16,256]{4,3,2,1,0:T(8,128)(2,1)S(1)} %bitcast.47, bf16[3,3,3,256,256]{4,3,2,1,0:T(8,128)(2,1)} %weights.9, f32[16,256]{1,0:T(8,128)S(1)} %broadcast_in_dim.19.mask), custom_call_target="tpu_custom_call" | custom-call | flops 5368709120 | bytes 6438912 | tf_op jit(solution)/shard_map/pallas_call | solution.py:302
  52.6 6.3 %all-to-all-done.1 = bf16[8,2,4,16,512]{4,3,2,1,0:T(8,128)(2,1)S(1)} async-done(((bf16[8,2,4,16,512]{4,3,2,1,0:T(8,128)(2,1)}), bf16[8,2,4,16,512]{4,3,2,1,0:T(8,128)(2,1)S(1)}, u32[]{:S(2)}, u32[]{:S(2)}) %all-to-all-start.1) | async-done | bytes 1048608 | tf_op jit(solution)/shard_map/all_to_all | solution.py:359
  60.1 6.2 %shard_map.85 = (f32[4,16,16,256]{3,2,1,0:T(8,128)S(1)}, bf16[4,16,16,256]{3,2,1,0:T(8,128)(2,1)S(1)}) custom-call(bf16[6,16,16,256]{3,2,1,0:T(8,128)(2,1)S(1)} %copy-done.8, bf16[2,16,4,16,256]{4,3,2,1,0:T(8,128)(2,1)S(1)} %bitcast.48, bf16[3,3,3,256,256]{4,3,2,1,0:T(8,128)(2,1)} %weights.8), custom_call_target="tpu_custom_call" | custom-call | flops 3623878656 | bytes 6946816 | tf_op jit(solution)/shard_map/pallas_call | solution.py:302
  66.4 3.5 %shard_map.86 = (bf16[4,16,16,256]{3,2,1,0:T(8,128)(2,1)S(1)}, bf16[2,16,16,256]{3,2,1,0:T(8,128)(2,1)S(1)}) custom-call(s32[1]{0:T(128)} %bitcast.core_ref, bf16[8,2,2,2,16,512]{5,4,3,2,1,0:T(8,128)(2,1)S(1)} %bitcast.45, bf16[8,2,2,2,16,512]{5,4,3,2,1,0:T(8,128)(2,1)S(1)} %collective-permute-done.2.other, bf16[4,4,256,256]{3,2,1,0:T(8,128)(2,1)S(1)} %copy-done.4, ...), custom_call_target="tpu_custom_call" | custom-call | flops 2147483648 | bytes 6045700 | tf_op jit(solution)/shard_map/pallas_call | solution.py:302
  73.3 6.4 %shard_map.88 = bf16[64,88,256]{2,1,0:T(8,128)(2,1)} custom-call(s32[2]{0:T(128)S(1)} %pad_add_fusion.place, bf16[6,16,16,256]{3,2,1,0:T(8,128)(2,1)S(1)} %copy-done.9, bf16[4,16,16,256]{3,2,1,0:T(8,128)(2,1)S(1)} %get-tuple-element.39.block.grad_sum, bf16[64,32,256]{2,1,0:T(8,128)(2,1)S(1)} %shard_map.87.up), custom_call_target="tpu_custom_call" | custom-call | flops 3623878656 | bytes 5242888 | tf_op jit(solution)/shard_map/pallas_call | solution.py:302
  80.7 4.6 %all-to-all-start.2 = ((bf16[64,88,256]{2,1,0:T(8,128)(2,1)}), bf16[64,88,256]{2,1,0:T(8,128)(2,1)}, u32[]{:S(2)}, u32[]{:S(2)}) async-start(bf16[64,88,256]{2,1,0:T(8,128)(2,1)} %shard_map.88), calls=%async_computation.2 | async-start | bytes 5767168 | tf_op jit(solution)/shard_map/all_to_all | solution.py:396
  85.3 2.0 %copy-done.3 = bf16[3,3,3,256,256]{4,3,2,1,0:T(8,128)(2,1)S(1)} copy-done((bf16[3,3,3,256,256]{4,3,2,1,0:T(8,128)(2,1)S(1)}, bf16[3,3,3,256,256]{4,3,2,1,0:T(8,128)(2,1)}, u32[]{:S(2)}) %copy-start.3) | copy-done | bytes 3538968
  87.3 4.8 %shard_map.89 = (bf16[4,16,16,256]{3,2,1,0:T(8,128)(2,1)S(1)}, bf16[2,16,16,256]{3,2,1,0:T(8,128)(2,1)S(1)}) custom-call(bf16[4,16,16,256]{3,2,1,0:T(8,128)(2,1)S(1)} %copy-done.2, bf16[2,16,16,256]{3,2,1,0:T(8,128)(2,1)S(1)} %collective-permute-done.3.later, f32[4,16,16,256]{3,2,1,0:T(8,128)S(1)} %copy-done.6, bf16[3,3,3,256,256]{4,3,2,1,0:T(8,128)(2,1)S(1)} %copy-done.3, ...), custom_call_target="tpu_custom_call" | custom-call | flops 3623878656 | bytes 6176768 | tf_op jit(solution)/shard_map/pallas_call | solution.py:302
  92.1 4.8 %shard_map.90 = (bf16[16,56,256]{2,1,0:T(8,128)(2,1)S(1)}, bf16[16,56,256]{2,1,0:T(8,128)(2,1)S(1)}, bf16[16,56,256]{2,1,0:T(8,128)(2,1)S(1)}, bf16[16,56,256]{2,1,0:T(8,128)(2,1)S(1)}) custom-call(s32[2]{0:T(128)S(1)} %pad_add_fusion.place, bf16[2,16,4,16,256]{4,3,2,1,0:T(8,128)(2,1)S(1)} %bitcast.49, bf16[4,16,16,256]{3,2,1,0:T(8,128)(2,1)S(1)} %get-tuple-element.46.block), custom_call_target="tpu_custom_call" | custom-call | flops 3623878656 | bytes 3407880 | tf_op jit(solution)/shard_map/pallas_call | solution.py:302
  96.9 3.2 %collective-permute-start.7 = (bf16[16,56,256]{2,1,0:T(8,128)(2,1)S(1)}, bf16[16,56,256]{2,1,0:T(8,128)(2,1)S(1)}, u32[]{:S(2)}, u32[]{:S(2)}) collective-permute-start(bf16[16,56,256]{2,1,0:T(8,128)(2,1)S(1)} %get-tuple-element.52), channel_id=1, source_target_pairs={{0,96},{32,0},{64,32},{96,64},{1,97},{33,1},{65,33},{97,65},{2,98}... | collective-permute-start | bytes 1376264 | tf_op jit(solution)/shard_map/ppermute | solution.py:320
  100.2 2.2 %collective-permute-start.5 = (bf16[16,56,256]{2,1,0:T(8,128)(2,1)S(1)}, bf16[16,56,256]{2,1,0:T(8,128)(2,1)S(1)}, u32[]{:S(2)}, u32[]{:S(2)}) collective-permute-start(bf16[16,56,256]{2,1,0:T(8,128)(2,1)S(1)} %get-tuple-element.50), channel_id=1, source_target_pairs={{0,64},{32,96},{64,0},{96,32},{1,65},{33,97},{65,1},{97,33},{2,66}... | collective-permute-start | bytes 1376264 | tf_op jit(solution)/shard_map/ppermute | solution.py:320
  103.8 21.3 %collective-permute-done.4.later = bf16[2,16,16,256]{3,2,1,0:T(8,128)(2,1)S(1)} collective-permute-done((bf16[2,16,16,256]{3,2,1,0:T(8,128)(2,1)S(1)}, bf16[2,16,16,256]{3,2,1,0:T(8,128)(2,1)S(1)}, u32[]{:S(2)}, u32[]{:S(2)}) %collective-permute-start.4) | collective-permute-done | bytes 262176 | tf_op jit(solution)/shard_map/ppermute | solution.py:316
  125.1 1.9 %shard_map.91 = bf16[16,2,8,256]{3,2,1,0:T(8,128)(2,1)S(1)} custom-call(s32[1]{0:T(128)} %bitcast.core_ref, bf16[4,16,16,256]{3,2,1,0:T(8,128)(2,1)S(1)} %get-tuple-element.46.block, bf16[2,16,16,256]{3,2,1,0:T(8,128)(2,1)S(1)} %collective-permute-done.4.later, bf16[4,16,16,256]{3,2,1,0:T(8,128)(2,1)S(1)} %copy-done.2, bf16[3,3,3,256,256]{4,3,2,1,0:T(8,128)(2,1)S(1)} %copy-done), custom_call_target="tpu_custom_call" | custom-call | flops 939524096 | bytes 4980740 | tf_op jit(solution)/shard_map/pallas_call | solution.py:302
  127.3 2.0 %all-to-all-done.2 = bf16[64,88,256]{2,1,0:T(8,128)(2,1)} async-done(((bf16[64,88,256]{2,1,0:T(8,128)(2,1)}), bf16[64,88,256]{2,1,0:T(8,128)(2,1)}, u32[]{:S(2)}, u32[]{:S(2)}) %all-to-all-start.2) | async-done | bytes 2883616 | tf_op jit(solution)/shard_map/all_to_all | solution.py:396
  130.2 4.9 %all-to-all-start.3 = ((bf16[16,72,256]{2,1,0:T(8,128)(2,1)}), bf16[16,72,256]{2,1,0:T(8,128)(2,1)S(1)}, u32[]{:S(2)}, u32[]{:S(2)}) async-start(bf16[16,72,256]{2,1,0:T(8,128)(2,1)} %pad_maximum_fusion), calls=%async_computation.3 | async-start | bytes 1179648 | tf_op jit(solution)/shard_map/all_to_all | solution.py:426
  135.0 2.2 %convert_reduce_fusion = f32[4,88,256]{2,1,0:T(8,128)S(1)} fusion(bf16[16,4,88,256]{3,2,1,0:T(8,128)(2,1)} %bitcast.23), kind=kLoop, calls=%fused_computation | loop fusion | flops 2793472 | bytes 3244032 | tf_op jit(solution)/shard_map/reduce_sum | solution.py:420
  137.3 4.1 %collective-permute-start.10 = (bf16[88,256]{1,0:T(8,128)(2,1)S(1)}, bf16[88,256]{1,0:T(8,128)(2,1)S(1)}, u32[]{:S(2)}, u32[]{:S(2)}) collective-permute-start(bf16[88,256]{1,0:T(8,128)(2,1)S(1)} %get-tuple-element.59), channel_id=1, source_target_pairs={{0,96},{32,0},{64,32},{96,64},{1,97},{33,1},{65,33},{97,65},{2,98}... | collective-permute-start | bytes 135176 | tf_op jit(solution)/shard_map/ppermute | solution.py:320
  141.4 2.2 %collective-permute-start.8 = (bf16[88,256]{1,0:T(8,128)(2,1)S(1)}, bf16[88,256]{1,0:T(8,128)(2,1)S(1)}, u32[]{:S(2)}, u32[]{:S(2)}) collective-permute-start(bf16[88,256]{1,0:T(8,128)(2,1)S(1)} %get-tuple-element.58), channel_id=1, source_target_pairs={{0,64},{32,96},{64,0},{96,32},{1,65},{33,97},{65,1},{97,33},{2,66}... | collective-permute-start | bytes 135176 | tf_op jit(solution)/shard_map/ppermute | solution.py:320
  143.6 3.5 %collective-permute-done.9 = bf16[88,256]{1,0:T(8,128)(2,1)S(1)} collective-permute-done((bf16[88,256]{1,0:T(8,128)(2,1)S(1)}, bf16[88,256]{1,0:T(8,128)(2,1)S(1)}, u32[]{:S(2)}, u32[]{:S(2)}) %collective-permute-start.9) | collective-permute-done | bytes 45088 | tf_op jit(solution)/shard_map/ppermute | solution.py:320
  (64 shorter events, 19.4 us)
Async XLA Ops:
  0.6 8.8 %collective-permute-start = (bf16[2,128,256]{2,1,0:T(8,128)(2,1)}, bf16[2,128,256]{2,1,0:T(8,128)(2,1)S(1)}, u32[]{:S(2)}, u32[]{:S(2)}) collective-permute-start(bf16[2,128,256]{2,1,0:T(8,128)(2,1)} %bitcast.55), channel_id=1, source_target_pairs={{0,32},{32,64},{64,96},{1,33},{33,65},{65,97},{2,34},{34,66},{66,9... | collective-permute-start | bytes 393224 | tf_op jit(solution)/shard_map/ppermute | solution.py:316
  5.5 4.0 %collective-permute-start.1 = (bf16[2,4,4,512]{3,2,1,0:T(4,128)(2,1)S(1)}, bf16[2,4,4,512]{3,2,1,0:T(4,128)(2,1)S(1)}, u32[]{:S(2)}, u32[]{:S(2)}) collective-permute-start(bf16[2,4,4,512]{3,2,1,0:T(4,128)(2,1)S(1)} %slice_select_fusion), channel_id=1, source_target_pairs={{0,1},{1,0},{2,3},{3,2},{4,5},{5,4},{6,7},{7,6},{8,9},{9,8},{10,11... | collective-permute-start | bytes 98312 | tf_op jit(solution)/shard_map/ppermute | solution.py:343
  11.7 25.9 %all-to-all-start = ((bf16[32,4,16,256]{3,2,1,0:T(8,128)(2,1)}), bf16[32,4,16,256]{3,2,1,0:T(8,128)(2,1)S(1)}, u32[]{:S(2)}, u32[]{:S(2)}) async-start(bf16[32,4,16,256]{3,2,1,0:T(8,128)(2,1)} %bitcast.8), calls=%async_computation | async-start | bytes 2097152 | tf_op jit(solution)/shard_map/all_to_all | solution.py:351
  38.7 20.2 %all-to-all-start.1 = ((bf16[8,2,4,16,512]{4,3,2,1,0:T(8,128)(2,1)}), bf16[8,2,4,16,512]{4,3,2,1,0:T(8,128)(2,1)S(1)}, u32[]{:S(2)}, u32[]{:S(2)}) async-start(bf16[8,2,4,16,512]{4,3,2,1,0:T(8,128)(2,1)} %copy.16), calls=%async_computation.1 | async-start | bytes 2097152 | tf_op jit(solution)/shard_map/all_to_all | solution.py:359
  50.7 1.0 copy-start.5
  58.9 7.5 %collective-permute-start.2 = (bf16[8,2,2,2,16,512]{5,4,3,2,1,0:T(8,128)(2,1)S(1)}, bf16[8,2,2,2,16,512]{5,4,3,2,1,0:T(8,128)(2,1)S(1)}, u32[]{:S(2)}, u32[]{:S(2)}) collective-permute-start(bf16[8,2,2,2,16,512]{5,4,3,2,1,0:T(8,128)(2,1)S(1)} %bitcast.44), channel_id=1, source_target_pairs={{0,16},{16,0},{1,17},{17,1},{2,18},{18,2},{3,19},{19,3},{4,20},{20... | collective-permute-start | bytes 3145736 | tf_op jit(solution)/shard_map/ppermute | solution.py:369
  59.0 1.1 copy-start.8
  60.1 6.3 %copy-start.4 = (bf16[4,4,256,256]{3,2,1,0:T(8,128)(2,1)S(1)}, bf16[4,4,256,256]{3,2,1,0:T(8,128)(2,1)}, u32[]{:S(2)}) copy-start(bf16[4,4,256,256]{3,2,1,0:T(8,128)(2,1)} %weights.7) | copy-start | bytes 6291460
  69.9 9.8 %copy-start.1 = (bf16[4,16,16,256]{3,2,1,0:T(8,128)(2,1)}, bf16[4,16,16,256]{3,2,1,0:T(8,128)(2,1)S(1)}, u32[]{:S(2)}) copy-start(bf16[4,16,16,256]{3,2,1,0:T(8,128)(2,1)S(1)} %get-tuple-element.39.block.grad_sum) | copy-start | bytes 1572868
  69.9 3.4 %copy-start.9 = (bf16[6,16,16,256]{3,2,1,0:T(8,128)(2,1)S(1)}, bf16[6,16,16,256]{3,2,1,0:T(8,128)(2,1)}, u32[]{:S(2)}) copy-start(bf16[6,16,16,256]{3,2,1,0:T(8,128)(2,1)} %copy-done.7) | copy-start | bytes 2359300
  69.9 10.7 %collective-permute-start.3 = (bf16[2,16,16,256]{3,2,1,0:T(8,128)(2,1)S(1)}, bf16[2,16,16,256]{3,2,1,0:T(8,128)(2,1)S(1)}, u32[]{:S(2)}, u32[]{:S(2)}) collective-permute-start(bf16[2,16,16,256]{3,2,1,0:T(8,128)(2,1)S(1)} %get-tuple-element.41), channel_id=1, source_target_pairs={{32,0},{64,32},{96,64},{33,1},{65,33},{97,65},{34,2},{66,34},{98,6... | collective-permute-start | bytes 786440 | tf_op jit(solution)/shard_map/ppermute | solution.py:316
  79.7 5.6 %copy-start.6 = (f32[4,16,16,256]{3,2,1,0:T(8,128)S(1)}, f32[4,16,16,256]{3,2,1,0:T(8,128)}, u32[]{:S(2)}) copy-start(f32[4,16,16,256]{3,2,1,0:T(8,128)} %copy-done.5) | copy-start | bytes 3145732
  80.7 4.6 %copy-start.2 = (bf16[4,16,16,256]{3,2,1,0:T(8,128)(2,1)S(1)}, bf16[4,16,16,256]{3,2,1,0:T(8,128)(2,1)}, u32[]{:S(2)}) copy-start(bf16[4,16,16,256]{3,2,1,0:T(8,128)(2,1)} %copy-done.1) | copy-start | bytes 1572868
  80.7 48.6 %all-to-all-start.2 = ((bf16[64,88,256]{2,1,0:T(8,128)(2,1)}), bf16[64,88,256]{2,1,0:T(8,128)(2,1)}, u32[]{:S(2)}, u32[]{:S(2)}) async-start(bf16[64,88,256]{2,1,0:T(8,128)(2,1)} %shard_map.88), calls=%async_computation.2 | async-start | bytes 5767168 | tf_op jit(solution)/shard_map/all_to_all | solution.py:396
  85.3 2.0 %copy-start.3 = (bf16[3,3,3,256,256]{4,3,2,1,0:T(8,128)(2,1)S(1)}, bf16[3,3,3,256,256]{4,3,2,1,0:T(8,128)(2,1)}, u32[]{:S(2)}) copy-start(bf16[3,3,3,256,256]{4,3,2,1,0:T(8,128)(2,1)} %weights.8) | copy-start | bytes 10616836
  92.1 33.0 %copy-start = (bf16[3,3,3,256,256]{4,3,2,1,0:T(8,128)(2,1)S(1)}, bf16[3,3,3,256,256]{4,3,2,1,0:T(8,128)(2,1)}, u32[]{:S(2)}) copy-start(bf16[3,3,3,256,256]{4,3,2,1,0:T(8,128)(2,1)} %weights.9) | copy-start | bytes 10616836
  96.9 30.1 %collective-permute-start.7 = (bf16[16,56,256]{2,1,0:T(8,128)(2,1)S(1)}, bf16[16,56,256]{2,1,0:T(8,128)(2,1)S(1)}, u32[]{:S(2)}, u32[]{:S(2)}) collective-permute-start(bf16[16,56,256]{2,1,0:T(8,128)(2,1)S(1)} %get-tuple-element.52), channel_id=1, source_target_pairs={{0,96},{32,0},{64,32},{96,64},{1,97},{33,1},{65,33},{97,65},{2,98}... | collective-permute-start | bytes 1376264 | tf_op jit(solution)/shard_map/ppermute | solution.py:320
  100.1 26.9 %collective-permute-start.6 = (bf16[16,56,256]{2,1,0:T(8,128)(2,1)S(1)}, bf16[16,56,256]{2,1,0:T(8,128)(2,1)S(1)}, u32[]{:S(2)}, u32[]{:S(2)}) collective-permute-start(bf16[16,56,256]{2,1,0:T(8,128)(2,1)S(1)} %get-tuple-element.51), channel_id=1, source_target_pairs={{0,32},{32,64},{64,96},{96,0},{1,33},{33,65},{65,97},{97,1},{2,34}... | collective-permute-start | bytes 1376264 | tf_op jit(solution)/shard_map/ppermute | solution.py:320
  100.2 26.9 %collective-permute-start.5 = (bf16[16,56,256]{2,1,0:T(8,128)(2,1)S(1)}, bf16[16,56,256]{2,1,0:T(8,128)(2,1)S(1)}, u32[]{:S(2)}, u32[]{:S(2)}) collective-permute-start(bf16[16,56,256]{2,1,0:T(8,128)(2,1)S(1)} %get-tuple-element.50), channel_id=1, source_target_pairs={{0,64},{32,96},{64,0},{96,32},{1,65},{33,97},{65,1},{97,33},{2,66}... | collective-permute-start | bytes 1376264 | tf_op jit(solution)/shard_map/ppermute | solution.py:320
  102.3 22.8 %collective-permute-start.4 = (bf16[2,16,16,256]{3,2,1,0:T(8,128)(2,1)S(1)}, bf16[2,16,16,256]{3,2,1,0:T(8,128)(2,1)S(1)}, u32[]{:S(2)}, u32[]{:S(2)}) collective-permute-start(bf16[2,16,16,256]{3,2,1,0:T(8,128)(2,1)S(1)} %get-tuple-element.47), channel_id=1, source_target_pairs={{32,0},{64,32},{96,64},{33,1},{65,33},{97,65},{34,2},{66,34},{98,6... | collective-permute-start | bytes 786440 | tf_op jit(solution)/shard_map/ppermute | solution.py:316
  130.2 18.3 %all-to-all-start.3 = ((bf16[16,72,256]{2,1,0:T(8,128)(2,1)}), bf16[16,72,256]{2,1,0:T(8,128)(2,1)S(1)}, u32[]{:S(2)}, u32[]{:S(2)}) async-start(bf16[16,72,256]{2,1,0:T(8,128)(2,1)} %pad_maximum_fusion), calls=%async_computation.3 | async-start | bytes 1179648 | tf_op jit(solution)/shard_map/all_to_all | solution.py:426
  137.3 6.3 %collective-permute-start.10 = (bf16[88,256]{1,0:T(8,128)(2,1)S(1)}, bf16[88,256]{1,0:T(8,128)(2,1)S(1)}, u32[]{:S(2)}, u32[]{:S(2)}) collective-permute-start(bf16[88,256]{1,0:T(8,128)(2,1)S(1)} %get-tuple-element.59), channel_id=1, source_target_pairs={{0,96},{32,0},{64,32},{96,64},{1,97},{33,1},{65,33},{97,65},{2,98}... | collective-permute-start | bytes 135176 | tf_op jit(solution)/shard_map/ppermute | solution.py:320
  141.4 5.7 %collective-permute-start.9 = (bf16[88,256]{1,0:T(8,128)(2,1)S(1)}, bf16[88,256]{1,0:T(8,128)(2,1)S(1)}, u32[]{:S(2)}, u32[]{:S(2)}) collective-permute-start(bf16[88,256]{1,0:T(8,128)(2,1)S(1)} %get-tuple-element.60), channel_id=1, source_target_pairs={{0,32},{32,64},{64,96},{96,0},{1,33},{33,65},{65,97},{97,1},{2,34}... | collective-permute-start | bytes 135176 | tf_op jit(solution)/shard_map/ppermute | solution.py:320
  141.4 5.7 %collective-permute-start.8 = (bf16[88,256]{1,0:T(8,128)(2,1)S(1)}, bf16[88,256]{1,0:T(8,128)(2,1)S(1)}, u32[]{:S(2)}, u32[]{:S(2)}) collective-permute-start(bf16[88,256]{1,0:T(8,128)(2,1)S(1)} %get-tuple-element.58), channel_id=1, source_target_pairs={{0,64},{32,96},{64,0},{96,32},{1,65},{33,97},{65,1},{97,33},{2,66}... | collective-permute-start | bytes 135176 | tf_op jit(solution)/shard_map/ppermute | solution.py:320
  (1 other events, 0.9 us)

commit v9 on v8

--- a/solution.py
+++ b/solution.py
@@ -62,11 +62,11 @@
     return pltpu.roll(block.astype(F32), WIN - EDGE, axis=1)[:, :OWN]
 
 
-def forward_taps(table, frames, weights, total):
-    step = pl.program_id(0)
+def forward_taps(table, step, frames, weights, total):
+    rows = frames * ROWS * WIN
     for tap in range(3):
-        lhs = table[pl.ds(step, frames), tap : tap + ROWS].reshape(frames * ROWS * WIN, 3 * CH)
-        total[...] += nn(lhs, weights[0, tap].reshape(3 * CH, CH))
+        lhs = table[pl.ds(step, frames), tap : tap + ROWS].reshape(rows, 3 * CH)
+        total[:rows] += nn(lhs, weights[0, tap].reshape(3 * CH, CH))
 
 
 def backward_taps(table, start, frames, columns, weights, total):
@@ -86,44 +86,50 @@
     return total[frame * rows : (frame + 1) * rows].reshape(ROWS, columns, CH)
 
 
-def first_kernel(block, weights, mask, act, slope, table, total):
-    @pl.when(pl.program_id(0) == 0)
+def forward_kernel(core_ref, mine, other, first, second, mask, act, slope, summed, up_act, table, total):
+    step = pl.program_id(0)
+    core = core_ref[0]
+    sources = ((mine, core), (other, 1 - core))
+
+    @pl.when(step == 0)
     def _():
         clear_border(table)
-        for core in range(2):
+        for source, which in sources:
             for frame in range(FR):
-                slot = 2 * core + frame if frame < 2 else 2 + 2 * core + frame
-                fill_table(table, slot, block[core, :, frame], True)
+                slot = 2 * which + (frame if frame < 2 else frame + 2)
+                fill_table(table, slot, source[:, frame], True)
         total[...] = jnp.zeros_like(total)
 
-    forward_taps(table, FR + 2, weights, total)
-
-    @pl.when(pl.program_id(0) == 2)
+    @pl.when(step < 3)
+    def _():
+        forward_taps(table, step, FR + 2, first, total)
+
+    @pl.when(step == 2)
     def _():
         for frame in range(FR + 2):
             values = frame_of(total, frame, WIN)
             sigma = jax.nn.sigmoid(values)
-            act[frame] = (values * sigma * mask[...]).astype(BF16)
+            result = (values * sigma * mask[...]).astype(BF16)
+            act[frame] = result
+            fill_table(table, frame, result, True)
             if frame >= 2:
                 slope[frame - 2] = slope_of(values, sigma)
-
-
-def second_kernel(act, features, weights, summed, up_act, table, total):
-    @pl.when(pl.program_id(0) == 0)
-    def _():
-        clear_border(table)
-        for frame in range(FR + 2):
-            fill_table(table, frame, act[frame], True)
         total[...] = jnp.zeros_like(total)
 
-    forward_taps(table, FR, weights, total)
-
-    @pl.when(pl.program_id(0) == 2)
-    def _():
-        for frame in range(FR):
-            values = frame_of(total, frame, WIN) + features[frame // 2, :, 2 + frame % 2].astype(F32)
-            summed[frame] = values
-            up_act[frame] = (values * jax.nn.sigmoid(values)).astype(BF16)
+    @pl.when(step >= 3)
+    def _():
+        forward_taps(table, step - 3, FR, second, total)
+
+    @pl.when(step == 5)
+    def _():
+        rows = ROWS * WIN
+        for source, which in sources:
+            for frame in range(2):
+                place = 2 * which + frame
+                values = total[pl.ds(pl.multiple_of(place * rows, rows), rows)].reshape(ROWS, WIN, CH)
+                values = values + source[:, 2 + frame].astype(F32)
+                summed[place] = values
+                up_act[place] = (values * jax.nn.sigmoid(values)).astype(BF16)
 
 
 def hidden_kernel(block, later, slope, weights, mask, grad_hidden, head, table, total):
@@ -234,16 +240,16 @@
                 ].astype(BF16)
 
 
-def tap_sums(act_of, block, table, flipped, sums):
+def tap_sums(frames, block, table, flipped, sums):
     clear_border(table)
     column = lax.broadcasted_iota(jnp.int32, (ROWS, WIN, CH), 1)
     own = (column >= EDGE) & (column < EDGE + OWN)
     for frame in range(FR):
         fill_table(table, frame, jnp.where(own, block[frame].astype(F32), 0.0).astype(BF16), False)
     rows = ROWS * WIN
-    for frame in range(FR + 2):
-        values = act_of(frame).astype(F32).reshape(rows, CH)
-        flipped[:, frame * rows : (frame + 1) * rows] = jnp.transpose(values).astype(BF16)
+    for slot, values in frames:
+        lanes = pl.ds(pl.multiple_of(slot * rows, rows), rows)
+        flipped[:, lanes] = jnp.transpose(values.astype(F32).reshape(rows, CH)).astype(BF16)
     sums[TAPS * CH :] = jnp.zeros((8, CH), F32)
     for tap_t in range(3):
         lhs = flipped[:, tap_t * rows : (tap_t + FR) * rows]
@@ -262,7 +268,7 @@
 
 
 def second_grad_kernel(place, act, block, up, out, table, flipped, sums):
-    tap_sums(lambda frame: act[frame], block, table, flipped, sums)
+    tap_sums([(frame, act[frame]) for frame in range(FR + 2)], block, table, flipped, sums)
     for step in range(4):
         group = lax.rem(place[1] + step, 4)
         for member in range(16):
@@ -271,11 +277,15 @@
             out[chunk, UP_ROWS:] = piece_of(sums, 2 * group + place[0], member).astype(BF16)
 
 
-def first_grad_kernel(place, act, block, own, next_one, next_two, next_three, table, flipped, sums):
-    def frame_at(frame):
-        return act[1, :, frame] if frame < 2 else act[(frame - 2) // 2, :, 2 + frame % 2]
-
-    tap_sums(frame_at, block, table, flipped, sums)
+def first_grad_kernel(place, mine, other, block, own, next_one, next_two, next_three, table, flipped, sums):
+    core = place[0]
+    frames = []
+    for frame in range(2):
+        before = jnp.where(core == 1, mine[:, frame].astype(F32), other[:, frame].astype(F32))
+        frames.append((frame, before))
+        frames.append((2 + 2 * core + frame, mine[:, 2 + frame]))
+        frames.append((4 - 2 * core + frame, other[:, 2 + frame]))
+    tap_sums(frames, block, table, flipped, sums)
     for step, out in enumerate((own, next_one, next_two, next_three)):
         group = lax.rem(place[1] + step, 4)
         for member in range(16):
@@ -290,8 +300,8 @@
 SMEM = pl.BlockSpec(memory_space=pltpu.SMEM)
 
 
-def tap_weights():
-    return pl.BlockSpec((1, 3, 3, CH, CH), lambda step: (step, 0, 0, 0, 0))
+def tap_weights(begin=0):
+    return pl.BlockSpec((1, 3, 3, CH, CH), lambda step: (jnp.clip(step - begin, 0, 2), 0, 0, 0, 0))
 
 
 def call(kernel, grid, args, specs, outs, scratch, flops):
@@ -346,32 +356,27 @@
     frames = jnp.concatenate([before, frames], axis=0)
     padded = jnp.pad(frames, ((0, 0), (EDGE, EDGE), (0, 0))).reshape(4, 17, OWN, CH)
     windows = jnp.concatenate([padded[:, :-1], padded[:, 1:]], axis=2)
-    windows = windows.reshape(4, 2, 8, WIN, CH).transpose(2, 1, 0, 3, 4).reshape(1, 16, 4, WIN, CH)
-    windows = jnp.broadcast_to(windows, (2, 16, 4, WIN, CH)).reshape(32, 4, WIN, CH)
-    block = lax.all_to_all(windows, ("core", "z", "x_hi", "width"), 0, 0, tiled=True)
+    windows = windows.reshape(4, 2, 8, WIN, CH).transpose(2, 1, 0, 3, 4).reshape(16, 4, WIN, CH)
+    block = lax.all_to_all(windows, ("z", "x_hi", "width"), 0, 0, tiled=True)
 
     nothing = jnp.zeros_like(edge)
     low, high = jnp.where(width == 0, nothing, edge), jnp.where(width == 0, edge, nothing)
     paired = jnp.concatenate([low, paired, high], axis=2).reshape(2, 4, 9, OWN, 2 * CH)
     fine = jnp.concatenate([paired[:, :, :-1], paired[:, :, 1:]], axis=3).transpose(2, 0, 1, 3, 4)
     fine, block = lax.optimization_barrier((fine, block))
-    block = block.reshape(2, ROWS, 4, WIN, CH)
+    swap = [(0, 1), (1, 0)]
+    other_block = lax.ppermute(block, "core", swap)
     mine = lax.all_to_all(fine, ("z", "x_hi"), 0, 0, tiled=True).reshape(8, 2, 2, 2, WIN, 2 * CH)
 
-    first_act, first_slope = call(
-        first_kernel, (3,), (block, conv_first, mask),
-        [whole(block.shape), tap_weights(), whole(mask.shape)],
-        [(six_frames, BF16), (act_shape, F32)],
+    first_act, first_slope, summed, up_act = call(
+        forward_kernel, (6,), (core_arg, block, other_block, conv_first, conv_second, mask),
+        [SMEM, whole(block.shape), whole(block.shape), tap_weights(0), tap_weights(3), whole(mask.shape)],
+        [(six_frames, BF16), (act_shape, F32), (act_shape, F32), (act_shape, BF16)],
         [pltpu.VMEM((FR + 4, ROWS + 2, WIN, 3 * CH), BF16), pltpu.VMEM(((FR + 2) * ROWS * WIN, CH), F32)],
-        40 * tap_flops,
-    )
-    mine, first_slope = lax.optimization_barrier((mine, first_slope))
-    other = lax.ppermute(mine, "core", [(0, 1), (1, 0)])
-    summed, up_act = call(
-        second_kernel, (3,), (first_act, block, conv_second),
-        [whole(six_frames), whole(block.shape), tap_weights()],
-        [(act_shape, F32), (act_shape, BF16)], [table, total], 27 * tap_flops,
-    )
+        67 * tap_flops,
+    )
+    mine, up_act = lax.optimization_barrier((mine, up_act))
+    other = lax.ppermute(mine, "core", swap)
     grad_sum, sum_head = call(
         cotangent_kernel, (), (core_arg, mine, other, up_kernel, summed, mask),
         [SMEM, whole(mine.shape), whole(mine.shape), whole(up_kernel.shape), whole(act_shape), whole(mask.shape)],
@@ -402,8 +407,8 @@
     )
     later_hidden = shift(hidden_head, "y", -1)
     blocks = call(
-        first_grad_kernel, (), (place, block, grad_hidden),
-        [SMEM, whole(block.shape), whole(act_shape)],
+        first_grad_kernel, (), (place, block, other_block, grad_hidden),
+        [SMEM, whole(block.shape), whole(block.shape), whole(act_shape)],
         [((16, PIECE, CH), BF16)] * 4, grad_scratch, 27 * tap_flops,
     )
     arrived = [blocks[0]]

time: 151 us -> 143 us (0.947)
  waiting for transfers between devices: 53.8 us -> 41 us
  local copies, waits for them, and re-layouts: 11.3 us -> 14.4 us
  starting transfers between devices: 41.1 us -> 43.7 us
    all_to_all x1, waiting for transfers between devices: 17.3 us -> 9.7 us  [shards(): block = lax.all_to_all(windows, ('z', 'x_hi', 'width'), 0, 0, tiled=True)]
    all_to_all x1, waiting for transfers between devices: 6.28 us -> 0.55 us  [shards(): lax.all_to_all(fine, ('z', 'x_hi'), 0, 0, tiled=True)]
    unnamed x22 -> x28, local copies, waits for them, and re-layouts: 5.69 us -> 9.1 us
    ppermute x1 -> x2, waiting for transfers between devices: 0.01 us -> 2.58 us  [the longest x1 2.58 us: shards(): other = lax.ppermute(mine, 'core', swap)]
    all_to_all x1, starting transfers between devices: 4.61 us -> 6.82 us  [shards(): early = lax.all_to_all(early, ('z', 'x_hi', 'width'), 0, 0, tiled=True)]
    pallas_call x8 -> x7, Pallas kernels: 37.8 us -> 37.2 us  [call(): pl.pallas_call(kernel, out_shape=shapes[0] if single else shapes, grid=gr...]
  transfers between devices with their start and end apart: 15 -> 16, of which waited for: 7 -> 8; matrix products, arithmetic and copies ran while one was open for 4% -> 5% of each run, Pallas kernels for 23% -> 24%
where the time goes in v9:
time: 143 us; the launch traced here: 142 us
  starting transfers between devices  43.7 us (31%)
  waiting for transfers between devices  41 us (29%)
  Pallas kernels  37.2 us (26%)
  local copies, waits for them, and re-layouts  14.4 us (10%)
  other arithmetic  4.94 us (3%)
    pallas_call x7, Pallas kernels, call(): pl.pallas_call(kernel, out_shape=shapes[0] if single else shapes, grid=gr...  37.2 us
    ppermute x3, waiting for transfers between devices, shift(): lax.ppermute(value, axis, [(i, i + step) for i in range(count) if 0 <= i...  21.3 us
    ppermute x6, starting transfers between devices, over_y(): return lax.ppermute(value, 'y', [(i, (i + step) % 4) for i in range(4)])  11.6 us
    all_to_all x1, waiting for transfers between devices, shards(): block = lax.all_to_all(windows, ('z', 'x_hi', 'width'), 0, 0, tiled=True)  9.7 us
    unnamed x28, local copies, waits for them, and re-layouts  9.1 us
    all_to_all x1, starting transfers between devices, shards(): block = lax.all_to_all(windows, ('z', 'x_hi', 'width'), 0, 0, tiled=True)  7.88 us
    all_to_all x1, starting transfers between devices, shards(): early = lax.all_to_all(early, ('z', 'x_hi', 'width'), 0, 0, tiled=True)  6.82 us
    ppermute x3, starting transfers between devices, shift(): lax.ppermute(value, axis, [(i, i + step) for i in range(count) if 0 <= i...  6.68 us
  transfers between devices with their start and end apart: 16, of which 8 were waited for; matrix products, arithmetic and copies ran while one was open for 5% of the time, Pallas kernels for 24%

profile of v9, /device:TPU:0, one launch (start us, length us, event | category | flops | bytes accessed | tf_op | source)
XLA Modules:
  0.0 142.1 jit_solution(6558594318814784600)
XLA Ops:
  0.6 3.6 %collective-permute-start = (bf16[2,128,256]{2,1,0:T(8,128)(2,1)}, bf16[2,128,256]{2,1,0:T(8,128)(2,1)S(1)}, u32[]{:S(2)}, u32[]{:S(2)}) collective-permute-start(bf16[2,128,256]{2,1,0:T(8,128)(2,1)} %bitcast.49), channel_id=1, source_target_pairs={{0,32},{32,64},{64,96},{1,33},{33,65},{65,97},{2,34},{34,66},{66,9... | collective-permute-start | bytes 393224 | tf_op jit(solution)/shard_map/ppermute | solution.py:326
  7.0 2.4 %collective-permute-done.1 = bf16[2,4,4,512]{3,2,1,0:T(4,128)(2,1)S(1)} collective-permute-done((bf16[2,4,4,512]{3,2,1,0:T(4,128)(2,1)S(1)}, bf16[2,4,4,512]{3,2,1,0:T(4,128)(2,1)S(1)}, u32[]{:S(2)}, u32[]{:S(2)}) %collective-permute-start.1) | collective-permute-done | bytes 32800 | tf_op jit(solution)/shard_map/ppermute | solution.py:353
  11.4 7.9 %all-to-all-start = ((bf16[16,4,16,256]{3,2,1,0:T(8,128)(2,1)}), bf16[16,4,16,256]{3,2,1,0:T(8,128)(2,1)S(1)}, u32[]{:S(2)}, u32[]{:S(2)}) async-start(bf16[16,4,16,256]{3,2,1,0:T(8,128)(2,1)} %bitcast.7), calls=%async_computation | async-start | bytes 1048576 | tf_op jit(solution)/shard_map/all_to_all | solution.py:360
  19.7 9.7 %all-to-all-done.mine = bf16[16,4,16,256]{3,2,1,0:T(8,128)(2,1)S(1)} async-done(((bf16[16,4,16,256]{3,2,1,0:T(8,128)(2,1)}), bf16[16,4,16,256]{3,2,1,0:T(8,128)(2,1)S(1)}, u32[]{:S(2)}, u32[]{:S(2)}) %all-to-all-start) | async-done | bytes 524320 | tf_op jit(solution)/shard_map/all_to_all | solution.py:360
  30.5 3.6 %all-to-all-start.1 = ((bf16[8,2,4,16,512]{4,3,2,1,0:T(8,128)(2,1)}), bf16[8,2,4,16,512]{4,3,2,1,0:T(8,128)(2,1)S(1)}, u32[]{:S(2)}, u32[]{:S(2)}) async-start(bf16[8,2,4,16,512]{4,3,2,1,0:T(8,128)(2,1)} %copy.14), calls=%async_computation.1 | async-start | bytes 2097152 | tf_op jit(solution)/shard_map/all_to_all | solution.py:369
  34.2 13.8 %shard_map.84 = (bf16[6,16,16,256]{3,2,1,0:T(8,128)(2,1)S(1)}, f32[4,16,16,256]{3,2,1,0:T(8,128)S(1)}, f32[4,16,16,256]{3,2,1,0:T(8,128)S(1)}, bf16[4,16,16,256]{3,2,1,0:T(8,128)(2,1)S(1)}) custom-call(s32[1]{0:T(128)} %bitcast.core_ref, bf16[16,4,16,256]{3,2,1,0:T(8,128)(2,1)S(1)} %all-to-all-done.mine, ...), custom_call_target="tpu_custom_call" | custom-call | flops 8992587776 | bytes 11550724 | tf_op jit(solution)/shard_map/pallas_call | solution.py:312
  52.3 2.6 %collective-permute-done.3.other = bf16[8,2,2,2,16,512]{5,4,3,2,1,0:T(8,128)(2,1)S(1)} collective-permute-done((bf16[8,2,2,2,16,512]{5,4,3,2,1,0:T(8,128)(2,1)S(1)}, bf16[8,2,2,2,16,512]{5,4,3,2,1,0:T(8,128)(2,1)S(1)}, u32[]{:S(2)}, u32[]{:S(2)}) %collective-permute-start.3) | collective-permute-done | bytes 1048608 | tf_op jit(solution)/shard_map/ppermute | solution.py:379
  57.7 3.5 %shard_map.85 = (bf16[4,16,16,256]{3,2,1,0:T(8,128)(2,1)S(1)}, bf16[2,16,16,256]{3,2,1,0:T(8,128)(2,1)S(1)}) custom-call(s32[1]{0:T(128)} %bitcast.core_ref, bf16[8,2,2,2,16,512]{5,4,3,2,1,0:T(8,128)(2,1)S(1)} %bitcast.43, bf16[8,2,2,2,16,512]{5,4,3,2,1,0:T(8,128)(2,1)S(1)} %collective-permute-done.3.other, bf16[4,4,256,256]{3,2,1,0:T(8,128)(2,1)S(1)} %copy-done.4, ...), custom_call_target="tpu_custom_call" | custom-call | flops 2147483648 | bytes 6045700 | tf_op jit(solution)/shard_map/pallas_call | solution.py:312
  61.2 1.6 %collective-permute-start.4 = (bf16[2,16,16,256]{3,2,1,0:T(8,128)(2,1)S(1)}, bf16[2,16,16,256]{3,2,1,0:T(8,128)(2,1)S(1)}, u32[]{:S(2)}, u32[]{:S(2)}) collective-permute-start(bf16[2,16,16,256]{3,2,1,0:T(8,128)(2,1)S(1)} %get-tuple-element.41), channel_id=1, source_target_pairs={{32,0},{64,32},{96,64},{33,1},{65,33},{97,65},{34,2},{66,34},{98,6... | collective-permute-start | bytes 786440 | tf_op jit(solution)/shard_map/ppermute | solution.py:326
  62.8 1.7 %shard_map.86.up = bf16[64,32,256]{2,1,0:T(8,128)(2,1)S(1)} custom-call(s32[1]{0:T(128)} %bitcast.core_ref, bf16[4,16,16,256]{3,2,1,0:T(8,128)(2,1)S(1)} %copy-done.2, bf16[8,2,2,2,16,512]{5,4,3,2,1,0:T(8,128)(2,1)S(1)} %bitcast.44, bf16[8,2,2,2,16,512]{5,4,3,2,1,0:T(8,128)(2,1)S(1)} %collective-permute-done.3.other), custom_call_target="tpu_custom_call" | custom-call | flops 536870912 | bytes 3670020 | tf_op jit(solution)/shard_map/pallas_call | solution.py:312
  64.6 6.4 %shard_map.87 = bf16[64,88,256]{2,1,0:T(8,128)(2,1)} custom-call(s32[2]{0:T(128)S(1)} %pad_add_fusion.place, bf16[6,16,16,256]{3,2,1,0:T(8,128)(2,1)S(1)} %copy-done.12, bf16[4,16,16,256]{3,2,1,0:T(8,128)(2,1)S(1)} %get-tuple-element.38.block.grad_sum, bf16[64,32,256]{2,1,0:T(8,128)(2,1)S(1)} %shard_map.86.up), custom_call_target="tpu_custom_call" | custom-call | flops 3623878656 | bytes 5242888 | tf_op jit(solution)/shard_map/pallas_call | solution.py:312
  71.8 6.8 %all-to-all-start.2 = ((bf16[64,88,256]{2,1,0:T(8,128)(2,1)}), bf16[64,88,256]{2,1,0:T(8,128)(2,1)}, u32[]{:S(2)}, u32[]{:S(2)}) async-start(bf16[64,88,256]{2,1,0:T(8,128)(2,1)} %shard_map.87), calls=%async_computation.2 | async-start | bytes 5767168 | tf_op jit(solution)/shard_map/all_to_all | solution.py:401
  78.6 2.0 %copy-done.3 = bf16[3,3,3,256,256]{4,3,2,1,0:T(8,128)(2,1)S(1)} copy-done((bf16[3,3,3,256,256]{4,3,2,1,0:T(8,128)(2,1)S(1)}, bf16[3,3,3,256,256]{4,3,2,1,0:T(8,128)(2,1)}, u32[]{:S(2)}) %copy-start.3) | copy-done | bytes 3538968
  80.6 4.8 %shard_map.88 = (bf16[4,16,16,256]{3,2,1,0:T(8,128)(2,1)S(1)}, bf16[2,16,16,256]{3,2,1,0:T(8,128)(2,1)S(1)}) custom-call(bf16[4,16,16,256]{3,2,1,0:T(8,128)(2,1)S(1)} %get-tuple-element.38.block.grad_sum, bf16[2,16,16,256]{3,2,1,0:T(8,128)(2,1)S(1)} %collective-permute-done.4.later, f32[4,16,16,256]{3,2,1,0:T(8,128)S(1)} %copy-done.10, ...), custom_call_target="tpu_custom_call" | custom-call | flops 3623878656 | bytes 6176768 | tf_op jit(solution)/shard_map/pallas_call | solution.py:312
  85.4 4.9 %shard_map.89 = (bf16[16,56,256]{2,1,0:T(8,128)(2,1)S(1)}, bf16[16,56,256]{2,1,0:T(8,128)(2,1)S(1)}, bf16[16,56,256]{2,1,0:T(8,128)(2,1)S(1)}, bf16[16,56,256]{2,1,0:T(8,128)(2,1)S(1)}) custom-call(s32[2]{0:T(128)S(1)} %pad_add_fusion.place, bf16[16,4,16,256]{3,2,1,0:T(8,128)(2,1)S(1)} %all-to-all-done.mine, bf16[16,4,16,256]{3,2,1,0:T(8,128)(2,1)S(1)} %copy-done.6, ...), custom_call_target="tpu_custom_call" | custom-call | flops 3623878656 | bytes 3407880 | tf_op jit(solution)/shard_map/pallas_call | solution.py:312
  90.4 3.8 %collective-permute-start.8 = (bf16[16,56,256]{2,1,0:T(8,128)(2,1)S(1)}, bf16[16,56,256]{2,1,0:T(8,128)(2,1)S(1)}, u32[]{:S(2)}, u32[]{:S(2)}) collective-permute-start(bf16[16,56,256]{2,1,0:T(8,128)(2,1)S(1)} %get-tuple-element.52), channel_id=1, source_target_pairs={{0,96},{32,0},{64,32},{96,64},{1,97},{33,1},{65,33},{97,65},{2,98}... | collective-permute-start | bytes 1376264 | tf_op jit(solution)/shard_map/ppermute | solution.py:330
  94.2 2.2 %collective-permute-start.6 = (bf16[16,56,256]{2,1,0:T(8,128)(2,1)S(1)}, bf16[16,56,256]{2,1,0:T(8,128)(2,1)S(1)}, u32[]{:S(2)}, u32[]{:S(2)}) collective-permute-start(bf16[16,56,256]{2,1,0:T(8,128)(2,1)S(1)} %get-tuple-element.50), channel_id=1, source_target_pairs={{0,64},{32,96},{64,0},{96,32},{1,65},{33,97},{65,1},{97,33},{2,66}... | collective-permute-start | bytes 1376264 | tf_op jit(solution)/shard_map/ppermute | solution.py:330
  97.8 20.5 %collective-permute-done.5.later = bf16[2,16,16,256]{3,2,1,0:T(8,128)(2,1)S(1)} collective-permute-done((bf16[2,16,16,256]{3,2,1,0:T(8,128)(2,1)S(1)}, bf16[2,16,16,256]{3,2,1,0:T(8,128)(2,1)S(1)}, u32[]{:S(2)}, u32[]{:S(2)}) %collective-permute-start.5) | collective-permute-done | bytes 262176 | tf_op jit(solution)/shard_map/ppermute | solution.py:326
  118.4 1.9 %shard_map.90 = bf16[16,2,8,256]{3,2,1,0:T(8,128)(2,1)S(1)} custom-call(s32[1]{0:T(128)} %bitcast.core_ref, bf16[4,16,16,256]{3,2,1,0:T(8,128)(2,1)S(1)} %get-tuple-element.46.block, bf16[2,16,16,256]{3,2,1,0:T(8,128)(2,1)S(1)} %collective-permute-done.5.later, bf16[4,16,16,256]{3,2,1,0:T(8,128)(2,1)S(1)} %get-tuple-element.38.block.grad_sum, ...), custom_call_target="tpu_custom_call" | custom-call | flops 939524096 | bytes 4980740 | tf_op jit(solution)/shard_map/pallas_call | solution.py:312
  122.8 5.6 %all-to-all-start.3 = ((bf16[16,72,256]{2,1,0:T(8,128)(2,1)}), bf16[16,72,256]{2,1,0:T(8,128)(2,1)S(1)}, u32[]{:S(2)}, u32[]{:S(2)}) async-start(bf16[16,72,256]{2,1,0:T(8,128)(2,1)} %pad_maximum_fusion), calls=%async_computation.3 | async-start | bytes 1179648 | tf_op jit(solution)/shard_map/all_to_all | solution.py:431
  128.4 2.2 %convert_reduce_fusion = f32[4,88,256]{2,1,0:T(8,128)S(1)} fusion(bf16[16,4,88,256]{3,2,1,0:T(8,128)(2,1)} %bitcast.21), kind=kLoop, calls=%fused_computation | loop fusion | flops 2793472 | bytes 3244032 | tf_op jit(solution)/shard_map/reduce_sum | solution.py:425
  130.7 2.9 %collective-permute-start.11 = (bf16[88,256]{1,0:T(8,128)(2,1)S(1)}, bf16[88,256]{1,0:T(8,128)(2,1)S(1)}, u32[]{:S(2)}, u32[]{:S(2)}) collective-permute-start(bf16[88,256]{1,0:T(8,128)(2,1)S(1)} %get-tuple-element.59), channel_id=1, source_target_pairs={{0,96},{32,0},{64,32},{96,64},{1,97},{33,1},{65,33},{97,65},{2,98}... | collective-permute-start | bytes 135176 | tf_op jit(solution)/shard_map/ppermute | solution.py:330
  133.6 2.7 %collective-permute-start.9 = (bf16[88,256]{1,0:T(8,128)(2,1)S(1)}, bf16[88,256]{1,0:T(8,128)(2,1)S(1)}, u32[]{:S(2)}, u32[]{:S(2)}) collective-permute-start(bf16[88,256]{1,0:T(8,128)(2,1)S(1)} %get-tuple-element.58), channel_id=1, source_target_pairs={{0,64},{32,96},{64,0},{96,32},{1,65},{33,97},{65,1},{97,33},{2,66}... | collective-permute-start | bytes 135176 | tf_op jit(solution)/shard_map/ppermute | solution.py:330
  136.3 3.1 %collective-permute-done.10 = bf16[88,256]{1,0:T(8,128)(2,1)S(1)} collective-permute-done((bf16[88,256]{1,0:T(8,128)(2,1)S(1)}, bf16[88,256]{1,0:T(8,128)(2,1)S(1)}, u32[]{:S(2)}, u32[]{:S(2)}) %collective-permute-start.10) | collective-permute-done | bytes 45088 | tf_op jit(solution)/shard_map/ppermute | solution.py:330
  (70 shorter events, 20.8 us)
Async XLA Ops:
  0.6 8.8 %collective-permute-start = (bf16[2,128,256]{2,1,0:T(8,128)(2,1)}, bf16[2,128,256]{2,1,0:T(8,128)(2,1)S(1)}, u32[]{:S(2)}, u32[]{:S(2)}) collective-permute-start(bf16[2,128,256]{2,1,0:T(8,128)(2,1)} %bitcast.49), channel_id=1, source_target_pairs={{0,32},{32,64},{64,96},{1,33},{33,65},{65,97},{2,34},{34,66},{66,9... | collective-permute-start | bytes 393224 | tf_op jit(solution)/shard_map/ppermute | solution.py:326
  5.5 4.0 %collective-permute-start.1 = (bf16[2,4,4,512]{3,2,1,0:T(4,128)(2,1)S(1)}, bf16[2,4,4,512]{3,2,1,0:T(4,128)(2,1)S(1)}, u32[]{:S(2)}, u32[]{:S(2)}) collective-permute-start(bf16[2,4,4,512]{3,2,1,0:T(4,128)(2,1)S(1)} %slice_select_fusion), channel_id=1, source_target_pairs={{0,1},{1,0},{2,3},{3,2},{4,5},{5,4},{6,7},{7,6},{8,9},{9,8},{10,11... | collective-permute-start | bytes 98312 | tf_op jit(solution)/shard_map/ppermute | solution.py:353
  11.4 18.0 %all-to-all-start = ((bf16[16,4,16,256]{3,2,1,0:T(8,128)(2,1)}), bf16[16,4,16,256]{3,2,1,0:T(8,128)(2,1)S(1)}, u32[]{:S(2)}, u32[]{:S(2)}) async-start(bf16[16,4,16,256]{3,2,1,0:T(8,128)(2,1)} %bitcast.7), calls=%async_computation | async-start | bytes 1048576 | tf_op jit(solution)/shard_map/all_to_all | solution.py:360
  29.4 4.7 %collective-permute-start.2 = (bf16[16,4,16,256]{3,2,1,0:T(8,128)(2,1)S(1)}, bf16[16,4,16,256]{3,2,1,0:T(8,128)(2,1)S(1)}, u32[]{:S(2)}, u32[]{:S(2)}) collective-permute-start(bf16[16,4,16,256]{3,2,1,0:T(8,128)(2,1)S(1)} %all-to-all-done.mine), channel_id=1, source_target_pairs={{0,16},{16,0},{1,17},{17,1},{2,18},{18,2},{3,19},{19,3},{4,20},{20... | collective-permute-start | bytes 1572872 | tf_op jit(solution)/shard_map/ppermute | solution.py:368
  30.5 21.7 %all-to-all-start.1 = ((bf16[8,2,4,16,512]{4,3,2,1,0:T(8,128)(2,1)}), bf16[8,2,4,16,512]{4,3,2,1,0:T(8,128)(2,1)S(1)}, u32[]{:S(2)}, u32[]{:S(2)}) async-start(bf16[8,2,4,16,512]{4,3,2,1,0:T(8,128)(2,1)} %copy.14), calls=%async_computation.1 | async-start | bytes 2097152 | tf_op jit(solution)/shard_map/all_to_all | solution.py:369
  34.1 13.9 %copy-start.5 = (bf16[16,4,16,256]{3,2,1,0:T(8,128)(2,1)}, bf16[16,4,16,256]{3,2,1,0:T(8,128)(2,1)S(1)}, u32[]{:S(2)}) copy-start(bf16[16,4,16,256]{3,2,1,0:T(8,128)(2,1)S(1)} %collective-permute-done.2.other) | copy-start | bytes 1572868
  52.2 2.7 %collective-permute-start.3 = (bf16[8,2,2,2,16,512]{5,4,3,2,1,0:T(8,128)(2,1)S(1)}, bf16[8,2,2,2,16,512]{5,4,3,2,1,0:T(8,128)(2,1)S(1)}, u32[]{:S(2)}, u32[]{:S(2)}) collective-permute-start(bf16[8,2,2,2,16,512]{5,4,3,2,1,0:T(8,128)(2,1)S(1)} %bitcast.42), channel_id=1, source_target_pairs={{0,16},{16,0},{1,17},{17,1},{2,18},{18,2},{3,19},{19,3},{4,20},{20... | collective-permute-start | bytes 3145736 | tf_op jit(solution)/shard_map/ppermute | solution.py:379
  54.9 1.6 %copy-start.4 = (bf16[4,4,256,256]{3,2,1,0:T(8,128)(2,1)S(1)}, bf16[4,4,256,256]{3,2,1,0:T(8,128)(2,1)}, u32[]{:S(2)}) copy-start(bf16[4,4,256,256]{3,2,1,0:T(8,128)(2,1)} %weights.3) | copy-start | bytes 6291460
  57.7 5.2 %copy-start.2 = (bf16[4,16,16,256]{3,2,1,0:T(8,128)(2,1)S(1)}, bf16[4,16,16,256]{3,2,1,0:T(8,128)(2,1)}, u32[]{:S(2)}) copy-start(bf16[4,16,16,256]{3,2,1,0:T(8,128)(2,1)} %copy-done.1) | copy-start | bytes 1572868
  61.2 3.4 %copy-start.12 = (bf16[6,16,16,256]{3,2,1,0:T(8,128)(2,1)S(1)}, bf16[6,16,16,256]{3,2,1,0:T(8,128)(2,1)}, u32[]{:S(2)}) copy-start(bf16[6,16,16,256]{3,2,1,0:T(8,128)(2,1)} %copy-done.11) | copy-start | bytes 2359300
  61.2 10.5 %collective-permute-start.4 = (bf16[2,16,16,256]{3,2,1,0:T(8,128)(2,1)S(1)}, bf16[2,16,16,256]{3,2,1,0:T(8,128)(2,1)S(1)}, u32[]{:S(2)}, u32[]{:S(2)}) collective-permute-start(bf16[2,16,16,256]{3,2,1,0:T(8,128)(2,1)S(1)} %get-tuple-element.41), channel_id=1, source_target_pairs={{32,0},{64,32},{96,64},{33,1},{65,33},{97,65},{34,2},{66,34},{98,6... | collective-permute-start | bytes 786440 | tf_op jit(solution)/shard_map/ppermute | solution.py:326
  71.0 7.6 %copy-start.10 = (f32[4,16,16,256]{3,2,1,0:T(8,128)S(1)}, f32[4,16,16,256]{3,2,1,0:T(8,128)}, u32[]{:S(2)}) copy-start(f32[4,16,16,256]{3,2,1,0:T(8,128)} %copy-done.9) | copy-start | bytes 3145732
  71.8 50.2 %all-to-all-start.2 = ((bf16[64,88,256]{2,1,0:T(8,128)(2,1)}), bf16[64,88,256]{2,1,0:T(8,128)(2,1)}, u32[]{:S(2)}, u32[]{:S(2)}) async-start(bf16[64,88,256]{2,1,0:T(8,128)(2,1)} %shard_map.87), calls=%async_computation.2 | async-start | bytes 5767168 | tf_op jit(solution)/shard_map/all_to_all | solution.py:401
  78.6 2.0 %copy-start.3 = (bf16[3,3,3,256,256]{4,3,2,1,0:T(8,128)(2,1)S(1)}, bf16[3,3,3,256,256]{4,3,2,1,0:T(8,128)(2,1)}, u32[]{:S(2)}) copy-start(bf16[3,3,3,256,256]{4,3,2,1,0:T(8,128)(2,1)} %weights.4) | copy-start | bytes 10616836
  80.6 4.8 %copy-start.6 = (bf16[16,4,16,256]{3,2,1,0:T(8,128)(2,1)S(1)}, bf16[16,4,16,256]{3,2,1,0:T(8,128)(2,1)}, u32[]{:S(2)}) copy-start(bf16[16,4,16,256]{3,2,1,0:T(8,128)(2,1)} %copy-done.5) | copy-start | bytes 1572868
  85.4 33.0 %copy-start = (bf16[3,3,3,256,256]{4,3,2,1,0:T(8,128)(2,1)S(1)}, bf16[3,3,3,256,256]{4,3,2,1,0:T(8,128)(2,1)}, u32[]{:S(2)}) copy-start(bf16[3,3,3,256,256]{4,3,2,1,0:T(8,128)(2,1)} %weights.5) | copy-start | bytes 10616836
  90.4 30.0 %collective-permute-start.8 = (bf16[16,56,256]{2,1,0:T(8,128)(2,1)S(1)}, bf16[16,56,256]{2,1,0:T(8,128)(2,1)S(1)}, u32[]{:S(2)}, u32[]{:S(2)}) collective-permute-start(bf16[16,56,256]{2,1,0:T(8,128)(2,1)S(1)} %get-tuple-element.52), channel_id=1, source_target_pairs={{0,96},{32,0},{64,32},{96,64},{1,97},{33,1},{65,33},{97,65},{2,98}... | collective-permute-start | bytes 1376264 | tf_op jit(solution)/shard_map/ppermute | solution.py:330
  94.2 26.2 %collective-permute-start.7 = (bf16[16,56,256]{2,1,0:T(8,128)(2,1)S(1)}, bf16[16,56,256]{2,1,0:T(8,128)(2,1)S(1)}, u32[]{:S(2)}, u32[]{:S(2)}) collective-permute-start(bf16[16,56,256]{2,1,0:T(8,128)(2,1)S(1)} %get-tuple-element.51), channel_id=1, source_target_pairs={{0,32},{32,64},{64,96},{96,0},{1,33},{33,65},{65,97},{97,1},{2,34}... | collective-permute-start | bytes 1376264 | tf_op jit(solution)/shard_map/ppermute | solution.py:330
  94.2 26.2 %collective-permute-start.6 = (bf16[16,56,256]{2,1,0:T(8,128)(2,1)S(1)}, bf16[16,56,256]{2,1,0:T(8,128)(2,1)S(1)}, u32[]{:S(2)}, u32[]{:S(2)}) collective-permute-start(bf16[16,56,256]{2,1,0:T(8,128)(2,1)S(1)} %get-tuple-element.50), channel_id=1, source_target_pairs={{0,64},{32,96},{64,0},{96,32},{1,65},{33,97},{65,1},{97,33},{2,66}... | collective-permute-start | bytes 1376264 | tf_op jit(solution)/shard_map/ppermute | solution.py:330
  96.3 22.0 %collective-permute-start.5 = (bf16[2,16,16,256]{3,2,1,0:T(8,128)(2,1)S(1)}, bf16[2,16,16,256]{3,2,1,0:T(8,128)(2,1)S(1)}, u32[]{:S(2)}, u32[]{:S(2)}) collective-permute-start(bf16[2,16,16,256]{3,2,1,0:T(8,128)(2,1)S(1)} %get-tuple-element.47), channel_id=1, source_target_pairs={{32,0},{64,32},{96,64},{33,1},{65,33},{97,65},{34,2},{66,34},{98,6... | collective-permute-start | bytes 786440 | tf_op jit(solution)/shard_map/ppermute | solution.py:326
  122.8 17.9 %all-to-all-start.3 = ((bf16[16,72,256]{2,1,0:T(8,128)(2,1)}), bf16[16,72,256]{2,1,0:T(8,128)(2,1)S(1)}, u32[]{:S(2)}, u32[]{:S(2)}) async-start(bf16[16,72,256]{2,1,0:T(8,128)(2,1)} %pad_maximum_fusion), calls=%async_computation.3 | async-start | bytes 1179648 | tf_op jit(solution)/shard_map/all_to_all | solution.py:431
  130.7 5.6 %collective-permute-start.11 = (bf16[88,256]{1,0:T(8,128)(2,1)S(1)}, bf16[88,256]{1,0:T(8,128)(2,1)S(1)}, u32[]{:S(2)}, u32[]{:S(2)}) collective-permute-start(bf16[88,256]{1,0:T(8,128)(2,1)S(1)} %get-tuple-element.59), channel_id=1, source_target_pairs={{0,96},{32,0},{64,32},{96,64},{1,97},{33,1},{65,33},{97,65},{2,98}... | collective-permute-start | bytes 135176 | tf_op jit(solution)/shard_map/ppermute | solution.py:330
  133.6 5.7 %collective-permute-start.10 = (bf16[88,256]{1,0:T(8,128)(2,1)S(1)}, bf16[88,256]{1,0:T(8,128)(2,1)S(1)}, u32[]{:S(2)}, u32[]{:S(2)}) collective-permute-start(bf16[88,256]{1,0:T(8,128)(2,1)S(1)} %get-tuple-element.60), channel_id=1, source_target_pairs={{0,32},{32,64},{64,96},{96,0},{1,33},{33,65},{65,97},{97,1},{2,34}... | collective-permute-start | bytes 135176 | tf_op jit(solution)/shard_map/ppermute | solution.py:330
  133.6 5.7 %collective-permute-start.9 = (bf16[88,256]{1,0:T(8,128)(2,1)S(1)}, bf16[88,256]{1,0:T(8,128)(2,1)S(1)}, u32[]{:S(2)}, u32[]{:S(2)}) collective-permute-start(bf16[88,256]{1,0:T(8,128)(2,1)S(1)} %get-tuple-element.58), channel_id=1, source_target_pairs={{0,64},{32,96},{64,0},{96,32},{1,65},{33,97},{65,1},{97,33},{2,66}... | collective-permute-start | bytes 135176 | tf_op jit(solution)/shard_map/ppermute | solution.py:330
  (5 other events, 4.9 us)

commit v10 on v9

--- a/solution.py
+++ b/solution.py
@@ -86,7 +86,7 @@
     return total[frame * rows : (frame + 1) * rows].reshape(ROWS, columns, CH)
 
 
-def forward_kernel(core_ref, mine, other, first, second, mask, act, slope, summed, up_act, table, total):
+def forward_kernel(core_ref, mine, other, first, second, mask, act, slope, late_slope, up_act, table, total):
     step = pl.program_id(0)
     core = core_ref[0]
     sources = ((mine, core), (other, 1 - core))
@@ -113,7 +113,7 @@
             act[frame] = result
             fill_table(table, frame, result, True)
             if frame >= 2:
-                slope[frame - 2] = slope_of(values, sigma)
+                slope[frame - 2] = slope_of(values, sigma).astype(BF16)
         total[...] = jnp.zeros_like(total)
 
     @pl.when(step >= 3)
@@ -128,8 +128,9 @@
                 place = 2 * which + frame
                 values = total[pl.ds(pl.multiple_of(place * rows, rows), rows)].reshape(ROWS, WIN, CH)
                 values = values + source[:, 2 + frame].astype(F32)
-                summed[place] = values
-                up_act[place] = (values * jax.nn.sigmoid(values)).astype(BF16)
+                sigma = jax.nn.sigmoid(values)
+                late_slope[place] = slope_of(values, sigma).astype(BF16)
+                up_act[place] = (values * sigma).astype(BF16)
 
 
 def hidden_kernel(block, later, slope, weights, mask, grad_hidden, head, table, total):
@@ -147,7 +148,7 @@
     @pl.when(pl.program_id(0) == 2)
     def _():
         for frame in range(FR):
-            result = (frame_of(total, frame, WIN) * slope[frame] * mask[...]).astype(BF16)
+            result = (frame_of(total, frame, WIN) * slope[frame].astype(F32) * mask[...]).astype(BF16)
             grad_hidden[frame] = result
             if frame < 2:
                 head[frame] = result
@@ -174,7 +175,7 @@
             grad_features[:, frame] = values.astype(BF16)
 
 
-def cotangent_kernel(core_ref, mine, other, weights, summed, mask, grad_sum, head, table):
+def cotangent_kernel(core_ref, mine, other, weights, slope, mask, grad_sum, head, table):
     core = core_ref[0]
     border = jnp.zeros((FR, WIN, 4 * CH), BF16)
     table[:, 0, 0] = border
@@ -201,8 +202,7 @@
                 more = nt(lhs.reshape(ROWS * WIN, CH), weights[tap, column])
                 part = more if part is None else part + more
         grad_act = part.reshape(ROWS, WIN, CH).astype(BF16).astype(F32)
-        values = summed[frame]
-        grad = grad_act * slope_of(values, jax.nn.sigmoid(values)) * mask[...]
+        grad = grad_act * slope[frame].astype(F32) * mask[...]
         grad_sum[frame] = grad.astype(BF16)
         if frame < 2:
             head[frame] = grad.astype(BF16)
@@ -240,7 +240,12 @@
                 ].astype(BF16)
 
 
-def tap_sums(frames, block, table, flipped, sums):
+def owners_of(tap):
+    first, last = tap * CH // (16 * SHARE), ((tap + 1) * CH - 1) // (16 * SHARE)
+    return sorted({k % 2 for k in range(first, last + 1)})
+
+
+def tap_sums(core, frames, block, table, flipped, sums):
     clear_border(table)
     column = lax.broadcasted_iota(jnp.int32, (ROWS, WIN, CH), 1)
     own = (column >= EDGE) & (column < EDGE + OWN)
@@ -254,11 +259,17 @@
     for tap_t in range(3):
         lhs = flipped[:, tap_t * rows : (tap_t + FR) * rows]
         for tap_h in range(3):
-            rhs = table[:, 2 - tap_h : 2 - tap_h + ROWS]
-            result = nn(lhs, rhs.reshape(FR * rows, 3 * CH))
             for tap_w in range(3):
-                at = (tap_t * 9 + tap_h * 3 + tap_w) * CH
-                sums[at : at + CH] = result[:, tap_w * CH : (tap_w + 1) * CH]
+
+                def fill(tap_h=tap_h, tap_w=tap_w, at=(tap_t * 9 + tap_h * 3 + tap_w) * CH, lhs=lhs):
+                    rhs = table[:, 2 - tap_h : 2 - tap_h + ROWS, :, tap_w * CH : (tap_w + 1) * CH]
+                    sums[at : at + CH] = nn(lhs, rhs.reshape(FR * rows, CH))
+
+                owners = owners_of(tap_t * 9 + tap_h * 3 + tap_w)
+                if len(owners) == 2:
+                    fill()
+                else:
+                    pl.when(core == owners[0])(fill)
 
 
 def piece_of(sums, owner, member):
@@ -268,7 +279,7 @@
 
 
 def second_grad_kernel(place, act, block, up, out, table, flipped, sums):
-    tap_sums([(frame, act[frame]) for frame in range(FR + 2)], block, table, flipped, sums)
+    tap_sums(place[0], [(frame, act[frame]) for frame in range(FR + 2)], block, table, flipped, sums)
     for step in range(4):
         group = lax.rem(place[1] + step, 4)
         for member in range(16):
@@ -285,7 +296,7 @@
         frames.append((frame, before))
         frames.append((2 + 2 * core + frame, mine[:, 2 + frame]))
         frames.append((4 - 2 * core + frame, other[:, 2 + frame]))
-    tap_sums(frames, block, table, flipped, sums)
+    tap_sums(core, frames, block, table, flipped, sums)
     for step, out in enumerate((own, next_one, next_two, next_three)):
         group = lax.rem(place[1] + step, 4)
         for member in range(16):
@@ -368,17 +379,17 @@
     other_block = lax.ppermute(block, "core", swap)
     mine = lax.all_to_all(fine, ("z", "x_hi"), 0, 0, tiled=True).reshape(8, 2, 2, 2, WIN, 2 * CH)
 
-    first_act, first_slope, summed, up_act = call(
+    first_act, first_slope, late_slope, up_act = call(
         forward_kernel, (6,), (core_arg, block, other_block, conv_first, conv_second, mask),
         [SMEM, whole(block.shape), whole(block.shape), tap_weights(0), tap_weights(3), whole(mask.shape)],
-        [(six_frames, BF16), (act_shape, F32), (act_shape, F32), (act_shape, BF16)],
+        [(six_frames, BF16), (act_shape, BF16), (act_shape, BF16), (act_shape, BF16)],
         [pltpu.VMEM((FR + 4, ROWS + 2, WIN, 3 * CH), BF16), pltpu.VMEM(((FR + 2) * ROWS * WIN, CH), F32)],
         67 * tap_flops,
     )
     mine, up_act = lax.optimization_barrier((mine, up_act))
     other = lax.ppermute(mine, "core", swap)
     grad_sum, sum_head = call(
-        cotangent_kernel, (), (core_arg, mine, other, up_kernel, summed, mask),
+        cotangent_kernel, (), (core_arg, mine, other, up_kernel, late_slope, mask),
         [SMEM, whole(mine.shape), whole(mine.shape), whole(up_kernel.shape), whole(act_shape), whole(mask.shape)],
         [(act_shape, BF16), (two_frames, BF16)], [pltpu.VMEM((FR, ROWS + 1, 2, WIN, 4 * CH), BF16)], 16 * tap_flops,
     )
@@ -405,7 +416,7 @@
         [whole(act_shape), whole(later.shape), whole(act_shape), tap_weights(), whole(mask.shape)],
         [(act_shape, BF16), (two_frames, BF16)], [table, total], 27 * tap_flops,
     )
-    later_hidden = shift(hidden_head, "y", -1)
+    later_hidden = lax.ppermute(hidden_head, ("y", "core"), [(2 * i + 1, 2 * i - 1) for i in range(1, 4)])
     blocks = call(
         first_grad_kernel, (), (place, block, other_block, grad_hidden),
         [SMEM, whole(block.shape), whole(block.shape), whole(act_shape)],

time: 143 us -> 144 us (level)
  Pallas kernels: 37.2 us -> 39.4 us
    ppermute x3 -> x2, waiting for transfers between devices: 21.3 us -> 0.01 us  [shift(): lax.ppermute(value, axis, [(i, i + step) for i in range(count) if 0 <= i...]
    ppermute x6, waiting for transfers between devices: 3.08 us -> 21.5 us  [over_y(): return lax.ppermute(value, 'y', [(i, (i + step) % 4) for i in range(4)])]
    all_to_all x1, waiting for transfers between devices: 1.31 us -> 4.17 us  [shards(): early = lax.all_to_all(early, ('z', 'x_hi', 'width'), 0, 0, tiled=True)]
    pallas_call x7, Pallas kernels: 37.2 us -> 39.4 us  [call(): pl.pallas_call(kernel, out_shape=shapes[0] if single else shapes, grid=gr...]
    ppermute x3 -> x2, starting transfers between devices: 6.68 us -> 5.18 us  [shift(): lax.ppermute(value, axis, [(i, i + step) for i in range(count) if 0 <= i...]
  transfers between devices with their start and end apart: 16 -> 16, of which waited for: 8 -> 8; matrix products, arithmetic and copies ran while one was open for 5% -> 5% of each run, Pallas kernels for 24% -> 25%
where the time goes in v10:
time: 144 us; the launch traced here: 143 us
  starting transfers between devices  42.4 us (29%)
  waiting for transfers between devices  41.1 us (29%)
  Pallas kernels  39.4 us (27%)
  local copies, waits for them, and re-layouts  13.9 us (10%)
  other arithmetic  4.93 us (3%)
    pallas_call x7, Pallas kernels, call(): pl.pallas_call(kernel, out_shape=shapes[0] if single else shapes, grid=gr...  39.4 us
    ppermute x6, waiting for transfers between devices, over_y(): return lax.ppermute(value, 'y', [(i, (i + step) % 4) for i in range(4)])  21.5 us
    ppermute x6, starting transfers between devices, over_y(): return lax.ppermute(value, 'y', [(i, (i + step) % 4) for i in range(4)])  12.3 us
    all_to_all x1, waiting for transfers between devices, shards(): block = lax.all_to_all(windows, ('z', 'x_hi', 'width'), 0, 0, tiled=True)  9.7 us
    unnamed x28, local copies, waits for them, and re-layouts  8.59 us
    all_to_all x1, starting transfers between devices, shards(): block = lax.all_to_all(windows, ('z', 'x_hi', 'width'), 0, 0, tiled=True)  7.88 us
    all_to_all x1, starting transfers between devices, shards(): early = lax.all_to_all(early, ('z', 'x_hi', 'width'), 0, 0, tiled=True)  6.74 us
    ppermute x2, starting transfers between devices, shift(): lax.ppermute(value, axis, [(i, i + step) for i in range(count) if 0 <= i...  5.18 us
  transfers between devices with their start and end apart: 16, of which 8 were waited for; matrix products, arithmetic and copies ran while one was open for 5% of the time, Pallas kernels for 25%

profile of v10, /device:TPU:0, one launch (start us, length us, event | category | flops | bytes accessed | tf_op | source)
XLA Modules:
  0.0 142.7 jit_solution(14976441366809958791)
XLA Ops:
  0.6 3.6 %collective-permute-start = (bf16[2,128,256]{2,1,0:T(8,128)(2,1)}, bf16[2,128,256]{2,1,0:T(8,128)(2,1)S(1)}, u32[]{:S(2)}, u32[]{:S(2)}) collective-permute-start(bf16[2,128,256]{2,1,0:T(8,128)(2,1)} %bitcast.49), channel_id=1, source_target_pairs={{0,32},{32,64},{64,96},{1,33},{33,65},{65,97},{2,34},{34,66},{66,9... | collective-permute-start | bytes 393224 | tf_op jit(solution)/shard_map/ppermute | solution.py:337
  7.0 2.4 %collective-permute-done.1 = bf16[2,4,4,512]{3,2,1,0:T(4,128)(2,1)S(1)} collective-permute-done((bf16[2,4,4,512]{3,2,1,0:T(4,128)(2,1)S(1)}, bf16[2,4,4,512]{3,2,1,0:T(4,128)(2,1)S(1)}, u32[]{:S(2)}, u32[]{:S(2)}) %collective-permute-start.1) | collective-permute-done | bytes 32800 | tf_op jit(solution)/shard_map/ppermute | solution.py:364
  11.4 7.9 %all-to-all-start = ((bf16[16,4,16,256]{3,2,1,0:T(8,128)(2,1)}), bf16[16,4,16,256]{3,2,1,0:T(8,128)(2,1)S(1)}, u32[]{:S(2)}, u32[]{:S(2)}) async-start(bf16[16,4,16,256]{3,2,1,0:T(8,128)(2,1)} %bitcast.7), calls=%async_computation | async-start | bytes 1048576 | tf_op jit(solution)/shard_map/all_to_all | solution.py:371
  19.7 9.7 %all-to-all-done.mine = bf16[16,4,16,256]{3,2,1,0:T(8,128)(2,1)S(1)} async-done(((bf16[16,4,16,256]{3,2,1,0:T(8,128)(2,1)}), bf16[16,4,16,256]{3,2,1,0:T(8,128)(2,1)S(1)}, u32[]{:S(2)}, u32[]{:S(2)}) %all-to-all-start) | async-done | bytes 524320 | tf_op jit(solution)/shard_map/all_to_all | solution.py:371
  30.5 3.6 %all-to-all-start.1 = ((bf16[8,2,4,16,512]{4,3,2,1,0:T(8,128)(2,1)}), bf16[8,2,4,16,512]{4,3,2,1,0:T(8,128)(2,1)S(1)}, u32[]{:S(2)}, u32[]{:S(2)}) async-start(bf16[8,2,4,16,512]{4,3,2,1,0:T(8,128)(2,1)} %copy.14), calls=%async_computation.1 | async-start | bytes 2097152 | tf_op jit(solution)/shard_map/all_to_all | solution.py:380
  34.2 14.0 %shard_map.84 = (bf16[6,16,16,256]{3,2,1,0:T(8,128)(2,1)S(1)}, bf16[4,16,16,256]{3,2,1,0:T(8,128)(2,1)S(1)}, bf16[4,16,16,256]{3,2,1,0:T(8,128)(2,1)S(1)}, bf16[4,16,16,256]{3,2,1,0:T(8,128)(2,1)S(1)}) custom-call(s32[1]{0:T(128)} %bitcast.core_ref, bf16[16,4,16,256]{3,2,1,0:T(8,128)(2,1)S(1)} %all-to-all-done.mine, ...), custom_call_target="tpu_custom_call" | custom-call | flops 8992587776 | bytes 10502148 | tf_op jit(solution)/shard_map/pallas_call | solution.py:323
  52.3 2.6 %collective-permute-done.3.other = bf16[8,2,2,2,16,512]{5,4,3,2,1,0:T(8,128)(2,1)S(1)} collective-permute-done((bf16[8,2,2,2,16,512]{5,4,3,2,1,0:T(8,128)(2,1)S(1)}, bf16[8,2,2,2,16,512]{5,4,3,2,1,0:T(8,128)(2,1)S(1)}, u32[]{:S(2)}, u32[]{:S(2)}) %collective-permute-start.3) | collective-permute-done | bytes 1048608 | tf_op jit(solution)/shard_map/ppermute | solution.py:390
  57.5 3.4 %shard_map.85 = (bf16[4,16,16,256]{3,2,1,0:T(8,128)(2,1)S(1)}, bf16[2,16,16,256]{3,2,1,0:T(8,128)(2,1)S(1)}) custom-call(s32[1]{0:T(128)} %bitcast.core_ref, bf16[8,2,2,2,16,512]{5,4,3,2,1,0:T(8,128)(2,1)S(1)} %bitcast.43, bf16[8,2,2,2,16,512]{5,4,3,2,1,0:T(8,128)(2,1)S(1)} %collective-permute-done.3.other, bf16[4,4,256,256]{3,2,1,0:T(8,128)(2,1)S(1)} %copy-done.4, ...), custom_call_target="tpu_custom_call" | custom-call | flops 2147483648 | bytes 5521412 | tf_op jit(solution)/shard_map/pallas_call | solution.py:323
  64.3 7.4 %shard_map.87 = bf16[64,88,256]{2,1,0:T(8,128)(2,1)} custom-call(s32[2]{0:T(128)S(1)} %pad_add_fusion.place, bf16[6,16,16,256]{3,2,1,0:T(8,128)(2,1)S(1)} %copy-done.10, bf16[4,16,16,256]{3,2,1,0:T(8,128)(2,1)S(1)} %get-tuple-element.38.block.grad_sum, bf16[64,32,256]{2,1,0:T(8,128)(2,1)S(1)} %shard_map.86.up), custom_call_target="tpu_custom_call" | custom-call | flops 3623878656 | bytes 5242888 | tf_op jit(solution)/shard_map/pallas_call | solution.py:323
  71.8 6.7 %all-to-all-start.2 = ((bf16[64,88,256]{2,1,0:T(8,128)(2,1)}), bf16[64,88,256]{2,1,0:T(8,128)(2,1)}, u32[]{:S(2)}, u32[]{:S(2)}) async-start(bf16[64,88,256]{2,1,0:T(8,128)(2,1)} %shard_map.87), calls=%async_computation.2 | async-start | bytes 5767168 | tf_op jit(solution)/shard_map/all_to_all | solution.py:412
  78.5 2.0 %copy-done.3 = bf16[3,3,3,256,256]{4,3,2,1,0:T(8,128)(2,1)S(1)} copy-done((bf16[3,3,3,256,256]{4,3,2,1,0:T(8,128)(2,1)S(1)}, bf16[3,3,3,256,256]{4,3,2,1,0:T(8,128)(2,1)}, u32[]{:S(2)}) %copy-start.3) | copy-done | bytes 3538968
  80.5 4.8 %shard_map.88 = (bf16[4,16,16,256]{3,2,1,0:T(8,128)(2,1)S(1)}, bf16[2,16,16,256]{3,2,1,0:T(8,128)(2,1)S(1)}) custom-call(bf16[4,16,16,256]{3,2,1,0:T(8,128)(2,1)S(1)} %get-tuple-element.38.block.grad_sum, bf16[2,16,16,256]{3,2,1,0:T(8,128)(2,1)S(1)} %collective-permute-done.4.later, bf16[4,16,16,256]{3,2,1,0:T(8,128)(2,1)S(1)} %copy-done.12, ...), custom_call_target="tpu_custom_call" | custom-call | flops 3623878656 | bytes 5652480 | tf_op jit(solution)/shard_map/pallas_call | solution.py:323
  85.4 6.0 %shard_map.89 = (bf16[16,56,256]{2,1,0:T(8,128)(2,1)S(1)}, bf16[16,56,256]{2,1,0:T(8,128)(2,1)S(1)}, bf16[16,56,256]{2,1,0:T(8,128)(2,1)S(1)}, bf16[16,56,256]{2,1,0:T(8,128)(2,1)S(1)}) custom-call(s32[2]{0:T(128)S(1)} %pad_add_fusion.place, bf16[16,4,16,256]{3,2,1,0:T(8,128)(2,1)S(1)} %all-to-all-done.mine, bf16[16,4,16,256]{3,2,1,0:T(8,128)(2,1)S(1)} %copy-done.6, ...), custom_call_target="tpu_custom_call" | custom-call | flops 3623878656 | bytes 3407880 | tf_op jit(solution)/shard_map/pallas_call | solution.py:323
  91.4 4.5 %collective-permute-start.8 = (bf16[16,56,256]{2,1,0:T(8,128)(2,1)S(1)}, bf16[16,56,256]{2,1,0:T(8,128)(2,1)S(1)}, u32[]{:S(2)}, u32[]{:S(2)}) collective-permute-start(bf16[16,56,256]{2,1,0:T(8,128)(2,1)S(1)} %get-tuple-element.52), channel_id=1, source_target_pairs={{0,96},{32,0},{64,32},{96,64},{1,97},{33,1},{65,33},{97,65},{2,98}... | collective-permute-start | bytes 1376264 | tf_op jit(solution)/shard_map/ppermute | solution.py:341
  95.9 2.2 %collective-permute-start.6 = (bf16[16,56,256]{2,1,0:T(8,128)(2,1)S(1)}, bf16[16,56,256]{2,1,0:T(8,128)(2,1)S(1)}, u32[]{:S(2)}, u32[]{:S(2)}) collective-permute-start(bf16[16,56,256]{2,1,0:T(8,128)(2,1)S(1)} %get-tuple-element.50), channel_id=1, source_target_pairs={{0,64},{32,96},{64,0},{96,32},{1,65},{33,97},{65,1},{97,33},{2,66}... | collective-permute-start | bytes 1376264 | tf_op jit(solution)/shard_map/ppermute | solution.py:341
  98.8 2.0 %shard_map.90 = bf16[16,2,8,256]{3,2,1,0:T(8,128)(2,1)S(1)} custom-call(s32[1]{0:T(128)} %bitcast.core_ref, bf16[4,16,16,256]{3,2,1,0:T(8,128)(2,1)S(1)} %get-tuple-element.46.block, bf16[2,16,16,256]{3,2,1,0:T(8,128)(2,1)S(1)} %collective-permute-done.5.later, bf16[4,16,16,256]{3,2,1,0:T(8,128)(2,1)S(1)} %get-tuple-element.38.block.grad_sum, ...), custom_call_target="tpu_custom_call" | custom-call | flops 939524096 | bytes 4980740 | tf_op jit(solution)/shard_map/pallas_call | solution.py:323
  100.8 14.6 %collective-permute-done.8 = bf16[16,56,256]{2,1,0:T(8,128)(2,1)S(1)} collective-permute-done((bf16[16,56,256]{2,1,0:T(8,128)(2,1)S(1)}, bf16[16,56,256]{2,1,0:T(8,128)(2,1)S(1)}, u32[]{:S(2)}, u32[]{:S(2)}) %collective-permute-start.8) | collective-permute-done | bytes 458784 | tf_op jit(solution)/shard_map/ppermute | solution.py:341
  115.4 3.4 %collective-permute-done.7 = bf16[16,56,256]{2,1,0:T(8,128)(2,1)S(1)} collective-permute-done((bf16[16,56,256]{2,1,0:T(8,128)(2,1)S(1)}, bf16[16,56,256]{2,1,0:T(8,128)(2,1)S(1)}, u32[]{:S(2)}, u32[]{:S(2)}) %collective-permute-start.7) | collective-permute-done | bytes 458784 | tf_op jit(solution)/shard_map/ppermute | solution.py:341
  119.0 4.2 %all-to-all-done.2 = bf16[64,88,256]{2,1,0:T(8,128)(2,1)} async-done(((bf16[64,88,256]{2,1,0:T(8,128)(2,1)}), bf16[64,88,256]{2,1,0:T(8,128)(2,1)}, u32[]{:S(2)}, u32[]{:S(2)}) %all-to-all-start.2) | async-done | bytes 2883616 | tf_op jit(solution)/shard_map/all_to_all | solution.py:412
  124.0 4.5 %all-to-all-start.3 = ((bf16[16,72,256]{2,1,0:T(8,128)(2,1)}), bf16[16,72,256]{2,1,0:T(8,128)(2,1)S(1)}, u32[]{:S(2)}, u32[]{:S(2)}) async-start(bf16[16,72,256]{2,1,0:T(8,128)(2,1)} %pad_maximum_fusion), calls=%async_computation.3 | async-start | bytes 1179648 | tf_op jit(solution)/shard_map/all_to_all | solution.py:442
  128.5 2.2 %convert_reduce_fusion = f32[4,88,256]{2,1,0:T(8,128)S(1)} fusion(bf16[16,4,88,256]{3,2,1,0:T(8,128)(2,1)} %bitcast.21), kind=kLoop, calls=%fused_computation | loop fusion | flops 2793472 | bytes 3244032 | tf_op jit(solution)/shard_map/reduce_sum | solution.py:436
  130.8 3.4 %collective-permute-start.11 = (bf16[88,256]{1,0:T(8,128)(2,1)S(1)}, bf16[88,256]{1,0:T(8,128)(2,1)S(1)}, u32[]{:S(2)}, u32[]{:S(2)}) collective-permute-start(bf16[88,256]{1,0:T(8,128)(2,1)S(1)} %get-tuple-element.59), channel_id=1, source_target_pairs={{0,96},{32,0},{64,32},{96,64},{1,97},{33,1},{65,33},{97,65},{2,98}... | collective-permute-start | bytes 135176 | tf_op jit(solution)/shard_map/ppermute | solution.py:341
  134.3 2.2 %collective-permute-start.9 = (bf16[88,256]{1,0:T(8,128)(2,1)S(1)}, bf16[88,256]{1,0:T(8,128)(2,1)S(1)}, u32[]{:S(2)}, u32[]{:S(2)}) collective-permute-start(bf16[88,256]{1,0:T(8,128)(2,1)S(1)} %get-tuple-element.58), channel_id=1, source_target_pairs={{0,64},{32,96},{64,0},{96,32},{1,65},{33,97},{65,1},{97,33},{2,66}... | collective-permute-start | bytes 135176 | tf_op jit(solution)/shard_map/ppermute | solution.py:341
  136.5 3.5 %collective-permute-done.10 = bf16[88,256]{1,0:T(8,128)(2,1)S(1)} collective-permute-done((bf16[88,256]{1,0:T(8,128)(2,1)S(1)}, bf16[88,256]{1,0:T(8,128)(2,1)S(1)}, u32[]{:S(2)}, u32[]{:S(2)}) %collective-permute-start.10) | collective-permute-done | bytes 45088 | tf_op jit(solution)/shard_map/ppermute | solution.py:341
  (70 shorter events, 20.8 us)
Async XLA Ops:
  0.6 8.8 %collective-permute-start = (bf16[2,128,256]{2,1,0:T(8,128)(2,1)}, bf16[2,128,256]{2,1,0:T(8,128)(2,1)S(1)}, u32[]{:S(2)}, u32[]{:S(2)}) collective-permute-start(bf16[2,128,256]{2,1,0:T(8,128)(2,1)} %bitcast.49), channel_id=1, source_target_pairs={{0,32},{32,64},{64,96},{1,33},{33,65},{65,97},{2,34},{34,66},{66,9... | collective-permute-start | bytes 393224 | tf_op jit(solution)/shard_map/ppermute | solution.py:337
  5.5 4.0 %collective-permute-start.1 = (bf16[2,4,4,512]{3,2,1,0:T(4,128)(2,1)S(1)}, bf16[2,4,4,512]{3,2,1,0:T(4,128)(2,1)S(1)}, u32[]{:S(2)}, u32[]{:S(2)}) collective-permute-start(bf16[2,4,4,512]{3,2,1,0:T(4,128)(2,1)S(1)} %slice_select_fusion), channel_id=1, source_target_pairs={{0,1},{1,0},{2,3},{3,2},{4,5},{5,4},{6,7},{7,6},{8,9},{9,8},{10,11... | collective-permute-start | bytes 98312 | tf_op jit(solution)/shard_map/ppermute | solution.py:364
  11.4 18.0 %all-to-all-start = ((bf16[16,4,16,256]{3,2,1,0:T(8,128)(2,1)}), bf16[16,4,16,256]{3,2,1,0:T(8,128)(2,1)S(1)}, u32[]{:S(2)}, u32[]{:S(2)}) async-start(bf16[16,4,16,256]{3,2,1,0:T(8,128)(2,1)} %bitcast.7), calls=%async_computation | async-start | bytes 1048576 | tf_op jit(solution)/shard_map/all_to_all | solution.py:371
  29.4 4.7 %collective-permute-start.2 = (bf16[16,4,16,256]{3,2,1,0:T(8,128)(2,1)S(1)}, bf16[16,4,16,256]{3,2,1,0:T(8,128)(2,1)S(1)}, u32[]{:S(2)}, u32[]{:S(2)}) collective-permute-start(bf16[16,4,16,256]{3,2,1,0:T(8,128)(2,1)S(1)} %all-to-all-done.mine), channel_id=1, source_target_pairs={{0,16},{16,0},{1,17},{17,1},{2,18},{18,2},{3,19},{19,3},{4,20},{20... | collective-permute-start | bytes 1572872 | tf_op jit(solution)/shard_map/ppermute | solution.py:379
  30.5 21.7 %all-to-all-start.1 = ((bf16[8,2,4,16,512]{4,3,2,1,0:T(8,128)(2,1)}), bf16[8,2,4,16,512]{4,3,2,1,0:T(8,128)(2,1)S(1)}, u32[]{:S(2)}, u32[]{:S(2)}) async-start(bf16[8,2,4,16,512]{4,3,2,1,0:T(8,128)(2,1)} %copy.14), calls=%async_computation.1 | async-start | bytes 2097152 | tf_op jit(solution)/shard_map/all_to_all | solution.py:380
  34.1 14.1 %copy-start.5 = (bf16[16,4,16,256]{3,2,1,0:T(8,128)(2,1)}, bf16[16,4,16,256]{3,2,1,0:T(8,128)(2,1)S(1)}, u32[]{:S(2)}) copy-start(bf16[16,4,16,256]{3,2,1,0:T(8,128)(2,1)S(1)} %collective-permute-done.2.other) | copy-start | bytes 1572868
  52.2 2.7 %collective-permute-start.3 = (bf16[8,2,2,2,16,512]{5,4,3,2,1,0:T(8,128)(2,1)S(1)}, bf16[8,2,2,2,16,512]{5,4,3,2,1,0:T(8,128)(2,1)S(1)}, u32[]{:S(2)}, u32[]{:S(2)}) collective-permute-start(bf16[8,2,2,2,16,512]{5,4,3,2,1,0:T(8,128)(2,1)S(1)} %bitcast.42), channel_id=1, source_target_pairs={{0,16},{16,0},{1,17},{17,1},{2,18},{18,2},{3,19},{19,3},{4,20},{20... | collective-permute-start | bytes 3145736 | tf_op jit(solution)/shard_map/ppermute | solution.py:390
  54.9 1.6 %copy-start.4 = (bf16[4,4,256,256]{3,2,1,0:T(8,128)(2,1)S(1)}, bf16[4,4,256,256]{3,2,1,0:T(8,128)(2,1)}, u32[]{:S(2)}) copy-start(bf16[4,4,256,256]{3,2,1,0:T(8,128)(2,1)} %weights.3) | copy-start | bytes 6291460
  57.5 5.1 %copy-start.2 = (bf16[4,16,16,256]{3,2,1,0:T(8,128)(2,1)S(1)}, bf16[4,16,16,256]{3,2,1,0:T(8,128)(2,1)}, u32[]{:S(2)}) copy-start(bf16[4,16,16,256]{3,2,1,0:T(8,128)(2,1)} %copy-done.1) | copy-start | bytes 1572868
  60.9 3.4 %copy-start.10 = (bf16[6,16,16,256]{3,2,1,0:T(8,128)(2,1)S(1)}, bf16[6,16,16,256]{3,2,1,0:T(8,128)(2,1)}, u32[]{:S(2)}) copy-start(bf16[6,16,16,256]{3,2,1,0:T(8,128)(2,1)} %copy-done.9) | copy-start | bytes 2359300
  60.9 10.8 %collective-permute-start.4 = (bf16[2,16,16,256]{3,2,1,0:T(8,128)(2,1)S(1)}, bf16[2,16,16,256]{3,2,1,0:T(8,128)(2,1)S(1)}, u32[]{:S(2)}, u32[]{:S(2)}) collective-permute-start(bf16[2,16,16,256]{3,2,1,0:T(8,128)(2,1)S(1)} %get-tuple-element.41), channel_id=1, source_target_pairs={{32,0},{64,32},{96,64},{33,1},{65,33},{97,65},{34,2},{66,34},{98,6... | collective-permute-start | bytes 786440 | tf_op jit(solution)/shard_map/ppermute | solution.py:337
  71.8 6.8 %copy-start.12 = (bf16[4,16,16,256]{3,2,1,0:T(8,128)(2,1)S(1)}, bf16[4,16,16,256]{3,2,1,0:T(8,128)(2,1)}, u32[]{:S(2)}) copy-start(bf16[4,16,16,256]{3,2,1,0:T(8,128)(2,1)} %copy-done.11) | copy-start | bytes 1572868
  71.8 51.4 %all-to-all-start.2 = ((bf16[64,88,256]{2,1,0:T(8,128)(2,1)}), bf16[64,88,256]{2,1,0:T(8,128)(2,1)}, u32[]{:S(2)}, u32[]{:S(2)}) async-start(bf16[64,88,256]{2,1,0:T(8,128)(2,1)} %shard_map.87), calls=%async_computation.2 | async-start | bytes 5767168 | tf_op jit(solution)/shard_map/all_to_all | solution.py:412
  78.5 2.0 %copy-start.3 = (bf16[3,3,3,256,256]{4,3,2,1,0:T(8,128)(2,1)S(1)}, bf16[3,3,3,256,256]{4,3,2,1,0:T(8,128)(2,1)}, u32[]{:S(2)}) copy-start(bf16[3,3,3,256,256]{4,3,2,1,0:T(8,128)(2,1)} %weights.4) | copy-start | bytes 10616836
  80.5 4.8 %copy-start.6 = (bf16[16,4,16,256]{3,2,1,0:T(8,128)(2,1)S(1)}, bf16[16,4,16,256]{3,2,1,0:T(8,128)(2,1)}, u32[]{:S(2)}) copy-start(bf16[16,4,16,256]{3,2,1,0:T(8,128)(2,1)} %copy-done.5) | copy-start | bytes 1572868
  85.3 13.4 %copy-start = (bf16[3,3,3,256,256]{4,3,2,1,0:T(8,128)(2,1)S(1)}, bf16[3,3,3,256,256]{4,3,2,1,0:T(8,128)(2,1)}, u32[]{:S(2)}) copy-start(bf16[3,3,3,256,256]{4,3,2,1,0:T(8,128)(2,1)} %weights.5) | copy-start | bytes 10616836
  91.4 24.0 %collective-permute-start.8 = (bf16[16,56,256]{2,1,0:T(8,128)(2,1)S(1)}, bf16[16,56,256]{2,1,0:T(8,128)(2,1)S(1)}, u32[]{:S(2)}, u32[]{:S(2)}) collective-permute-start(bf16[16,56,256]{2,1,0:T(8,128)(2,1)S(1)} %get-tuple-element.52), channel_id=1, source_target_pairs={{0,96},{32,0},{64,32},{96,64},{1,97},{33,1},{65,33},{97,65},{2,98}... | collective-permute-start | bytes 1376264 | tf_op jit(solution)/shard_map/ppermute | solution.py:341
  95.9 22.8 %collective-permute-start.7 = (bf16[16,56,256]{2,1,0:T(8,128)(2,1)S(1)}, bf16[16,56,256]{2,1,0:T(8,128)(2,1)S(1)}, u32[]{:S(2)}, u32[]{:S(2)}) collective-permute-start(bf16[16,56,256]{2,1,0:T(8,128)(2,1)S(1)} %get-tuple-element.51), channel_id=1, source_target_pairs={{0,32},{32,64},{64,96},{96,0},{1,33},{33,65},{65,97},{97,1},{2,34}... | collective-permute-start | bytes 1376264 | tf_op jit(solution)/shard_map/ppermute | solution.py:341
  95.9 22.8 %collective-permute-start.6 = (bf16[16,56,256]{2,1,0:T(8,128)(2,1)S(1)}, bf16[16,56,256]{2,1,0:T(8,128)(2,1)S(1)}, u32[]{:S(2)}, u32[]{:S(2)}) collective-permute-start(bf16[16,56,256]{2,1,0:T(8,128)(2,1)S(1)} %get-tuple-element.50), channel_id=1, source_target_pairs={{0,64},{32,96},{64,0},{96,32},{1,65},{33,97},{65,1},{97,33},{2,66}... | collective-permute-start | bytes 1376264 | tf_op jit(solution)/shard_map/ppermute | solution.py:341
  98.1 0.7 collective-permute-start.5
  124.0 17.3 %all-to-all-start.3 = ((bf16[16,72,256]{2,1,0:T(8,128)(2,1)}), bf16[16,72,256]{2,1,0:T(8,128)(2,1)S(1)}, u32[]{:S(2)}, u32[]{:S(2)}) async-start(bf16[16,72,256]{2,1,0:T(8,128)(2,1)} %pad_maximum_fusion), calls=%async_computation.3 | async-start | bytes 1179648 | tf_op jit(solution)/shard_map/all_to_all | solution.py:442
  130.8 5.6 %collective-permute-start.11 = (bf16[88,256]{1,0:T(8,128)(2,1)S(1)}, bf16[88,256]{1,0:T(8,128)(2,1)S(1)}, u32[]{:S(2)}, u32[]{:S(2)}) collective-permute-start(bf16[88,256]{1,0:T(8,128)(2,1)S(1)} %get-tuple-element.59), channel_id=1, source_target_pairs={{0,96},{32,0},{64,32},{96,64},{1,97},{33,1},{65,33},{97,65},{2,98}... | collective-permute-start | bytes 135176 | tf_op jit(solution)/shard_map/ppermute | solution.py:341
  134.3 5.7 %collective-permute-start.10 = (bf16[88,256]{1,0:T(8,128)(2,1)S(1)}, bf16[88,256]{1,0:T(8,128)(2,1)S(1)}, u32[]{:S(2)}, u32[]{:S(2)}) collective-permute-start(bf16[88,256]{1,0:T(8,128)(2,1)S(1)} %get-tuple-element.60), channel_id=1, source_target_pairs={{0,32},{32,64},{64,96},{96,0},{1,33},{33,65},{65,97},{97,1},{2,34}... | collective-permute-start | bytes 135176 | tf_op jit(solution)/shard_map/ppermute | solution.py:341
  134.3 5.7 %collective-permute-start.9 = (bf16[88,256]{1,0:T(8,128)(2,1)S(1)}, bf16[88,256]{1,0:T(8,128)(2,1)S(1)}, u32[]{:S(2)}, u32[]{:S(2)}) collective-permute-start(bf16[88,256]{1,0:T(8,128)(2,1)S(1)} %get-tuple-element.58), channel_id=1, source_target_pairs={{0,64},{32,96},{64,0},{96,32},{1,65},{33,97},{65,1},{97,33},{2,66}... | collective-permute-start | bytes 135176 | tf_op jit(solution)/shard_map/ppermute | solution.py:341
  (5 other events, 4.4 us)

commit v11 on v9

--- a/solution.py
+++ b/solution.py
@@ -86,7 +86,7 @@
     return total[frame * rows : (frame + 1) * rows].reshape(ROWS, columns, CH)
 
 
-def forward_kernel(core_ref, mine, other, first, second, mask, act, slope, summed, up_act, table, total):
+def forward_kernel(core_ref, mine, other, mine_before, other_before, first, second, mask, act, slope, summed, up_act, table, total):
     step = pl.program_id(0)
     core = core_ref[0]
     sources = ((mine, core), (other, 1 - core))
@@ -95,9 +95,11 @@
     def _():
         clear_border(table)
         for source, which in sources:
-            for frame in range(FR):
-                slot = 2 * which + (frame if frame < 2 else frame + 2)
-                fill_table(table, slot, source[:, frame], True)
+            for frame in range(2):
+                fill_table(table, 4 + 2 * which + frame, source[:, frame], True)
+        for source, which in ((mine_before, core), (other_before, 1 - core)):
+            for frame in range(2):
+                fill_table(table, 2 * which + frame, source[:, frame], True)
         total[...] = jnp.zeros_like(total)
 
     @pl.when(step < 3)
@@ -127,7 +129,7 @@
             for frame in range(2):
                 place = 2 * which + frame
                 values = total[pl.ds(pl.multiple_of(place * rows, rows), rows)].reshape(ROWS, WIN, CH)
-                values = values + source[:, 2 + frame].astype(F32)
+                values = values + source[:, frame].astype(F32)
                 summed[place] = values
                 up_act[place] = (values * jax.nn.sigmoid(values)).astype(BF16)
 
@@ -277,14 +279,14 @@
             out[chunk, UP_ROWS:] = piece_of(sums, 2 * group + place[0], member).astype(BF16)
 
 
-def first_grad_kernel(place, mine, other, block, own, next_one, next_two, next_three, table, flipped, sums):
+def first_grad_kernel(place, mine, other, mine_before, other_before, block, own, next_one, next_two, next_three, table, flipped, sums):
     core = place[0]
     frames = []
     for frame in range(2):
-        before = jnp.where(core == 1, mine[:, frame].astype(F32), other[:, frame].astype(F32))
+        before = jnp.where(core == 1, mine_before[:, frame].astype(F32), other_before[:, frame].astype(F32))
         frames.append((frame, before))
-        frames.append((2 + 2 * core + frame, mine[:, 2 + frame]))
-        frames.append((4 - 2 * core + frame, other[:, 2 + frame]))
+        frames.append((2 + 2 * core + frame, mine[:, frame]))
+        frames.append((4 - 2 * core + frame, other[:, frame]))
     tap_sums(frames, block, table, flipped, sums)
     for step, out in enumerate((own, next_one, next_two, next_three)):
         group = lax.rem(place[1] + step, 4)
@@ -352,11 +354,10 @@
     edge = jnp.where(width == 0, paired[:, :, 64 - EDGE :], paired[:, :, :EDGE])
     edge = lax.ppermute(edge, "width", [(0, 1), (1, 0)])
     frames = features[:, 0]
-    before, edge = lax.optimization_barrier((shift(frames, "y", 1), edge))
-    frames = jnp.concatenate([before, frames], axis=0)
-    padded = jnp.pad(frames, ((0, 0), (EDGE, EDGE), (0, 0))).reshape(4, 17, OWN, CH)
+    padded = jnp.pad(frames, ((0, 0), (EDGE, EDGE), (0, 0))).reshape(2, 17, OWN, CH)
     windows = jnp.concatenate([padded[:, :-1], padded[:, 1:]], axis=2)
-    windows = windows.reshape(4, 2, 8, WIN, CH).transpose(2, 1, 0, 3, 4).reshape(16, 4, WIN, CH)
+    windows = windows.reshape(2, 2, 8, WIN, CH).transpose(2, 1, 0, 3, 4).reshape(16, 2, WIN, CH)
+    windows, edge = lax.optimization_barrier((windows, edge))
     block = lax.all_to_all(windows, ("z", "x_hi", "width"), 0, 0, tiled=True)
 
     nothing = jnp.zeros_like(edge)
@@ -365,12 +366,16 @@
     fine = jnp.concatenate([paired[:, :, :-1], paired[:, :, 1:]], axis=3).transpose(2, 0, 1, 3, 4)
     fine, block = lax.optimization_barrier((fine, block))
     swap = [(0, 1), (1, 0)]
+    before = shift(block, "y", 1)
     other_block = lax.ppermute(block, "core", swap)
+    crossed = [(2 * i + j, 2 * i + 3 - j) for i in range(3) for j in range(2)]
+    other_before = lax.ppermute(block, ("y", "core"), crossed)
+    blocks_in = (block, other_block, before, other_before)
     mine = lax.all_to_all(fine, ("z", "x_hi"), 0, 0, tiled=True).reshape(8, 2, 2, 2, WIN, 2 * CH)
 
     first_act, first_slope, summed, up_act = call(
-        forward_kernel, (6,), (core_arg, block, other_block, conv_first, conv_second, mask),
-        [SMEM, whole(block.shape), whole(block.shape), tap_weights(0), tap_weights(3), whole(mask.shape)],
+        forward_kernel, (6,), (core_arg, *blocks_in, conv_first, conv_second, mask),
+        [SMEM, *[whole(block.shape)] * 4, tap_weights(0), tap_weights(3), whole(mask.shape)],
         [(six_frames, BF16), (act_shape, F32), (act_shape, F32), (act_shape, BF16)],
         [pltpu.VMEM((FR + 4, ROWS + 2, WIN, 3 * CH), BF16), pltpu.VMEM(((FR + 2) * ROWS * WIN, CH), F32)],
         67 * tap_flops,
@@ -405,10 +410,10 @@
         [whole(act_shape), whole(later.shape), whole(act_shape), tap_weights(), whole(mask.shape)],
         [(act_shape, BF16), (two_frames, BF16)], [table, total], 27 * tap_flops,
     )
-    later_hidden = shift(hidden_head, "y", -1)
+    later_hidden = lax.ppermute(hidden_head, ("y", "core"), [(2 * i + 1, 2 * i - 1) for i in range(1, 4)])
     blocks = call(
-        first_grad_kernel, (), (place, block, other_block, grad_hidden),
-        [SMEM, whole(block.shape), whole(block.shape), whole(act_shape)],
+        first_grad_kernel, (), (place, *blocks_in, grad_hidden),
+        [SMEM, *[whole(block.shape)] * 4, whole(act_shape)],
         [((16, PIECE, CH), BF16)] * 4, grad_scratch, 27 * tap_flops,
     )
     arrived = [blocks[0]]

time: 143 us -> 146 us (1.021)
  waiting for transfers between devices: 41 us -> 43 us
  local copies, waits for them, and re-layouts: 14.4 us -> 16.1 us
    ppermute x3 -> x2, waiting for transfers between devices: 21.3 us -> 1.32 us  [shift(): lax.ppermute(value, axis, [(i, i + step) for i in range(count) if 0 <= i...]
    ppermute x6, waiting for transfers between devices: 3.08 us -> 22.3 us  [over_y(): return lax.ppermute(value, 'y', [(i, (i + step) % 4) for i in range(4)])]
    ppermute x0 -> x2, starting transfers between devices: none -> 4.2 us  [the longest x1 3.32 us: shards(): other_before = lax.ppermute(block, ('y', 'core'), crossed)]
    ppermute x0 -> x2, waiting for transfers between devices: none -> 3.8 us  [the longest x1 3.79 us: shards(): other_before = lax.ppermute(block, ('y', 'core'), crossed)]
    all_to_all x1, waiting for transfers between devices: 1.31 us -> 4.1 us  [shards(): early = lax.all_to_all(early, ('z', 'x_hi', 'width'), 0, 0, tiled=True)]
    all_to_all x1, starting transfers between devices: 6.82 us -> 4.47 us  [shards(): early = lax.all_to_all(early, ('z', 'x_hi', 'width'), 0, 0, tiled=True)]
    ppermute x1, waiting for transfers between devices: 2.42 us -> 0.61 us  [shards(): edge = lax.ppermute(edge, 'width', [(0, 1), (1, 0)])]
    ppermute x3 -> x2, starting transfers between devices: 6.68 us -> 5.09 us  [shift(): lax.ppermute(value, axis, [(i, i + step) for i in range(count) if 0 <= i...]
  transfers between devices with their start and end apart: 16 -> 17, of which waited for: 8 -> 9; matrix products, arithmetic and copies ran while one was open for 5% -> 5% of each run, Pallas kernels for 24% -> 23%
where the time goes in v11:
time: 146 us; the launch traced here: 145 us
  starting transfers between devices  43.5 us (30%)
  waiting for transfers between devices  43 us (29%)
  Pallas kernels  37.2 us (25%)
  local copies, waits for them, and re-layouts  16.1 us (11%)
  other arithmetic  3.95 us (3%)
    pallas_call x7, Pallas kernels, call(): pl.pallas_call(kernel, out_shape=shapes[0] if single else shapes, grid=gr...  37.2 us
    ppermute x6, waiting for transfers between devices, over_y(): return lax.ppermute(value, 'y', [(i, (i + step) % 4) for i in range(4)])  22.3 us
    ppermute x6, starting transfers between devices, over_y(): return lax.ppermute(value, 'y', [(i, (i + step) % 4) for i in range(4)])  12.2 us
    unnamed x36, local copies, waits for them, and re-layouts  10.1 us
    all_to_all x1, waiting for transfers between devices, shards(): block = lax.all_to_all(windows, ('z', 'x_hi', 'width'), 0, 0, tiled=True)  8.29 us
    all_to_all x1, starting transfers between devices, shards(): block = lax.all_to_all(windows, ('z', 'x_hi', 'width'), 0, 0, tiled=True)  7.97 us
    ppermute x2, starting transfers between devices, shift(): lax.ppermute(value, axis, [(i, i + step) for i in range(count) if 0 <= i...  5.09 us
    all_to_all x1, starting transfers between devices, shards(): early = lax.all_to_all(early, ('z', 'x_hi', 'width'), 0, 0, tiled=True)  4.47 us
  transfers between devices with their start and end apart: 17, of which 9 were waited for; matrix products, arithmetic and copies ran while one was open for 5% of the time, Pallas kernels for 23%

profile of v11, /device:TPU:0, one launch (start us, length us, event | category | flops | bytes accessed | tf_op | source)
XLA Modules:
  0.0 144.9 jit_solution(9667818779039872008)
XLA Ops:
  5.9 8.0 %all-to-all-start = ((bf16[16,2,16,256]{3,2,1,0:T(8,128)(2,1)}), bf16[16,2,16,256]{3,2,1,0:T(8,128)(2,1)S(1)}, u32[]{:S(2)}, u32[]{:S(2)}) async-start(bf16[16,2,16,256]{3,2,1,0:T(8,128)(2,1)} %bitcast.5), calls=%async_computation | async-start | bytes 524288 | tf_op jit(solution)/shard_map/all_to_all | solution.py:361
  14.3 8.3 %all-to-all-done.mine = bf16[16,2,16,256]{3,2,1,0:T(8,128)(2,1)S(1)} async-done(((bf16[16,2,16,256]{3,2,1,0:T(8,128)(2,1)}), bf16[16,2,16,256]{3,2,1,0:T(8,128)(2,1)S(1)}, u32[]{:S(2)}, u32[]{:S(2)}) %all-to-all-start) | async-done | bytes 262176 | tf_op jit(solution)/shard_map/all_to_all | solution.py:361
  22.6 3.5 %collective-permute-start.2 = (bf16[16,2,16,256]{3,2,1,0:T(8,128)(2,1)S(1)}, bf16[16,2,16,256]{3,2,1,0:T(8,128)(2,1)S(1)}, u32[]{:S(2)}, u32[]{:S(2)}) collective-permute-start(bf16[16,2,16,256]{3,2,1,0:T(8,128)(2,1)S(1)} %all-to-all-done.mine), channel_id=1, source_target_pairs={{0,32},{32,64},{64,96},{1,33},{33,65},{65,97},{2,34},{34,66},{66,9... | collective-permute-start | bytes 786440 | tf_op jit(solution)/shard_map/ppermute | solution.py:328
  26.1 3.3 %collective-permute-start.3 = (bf16[16,2,16,256]{3,2,1,0:T(8,128)(2,1)S(1)}, bf16[16,2,16,256]{3,2,1,0:T(8,128)(2,1)S(1)}, u32[]{:S(2)}, u32[]{:S(2)}) collective-permute-start(bf16[16,2,16,256]{3,2,1,0:T(8,128)(2,1)S(1)} %all-to-all-done.mine), channel_id=1, source_target_pairs={{0,48},{16,32},{32,80},{48,64},{64,112},{80,96},{1,49},{17,33},{33... | collective-permute-start | bytes 786440 | tf_op jit(solution)/shard_map/ppermute | solution.py:372
  30.5 3.6 %all-to-all-start.1 = ((bf16[8,2,4,16,512]{4,3,2,1,0:T(8,128)(2,1)}), bf16[8,2,4,16,512]{4,3,2,1,0:T(8,128)(2,1)S(1)}, u32[]{:S(2)}, u32[]{:S(2)}) async-start(bf16[8,2,4,16,512]{4,3,2,1,0:T(8,128)(2,1)} %copy.14), calls=%async_computation.1 | async-start | bytes 2097152 | tf_op jit(solution)/shard_map/all_to_all | solution.py:374
  34.1 3.8 %collective-permute-done.3.other_before = bf16[16,2,16,256]{3,2,1,0:T(8,128)(2,1)S(1)} collective-permute-done((bf16[16,2,16,256]{3,2,1,0:T(8,128)(2,1)S(1)}, bf16[16,2,16,256]{3,2,1,0:T(8,128)(2,1)S(1)}, u32[]{:S(2)}, u32[]{:S(2)}) %collective-permute-start.3) | collective-permute-done | bytes 262176 | tf_op jit(solution)/shard_map/ppermute | solution.py:372
  38.0 13.8 %shard_map.84 = (bf16[6,16,16,256]{3,2,1,0:T(8,128)(2,1)S(1)}, f32[4,16,16,256]{3,2,1,0:T(8,128)S(1)}, f32[4,16,16,256]{3,2,1,0:T(8,128)S(1)}, bf16[4,16,16,256]{3,2,1,0:T(8,128)(2,1)S(1)}) custom-call(s32[1]{0:T(128)} %bitcast.core_ref, bf16[16,2,16,256]{3,2,1,0:T(8,128)(2,1)S(1)} %all-to-all-done.mine, ...), custom_call_target="tpu_custom_call" | custom-call | flops 8992587776 | bytes 11550724 | tf_op jit(solution)/shard_map/pallas_call | solution.py:314
  54.8 2.6 %collective-permute-done.4.other = bf16[8,2,2,2,16,512]{5,4,3,2,1,0:T(8,128)(2,1)S(1)} collective-permute-done((bf16[8,2,2,2,16,512]{5,4,3,2,1,0:T(8,128)(2,1)S(1)}, bf16[8,2,2,2,16,512]{5,4,3,2,1,0:T(8,128)(2,1)S(1)}, u32[]{:S(2)}, u32[]{:S(2)}) %collective-permute-start.4) | collective-permute-done | bytes 1048608 | tf_op jit(solution)/shard_map/ppermute | solution.py:384
  60.2 3.5 %shard_map.85 = (bf16[4,16,16,256]{3,2,1,0:T(8,128)(2,1)S(1)}, bf16[2,16,16,256]{3,2,1,0:T(8,128)(2,1)S(1)}) custom-call(s32[1]{0:T(128)} %bitcast.core_ref, bf16[8,2,2,2,16,512]{5,4,3,2,1,0:T(8,128)(2,1)S(1)} %bitcast.43, bf16[8,2,2,2,16,512]{5,4,3,2,1,0:T(8,128)(2,1)S(1)} %collective-permute-done.4.other, bf16[4,4,256,256]{3,2,1,0:T(8,128)(2,1)S(1)} %copy-done.2, ...), custom_call_target="tpu_custom_call" | custom-call | flops 2147483648 | bytes 6045700 | tf_op jit(solution)/shard_map/pallas_call | solution.py:314
  67.1 6.4 %shard_map.87 = bf16[64,88,256]{2,1,0:T(8,128)(2,1)} custom-call(s32[2]{0:T(128)S(1)} %pad_add_fusion.place, bf16[6,16,16,256]{3,2,1,0:T(8,128)(2,1)S(1)} %copy-done.16, bf16[4,16,16,256]{3,2,1,0:T(8,128)(2,1)S(1)} %get-tuple-element.38.block.grad_sum, bf16[64,32,256]{2,1,0:T(8,128)(2,1)S(1)} %shard_map.86.up), custom_call_target="tpu_custom_call" | custom-call | flops 3623878656 | bytes 5242888 | tf_op jit(solution)/shard_map/pallas_call | solution.py:314
  75.6 4.5 %all-to-all-start.2 = ((bf16[64,88,256]{2,1,0:T(8,128)(2,1)}), bf16[64,88,256]{2,1,0:T(8,128)(2,1)}, u32[]{:S(2)}, u32[]{:S(2)}) async-start(bf16[64,88,256]{2,1,0:T(8,128)(2,1)} %shard_map.87), calls=%async_computation.2 | async-start | bytes 5767168 | tf_op jit(solution)/shard_map/all_to_all | solution.py:406
  80.1 2.0 %copy-done.1 = bf16[3,3,3,256,256]{4,3,2,1,0:T(8,128)(2,1)S(1)} copy-done((bf16[3,3,3,256,256]{4,3,2,1,0:T(8,128)(2,1)S(1)}, bf16[3,3,3,256,256]{4,3,2,1,0:T(8,128)(2,1)}, u32[]{:S(2)}) %copy-start.1) | copy-done | bytes 3538968
  83.0 4.8 %shard_map.88 = (bf16[4,16,16,256]{3,2,1,0:T(8,128)(2,1)S(1)}, bf16[2,16,16,256]{3,2,1,0:T(8,128)(2,1)S(1)}) custom-call(bf16[4,16,16,256]{3,2,1,0:T(8,128)(2,1)S(1)} %get-tuple-element.38.block.grad_sum, bf16[2,16,16,256]{3,2,1,0:T(8,128)(2,1)S(1)} %copy-done.10, f32[4,16,16,256]{3,2,1,0:T(8,128)S(1)} %copy-done.14, ...), custom_call_target="tpu_custom_call" | custom-call | flops 3623878656 | bytes 6176768 | tf_op jit(solution)/shard_map/pallas_call | solution.py:314
  87.9 4.9 %shard_map.89 = (bf16[16,56,256]{2,1,0:T(8,128)(2,1)S(1)}, bf16[16,56,256]{2,1,0:T(8,128)(2,1)S(1)}, bf16[16,56,256]{2,1,0:T(8,128)(2,1)S(1)}, bf16[16,56,256]{2,1,0:T(8,128)(2,1)S(1)}) custom-call(s32[2]{0:T(128)S(1)} %pad_add_fusion.place, bf16[16,2,16,256]{3,2,1,0:T(8,128)(2,1)S(1)} %all-to-all-done.mine, bf16[16,2,16,256]{3,2,1,0:T(8,128)(2,1)S(1)} %copy-done.4, ...), custom_call_target="tpu_custom_call" | custom-call | flops 3623878656 | bytes 3407880 | tf_op jit(solution)/shard_map/pallas_call | solution.py:314
  92.8 3.8 %collective-permute-start.9 = (bf16[16,56,256]{2,1,0:T(8,128)(2,1)S(1)}, bf16[16,56,256]{2,1,0:T(8,128)(2,1)S(1)}, u32[]{:S(2)}, u32[]{:S(2)}) collective-permute-start(bf16[16,56,256]{2,1,0:T(8,128)(2,1)S(1)} %get-tuple-element.52), channel_id=1, source_target_pairs={{0,96},{32,0},{64,32},{96,64},{1,97},{33,1},{65,33},{97,65},{2,98}... | collective-permute-start | bytes 1376264 | tf_op jit(solution)/shard_map/ppermute | solution.py:332
  96.6 1.9 %collective-permute-start.7 = (bf16[16,56,256]{2,1,0:T(8,128)(2,1)S(1)}, bf16[16,56,256]{2,1,0:T(8,128)(2,1)S(1)}, u32[]{:S(2)}, u32[]{:S(2)}) collective-permute-start(bf16[16,56,256]{2,1,0:T(8,128)(2,1)S(1)} %get-tuple-element.50), channel_id=1, source_target_pairs={{0,64},{32,96},{64,0},{96,32},{1,65},{33,97},{65,1},{97,33},{2,66}... | collective-permute-start | bytes 1376264 | tf_op jit(solution)/shard_map/ppermute | solution.py:332
  99.4 2.0 %shard_map.90 = bf16[16,2,8,256]{3,2,1,0:T(8,128)(2,1)S(1)} custom-call(s32[1]{0:T(128)} %bitcast.core_ref, bf16[4,16,16,256]{3,2,1,0:T(8,128)(2,1)S(1)} %get-tuple-element.46.block, bf16[2,16,16,256]{3,2,1,0:T(8,128)(2,1)S(1)} %collective-permute-done.6.later, bf16[4,16,16,256]{3,2,1,0:T(8,128)(2,1)S(1)} %get-tuple-element.38.block.grad_sum, ...), custom_call_target="tpu_custom_call" | custom-call | flops 939524096 | bytes 4980740 | tf_op jit(solution)/shard_map/pallas_call | solution.py:314
  101.4 15.1 %collective-permute-done.9 = bf16[16,56,256]{2,1,0:T(8,128)(2,1)S(1)} collective-permute-done((bf16[16,56,256]{2,1,0:T(8,128)(2,1)S(1)}, bf16[16,56,256]{2,1,0:T(8,128)(2,1)S(1)}, u32[]{:S(2)}, u32[]{:S(2)}) %collective-permute-start.9) | collective-permute-done | bytes 458784 | tf_op jit(solution)/shard_map/ppermute | solution.py:332
  116.5 3.4 %collective-permute-done.8 = bf16[16,56,256]{2,1,0:T(8,128)(2,1)S(1)} collective-permute-done((bf16[16,56,256]{2,1,0:T(8,128)(2,1)S(1)}, bf16[16,56,256]{2,1,0:T(8,128)(2,1)S(1)}, u32[]{:S(2)}, u32[]{:S(2)}) %collective-permute-start.8) | collective-permute-done | bytes 458784 | tf_op jit(solution)/shard_map/ppermute | solution.py:332
  120.2 4.1 %all-to-all-done.2 = bf16[64,88,256]{2,1,0:T(8,128)(2,1)} async-done(((bf16[64,88,256]{2,1,0:T(8,128)(2,1)}), bf16[64,88,256]{2,1,0:T(8,128)(2,1)}, u32[]{:S(2)}, u32[]{:S(2)}) %all-to-all-start.2) | async-done | bytes 2883616 | tf_op jit(solution)/shard_map/all_to_all | solution.py:406
  125.1 4.3 %all-to-all-start.3 = ((bf16[16,72,256]{2,1,0:T(8,128)(2,1)}), bf16[16,72,256]{2,1,0:T(8,128)(2,1)S(1)}, u32[]{:S(2)}, u32[]{:S(2)}) async-start(bf16[16,72,256]{2,1,0:T(8,128)(2,1)} %pad_maximum_fusion), calls=%async_computation.3 | async-start | bytes 1179648 | tf_op jit(solution)/shard_map/all_to_all | solution.py:436
  129.5 2.2 %convert_reduce_fusion = f32[4,88,256]{2,1,0:T(8,128)S(1)} fusion(bf16[16,4,88,256]{3,2,1,0:T(8,128)(2,1)} %bitcast.21), kind=kLoop, calls=%fused_computation | loop fusion | flops 2793472 | bytes 3244032 | tf_op jit(solution)/shard_map/reduce_sum | solution.py:430
  131.8 4.6 %collective-permute-start.12 = (bf16[88,256]{1,0:T(8,128)(2,1)S(1)}, bf16[88,256]{1,0:T(8,128)(2,1)S(1)}, u32[]{:S(2)}, u32[]{:S(2)}) collective-permute-start(bf16[88,256]{1,0:T(8,128)(2,1)S(1)} %get-tuple-element.57), channel_id=1, source_target_pairs={{0,96},{32,0},{64,32},{96,64},{1,97},{33,1},{65,33},{97,65},{2,98}... | collective-permute-start | bytes 135176 | tf_op jit(solution)/shard_map/ppermute | solution.py:332
  138.3 3.9 %collective-permute-done.11 = bf16[88,256]{1,0:T(8,128)(2,1)S(1)} collective-permute-done((bf16[88,256]{1,0:T(8,128)(2,1)S(1)}, bf16[88,256]{1,0:T(8,128)(2,1)S(1)}, u32[]{:S(2)}, u32[]{:S(2)}) %collective-permute-start.11) | collective-permute-done | bytes 45088 | tf_op jit(solution)/shard_map/ppermute | solution.py:332
  (80 shorter events, 25.6 us)
Async XLA Ops:
  1.9 4.0 %collective-permute-start = (bf16[2,4,4,512]{3,2,1,0:T(4,128)(2,1)S(1)}, bf16[2,4,4,512]{3,2,1,0:T(4,128)(2,1)S(1)}, u32[]{:S(2)}, u32[]{:S(2)}) collective-permute-start(bf16[2,4,4,512]{3,2,1,0:T(4,128)(2,1)S(1)} %slice_select_fusion), channel_id=1, source_target_pairs={{0,1},{1,0},{2,3},{3,2},{4,5},{5,4},{6,7},{7,6},{8,9},{9,8},{10,11... | collective-permute-start | bytes 98312 | tf_op jit(solution)/shard_map/ppermute | solution.py:355
  5.9 16.7 %all-to-all-start = ((bf16[16,2,16,256]{3,2,1,0:T(8,128)(2,1)}), bf16[16,2,16,256]{3,2,1,0:T(8,128)(2,1)S(1)}, u32[]{:S(2)}, u32[]{:S(2)}) async-start(bf16[16,2,16,256]{3,2,1,0:T(8,128)(2,1)} %bitcast.5), calls=%async_computation | async-start | bytes 524288 | tf_op jit(solution)/shard_map/all_to_all | solution.py:361
  22.6 11.5 %collective-permute-start.1 = (bf16[16,2,16,256]{3,2,1,0:T(8,128)(2,1)S(1)}, bf16[16,2,16,256]{3,2,1,0:T(8,128)(2,1)S(1)}, u32[]{:S(2)}, u32[]{:S(2)}) collective-permute-start(bf16[16,2,16,256]{3,2,1,0:T(8,128)(2,1)S(1)} %all-to-all-done.mine), channel_id=1, source_target_pairs={{0,16},{16,0},{1,17},{17,1},{2,18},{18,2},{3,19},{19,3},{4,20},{20... | collective-permute-start | bytes 786440 | tf_op jit(solution)/shard_map/ppermute | solution.py:370
  22.6 11.5 %collective-permute-start.2 = (bf16[16,2,16,256]{3,2,1,0:T(8,128)(2,1)S(1)}, bf16[16,2,16,256]{3,2,1,0:T(8,128)(2,1)S(1)}, u32[]{:S(2)}, u32[]{:S(2)}) collective-permute-start(bf16[16,2,16,256]{3,2,1,0:T(8,128)(2,1)S(1)} %all-to-all-done.mine), channel_id=1, source_target_pairs={{0,32},{32,64},{64,96},{1,33},{33,65},{65,97},{2,34},{34,66},{66,9... | collective-permute-start | bytes 786440 | tf_op jit(solution)/shard_map/ppermute | solution.py:328
  26.1 11.8 %collective-permute-start.3 = (bf16[16,2,16,256]{3,2,1,0:T(8,128)(2,1)S(1)}, bf16[16,2,16,256]{3,2,1,0:T(8,128)(2,1)S(1)}, u32[]{:S(2)}, u32[]{:S(2)}) collective-permute-start(bf16[16,2,16,256]{3,2,1,0:T(8,128)(2,1)S(1)} %all-to-all-done.mine), channel_id=1, source_target_pairs={{0,48},{16,32},{32,80},{48,64},{64,112},{80,96},{1,49},{17,33},{33... | collective-permute-start | bytes 786440 | tf_op jit(solution)/shard_map/ppermute | solution.py:372
  30.5 24.2 %all-to-all-start.1 = ((bf16[8,2,4,16,512]{4,3,2,1,0:T(8,128)(2,1)}), bf16[8,2,4,16,512]{4,3,2,1,0:T(8,128)(2,1)S(1)}, u32[]{:S(2)}, u32[]{:S(2)}) async-start(bf16[8,2,4,16,512]{4,3,2,1,0:T(8,128)(2,1)} %copy.14), calls=%async_computation.1 | async-start | bytes 2097152 | tf_op jit(solution)/shard_map/all_to_all | solution.py:374
  34.1 17.7 %copy-start.3 = (bf16[16,2,16,256]{3,2,1,0:T(8,128)(2,1)}, bf16[16,2,16,256]{3,2,1,0:T(8,128)(2,1)S(1)}, u32[]{:S(2)}) copy-start(bf16[16,2,16,256]{3,2,1,0:T(8,128)(2,1)S(1)} %collective-permute-done.1.other) | copy-start | bytes 786436
  34.1 17.7 %copy-start.5 = (bf16[16,2,16,256]{3,2,1,0:T(8,128)(2,1)}, bf16[16,2,16,256]{3,2,1,0:T(8,128)(2,1)S(1)}, u32[]{:S(2)}) copy-start(bf16[16,2,16,256]{3,2,1,0:T(8,128)(2,1)S(1)} %collective-permute-done.2.mine_before) | copy-start | bytes 786436
  37.9 13.9 %copy-start.7 = (bf16[16,2,16,256]{3,2,1,0:T(8,128)(2,1)}, bf16[16,2,16,256]{3,2,1,0:T(8,128)(2,1)S(1)}, u32[]{:S(2)}) copy-start(bf16[16,2,16,256]{3,2,1,0:T(8,128)(2,1)S(1)} %collective-permute-done.3.other_before) | copy-start | bytes 786436
  54.7 2.7 %collective-permute-start.4 = (bf16[8,2,2,2,16,512]{5,4,3,2,1,0:T(8,128)(2,1)S(1)}, bf16[8,2,2,2,16,512]{5,4,3,2,1,0:T(8,128)(2,1)S(1)}, u32[]{:S(2)}, u32[]{:S(2)}) collective-permute-start(bf16[8,2,2,2,16,512]{5,4,3,2,1,0:T(8,128)(2,1)S(1)} %bitcast.42), channel_id=1, source_target_pairs={{0,16},{16,0},{1,17},{17,1},{2,18},{18,2},{3,19},{19,3},{4,20},{20... | collective-permute-start | bytes 3145736 | tf_op jit(solution)/shard_map/ppermute | solution.py:384
  63.7 11.1 %collective-permute-start.5 = (bf16[2,16,16,256]{3,2,1,0:T(8,128)(2,1)S(1)}, bf16[2,16,16,256]{3,2,1,0:T(8,128)(2,1)S(1)}, u32[]{:S(2)}, u32[]{:S(2)}) collective-permute-start(bf16[2,16,16,256]{3,2,1,0:T(8,128)(2,1)S(1)} %get-tuple-element.41), channel_id=1, source_target_pairs={{32,0},{64,32},{96,64},{33,1},{65,33},{97,65},{34,2},{66,34},{98,6... | collective-permute-start | bytes 786440 | tf_op jit(solution)/shard_map/ppermute | solution.py:328
  73.5 6.6 %copy-start.14 = (f32[4,16,16,256]{3,2,1,0:T(8,128)S(1)}, f32[4,16,16,256]{3,2,1,0:T(8,128)}, u32[]{:S(2)}) copy-start(f32[4,16,16,256]{3,2,1,0:T(8,128)} %copy-done.13) | copy-start | bytes 3145732
  75.6 48.7 %all-to-all-start.2 = ((bf16[64,88,256]{2,1,0:T(8,128)(2,1)}), bf16[64,88,256]{2,1,0:T(8,128)(2,1)}, u32[]{:S(2)}, u32[]{:S(2)}) async-start(bf16[64,88,256]{2,1,0:T(8,128)(2,1)} %shard_map.87), calls=%async_computation.2 | async-start | bytes 5767168 | tf_op jit(solution)/shard_map/all_to_all | solution.py:406
  83.0 4.8 %copy-start.6 = (bf16[16,2,16,256]{3,2,1,0:T(8,128)(2,1)S(1)}, bf16[16,2,16,256]{3,2,1,0:T(8,128)(2,1)}, u32[]{:S(2)}) copy-start(bf16[16,2,16,256]{3,2,1,0:T(8,128)(2,1)} %copy-done.5) | copy-start | bytes 786436
  83.0 4.8 %copy-start.8 = (bf16[16,2,16,256]{3,2,1,0:T(8,128)(2,1)S(1)}, bf16[16,2,16,256]{3,2,1,0:T(8,128)(2,1)}, u32[]{:S(2)}) copy-start(bf16[16,2,16,256]{3,2,1,0:T(8,128)(2,1)} %copy-done.7) | copy-start | bytes 786436
  87.9 11.6 %copy-start = (bf16[3,3,3,256,256]{4,3,2,1,0:T(8,128)(2,1)S(1)}, bf16[3,3,3,256,256]{4,3,2,1,0:T(8,128)(2,1)}, u32[]{:S(2)}) copy-start(bf16[3,3,3,256,256]{4,3,2,1,0:T(8,128)(2,1)} %weights.5) | copy-start | bytes 10616836
  92.8 23.7 %collective-permute-start.9 = (bf16[16,56,256]{2,1,0:T(8,128)(2,1)S(1)}, bf16[16,56,256]{2,1,0:T(8,128)(2,1)S(1)}, u32[]{:S(2)}, u32[]{:S(2)}) collective-permute-start(bf16[16,56,256]{2,1,0:T(8,128)(2,1)S(1)} %get-tuple-element.52), channel_id=1, source_target_pairs={{0,96},{32,0},{64,32},{96,64},{1,97},{33,1},{65,33},{97,65},{2,98}... | collective-permute-start | bytes 1376264 | tf_op jit(solution)/shard_map/ppermute | solution.py:332
  96.6 23.3 %collective-permute-start.8 = (bf16[16,56,256]{2,1,0:T(8,128)(2,1)S(1)}, bf16[16,56,256]{2,1,0:T(8,128)(2,1)S(1)}, u32[]{:S(2)}, u32[]{:S(2)}) collective-permute-start(bf16[16,56,256]{2,1,0:T(8,128)(2,1)S(1)} %get-tuple-element.51), channel_id=1, source_target_pairs={{0,32},{32,64},{64,96},{96,0},{1,33},{33,65},{65,97},{97,1},{2,34}... | collective-permute-start | bytes 1376264 | tf_op jit(solution)/shard_map/ppermute | solution.py:332
  96.6 23.3 %collective-permute-start.7 = (bf16[16,56,256]{2,1,0:T(8,128)(2,1)S(1)}, bf16[16,56,256]{2,1,0:T(8,128)(2,1)S(1)}, u32[]{:S(2)}, u32[]{:S(2)}) collective-permute-start(bf16[16,56,256]{2,1,0:T(8,128)(2,1)S(1)} %get-tuple-element.50), channel_id=1, source_target_pairs={{0,64},{32,96},{64,0},{96,32},{1,65},{33,97},{65,1},{97,33},{2,66}... | collective-permute-start | bytes 1376264 | tf_op jit(solution)/shard_map/ppermute | solution.py:332
  98.5 0.9 collective-permute-start.6
  125.1 18.4 %all-to-all-start.3 = ((bf16[16,72,256]{2,1,0:T(8,128)(2,1)}), bf16[16,72,256]{2,1,0:T(8,128)(2,1)S(1)}, u32[]{:S(2)}, u32[]{:S(2)}) async-start(bf16[16,72,256]{2,1,0:T(8,128)(2,1)} %pad_maximum_fusion), calls=%async_computation.3 | async-start | bytes 1179648 | tf_op jit(solution)/shard_map/all_to_all | solution.py:436
  131.8 6.5 %collective-permute-start.12 = (bf16[88,256]{1,0:T(8,128)(2,1)S(1)}, bf16[88,256]{1,0:T(8,128)(2,1)S(1)}, u32[]{:S(2)}, u32[]{:S(2)}) collective-permute-start(bf16[88,256]{1,0:T(8,128)(2,1)S(1)} %get-tuple-element.57), channel_id=1, source_target_pairs={{0,96},{32,0},{64,32},{96,64},{1,97},{33,1},{65,33},{97,65},{2,98}... | collective-permute-start | bytes 135176 | tf_op jit(solution)/shard_map/ppermute | solution.py:332
  136.4 5.7 %collective-permute-start.11 = (bf16[88,256]{1,0:T(8,128)(2,1)S(1)}, bf16[88,256]{1,0:T(8,128)(2,1)S(1)}, u32[]{:S(2)}, u32[]{:S(2)}) collective-permute-start(bf16[88,256]{1,0:T(8,128)(2,1)S(1)} %get-tuple-element.58), channel_id=1, source_target_pairs={{0,32},{32,64},{64,96},{96,0},{1,33},{33,65},{65,97},{97,1},{2,34}... | collective-permute-start | bytes 135176 | tf_op jit(solution)/shard_map/ppermute | solution.py:332
  136.4 5.7 %collective-permute-start.10 = (bf16[88,256]{1,0:T(8,128)(2,1)S(1)}, bf16[88,256]{1,0:T(8,128)(2,1)S(1)}, u32[]{:S(2)}, u32[]{:S(2)}) collective-permute-start(bf16[88,256]{1,0:T(8,128)(2,1)S(1)} %get-tuple-element.56), channel_id=1, source_target_pairs={{0,64},{32,96},{64,0},{96,32},{1,65},{33,97},{65,1},{97,33},{2,66}... | collective-permute-start | bytes 135176 | tf_op jit(solution)/shard_map/ppermute | solution.py:332
  (10 other events, 17.6 us)

commit v12 on v9

--- a/solution.py
+++ b/solution.py
@@ -405,7 +405,7 @@
         [whole(act_shape), whole(later.shape), whole(act_shape), tap_weights(), whole(mask.shape)],
         [(act_shape, BF16), (two_frames, BF16)], [table, total], 27 * tap_flops,
     )
-    later_hidden = shift(hidden_head, "y", -1)
+    later_hidden = lax.ppermute(hidden_head, ("y", "core"), [(2 * i + 1, 2 * i - 1) for i in range(1, 4)])
     blocks = call(
         first_grad_kernel, (), (place, block, other_block, grad_hidden),
         [SMEM, whole(block.shape), whole(block.shape), whole(act_shape)],
@@ -421,13 +421,13 @@
         [((ROWS, 2, OWN, CH), BF16)], [own_table, pltpu.VMEM((2 * ROWS * OWN, CH), F32)], 7 * tap_flops,
     )
 
-    tied_rows, early = lax.optimization_barrier((rows_out, early))
+    first_sum = sum(value.astype(F32) for value in arrived).astype(BF16)
+    late = jnp.concatenate([rows_out.reshape(16, 2 * OWN, CH), first_sum], axis=1)
+    late, early = lax.optimization_barrier((late, early))
     early = jnp.sum(early.reshape(16, 4, UP_ROWS + PIECE, CH).astype(F32), axis=0)
     early_total = early[0]
     for step in (2, 1, 3):
         early_total += over_y(early[step].astype(BF16), step).astype(F32)
-    first_sum = sum(value.astype(F32) for value in arrived).astype(BF16)
-    late = jnp.concatenate([tied_rows.reshape(16, 2 * OWN, CH), first_sum], axis=1)
     late = lax.all_to_all(late, ("z", "x_hi", "width"), 0, 0, tiled=True)
 
     factor = 1.0 / math.sqrt(32768)

time: 143 us -> 145 us (1.014); the launches traced: 142 us -> 143 us
    ppermute x3 -> x2, waiting for transfers between devices: 21.3 us -> 0.77 us  [shift(): lax.ppermute(value, axis, [(i, i + step) for i in range(count) if 0 <= i...]
    ppermute x6, waiting for transfers between devices: 3.08 us -> 19.3 us  [over_y(): return lax.ppermute(value, 'y', [(i, (i + step) % 4) for i in range(4)])]
    all_to_all x1, waiting for transfers between devices: 1.31 us -> 4.51 us  [shards(): early = lax.all_to_all(early, ('z', 'x_hi', 'width'), 0, 0, tiled=True)]
    ppermute x6, starting transfers between devices: 11.6 us -> 14 us  [over_y(): return lax.ppermute(value, 'y', [(i, (i + step) % 4) for i in range(4)])]
    all_to_all x1, starting transfers between devices: 5.59 us -> 3.91 us  [shards(): late = lax.all_to_all(late, ('z', 'x_hi', 'width'), 0, 0, tiled=True)]
    all_to_all x1, waiting for transfers between devices: 0.01 us -> 1.51 us  [shards(): late = lax.all_to_all(late, ('z', 'x_hi', 'width'), 0, 0, tiled=True)]
    ppermute x3 -> x2, starting transfers between devices: 6.68 us -> 5.18 us  [shift(): lax.ppermute(value, axis, [(i, i + step) for i in range(count) if 0 <= i...]
  transfers between devices with their start and end apart: 16 -> 16, of which waited for: 8 -> 12; matrix products, arithmetic and copies ran while one was open for 5% -> 4% of each run, Pallas kernels for 24% -> 24%
where the time goes in v12:
time: 145 us; the launch traced here: 143 us
  starting transfers between devices  43.8 us (30%)
  waiting for transfers between devices  41.3 us (28%)
  Pallas kernels  37.2 us (26%)
  local copies, waits for them, and re-layouts  14.4 us (10%)
  other arithmetic  4.93 us (3%)
    pallas_call x7, Pallas kernels, call(): pl.pallas_call(kernel, out_shape=shapes[0] if single else shapes, grid=gr...  37.2 us
    ppermute x6, waiting for transfers between devices, over_y(): return lax.ppermute(value, 'y', [(i, (i + step) % 4) for i in range(4)])  19.3 us
    ppermute x6, starting transfers between devices, over_y(): return lax.ppermute(value, 'y', [(i, (i + step) % 4) for i in range(4)])  14 us
    all_to_all x1, waiting for transfers between devices, shards(): block = lax.all_to_all(windows, ('z', 'x_hi', 'width'), 0, 0, tiled=True)  9.7 us
    unnamed x28, local copies, waits for them, and re-layouts  9.1 us
    all_to_all x1, starting transfers between devices, shards(): block = lax.all_to_all(windows, ('z', 'x_hi', 'width'), 0, 0, tiled=True)  7.88 us
    all_to_all x1, starting transfers between devices, shards(): early = lax.all_to_all(early, ('z', 'x_hi', 'width'), 0, 0, tiled=True)  6.82 us
    ppermute x2, starting transfers between devices, shift(): lax.ppermute(value, axis, [(i, i + step) for i in range(count) if 0 <= i...  5.18 us
  transfers between devices with their start and end apart: 16, of which 12 were waited for; matrix products, arithmetic and copies ran while one was open for 4% of the time, Pallas kernels for 24%

profile of v12, /device:TPU:0, one launch (start us, length us, event | category | flops | bytes accessed | tf_op | source)
XLA Modules:
  0.0 142.6 jit_solution(17080731437920320921)
XLA Ops:
  0.6 3.6 %collective-permute-start = (bf16[2,128,256]{2,1,0:T(8,128)(2,1)}, bf16[2,128,256]{2,1,0:T(8,128)(2,1)S(1)}, u32[]{:S(2)}, u32[]{:S(2)}) collective-permute-start(bf16[2,128,256]{2,1,0:T(8,128)(2,1)} %bitcast.49), channel_id=1, source_target_pairs={{0,32},{32,64},{64,96},{1,33},{33,65},{65,97},{2,34},{34,66},{66,9... | collective-permute-start | bytes 393224 | tf_op jit(solution)/shard_map/ppermute | solution.py:326
  7.0 2.4 %collective-permute-done.1 = bf16[2,4,4,512]{3,2,1,0:T(4,128)(2,1)S(1)} collective-permute-done((bf16[2,4,4,512]{3,2,1,0:T(4,128)(2,1)S(1)}, bf16[2,4,4,512]{3,2,1,0:T(4,128)(2,1)S(1)}, u32[]{:S(2)}, u32[]{:S(2)}) %collective-permute-start.1) | collective-permute-done | bytes 32800 | tf_op jit(solution)/shard_map/ppermute | solution.py:353
  11.4 7.9 %all-to-all-start = ((bf16[16,4,16,256]{3,2,1,0:T(8,128)(2,1)}), bf16[16,4,16,256]{3,2,1,0:T(8,128)(2,1)S(1)}, u32[]{:S(2)}, u32[]{:S(2)}) async-start(bf16[16,4,16,256]{3,2,1,0:T(8,128)(2,1)} %bitcast.7), calls=%async_computation | async-start | bytes 1048576 | tf_op jit(solution)/shard_map/all_to_all | solution.py:360
  19.7 9.7 %all-to-all-done.mine = bf16[16,4,16,256]{3,2,1,0:T(8,128)(2,1)S(1)} async-done(((bf16[16,4,16,256]{3,2,1,0:T(8,128)(2,1)}), bf16[16,4,16,256]{3,2,1,0:T(8,128)(2,1)S(1)}, u32[]{:S(2)}, u32[]{:S(2)}) %all-to-all-start) | async-done | bytes 524320 | tf_op jit(solution)/shard_map/all_to_all | solution.py:360
  30.5 3.6 %all-to-all-start.1 = ((bf16[8,2,4,16,512]{4,3,2,1,0:T(8,128)(2,1)}), bf16[8,2,4,16,512]{4,3,2,1,0:T(8,128)(2,1)S(1)}, u32[]{:S(2)}, u32[]{:S(2)}) async-start(bf16[8,2,4,16,512]{4,3,2,1,0:T(8,128)(2,1)} %copy.14), calls=%async_computation.1 | async-start | bytes 2097152 | tf_op jit(solution)/shard_map/all_to_all | solution.py:369
  34.2 13.8 %shard_map.84 = (bf16[6,16,16,256]{3,2,1,0:T(8,128)(2,1)S(1)}, f32[4,16,16,256]{3,2,1,0:T(8,128)S(1)}, f32[4,16,16,256]{3,2,1,0:T(8,128)S(1)}, bf16[4,16,16,256]{3,2,1,0:T(8,128)(2,1)S(1)}) custom-call(s32[1]{0:T(128)} %bitcast.core_ref, bf16[16,4,16,256]{3,2,1,0:T(8,128)(2,1)S(1)} %all-to-all-done.mine, ...), custom_call_target="tpu_custom_call" | custom-call | flops 8992587776 | bytes 11550724 | tf_op jit(solution)/shard_map/pallas_call | solution.py:312
  52.3 2.6 %collective-permute-done.3.other = bf16[8,2,2,2,16,512]{5,4,3,2,1,0:T(8,128)(2,1)S(1)} collective-permute-done((bf16[8,2,2,2,16,512]{5,4,3,2,1,0:T(8,128)(2,1)S(1)}, bf16[8,2,2,2,16,512]{5,4,3,2,1,0:T(8,128)(2,1)S(1)}, u32[]{:S(2)}, u32[]{:S(2)}) %collective-permute-start.3) | collective-permute-done | bytes 1048608 | tf_op jit(solution)/shard_map/ppermute | solution.py:379
  57.7 3.5 %shard_map.85 = (bf16[4,16,16,256]{3,2,1,0:T(8,128)(2,1)S(1)}, bf16[2,16,16,256]{3,2,1,0:T(8,128)(2,1)S(1)}) custom-call(s32[1]{0:T(128)} %bitcast.core_ref, bf16[8,2,2,2,16,512]{5,4,3,2,1,0:T(8,128)(2,1)S(1)} %bitcast.43, bf16[8,2,2,2,16,512]{5,4,3,2,1,0:T(8,128)(2,1)S(1)} %collective-permute-done.3.other, bf16[4,4,256,256]{3,2,1,0:T(8,128)(2,1)S(1)} %copy-done.4, ...), custom_call_target="tpu_custom_call" | custom-call | flops 2147483648 | bytes 6045700 | tf_op jit(solution)/shard_map/pallas_call | solution.py:312
  64.6 6.4 %shard_map.87 = bf16[64,88,256]{2,1,0:T(8,128)(2,1)} custom-call(s32[2]{0:T(128)S(1)} %pad_add_fusion.place, bf16[6,16,16,256]{3,2,1,0:T(8,128)(2,1)S(1)} %copy-done.12, bf16[4,16,16,256]{3,2,1,0:T(8,128)(2,1)S(1)} %get-tuple-element.38.block.grad_sum, bf16[64,32,256]{2,1,0:T(8,128)(2,1)S(1)} %shard_map.86.up), custom_call_target="tpu_custom_call" | custom-call | flops 3623878656 | bytes 5242888 | tf_op jit(solution)/shard_map/pallas_call | solution.py:312
  71.8 6.8 %all-to-all-start.2 = ((bf16[64,88,256]{2,1,0:T(8,128)(2,1)}), bf16[64,88,256]{2,1,0:T(8,128)(2,1)}, u32[]{:S(2)}, u32[]{:S(2)}) async-start(bf16[64,88,256]{2,1,0:T(8,128)(2,1)} %shard_map.87), calls=%async_computation.2 | async-start | bytes 5767168 | tf_op jit(solution)/shard_map/all_to_all | solution.py:401
  78.6 2.0 %copy-done.3 = bf16[3,3,3,256,256]{4,3,2,1,0:T(8,128)(2,1)S(1)} copy-done((bf16[3,3,3,256,256]{4,3,2,1,0:T(8,128)(2,1)S(1)}, bf16[3,3,3,256,256]{4,3,2,1,0:T(8,128)(2,1)}, u32[]{:S(2)}) %copy-start.3) | copy-done | bytes 3538968
  80.6 4.8 %shard_map.88 = (bf16[4,16,16,256]{3,2,1,0:T(8,128)(2,1)S(1)}, bf16[2,16,16,256]{3,2,1,0:T(8,128)(2,1)S(1)}) custom-call(bf16[4,16,16,256]{3,2,1,0:T(8,128)(2,1)S(1)} %get-tuple-element.38.block.grad_sum, bf16[2,16,16,256]{3,2,1,0:T(8,128)(2,1)S(1)} %collective-permute-done.4.later, f32[4,16,16,256]{3,2,1,0:T(8,128)S(1)} %copy-done.10, ...), custom_call_target="tpu_custom_call" | custom-call | flops 3623878656 | bytes 6176768 | tf_op jit(solution)/shard_map/pallas_call | solution.py:312
  85.4 4.9 %shard_map.89 = (bf16[16,56,256]{2,1,0:T(8,128)(2,1)S(1)}, bf16[16,56,256]{2,1,0:T(8,128)(2,1)S(1)}, bf16[16,56,256]{2,1,0:T(8,128)(2,1)S(1)}, bf16[16,56,256]{2,1,0:T(8,128)(2,1)S(1)}) custom-call(s32[2]{0:T(128)S(1)} %pad_add_fusion.place, bf16[16,4,16,256]{3,2,1,0:T(8,128)(2,1)S(1)} %all-to-all-done.mine, bf16[16,4,16,256]{3,2,1,0:T(8,128)(2,1)S(1)} %copy-done.6, ...), custom_call_target="tpu_custom_call" | custom-call | flops 3623878656 | bytes 3407880 | tf_op jit(solution)/shard_map/pallas_call | solution.py:312
  90.4 3.9 %collective-permute-start.6 = (bf16[16,56,256]{2,1,0:T(8,128)(2,1)S(1)}, bf16[16,56,256]{2,1,0:T(8,128)(2,1)S(1)}, u32[]{:S(2)}, u32[]{:S(2)}) collective-permute-start(bf16[16,56,256]{2,1,0:T(8,128)(2,1)S(1)} %get-tuple-element.48), channel_id=1, source_target_pairs={{0,64},{32,96},{64,0},{96,32},{1,65},{33,97},{65,1},{97,33},{2,66}... | collective-permute-start | bytes 1376264 | tf_op jit(solution)/shard_map/ppermute | solution.py:330
  95.0 2.5 %collective-permute-start.8 = (bf16[16,56,256]{2,1,0:T(8,128)(2,1)S(1)}, bf16[16,56,256]{2,1,0:T(8,128)(2,1)S(1)}, u32[]{:S(2)}, u32[]{:S(2)}) collective-permute-start(bf16[16,56,256]{2,1,0:T(8,128)(2,1)S(1)} %get-tuple-element.50), channel_id=1, source_target_pairs={{0,96},{32,0},{64,32},{96,64},{1,97},{33,1},{65,33},{97,65},{2,98}... | collective-permute-start | bytes 1376264 | tf_op jit(solution)/shard_map/ppermute | solution.py:330
  98.5 2.0 %shard_map.90 = bf16[16,2,8,256]{3,2,1,0:T(8,128)(2,1)S(1)} custom-call(s32[1]{0:T(128)} %bitcast.core_ref, bf16[4,16,16,256]{3,2,1,0:T(8,128)(2,1)S(1)} %get-tuple-element.46.block, bf16[2,16,16,256]{3,2,1,0:T(8,128)(2,1)S(1)} %collective-permute-done.5.later, bf16[4,16,16,256]{3,2,1,0:T(8,128)(2,1)S(1)} %get-tuple-element.38.block.grad_sum, ...), custom_call_target="tpu_custom_call" | custom-call | flops 939524096 | bytes 4980740 | tf_op jit(solution)/shard_map/pallas_call | solution.py:312
  100.4 5.3 %collective-permute-done.6 = bf16[16,56,256]{2,1,0:T(8,128)(2,1)S(1)} collective-permute-done((bf16[16,56,256]{2,1,0:T(8,128)(2,1)S(1)}, bf16[16,56,256]{2,1,0:T(8,128)(2,1)S(1)}, u32[]{:S(2)}, u32[]{:S(2)}) %collective-permute-start.6) | collective-permute-done | bytes 458784 | tf_op jit(solution)/shard_map/ppermute | solution.py:330
  105.7 8.8 %collective-permute-done.7 = bf16[16,56,256]{2,1,0:T(8,128)(2,1)S(1)} collective-permute-done((bf16[16,56,256]{2,1,0:T(8,128)(2,1)S(1)}, bf16[16,56,256]{2,1,0:T(8,128)(2,1)S(1)}, u32[]{:S(2)}, u32[]{:S(2)}) %collective-permute-start.7) | collective-permute-done | bytes 458784 | tf_op jit(solution)/shard_map/ppermute | solution.py:330
  117.4 4.5 %all-to-all-done.2 = bf16[64,88,256]{2,1,0:T(8,128)(2,1)} async-done(((bf16[64,88,256]{2,1,0:T(8,128)(2,1)}), bf16[64,88,256]{2,1,0:T(8,128)(2,1)}, u32[]{:S(2)}, u32[]{:S(2)}) %all-to-all-start.2) | async-done | bytes 2883616 | tf_op jit(solution)/shard_map/all_to_all | solution.py:401
  121.9 2.2 %convert_reduce_fusion = f32[4,88,256]{2,1,0:T(8,128)S(1)} fusion(bf16[16,4,88,256]{3,2,1,0:T(8,128)(2,1)} %bitcast.21), kind=kLoop, calls=%fused_computation | loop fusion | flops 2793472 | bytes 3244032 | tf_op jit(solution)/shard_map/reduce_sum | solution.py:427
  124.2 3.9 %all-to-all-start.3 = ((bf16[16,72,256]{2,1,0:T(8,128)(2,1)}), bf16[16,72,256]{2,1,0:T(8,128)(2,1)S(1)}, u32[]{:S(2)}, u32[]{:S(2)}) async-start(bf16[16,72,256]{2,1,0:T(8,128)(2,1)} %pad_maximum_fusion), calls=%async_computation.3 | async-start | bytes 1179648 | tf_op jit(solution)/shard_map/all_to_all | solution.py:431
  128.1 3.6 %collective-permute-start.10 = (bf16[88,256]{1,0:T(8,128)(2,1)S(1)}, bf16[88,256]{1,0:T(8,128)(2,1)S(1)}, u32[]{:S(2)}, u32[]{:S(2)}) collective-permute-start(bf16[88,256]{1,0:T(8,128)(2,1)S(1)} %get-tuple-element.60), channel_id=1, source_target_pairs={{0,32},{32,64},{64,96},{96,0},{1,33},{33,65},{65,97},{97,1},{2,34}... | collective-permute-start | bytes 135176 | tf_op jit(solution)/shard_map/ppermute | solution.py:330
  132.9 2.1 %collective-permute-start.9 = (bf16[88,256]{1,0:T(8,128)(2,1)S(1)}, bf16[88,256]{1,0:T(8,128)(2,1)S(1)}, u32[]{:S(2)}, u32[]{:S(2)}) collective-permute-start(bf16[88,256]{1,0:T(8,128)(2,1)S(1)} %get-tuple-element.58), channel_id=1, source_target_pairs={{0,64},{32,96},{64,0},{96,32},{1,65},{33,97},{65,1},{97,33},{2,66}... | collective-permute-start | bytes 135176 | tf_op jit(solution)/shard_map/ppermute | solution.py:330
  135.8 2.6 %collective-permute-done.9 = bf16[88,256]{1,0:T(8,128)(2,1)S(1)} collective-permute-done((bf16[88,256]{1,0:T(8,128)(2,1)S(1)}, bf16[88,256]{1,0:T(8,128)(2,1)S(1)}, u32[]{:S(2)}, u32[]{:S(2)}) %collective-permute-start.9) | collective-permute-done | bytes 45088 | tf_op jit(solution)/shard_map/ppermute | solution.py:330
  (70 shorter events, 28.1 us)
Async XLA Ops:
  0.6 8.8 %collective-permute-start = (bf16[2,128,256]{2,1,0:T(8,128)(2,1)}, bf16[2,128,256]{2,1,0:T(8,128)(2,1)S(1)}, u32[]{:S(2)}, u32[]{:S(2)}) collective-permute-start(bf16[2,128,256]{2,1,0:T(8,128)(2,1)} %bitcast.49), channel_id=1, source_target_pairs={{0,32},{32,64},{64,96},{1,33},{33,65},{65,97},{2,34},{34,66},{66,9... | collective-permute-start | bytes 393224 | tf_op jit(solution)/shard_map/ppermute | solution.py:326
  5.5 4.0 %collective-permute-start.1 = (bf16[2,4,4,512]{3,2,1,0:T(4,128)(2,1)S(1)}, bf16[2,4,4,512]{3,2,1,0:T(4,128)(2,1)S(1)}, u32[]{:S(2)}, u32[]{:S(2)}) collective-permute-start(bf16[2,4,4,512]{3,2,1,0:T(4,128)(2,1)S(1)} %slice_select_fusion), channel_id=1, source_target_pairs={{0,1},{1,0},{2,3},{3,2},{4,5},{5,4},{6,7},{7,6},{8,9},{9,8},{10,11... | collective-permute-start | bytes 98312 | tf_op jit(solution)/shard_map/ppermute | solution.py:353
  11.4 18.0 %all-to-all-start = ((bf16[16,4,16,256]{3,2,1,0:T(8,128)(2,1)}), bf16[16,4,16,256]{3,2,1,0:T(8,128)(2,1)S(1)}, u32[]{:S(2)}, u32[]{:S(2)}) async-start(bf16[16,4,16,256]{3,2,1,0:T(8,128)(2,1)} %bitcast.7), calls=%async_computation | async-start | bytes 1048576 | tf_op jit(solution)/shard_map/all_to_all | solution.py:360
  29.4 4.7 %collective-permute-start.2 = (bf16[16,4,16,256]{3,2,1,0:T(8,128)(2,1)S(1)}, bf16[16,4,16,256]{3,2,1,0:T(8,128)(2,1)S(1)}, u32[]{:S(2)}, u32[]{:S(2)}) collective-permute-start(bf16[16,4,16,256]{3,2,1,0:T(8,128)(2,1)S(1)} %all-to-all-done.mine), channel_id=1, source_target_pairs={{0,16},{16,0},{1,17},{17,1},{2,18},{18,2},{3,19},{19,3},{4,20},{20... | collective-permute-start | bytes 1572872 | tf_op jit(solution)/shard_map/ppermute | solution.py:368
  30.5 21.7 %all-to-all-start.1 = ((bf16[8,2,4,16,512]{4,3,2,1,0:T(8,128)(2,1)}), bf16[8,2,4,16,512]{4,3,2,1,0:T(8,128)(2,1)S(1)}, u32[]{:S(2)}, u32[]{:S(2)}) async-start(bf16[8,2,4,16,512]{4,3,2,1,0:T(8,128)(2,1)} %copy.14), calls=%async_computation.1 | async-start | bytes 2097152 | tf_op jit(solution)/shard_map/all_to_all | solution.py:369
  34.1 13.9 %copy-start.5 = (bf16[16,4,16,256]{3,2,1,0:T(8,128)(2,1)}, bf16[16,4,16,256]{3,2,1,0:T(8,128)(2,1)S(1)}, u32[]{:S(2)}) copy-start(bf16[16,4,16,256]{3,2,1,0:T(8,128)(2,1)S(1)} %collective-permute-done.2.other) | copy-start | bytes 1572868
  52.2 2.7 %collective-permute-start.3 = (bf16[8,2,2,2,16,512]{5,4,3,2,1,0:T(8,128)(2,1)S(1)}, bf16[8,2,2,2,16,512]{5,4,3,2,1,0:T(8,128)(2,1)S(1)}, u32[]{:S(2)}, u32[]{:S(2)}) collective-permute-start(bf16[8,2,2,2,16,512]{5,4,3,2,1,0:T(8,128)(2,1)S(1)} %bitcast.42), channel_id=1, source_target_pairs={{0,16},{16,0},{1,17},{17,1},{2,18},{18,2},{3,19},{19,3},{4,20},{20... | collective-permute-start | bytes 3145736 | tf_op jit(solution)/shard_map/ppermute | solution.py:379
  54.9 1.6 %copy-start.4 = (bf16[4,4,256,256]{3,2,1,0:T(8,128)(2,1)S(1)}, bf16[4,4,256,256]{3,2,1,0:T(8,128)(2,1)}, u32[]{:S(2)}) copy-start(bf16[4,4,256,256]{3,2,1,0:T(8,128)(2,1)} %weights.3) | copy-start | bytes 6291460
  57.7 5.2 %copy-start.2 = (bf16[4,16,16,256]{3,2,1,0:T(8,128)(2,1)S(1)}, bf16[4,16,16,256]{3,2,1,0:T(8,128)(2,1)}, u32[]{:S(2)}) copy-start(bf16[4,16,16,256]{3,2,1,0:T(8,128)(2,1)} %copy-done.1) | copy-start | bytes 1572868
  61.2 3.4 %copy-start.12 = (bf16[6,16,16,256]{3,2,1,0:T(8,128)(2,1)S(1)}, bf16[6,16,16,256]{3,2,1,0:T(8,128)(2,1)}, u32[]{:S(2)}) copy-start(bf16[6,16,16,256]{3,2,1,0:T(8,128)(2,1)} %copy-done.11) | copy-start | bytes 2359300
  61.2 10.5 %collective-permute-start.4 = (bf16[2,16,16,256]{3,2,1,0:T(8,128)(2,1)S(1)}, bf16[2,16,16,256]{3,2,1,0:T(8,128)(2,1)S(1)}, u32[]{:S(2)}, u32[]{:S(2)}) collective-permute-start(bf16[2,16,16,256]{3,2,1,0:T(8,128)(2,1)S(1)} %get-tuple-element.41), channel_id=1, source_target_pairs={{32,0},{64,32},{96,64},{33,1},{65,33},{97,65},{34,2},{66,34},{98,6... | collective-permute-start | bytes 786440 | tf_op jit(solution)/shard_map/ppermute | solution.py:326
  71.0 7.6 %copy-start.10 = (f32[4,16,16,256]{3,2,1,0:T(8,128)S(1)}, f32[4,16,16,256]{3,2,1,0:T(8,128)}, u32[]{:S(2)}) copy-start(f32[4,16,16,256]{3,2,1,0:T(8,128)} %copy-done.9) | copy-start | bytes 3145732
  71.8 50.2 %all-to-all-start.2 = ((bf16[64,88,256]{2,1,0:T(8,128)(2,1)}), bf16[64,88,256]{2,1,0:T(8,128)(2,1)}, u32[]{:S(2)}, u32[]{:S(2)}) async-start(bf16[64,88,256]{2,1,0:T(8,128)(2,1)} %shard_map.87), calls=%async_computation.2 | async-start | bytes 5767168 | tf_op jit(solution)/shard_map/all_to_all | solution.py:401
  78.6 2.0 %copy-start.3 = (bf16[3,3,3,256,256]{4,3,2,1,0:T(8,128)(2,1)S(1)}, bf16[3,3,3,256,256]{4,3,2,1,0:T(8,128)(2,1)}, u32[]{:S(2)}) copy-start(bf16[3,3,3,256,256]{4,3,2,1,0:T(8,128)(2,1)} %weights.4) | copy-start | bytes 10616836
  80.6 4.8 %copy-start.6 = (bf16[16,4,16,256]{3,2,1,0:T(8,128)(2,1)S(1)}, bf16[16,4,16,256]{3,2,1,0:T(8,128)(2,1)}, u32[]{:S(2)}) copy-start(bf16[16,4,16,256]{3,2,1,0:T(8,128)(2,1)} %copy-done.5) | copy-start | bytes 1572868
  85.4 13.1 %copy-start = (bf16[3,3,3,256,256]{4,3,2,1,0:T(8,128)(2,1)S(1)}, bf16[3,3,3,256,256]{4,3,2,1,0:T(8,128)(2,1)}, u32[]{:S(2)}) copy-start(bf16[3,3,3,256,256]{4,3,2,1,0:T(8,128)(2,1)} %weights.5) | copy-start | bytes 10616836
  90.4 15.4 %collective-permute-start.6 = (bf16[16,56,256]{2,1,0:T(8,128)(2,1)S(1)}, bf16[16,56,256]{2,1,0:T(8,128)(2,1)S(1)}, u32[]{:S(2)}, u32[]{:S(2)}) collective-permute-start(bf16[16,56,256]{2,1,0:T(8,128)(2,1)S(1)} %get-tuple-element.48), channel_id=1, source_target_pairs={{0,64},{32,96},{64,0},{96,32},{1,65},{33,97},{65,1},{97,33},{2,66}... | collective-permute-start | bytes 1376264 | tf_op jit(solution)/shard_map/ppermute | solution.py:330
  94.3 20.2 %collective-permute-start.7 = (bf16[16,56,256]{2,1,0:T(8,128)(2,1)S(1)}, bf16[16,56,256]{2,1,0:T(8,128)(2,1)S(1)}, u32[]{:S(2)}, u32[]{:S(2)}) collective-permute-start(bf16[16,56,256]{2,1,0:T(8,128)(2,1)S(1)} %get-tuple-element.49), channel_id=1, source_target_pairs={{0,32},{32,64},{64,96},{96,0},{1,33},{33,65},{65,97},{97,1},{2,34}... | collective-permute-start | bytes 1376264 | tf_op jit(solution)/shard_map/ppermute | solution.py:330
  95.0 21.3 %collective-permute-start.8 = (bf16[16,56,256]{2,1,0:T(8,128)(2,1)S(1)}, bf16[16,56,256]{2,1,0:T(8,128)(2,1)S(1)}, u32[]{:S(2)}, u32[]{:S(2)}) collective-permute-start(bf16[16,56,256]{2,1,0:T(8,128)(2,1)S(1)} %get-tuple-element.50), channel_id=1, source_target_pairs={{0,96},{32,0},{64,32},{96,64},{1,97},{33,1},{65,33},{97,65},{2,98}... | collective-permute-start | bytes 1376264 | tf_op jit(solution)/shard_map/ppermute | solution.py:330
  97.6 0.9 collective-permute-start.5
  124.2 17.0 %all-to-all-start.3 = ((bf16[16,72,256]{2,1,0:T(8,128)(2,1)}), bf16[16,72,256]{2,1,0:T(8,128)(2,1)S(1)}, u32[]{:S(2)}, u32[]{:S(2)}) async-start(bf16[16,72,256]{2,1,0:T(8,128)(2,1)} %pad_maximum_fusion), calls=%async_computation.3 | async-start | bytes 1179648 | tf_op jit(solution)/shard_map/all_to_all | solution.py:431
  128.1 6.9 %collective-permute-start.10 = (bf16[88,256]{1,0:T(8,128)(2,1)S(1)}, bf16[88,256]{1,0:T(8,128)(2,1)S(1)}, u32[]{:S(2)}, u32[]{:S(2)}) collective-permute-start(bf16[88,256]{1,0:T(8,128)(2,1)S(1)} %get-tuple-element.60), channel_id=1, source_target_pairs={{0,32},{32,64},{64,96},{96,0},{1,33},{33,65},{65,97},{97,1},{2,34}... | collective-permute-start | bytes 135176 | tf_op jit(solution)/shard_map/ppermute | solution.py:330
  131.7 4.0 %collective-permute-start.11 = (bf16[88,256]{1,0:T(8,128)(2,1)S(1)}, bf16[88,256]{1,0:T(8,128)(2,1)S(1)}, u32[]{:S(2)}, u32[]{:S(2)}) collective-permute-start(bf16[88,256]{1,0:T(8,128)(2,1)S(1)} %get-tuple-element.59), channel_id=1, source_target_pairs={{0,96},{32,0},{64,32},{96,64},{1,97},{33,1},{65,33},{97,65},{2,98}... | collective-permute-start | bytes 135176 | tf_op jit(solution)/shard_map/ppermute | solution.py:330
  132.9 5.6 %collective-permute-start.9 = (bf16[88,256]{1,0:T(8,128)(2,1)S(1)}, bf16[88,256]{1,0:T(8,128)(2,1)S(1)}, u32[]{:S(2)}, u32[]{:S(2)}) collective-permute-start(bf16[88,256]{1,0:T(8,128)(2,1)S(1)} %get-tuple-element.58), channel_id=1, source_target_pairs={{0,64},{32,96},{64,0},{96,32},{1,65},{33,97},{65,1},{97,33},{2,66}... | collective-permute-start | bytes 135176 | tf_op jit(solution)/shard_map/ppermute | solution.py:330
  (5 other events, 4.9 us)

commit v13 on v12

--- a/solution.py
+++ b/solution.py
@@ -363,10 +363,10 @@
     low, high = jnp.where(width == 0, nothing, edge), jnp.where(width == 0, edge, nothing)
     paired = jnp.concatenate([low, paired, high], axis=2).reshape(2, 4, 9, OWN, 2 * CH)
     fine = jnp.concatenate([paired[:, :, :-1], paired[:, :, 1:]], axis=3).transpose(2, 0, 1, 3, 4)
-    fine, block = lax.optimization_barrier((fine, block))
+    fine, block = lax.optimization_barrier((fine.reshape(64, WIN, 2 * CH), block))
     swap = [(0, 1), (1, 0)]
     other_block = lax.ppermute(block, "core", swap)
-    mine = lax.all_to_all(fine, ("z", "x_hi"), 0, 0, tiled=True).reshape(8, 2, 2, 2, WIN, 2 * CH)
+    mine = lax.all_to_all(fine.reshape(8, 8, WIN, 2 * CH), ("z", "x_hi"), 0, 0, tiled=True).reshape(8, 2, 2, 2, WIN, 2 * CH)
 
     first_act, first_slope, summed, up_act = call(
         forward_kernel, (6,), (core_arg, block, other_block, conv_first, conv_second, mask),

time: 145 us -> 144 us (level)
  no operation moved by 1% of the time
where the time goes in v13:
time: 144 us; the launch traced here: 142 us
  starting transfers between devices  43.8 us (30%)
  waiting for transfers between devices  40.5 us (28%)
  Pallas kernels  37.2 us (26%)
  local copies, waits for them, and re-layouts  14.4 us (10%)
  other arithmetic  4.93 us (3%)
    pallas_call x7, Pallas kernels, call(): pl.pallas_call(kernel, out_shape=shapes[0] if single else shapes, grid=gr...  37.2 us
    ppermute x6, waiting for transfers between devices, over_y(): return lax.ppermute(value, 'y', [(i, (i + step) % 4) for i in range(4)])  19.3 us
    ppermute x6, starting transfers between devices, over_y(): return lax.ppermute(value, 'y', [(i, (i + step) % 4) for i in range(4)])  14 us
    unnamed x28, local copies, waits for them, and re-layouts  9.1 us
    all_to_all x1, waiting for transfers between devices, shards(): block = lax.all_to_all(windows, ('z', 'x_hi', 'width'), 0, 0, tiled=True)  8.62 us
    all_to_all x1, starting transfers between devices, shards(): block = lax.all_to_all(windows, ('z', 'x_hi', 'width'), 0, 0, tiled=True)  7.88 us
    all_to_all x1, starting transfers between devices, shards(): early = lax.all_to_all(early, ('z', 'x_hi', 'width'), 0, 0, tiled=True)  6.81 us
    ppermute x2, starting transfers between devices, shift(): lax.ppermute(value, axis, [(i, i + step) for i in range(count) if 0 <= i...  5.18 us
  transfers between devices with their start and end apart: 16, of which 12 were waited for; matrix products, arithmetic and copies ran while one was open for 4% of the time, Pallas kernels for 24%

profile of v13, /device:TPU:0, one launch (start us, length us, event | category | flops | bytes accessed | tf_op | source)
XLA Modules:
  0.0 141.7 jit_solution(2956133203416601139)
XLA Ops:
  0.6 3.6 %collective-permute-start = (bf16[2,128,256]{2,1,0:T(8,128)(2,1)}, bf16[2,128,256]{2,1,0:T(8,128)(2,1)S(1)}, u32[]{:S(2)}, u32[]{:S(2)}) collective-permute-start(bf16[2,128,256]{2,1,0:T(8,128)(2,1)} %bitcast.51), channel_id=1, source_target_pairs={{0,32},{32,64},{64,96},{1,33},{33,65},{65,97},{2,34},{34,66},{66,9... | collective-permute-start | bytes 393224 | tf_op jit(solution)/shard_map/ppermute | solution.py:326
  7.0 2.4 %collective-permute-done.1 = bf16[2,4,4,512]{3,2,1,0:T(4,128)(2,1)S(1)} collective-permute-done((bf16[2,4,4,512]{3,2,1,0:T(4,128)(2,1)S(1)}, bf16[2,4,4,512]{3,2,1,0:T(4,128)(2,1)S(1)}, u32[]{:S(2)}, u32[]{:S(2)}) %collective-permute-start.1) | collective-permute-done | bytes 32800 | tf_op jit(solution)/shard_map/ppermute | solution.py:353
  11.4 7.9 %all-to-all-start = ((bf16[16,4,16,256]{3,2,1,0:T(8,128)(2,1)}), bf16[16,4,16,256]{3,2,1,0:T(8,128)(2,1)S(1)}, u32[]{:S(2)}, u32[]{:S(2)}) async-start(bf16[16,4,16,256]{3,2,1,0:T(8,128)(2,1)} %bitcast.8), calls=%async_computation | async-start | bytes 1048576 | tf_op jit(solution)/shard_map/all_to_all | solution.py:360
  20.8 8.6 %all-to-all-done.mine = bf16[16,4,16,256]{3,2,1,0:T(8,128)(2,1)S(1)} async-done(((bf16[16,4,16,256]{3,2,1,0:T(8,128)(2,1)}), bf16[16,4,16,256]{3,2,1,0:T(8,128)(2,1)S(1)}, u32[]{:S(2)}, u32[]{:S(2)}) %all-to-all-start) | async-done | bytes 524320 | tf_op jit(solution)/shard_map/all_to_all | solution.py:360
  29.4 3.6 %all-to-all-start.1 = ((bf16[8,8,16,512]{3,2,1,0:T(8,128)(2,1)}), bf16[8,8,16,512]{3,2,1,0:T(8,128)(2,1)S(1)}, u32[]{:S(2)}, u32[]{:S(2)}) async-start(bf16[8,8,16,512]{3,2,1,0:T(8,128)(2,1)} %bitcast.9), calls=%async_computation.1 | async-start | bytes 2097152 | tf_op jit(solution)/shard_map/all_to_all | solution.py:369
  33.1 13.8 %shard_map.84 = (bf16[6,16,16,256]{3,2,1,0:T(8,128)(2,1)S(1)}, f32[4,16,16,256]{3,2,1,0:T(8,128)S(1)}, f32[4,16,16,256]{3,2,1,0:T(8,128)S(1)}, bf16[4,16,16,256]{3,2,1,0:T(8,128)(2,1)S(1)}) custom-call(s32[1]{0:T(128)} %bitcast.core_ref, bf16[16,4,16,256]{3,2,1,0:T(8,128)(2,1)S(1)} %all-to-all-done.mine, ...), custom_call_target="tpu_custom_call" | custom-call | flops 8992587776 | bytes 11550724 | tf_op jit(solution)/shard_map/pallas_call | solution.py:312
  51.2 2.6 %collective-permute-done.3.other = bf16[8,2,2,2,16,512]{5,4,3,2,1,0:T(8,128)(2,1)S(1)} collective-permute-done((bf16[8,2,2,2,16,512]{5,4,3,2,1,0:T(8,128)(2,1)S(1)}, bf16[8,2,2,2,16,512]{5,4,3,2,1,0:T(8,128)(2,1)S(1)}, u32[]{:S(2)}, u32[]{:S(2)}) %collective-permute-start.3) | collective-permute-done | bytes 1048608 | tf_op jit(solution)/shard_map/ppermute | solution.py:379
  56.6 3.5 %shard_map.85 = (bf16[4,16,16,256]{3,2,1,0:T(8,128)(2,1)S(1)}, bf16[2,16,16,256]{3,2,1,0:T(8,128)(2,1)S(1)}) custom-call(s32[1]{0:T(128)} %bitcast.core_ref, bf16[8,2,2,2,16,512]{5,4,3,2,1,0:T(8,128)(2,1)S(1)} %bitcast.45, bf16[8,2,2,2,16,512]{5,4,3,2,1,0:T(8,128)(2,1)S(1)} %collective-permute-done.3.other, bf16[4,4,256,256]{3,2,1,0:T(8,128)(2,1)S(1)} %copy-done.4, ...), custom_call_target="tpu_custom_call" | custom-call | flops 2147483648 | bytes 6045700 | tf_op jit(solution)/shard_map/pallas_call | solution.py:312
  63.5 6.4 %shard_map.87 = bf16[64,88,256]{2,1,0:T(8,128)(2,1)} custom-call(s32[2]{0:T(128)S(1)} %pad_add_fusion.place, bf16[6,16,16,256]{3,2,1,0:T(8,128)(2,1)S(1)} %copy-done.12, bf16[4,16,16,256]{3,2,1,0:T(8,128)(2,1)S(1)} %get-tuple-element.38.block.grad_sum, bf16[64,32,256]{2,1,0:T(8,128)(2,1)S(1)} %shard_map.86.up), custom_call_target="tpu_custom_call" | custom-call | flops 3623878656 | bytes 5242888 | tf_op jit(solution)/shard_map/pallas_call | solution.py:312
  70.7 6.8 %all-to-all-start.2 = ((bf16[64,88,256]{2,1,0:T(8,128)(2,1)}), bf16[64,88,256]{2,1,0:T(8,128)(2,1)}, u32[]{:S(2)}, u32[]{:S(2)}) async-start(bf16[64,88,256]{2,1,0:T(8,128)(2,1)} %shard_map.87), calls=%async_computation.2 | async-start | bytes 5767168 | tf_op jit(solution)/shard_map/all_to_all | solution.py:401
  77.5 2.0 %copy-done.3 = bf16[3,3,3,256,256]{4,3,2,1,0:T(8,128)(2,1)S(1)} copy-done((bf16[3,3,3,256,256]{4,3,2,1,0:T(8,128)(2,1)S(1)}, bf16[3,3,3,256,256]{4,3,2,1,0:T(8,128)(2,1)}, u32[]{:S(2)}) %copy-start.3) | copy-done | bytes 3538968
  79.5 4.8 %shard_map.88 = (bf16[4,16,16,256]{3,2,1,0:T(8,128)(2,1)S(1)}, bf16[2,16,16,256]{3,2,1,0:T(8,128)(2,1)S(1)}) custom-call(bf16[4,16,16,256]{3,2,1,0:T(8,128)(2,1)S(1)} %get-tuple-element.38.block.grad_sum, bf16[2,16,16,256]{3,2,1,0:T(8,128)(2,1)S(1)} %collective-permute-done.4.later, f32[4,16,16,256]{3,2,1,0:T(8,128)S(1)} %copy-done.10, ...), custom_call_target="tpu_custom_call" | custom-call | flops 3623878656 | bytes 6176768 | tf_op jit(solution)/shard_map/pallas_call | solution.py:312
  84.4 4.9 %shard_map.89 = (bf16[16,56,256]{2,1,0:T(8,128)(2,1)S(1)}, bf16[16,56,256]{2,1,0:T(8,128)(2,1)S(1)}, bf16[16,56,256]{2,1,0:T(8,128)(2,1)S(1)}, bf16[16,56,256]{2,1,0:T(8,128)(2,1)S(1)}) custom-call(s32[2]{0:T(128)S(1)} %pad_add_fusion.place, bf16[16,4,16,256]{3,2,1,0:T(8,128)(2,1)S(1)} %all-to-all-done.mine, bf16[16,4,16,256]{3,2,1,0:T(8,128)(2,1)S(1)} %copy-done.6, ...), custom_call_target="tpu_custom_call" | custom-call | flops 3623878656 | bytes 3407880 | tf_op jit(solution)/shard_map/pallas_call | solution.py:312
  89.3 3.9 %collective-permute-start.6 = (bf16[16,56,256]{2,1,0:T(8,128)(2,1)S(1)}, bf16[16,56,256]{2,1,0:T(8,128)(2,1)S(1)}, u32[]{:S(2)}, u32[]{:S(2)}) collective-permute-start(bf16[16,56,256]{2,1,0:T(8,128)(2,1)S(1)} %get-tuple-element.48), channel_id=1, source_target_pairs={{0,64},{32,96},{64,0},{96,32},{1,65},{33,97},{65,1},{97,33},{2,66}... | collective-permute-start | bytes 1376264 | tf_op jit(solution)/shard_map/ppermute | solution.py:330
  93.9 2.5 %collective-permute-start.8 = (bf16[16,56,256]{2,1,0:T(8,128)(2,1)S(1)}, bf16[16,56,256]{2,1,0:T(8,128)(2,1)S(1)}, u32[]{:S(2)}, u32[]{:S(2)}) collective-permute-start(bf16[16,56,256]{2,1,0:T(8,128)(2,1)S(1)} %get-tuple-element.50), channel_id=1, source_target_pairs={{0,96},{32,0},{64,32},{96,64},{1,97},{33,1},{65,33},{97,65},{2,98}... | collective-permute-start | bytes 1376264 | tf_op jit(solution)/shard_map/ppermute | solution.py:330
  97.4 2.0 %shard_map.90 = bf16[16,2,8,256]{3,2,1,0:T(8,128)(2,1)S(1)} custom-call(s32[1]{0:T(128)} %bitcast.core_ref, bf16[4,16,16,256]{3,2,1,0:T(8,128)(2,1)S(1)} %get-tuple-element.46.block, bf16[2,16,16,256]{3,2,1,0:T(8,128)(2,1)S(1)} %collective-permute-done.5.later, bf16[4,16,16,256]{3,2,1,0:T(8,128)(2,1)S(1)} %get-tuple-element.38.block.grad_sum, ...), custom_call_target="tpu_custom_call" | custom-call | flops 939524096 | bytes 4980740 | tf_op jit(solution)/shard_map/pallas_call | solution.py:312
  99.4 5.3 %collective-permute-done.6 = bf16[16,56,256]{2,1,0:T(8,128)(2,1)S(1)} collective-permute-done((bf16[16,56,256]{2,1,0:T(8,128)(2,1)S(1)}, bf16[16,56,256]{2,1,0:T(8,128)(2,1)S(1)}, u32[]{:S(2)}, u32[]{:S(2)}) %collective-permute-start.6) | collective-permute-done | bytes 458784 | tf_op jit(solution)/shard_map/ppermute | solution.py:330
  104.7 8.8 %collective-permute-done.7 = bf16[16,56,256]{2,1,0:T(8,128)(2,1)S(1)} collective-permute-done((bf16[16,56,256]{2,1,0:T(8,128)(2,1)S(1)}, bf16[16,56,256]{2,1,0:T(8,128)(2,1)S(1)}, u32[]{:S(2)}, u32[]{:S(2)}) %collective-permute-start.7) | collective-permute-done | bytes 458784 | tf_op jit(solution)/shard_map/ppermute | solution.py:330
  116.3 4.6 %all-to-all-done.2 = bf16[64,88,256]{2,1,0:T(8,128)(2,1)} async-done(((bf16[64,88,256]{2,1,0:T(8,128)(2,1)}), bf16[64,88,256]{2,1,0:T(8,128)(2,1)}, u32[]{:S(2)}, u32[]{:S(2)}) %all-to-all-start.2) | async-done | bytes 2883616 | tf_op jit(solution)/shard_map/all_to_all | solution.py:401
  120.9 2.2 %convert_reduce_fusion = f32[4,88,256]{2,1,0:T(8,128)S(1)} fusion(bf16[16,4,88,256]{3,2,1,0:T(8,128)(2,1)} %bitcast.23), kind=kLoop, calls=%fused_computation | loop fusion | flops 2793472 | bytes 3244032 | tf_op jit(solution)/shard_map/reduce_sum | solution.py:427
  123.2 4.0 %all-to-all-start.3 = ((bf16[16,72,256]{2,1,0:T(8,128)(2,1)}), bf16[16,72,256]{2,1,0:T(8,128)(2,1)S(1)}, u32[]{:S(2)}, u32[]{:S(2)}) async-start(bf16[16,72,256]{2,1,0:T(8,128)(2,1)} %pad_maximum_fusion), calls=%async_computation.3 | async-start | bytes 1179648 | tf_op jit(solution)/shard_map/all_to_all | solution.py:431
  127.2 3.5 %collective-permute-start.10 = (bf16[88,256]{1,0:T(8,128)(2,1)S(1)}, bf16[88,256]{1,0:T(8,128)(2,1)S(1)}, u32[]{:S(2)}, u32[]{:S(2)}) collective-permute-start(bf16[88,256]{1,0:T(8,128)(2,1)S(1)} %get-tuple-element.60), channel_id=1, source_target_pairs={{0,32},{32,64},{64,96},{96,0},{1,33},{33,65},{65,97},{97,1},{2,34}... | collective-permute-start | bytes 135176 | tf_op jit(solution)/shard_map/ppermute | solution.py:330
  131.8 2.1 %collective-permute-start.9 = (bf16[88,256]{1,0:T(8,128)(2,1)S(1)}, bf16[88,256]{1,0:T(8,128)(2,1)S(1)}, u32[]{:S(2)}, u32[]{:S(2)}) collective-permute-start(bf16[88,256]{1,0:T(8,128)(2,1)S(1)} %get-tuple-element.58), channel_id=1, source_target_pairs={{0,64},{32,96},{64,0},{96,32},{1,65},{33,97},{65,1},{97,33},{2,66}... | collective-permute-start | bytes 135176 | tf_op jit(solution)/shard_map/ppermute | solution.py:330
  134.7 2.7 %collective-permute-done.9 = bf16[88,256]{1,0:T(8,128)(2,1)S(1)} collective-permute-done((bf16[88,256]{1,0:T(8,128)(2,1)S(1)}, bf16[88,256]{1,0:T(8,128)(2,1)S(1)}, u32[]{:S(2)}, u32[]{:S(2)}) %collective-permute-start.9) | collective-permute-done | bytes 45088 | tf_op jit(solution)/shard_map/ppermute | solution.py:330
  (70 shorter events, 28.3 us)
Async XLA Ops:
  0.6 8.8 %collective-permute-start = (bf16[2,128,256]{2,1,0:T(8,128)(2,1)}, bf16[2,128,256]{2,1,0:T(8,128)(2,1)S(1)}, u32[]{:S(2)}, u32[]{:S(2)}) collective-permute-start(bf16[2,128,256]{2,1,0:T(8,128)(2,1)} %bitcast.51), channel_id=1, source_target_pairs={{0,32},{32,64},{64,96},{1,33},{33,65},{65,97},{2,34},{34,66},{66,9... | collective-permute-start | bytes 393224 | tf_op jit(solution)/shard_map/ppermute | solution.py:326
  5.5 4.0 %collective-permute-start.1 = (bf16[2,4,4,512]{3,2,1,0:T(4,128)(2,1)S(1)}, bf16[2,4,4,512]{3,2,1,0:T(4,128)(2,1)S(1)}, u32[]{:S(2)}, u32[]{:S(2)}) collective-permute-start(bf16[2,4,4,512]{3,2,1,0:T(4,128)(2,1)S(1)} %slice_select_fusion), channel_id=1, source_target_pairs={{0,1},{1,0},{2,3},{3,2},{4,5},{5,4},{6,7},{7,6},{8,9},{9,8},{10,11... | collective-permute-start | bytes 98312 | tf_op jit(solution)/shard_map/ppermute | solution.py:353
  11.4 18.0 %all-to-all-start = ((bf16[16,4,16,256]{3,2,1,0:T(8,128)(2,1)}), bf16[16,4,16,256]{3,2,1,0:T(8,128)(2,1)S(1)}, u32[]{:S(2)}, u32[]{:S(2)}) async-start(bf16[16,4,16,256]{3,2,1,0:T(8,128)(2,1)} %bitcast.8), calls=%async_computation | async-start | bytes 1048576 | tf_op jit(solution)/shard_map/all_to_all | solution.py:360
  29.4 3.6 %collective-permute-start.2 = (bf16[16,4,16,256]{3,2,1,0:T(8,128)(2,1)S(1)}, bf16[16,4,16,256]{3,2,1,0:T(8,128)(2,1)S(1)}, u32[]{:S(2)}, u32[]{:S(2)}) collective-permute-start(bf16[16,4,16,256]{3,2,1,0:T(8,128)(2,1)S(1)} %all-to-all-done.mine), channel_id=1, source_target_pairs={{0,16},{16,0},{1,17},{17,1},{2,18},{18,2},{3,19},{19,3},{4,20},{20... | collective-permute-start | bytes 1572872 | tf_op jit(solution)/shard_map/ppermute | solution.py:368
  29.4 21.7 %all-to-all-start.1 = ((bf16[8,8,16,512]{3,2,1,0:T(8,128)(2,1)}), bf16[8,8,16,512]{3,2,1,0:T(8,128)(2,1)S(1)}, u32[]{:S(2)}, u32[]{:S(2)}) async-start(bf16[8,8,16,512]{3,2,1,0:T(8,128)(2,1)} %bitcast.9), calls=%async_computation.1 | async-start | bytes 2097152 | tf_op jit(solution)/shard_map/all_to_all | solution.py:369
  33.0 13.9 %copy-start.5 = (bf16[16,4,16,256]{3,2,1,0:T(8,128)(2,1)}, bf16[16,4,16,256]{3,2,1,0:T(8,128)(2,1)S(1)}, u32[]{:S(2)}) copy-start(bf16[16,4,16,256]{3,2,1,0:T(8,128)(2,1)S(1)} %collective-permute-done.2.other) | copy-start | bytes 1572868
  51.1 2.7 %collective-permute-start.3 = (bf16[8,2,2,2,16,512]{5,4,3,2,1,0:T(8,128)(2,1)S(1)}, bf16[8,2,2,2,16,512]{5,4,3,2,1,0:T(8,128)(2,1)S(1)}, u32[]{:S(2)}, u32[]{:S(2)}) collective-permute-start(bf16[8,2,2,2,16,512]{5,4,3,2,1,0:T(8,128)(2,1)S(1)} %bitcast.44), channel_id=1, source_target_pairs={{0,16},{16,0},{1,17},{17,1},{2,18},{18,2},{3,19},{19,3},{4,20},{20... | collective-permute-start | bytes 3145736 | tf_op jit(solution)/shard_map/ppermute | solution.py:379
  53.8 1.6 %copy-start.4 = (bf16[4,4,256,256]{3,2,1,0:T(8,128)(2,1)S(1)}, bf16[4,4,256,256]{3,2,1,0:T(8,128)(2,1)}, u32[]{:S(2)}) copy-start(bf16[4,4,256,256]{3,2,1,0:T(8,128)(2,1)} %weights.3) | copy-start | bytes 6291460
  56.6 5.2 %copy-start.2 = (bf16[4,16,16,256]{3,2,1,0:T(8,128)(2,1)S(1)}, bf16[4,16,16,256]{3,2,1,0:T(8,128)(2,1)}, u32[]{:S(2)}) copy-start(bf16[4,16,16,256]{3,2,1,0:T(8,128)(2,1)} %copy-done.1) | copy-start | bytes 1572868
  60.1 3.4 %copy-start.12 = (bf16[6,16,16,256]{3,2,1,0:T(8,128)(2,1)S(1)}, bf16[6,16,16,256]{3,2,1,0:T(8,128)(2,1)}, u32[]{:S(2)}) copy-start(bf16[6,16,16,256]{3,2,1,0:T(8,128)(2,1)} %copy-done.11) | copy-start | bytes 2359300
  60.1 10.6 %collective-permute-start.4 = (bf16[2,16,16,256]{3,2,1,0:T(8,128)(2,1)S(1)}, bf16[2,16,16,256]{3,2,1,0:T(8,128)(2,1)S(1)}, u32[]{:S(2)}, u32[]{:S(2)}) collective-permute-start(bf16[2,16,16,256]{3,2,1,0:T(8,128)(2,1)S(1)} %get-tuple-element.41), channel_id=1, source_target_pairs={{32,0},{64,32},{96,64},{33,1},{65,33},{97,65},{34,2},{66,34},{98,6... | collective-permute-start | bytes 786440 | tf_op jit(solution)/shard_map/ppermute | solution.py:326
  69.9 7.6 %copy-start.10 = (f32[4,16,16,256]{3,2,1,0:T(8,128)S(1)}, f32[4,16,16,256]{3,2,1,0:T(8,128)}, u32[]{:S(2)}) copy-start(f32[4,16,16,256]{3,2,1,0:T(8,128)} %copy-done.9) | copy-start | bytes 3145732
  70.7 50.2 %all-to-all-start.2 = ((bf16[64,88,256]{2,1,0:T(8,128)(2,1)}), bf16[64,88,256]{2,1,0:T(8,128)(2,1)}, u32[]{:S(2)}, u32[]{:S(2)}) async-start(bf16[64,88,256]{2,1,0:T(8,128)(2,1)} %shard_map.87), calls=%async_computation.2 | async-start | bytes 5767168 | tf_op jit(solution)/shard_map/all_to_all | solution.py:401
  77.5 2.0 %copy-start.3 = (bf16[3,3,3,256,256]{4,3,2,1,0:T(8,128)(2,1)S(1)}, bf16[3,3,3,256,256]{4,3,2,1,0:T(8,128)(2,1)}, u32[]{:S(2)}) copy-start(bf16[3,3,3,256,256]{4,3,2,1,0:T(8,128)(2,1)} %weights.4) | copy-start | bytes 10616836
  79.5 4.8 %copy-start.6 = (bf16[16,4,16,256]{3,2,1,0:T(8,128)(2,1)S(1)}, bf16[16,4,16,256]{3,2,1,0:T(8,128)(2,1)}, u32[]{:S(2)}) copy-start(bf16[16,4,16,256]{3,2,1,0:T(8,128)(2,1)} %copy-done.5) | copy-start | bytes 1572868
  84.3 13.0 %copy-start = (bf16[3,3,3,256,256]{4,3,2,1,0:T(8,128)(2,1)S(1)}, bf16[3,3,3,256,256]{4,3,2,1,0:T(8,128)(2,1)}, u32[]{:S(2)}) copy-start(bf16[3,3,3,256,256]{4,3,2,1,0:T(8,128)(2,1)} %weights.5) | copy-start | bytes 10616836
  89.3 15.4 %collective-permute-start.6 = (bf16[16,56,256]{2,1,0:T(8,128)(2,1)S(1)}, bf16[16,56,256]{2,1,0:T(8,128)(2,1)S(1)}, u32[]{:S(2)}, u32[]{:S(2)}) collective-permute-start(bf16[16,56,256]{2,1,0:T(8,128)(2,1)S(1)} %get-tuple-element.48), channel_id=1, source_target_pairs={{0,64},{32,96},{64,0},{96,32},{1,65},{33,97},{65,1},{97,33},{2,66}... | collective-permute-start | bytes 1376264 | tf_op jit(solution)/shard_map/ppermute | solution.py:330
  93.2 20.2 %collective-permute-start.7 = (bf16[16,56,256]{2,1,0:T(8,128)(2,1)S(1)}, bf16[16,56,256]{2,1,0:T(8,128)(2,1)S(1)}, u32[]{:S(2)}, u32[]{:S(2)}) collective-permute-start(bf16[16,56,256]{2,1,0:T(8,128)(2,1)S(1)} %get-tuple-element.49), channel_id=1, source_target_pairs={{0,32},{32,64},{64,96},{96,0},{1,33},{33,65},{65,97},{97,1},{2,34}... | collective-permute-start | bytes 1376264 | tf_op jit(solution)/shard_map/ppermute | solution.py:330
  93.9 21.3 %collective-permute-start.8 = (bf16[16,56,256]{2,1,0:T(8,128)(2,1)S(1)}, bf16[16,56,256]{2,1,0:T(8,128)(2,1)S(1)}, u32[]{:S(2)}, u32[]{:S(2)}) collective-permute-start(bf16[16,56,256]{2,1,0:T(8,128)(2,1)S(1)} %get-tuple-element.50), channel_id=1, source_target_pairs={{0,96},{32,0},{64,32},{96,64},{1,97},{33,1},{65,33},{97,65},{2,98}... | collective-permute-start | bytes 1376264 | tf_op jit(solution)/shard_map/ppermute | solution.py:330
  96.5 0.9 collective-permute-start.5
  123.2 17.2 %all-to-all-start.3 = ((bf16[16,72,256]{2,1,0:T(8,128)(2,1)}), bf16[16,72,256]{2,1,0:T(8,128)(2,1)S(1)}, u32[]{:S(2)}, u32[]{:S(2)}) async-start(bf16[16,72,256]{2,1,0:T(8,128)(2,1)} %pad_maximum_fusion), calls=%async_computation.3 | async-start | bytes 1179648 | tf_op jit(solution)/shard_map/all_to_all | solution.py:431
  127.2 6.8 %collective-permute-start.10 = (bf16[88,256]{1,0:T(8,128)(2,1)S(1)}, bf16[88,256]{1,0:T(8,128)(2,1)S(1)}, u32[]{:S(2)}, u32[]{:S(2)}) collective-permute-start(bf16[88,256]{1,0:T(8,128)(2,1)S(1)} %get-tuple-element.60), channel_id=1, source_target_pairs={{0,32},{32,64},{64,96},{96,0},{1,33},{33,65},{65,97},{97,1},{2,34}... | collective-permute-start | bytes 135176 | tf_op jit(solution)/shard_map/ppermute | solution.py:330
  130.7 4.0 %collective-permute-start.11 = (bf16[88,256]{1,0:T(8,128)(2,1)S(1)}, bf16[88,256]{1,0:T(8,128)(2,1)S(1)}, u32[]{:S(2)}, u32[]{:S(2)}) collective-permute-start(bf16[88,256]{1,0:T(8,128)(2,1)S(1)} %get-tuple-element.59), channel_id=1, source_target_pairs={{0,96},{32,0},{64,32},{96,64},{1,97},{33,1},{65,33},{97,65},{2,98}... | collective-permute-start | bytes 135176 | tf_op jit(solution)/shard_map/ppermute | solution.py:330
  131.8 5.6 %collective-permute-start.9 = (bf16[88,256]{1,0:T(8,128)(2,1)S(1)}, bf16[88,256]{1,0:T(8,128)(2,1)S(1)}, u32[]{:S(2)}, u32[]{:S(2)}) collective-permute-start(bf16[88,256]{1,0:T(8,128)(2,1)S(1)} %get-tuple-element.58), channel_id=1, source_target_pairs={{0,64},{32,96},{64,0},{96,32},{1,65},{33,97},{65,1},{97,33},{2,66}... | collective-permute-start | bytes 135176 | tf_op jit(solution)/shard_map/ppermute | solution.py:330
  (5 other events, 4.9 us)

commit v14 on v13

--- a/solution.py
+++ b/solution.py
@@ -421,13 +421,13 @@
         [((ROWS, 2, OWN, CH), BF16)], [own_table, pltpu.VMEM((2 * ROWS * OWN, CH), F32)], 7 * tap_flops,
     )
 
-    first_sum = sum(value.astype(F32) for value in arrived).astype(BF16)
-    late = jnp.concatenate([rows_out.reshape(16, 2 * OWN, CH), first_sum], axis=1)
-    late, early = lax.optimization_barrier((late, early))
+    tied_rows, early = lax.optimization_barrier((rows_out, early))
     early = jnp.sum(early.reshape(16, 4, UP_ROWS + PIECE, CH).astype(F32), axis=0)
     early_total = early[0]
     for step in (2, 1, 3):
         early_total += over_y(early[step].astype(BF16), step).astype(F32)
+    first_sum = sum(value.astype(F32) for value in arrived).astype(BF16)
+    late = jnp.concatenate([tied_rows.reshape(16, 2 * OWN, CH), first_sum], axis=1)
     late = lax.all_to_all(late, ("z", "x_hi", "width"), 0, 0, tiled=True)
 
     factor = 1.0 / math.sqrt(32768)

time: 144 us -> 142 us (0.986)
    ppermute x6, waiting for transfers between devices: 19.3 us -> 21.3 us  [over_y(): return lax.ppermute(value, 'y', [(i, (i + step) % 4) for i in range(4)])]
    all_to_all x1, waiting for transfers between devices: 1.66 us -> 0.01 us  [shards(): late = lax.all_to_all(late, ('z', 'x_hi', 'width'), 0, 0, tiled=True)]
  transfers between devices with their start and end apart: 16 -> 16, of which waited for: 12 -> 9; matrix products, arithmetic and copies ran while one was open for 4% -> 5% of each run, Pallas kernels for 24% -> 24%
where the time goes in v14:
time: 142 us; the launch traced here: 141 us
  starting transfers between devices  42.6 us (30%)
  waiting for transfers between devices  41 us (29%)
  Pallas kernels  37.2 us (26%)
  local copies, waits for them, and re-layouts  14.4 us (10%)
  other arithmetic  4.94 us (3%)
    pallas_call x7, Pallas kernels, call(): pl.pallas_call(kernel, out_shape=shapes[0] if single else shapes, grid=gr...  37.2 us
    ppermute x6, waiting for transfers between devices, over_y(): return lax.ppermute(value, 'y', [(i, (i + step) % 4) for i in range(4)])  21.3 us
    ppermute x6, starting transfers between devices, over_y(): return lax.ppermute(value, 'y', [(i, (i + step) % 4) for i in range(4)])  12.7 us
    unnamed x28, local copies, waits for them, and re-layouts  9.1 us
    all_to_all x1, waiting for transfers between devices, shards(): block = lax.all_to_all(windows, ('z', 'x_hi', 'width'), 0, 0, tiled=True)  8.62 us
    all_to_all x1, starting transfers between devices, shards(): block = lax.all_to_all(windows, ('z', 'x_hi', 'width'), 0, 0, tiled=True)  7.88 us
    all_to_all x1, starting transfers between devices, shards(): early = lax.all_to_all(early, ('z', 'x_hi', 'width'), 0, 0, tiled=True)  6.81 us
    ppermute x2, starting transfers between devices, shift(): lax.ppermute(value, axis, [(i, i + step) for i in range(count) if 0 <= i...  5.18 us
  transfers between devices with their start and end apart: 16, of which 9 were waited for; matrix products, arithmetic and copies ran while one was open for 5% of the time, Pallas kernels for 24%

profile of v14, /device:TPU:0, one launch (start us, length us, event | category | flops | bytes accessed | tf_op | source)
XLA Modules:
  0.0 141.0 jit_solution(16512465973293339914)
XLA Ops:
  0.6 3.6 %collective-permute-start = (bf16[2,128,256]{2,1,0:T(8,128)(2,1)}, bf16[2,128,256]{2,1,0:T(8,128)(2,1)S(1)}, u32[]{:S(2)}, u32[]{:S(2)}) collective-permute-start(bf16[2,128,256]{2,1,0:T(8,128)(2,1)} %bitcast.51), channel_id=1, source_target_pairs={{0,32},{32,64},{64,96},{1,33},{33,65},{65,97},{2,34},{34,66},{66,9... | collective-permute-start | bytes 393224 | tf_op jit(solution)/shard_map/ppermute | solution.py:326
  7.0 2.4 %collective-permute-done.1 = bf16[2,4,4,512]{3,2,1,0:T(4,128)(2,1)S(1)} collective-permute-done((bf16[2,4,4,512]{3,2,1,0:T(4,128)(2,1)S(1)}, bf16[2,4,4,512]{3,2,1,0:T(4,128)(2,1)S(1)}, u32[]{:S(2)}, u32[]{:S(2)}) %collective-permute-start.1) | collective-permute-done | bytes 32800 | tf_op jit(solution)/shard_map/ppermute | solution.py:353
  11.4 7.9 %all-to-all-start = ((bf16[16,4,16,256]{3,2,1,0:T(8,128)(2,1)}), bf16[16,4,16,256]{3,2,1,0:T(8,128)(2,1)S(1)}, u32[]{:S(2)}, u32[]{:S(2)}) async-start(bf16[16,4,16,256]{3,2,1,0:T(8,128)(2,1)} %bitcast.8), calls=%async_computation | async-start | bytes 1048576 | tf_op jit(solution)/shard_map/all_to_all | solution.py:360
  20.8 8.6 %all-to-all-done.mine = bf16[16,4,16,256]{3,2,1,0:T(8,128)(2,1)S(1)} async-done(((bf16[16,4,16,256]{3,2,1,0:T(8,128)(2,1)}), bf16[16,4,16,256]{3,2,1,0:T(8,128)(2,1)S(1)}, u32[]{:S(2)}, u32[]{:S(2)}) %all-to-all-start) | async-done | bytes 524320 | tf_op jit(solution)/shard_map/all_to_all | solution.py:360
  29.4 3.6 %all-to-all-start.1 = ((bf16[8,8,16,512]{3,2,1,0:T(8,128)(2,1)}), bf16[8,8,16,512]{3,2,1,0:T(8,128)(2,1)S(1)}, u32[]{:S(2)}, u32[]{:S(2)}) async-start(bf16[8,8,16,512]{3,2,1,0:T(8,128)(2,1)} %bitcast.9), calls=%async_computation.1 | async-start | bytes 2097152 | tf_op jit(solution)/shard_map/all_to_all | solution.py:369
  33.1 13.8 %shard_map.84 = (bf16[6,16,16,256]{3,2,1,0:T(8,128)(2,1)S(1)}, f32[4,16,16,256]{3,2,1,0:T(8,128)S(1)}, f32[4,16,16,256]{3,2,1,0:T(8,128)S(1)}, bf16[4,16,16,256]{3,2,1,0:T(8,128)(2,1)S(1)}) custom-call(s32[1]{0:T(128)} %bitcast.core_ref, bf16[16,4,16,256]{3,2,1,0:T(8,128)(2,1)S(1)} %all-to-all-done.mine, ...), custom_call_target="tpu_custom_call" | custom-call | flops 8992587776 | bytes 11550724 | tf_op jit(solution)/shard_map/pallas_call | solution.py:312
  51.2 2.6 %collective-permute-done.3.other = bf16[8,2,2,2,16,512]{5,4,3,2,1,0:T(8,128)(2,1)S(1)} collective-permute-done((bf16[8,2,2,2,16,512]{5,4,3,2,1,0:T(8,128)(2,1)S(1)}, bf16[8,2,2,2,16,512]{5,4,3,2,1,0:T(8,128)(2,1)S(1)}, u32[]{:S(2)}, u32[]{:S(2)}) %collective-permute-start.3) | collective-permute-done | bytes 1048608 | tf_op jit(solution)/shard_map/ppermute | solution.py:379
  56.6 3.5 %shard_map.85 = (bf16[4,16,16,256]{3,2,1,0:T(8,128)(2,1)S(1)}, bf16[2,16,16,256]{3,2,1,0:T(8,128)(2,1)S(1)}) custom-call(s32[1]{0:T(128)} %bitcast.core_ref, bf16[8,2,2,2,16,512]{5,4,3,2,1,0:T(8,128)(2,1)S(1)} %bitcast.45, bf16[8,2,2,2,16,512]{5,4,3,2,1,0:T(8,128)(2,1)S(1)} %collective-permute-done.3.other, bf16[4,4,256,256]{3,2,1,0:T(8,128)(2,1)S(1)} %copy-done.4, ...), custom_call_target="tpu_custom_call" | custom-call | flops 2147483648 | bytes 6045700 | tf_op jit(solution)/shard_map/pallas_call | solution.py:312
  63.5 6.4 %shard_map.87 = bf16[64,88,256]{2,1,0:T(8,128)(2,1)} custom-call(s32[2]{0:T(128)S(1)} %pad_add_fusion.place, bf16[6,16,16,256]{3,2,1,0:T(8,128)(2,1)S(1)} %copy-done.12, bf16[4,16,16,256]{3,2,1,0:T(8,128)(2,1)S(1)} %get-tuple-element.38.block.grad_sum, bf16[64,32,256]{2,1,0:T(8,128)(2,1)S(1)} %shard_map.86.up), custom_call_target="tpu_custom_call" | custom-call | flops 3623878656 | bytes 5242888 | tf_op jit(solution)/shard_map/pallas_call | solution.py:312
  70.7 6.8 %all-to-all-start.2 = ((bf16[64,88,256]{2,1,0:T(8,128)(2,1)}), bf16[64,88,256]{2,1,0:T(8,128)(2,1)}, u32[]{:S(2)}, u32[]{:S(2)}) async-start(bf16[64,88,256]{2,1,0:T(8,128)(2,1)} %shard_map.87), calls=%async_computation.2 | async-start | bytes 5767168 | tf_op jit(solution)/shard_map/all_to_all | solution.py:401
  77.5 2.0 %copy-done.3 = bf16[3,3,3,256,256]{4,3,2,1,0:T(8,128)(2,1)S(1)} copy-done((bf16[3,3,3,256,256]{4,3,2,1,0:T(8,128)(2,1)S(1)}, bf16[3,3,3,256,256]{4,3,2,1,0:T(8,128)(2,1)}, u32[]{:S(2)}) %copy-start.3) | copy-done | bytes 3538968
  79.5 4.8 %shard_map.88 = (bf16[4,16,16,256]{3,2,1,0:T(8,128)(2,1)S(1)}, bf16[2,16,16,256]{3,2,1,0:T(8,128)(2,1)S(1)}) custom-call(bf16[4,16,16,256]{3,2,1,0:T(8,128)(2,1)S(1)} %get-tuple-element.38.block.grad_sum, bf16[2,16,16,256]{3,2,1,0:T(8,128)(2,1)S(1)} %collective-permute-done.4.later, f32[4,16,16,256]{3,2,1,0:T(8,128)S(1)} %copy-done.10, ...), custom_call_target="tpu_custom_call" | custom-call | flops 3623878656 | bytes 6176768 | tf_op jit(solution)/shard_map/pallas_call | solution.py:312
  84.4 4.9 %shard_map.89 = (bf16[16,56,256]{2,1,0:T(8,128)(2,1)S(1)}, bf16[16,56,256]{2,1,0:T(8,128)(2,1)S(1)}, bf16[16,56,256]{2,1,0:T(8,128)(2,1)S(1)}, bf16[16,56,256]{2,1,0:T(8,128)(2,1)S(1)}) custom-call(s32[2]{0:T(128)S(1)} %pad_add_fusion.place, bf16[16,4,16,256]{3,2,1,0:T(8,128)(2,1)S(1)} %all-to-all-done.mine, bf16[16,4,16,256]{3,2,1,0:T(8,128)(2,1)S(1)} %copy-done.6, ...), custom_call_target="tpu_custom_call" | custom-call | flops 3623878656 | bytes 3407880 | tf_op jit(solution)/shard_map/pallas_call | solution.py:312
  89.3 3.8 %collective-permute-start.8 = (bf16[16,56,256]{2,1,0:T(8,128)(2,1)S(1)}, bf16[16,56,256]{2,1,0:T(8,128)(2,1)S(1)}, u32[]{:S(2)}, u32[]{:S(2)}) collective-permute-start(bf16[16,56,256]{2,1,0:T(8,128)(2,1)S(1)} %get-tuple-element.52), channel_id=1, source_target_pairs={{0,96},{32,0},{64,32},{96,64},{1,97},{33,1},{65,33},{97,65},{2,98}... | collective-permute-start | bytes 1376264 | tf_op jit(solution)/shard_map/ppermute | solution.py:330
  93.1 2.2 %collective-permute-start.6 = (bf16[16,56,256]{2,1,0:T(8,128)(2,1)S(1)}, bf16[16,56,256]{2,1,0:T(8,128)(2,1)S(1)}, u32[]{:S(2)}, u32[]{:S(2)}) collective-permute-start(bf16[16,56,256]{2,1,0:T(8,128)(2,1)S(1)} %get-tuple-element.50), channel_id=1, source_target_pairs={{0,64},{32,96},{64,0},{96,32},{1,65},{33,97},{65,1},{97,33},{2,66}... | collective-permute-start | bytes 1376264 | tf_op jit(solution)/shard_map/ppermute | solution.py:330
  96.2 2.0 %shard_map.90 = bf16[16,2,8,256]{3,2,1,0:T(8,128)(2,1)S(1)} custom-call(s32[1]{0:T(128)} %bitcast.core_ref, bf16[4,16,16,256]{3,2,1,0:T(8,128)(2,1)S(1)} %get-tuple-element.46.block, bf16[2,16,16,256]{3,2,1,0:T(8,128)(2,1)S(1)} %collective-permute-done.5.later, bf16[4,16,16,256]{3,2,1,0:T(8,128)(2,1)S(1)} %get-tuple-element.38.block.grad_sum, ...), custom_call_target="tpu_custom_call" | custom-call | flops 939524096 | bytes 4980740 | tf_op jit(solution)/shard_map/pallas_call | solution.py:312
  98.1 14.4 %collective-permute-done.8 = bf16[16,56,256]{2,1,0:T(8,128)(2,1)S(1)} collective-permute-done((bf16[16,56,256]{2,1,0:T(8,128)(2,1)S(1)}, bf16[16,56,256]{2,1,0:T(8,128)(2,1)S(1)}, u32[]{:S(2)}, u32[]{:S(2)}) %collective-permute-start.8) | collective-permute-done | bytes 458784 | tf_op jit(solution)/shard_map/ppermute | solution.py:330
  112.5 3.4 %collective-permute-done.7 = bf16[16,56,256]{2,1,0:T(8,128)(2,1)S(1)} collective-permute-done((bf16[16,56,256]{2,1,0:T(8,128)(2,1)S(1)}, bf16[16,56,256]{2,1,0:T(8,128)(2,1)S(1)}, u32[]{:S(2)}, u32[]{:S(2)}) %collective-permute-start.7) | collective-permute-done | bytes 458784 | tf_op jit(solution)/shard_map/ppermute | solution.py:330
  116.2 4.7 %all-to-all-done.2 = bf16[64,88,256]{2,1,0:T(8,128)(2,1)} async-done(((bf16[64,88,256]{2,1,0:T(8,128)(2,1)}), bf16[64,88,256]{2,1,0:T(8,128)(2,1)}, u32[]{:S(2)}, u32[]{:S(2)}) %all-to-all-start.2) | async-done | bytes 2883616 | tf_op jit(solution)/shard_map/all_to_all | solution.py:401
  121.8 3.9 %all-to-all-start.3 = ((bf16[16,72,256]{2,1,0:T(8,128)(2,1)}), bf16[16,72,256]{2,1,0:T(8,128)(2,1)S(1)}, u32[]{:S(2)}, u32[]{:S(2)}) async-start(bf16[16,72,256]{2,1,0:T(8,128)(2,1)} %pad_maximum_fusion), calls=%async_computation.3 | async-start | bytes 1179648 | tf_op jit(solution)/shard_map/all_to_all | solution.py:431
  125.7 2.2 %convert_reduce_fusion = f32[4,88,256]{2,1,0:T(8,128)S(1)} fusion(bf16[16,4,88,256]{3,2,1,0:T(8,128)(2,1)} %bitcast.23), kind=kLoop, calls=%fused_computation | loop fusion | flops 2793472 | bytes 3244032 | tf_op jit(solution)/shard_map/reduce_sum | solution.py:425
  128.0 4.6 %collective-permute-start.11 = (bf16[88,256]{1,0:T(8,128)(2,1)S(1)}, bf16[88,256]{1,0:T(8,128)(2,1)S(1)}, u32[]{:S(2)}, u32[]{:S(2)}) collective-permute-start(bf16[88,256]{1,0:T(8,128)(2,1)S(1)} %get-tuple-element.59), channel_id=1, source_target_pairs={{0,96},{32,0},{64,32},{96,64},{1,97},{33,1},{65,33},{97,65},{2,98}... | collective-permute-start | bytes 135176 | tf_op jit(solution)/shard_map/ppermute | solution.py:330
  132.6 2.2 %collective-permute-start.9 = (bf16[88,256]{1,0:T(8,128)(2,1)S(1)}, bf16[88,256]{1,0:T(8,128)(2,1)S(1)}, u32[]{:S(2)}, u32[]{:S(2)}) collective-permute-start(bf16[88,256]{1,0:T(8,128)(2,1)S(1)} %get-tuple-element.58), channel_id=1, source_target_pairs={{0,64},{32,96},{64,0},{96,32},{1,65},{33,97},{65,1},{97,33},{2,66}... | collective-permute-start | bytes 135176 | tf_op jit(solution)/shard_map/ppermute | solution.py:330
  134.8 3.5 %collective-permute-done.10 = bf16[88,256]{1,0:T(8,128)(2,1)S(1)} collective-permute-done((bf16[88,256]{1,0:T(8,128)(2,1)S(1)}, bf16[88,256]{1,0:T(8,128)(2,1)S(1)}, u32[]{:S(2)}, u32[]{:S(2)}) %collective-permute-start.10) | collective-permute-done | bytes 45088 | tf_op jit(solution)/shard_map/ppermute | solution.py:330
  (70 shorter events, 22.2 us)
Async XLA Ops:
  0.6 8.8 %collective-permute-start = (bf16[2,128,256]{2,1,0:T(8,128)(2,1)}, bf16[2,128,256]{2,1,0:T(8,128)(2,1)S(1)}, u32[]{:S(2)}, u32[]{:S(2)}) collective-permute-start(bf16[2,128,256]{2,1,0:T(8,128)(2,1)} %bitcast.51), channel_id=1, source_target_pairs={{0,32},{32,64},{64,96},{1,33},{33,65},{65,97},{2,34},{34,66},{66,9... | collective-permute-start | bytes 393224 | tf_op jit(solution)/shard_map/ppermute | solution.py:326
  5.5 4.0 %collective-permute-start.1 = (bf16[2,4,4,512]{3,2,1,0:T(4,128)(2,1)S(1)}, bf16[2,4,4,512]{3,2,1,0:T(4,128)(2,1)S(1)}, u32[]{:S(2)}, u32[]{:S(2)}) collective-permute-start(bf16[2,4,4,512]{3,2,1,0:T(4,128)(2,1)S(1)} %slice_select_fusion), channel_id=1, source_target_pairs={{0,1},{1,0},{2,3},{3,2},{4,5},{5,4},{6,7},{7,6},{8,9},{9,8},{10,11... | collective-permute-start | bytes 98312 | tf_op jit(solution)/shard_map/ppermute | solution.py:353
  11.4 18.0 %all-to-all-start = ((bf16[16,4,16,256]{3,2,1,0:T(8,128)(2,1)}), bf16[16,4,16,256]{3,2,1,0:T(8,128)(2,1)S(1)}, u32[]{:S(2)}, u32[]{:S(2)}) async-start(bf16[16,4,16,256]{3,2,1,0:T(8,128)(2,1)} %bitcast.8), calls=%async_computation | async-start | bytes 1048576 | tf_op jit(solution)/shard_map/all_to_all | solution.py:360
  29.4 3.6 %collective-permute-start.2 = (bf16[16,4,16,256]{3,2,1,0:T(8,128)(2,1)S(1)}, bf16[16,4,16,256]{3,2,1,0:T(8,128)(2,1)S(1)}, u32[]{:S(2)}, u32[]{:S(2)}) collective-permute-start(bf16[16,4,16,256]{3,2,1,0:T(8,128)(2,1)S(1)} %all-to-all-done.mine), channel_id=1, source_target_pairs={{0,16},{16,0},{1,17},{17,1},{2,18},{18,2},{3,19},{19,3},{4,20},{20... | collective-permute-start | bytes 1572872 | tf_op jit(solution)/shard_map/ppermute | solution.py:368
  29.4 21.7 %all-to-all-start.1 = ((bf16[8,8,16,512]{3,2,1,0:T(8,128)(2,1)}), bf16[8,8,16,512]{3,2,1,0:T(8,128)(2,1)S(1)}, u32[]{:S(2)}, u32[]{:S(2)}) async-start(bf16[8,8,16,512]{3,2,1,0:T(8,128)(2,1)} %bitcast.9), calls=%async_computation.1 | async-start | bytes 2097152 | tf_op jit(solution)/shard_map/all_to_all | solution.py:369
  33.0 13.9 %copy-start.5 = (bf16[16,4,16,256]{3,2,1,0:T(8,128)(2,1)}, bf16[16,4,16,256]{3,2,1,0:T(8,128)(2,1)S(1)}, u32[]{:S(2)}) copy-start(bf16[16,4,16,256]{3,2,1,0:T(8,128)(2,1)S(1)} %collective-permute-done.2.other) | copy-start | bytes 1572868
  51.1 2.7 %collective-permute-start.3 = (bf16[8,2,2,2,16,512]{5,4,3,2,1,0:T(8,128)(2,1)S(1)}, bf16[8,2,2,2,16,512]{5,4,3,2,1,0:T(8,128)(2,1)S(1)}, u32[]{:S(2)}, u32[]{:S(2)}) collective-permute-start(bf16[8,2,2,2,16,512]{5,4,3,2,1,0:T(8,128)(2,1)S(1)} %bitcast.44), channel_id=1, source_target_pairs={{0,16},{16,0},{1,17},{17,1},{2,18},{18,2},{3,19},{19,3},{4,20},{20... | collective-permute-start | bytes 3145736 | tf_op jit(solution)/shard_map/ppermute | solution.py:379
  53.8 1.6 %copy-start.4 = (bf16[4,4,256,256]{3,2,1,0:T(8,128)(2,1)S(1)}, bf16[4,4,256,256]{3,2,1,0:T(8,128)(2,1)}, u32[]{:S(2)}) copy-start(bf16[4,4,256,256]{3,2,1,0:T(8,128)(2,1)} %weights.3) | copy-start | bytes 6291460
  56.6 5.2 %copy-start.2 = (bf16[4,16,16,256]{3,2,1,0:T(8,128)(2,1)S(1)}, bf16[4,16,16,256]{3,2,1,0:T(8,128)(2,1)}, u32[]{:S(2)}) copy-start(bf16[4,16,16,256]{3,2,1,0:T(8,128)(2,1)} %copy-done.1) | copy-start | bytes 1572868
  60.1 3.4 %copy-start.12 = (bf16[6,16,16,256]{3,2,1,0:T(8,128)(2,1)S(1)}, bf16[6,16,16,256]{3,2,1,0:T(8,128)(2,1)}, u32[]{:S(2)}) copy-start(bf16[6,16,16,256]{3,2,1,0:T(8,128)(2,1)} %copy-done.11) | copy-start | bytes 2359300
  60.1 10.6 %collective-permute-start.4 = (bf16[2,16,16,256]{3,2,1,0:T(8,128)(2,1)S(1)}, bf16[2,16,16,256]{3,2,1,0:T(8,128)(2,1)S(1)}, u32[]{:S(2)}, u32[]{:S(2)}) collective-permute-start(bf16[2,16,16,256]{3,2,1,0:T(8,128)(2,1)S(1)} %get-tuple-element.41), channel_id=1, source_target_pairs={{32,0},{64,32},{96,64},{33,1},{65,33},{97,65},{34,2},{66,34},{98,6... | collective-permute-start | bytes 786440 | tf_op jit(solution)/shard_map/ppermute | solution.py:326
  69.9 7.6 %copy-start.10 = (f32[4,16,16,256]{3,2,1,0:T(8,128)S(1)}, f32[4,16,16,256]{3,2,1,0:T(8,128)}, u32[]{:S(2)}) copy-start(f32[4,16,16,256]{3,2,1,0:T(8,128)} %copy-done.9) | copy-start | bytes 3145732
  70.7 50.2 %all-to-all-start.2 = ((bf16[64,88,256]{2,1,0:T(8,128)(2,1)}), bf16[64,88,256]{2,1,0:T(8,128)(2,1)}, u32[]{:S(2)}, u32[]{:S(2)}) async-start(bf16[64,88,256]{2,1,0:T(8,128)(2,1)} %shard_map.87), calls=%async_computation.2 | async-start | bytes 5767168 | tf_op jit(solution)/shard_map/all_to_all | solution.py:401
  77.5 2.0 %copy-start.3 = (bf16[3,3,3,256,256]{4,3,2,1,0:T(8,128)(2,1)S(1)}, bf16[3,3,3,256,256]{4,3,2,1,0:T(8,128)(2,1)}, u32[]{:S(2)}) copy-start(bf16[3,3,3,256,256]{4,3,2,1,0:T(8,128)(2,1)} %weights.4) | copy-start | bytes 10616836
  79.5 4.8 %copy-start.6 = (bf16[16,4,16,256]{3,2,1,0:T(8,128)(2,1)S(1)}, bf16[16,4,16,256]{3,2,1,0:T(8,128)(2,1)}, u32[]{:S(2)}) copy-start(bf16[16,4,16,256]{3,2,1,0:T(8,128)(2,1)} %copy-done.5) | copy-start | bytes 1572868
  84.3 11.8 %copy-start = (bf16[3,3,3,256,256]{4,3,2,1,0:T(8,128)(2,1)S(1)}, bf16[3,3,3,256,256]{4,3,2,1,0:T(8,128)(2,1)}, u32[]{:S(2)}) copy-start(bf16[3,3,3,256,256]{4,3,2,1,0:T(8,128)(2,1)} %weights.5) | copy-start | bytes 10616836
  89.3 23.2 %collective-permute-start.8 = (bf16[16,56,256]{2,1,0:T(8,128)(2,1)S(1)}, bf16[16,56,256]{2,1,0:T(8,128)(2,1)S(1)}, u32[]{:S(2)}, u32[]{:S(2)}) collective-permute-start(bf16[16,56,256]{2,1,0:T(8,128)(2,1)S(1)} %get-tuple-element.52), channel_id=1, source_target_pairs={{0,96},{32,0},{64,32},{96,64},{1,97},{33,1},{65,33},{97,65},{2,98}... | collective-permute-start | bytes 1376264 | tf_op jit(solution)/shard_map/ppermute | solution.py:330
  93.1 22.8 %collective-permute-start.7 = (bf16[16,56,256]{2,1,0:T(8,128)(2,1)S(1)}, bf16[16,56,256]{2,1,0:T(8,128)(2,1)S(1)}, u32[]{:S(2)}, u32[]{:S(2)}) collective-permute-start(bf16[16,56,256]{2,1,0:T(8,128)(2,1)S(1)} %get-tuple-element.51), channel_id=1, source_target_pairs={{0,32},{32,64},{64,96},{96,0},{1,33},{33,65},{65,97},{97,1},{2,34}... | collective-permute-start | bytes 1376264 | tf_op jit(solution)/shard_map/ppermute | solution.py:330
  93.1 22.8 %collective-permute-start.6 = (bf16[16,56,256]{2,1,0:T(8,128)(2,1)S(1)}, bf16[16,56,256]{2,1,0:T(8,128)(2,1)S(1)}, u32[]{:S(2)}, u32[]{:S(2)}) collective-permute-start(bf16[16,56,256]{2,1,0:T(8,128)(2,1)S(1)} %get-tuple-element.50), channel_id=1, source_target_pairs={{0,64},{32,96},{64,0},{96,32},{1,65},{33,97},{65,1},{97,33},{2,66}... | collective-permute-start | bytes 1376264 | tf_op jit(solution)/shard_map/ppermute | solution.py:330
  95.3 0.9 collective-permute-start.5
  121.8 17.9 %all-to-all-start.3 = ((bf16[16,72,256]{2,1,0:T(8,128)(2,1)}), bf16[16,72,256]{2,1,0:T(8,128)(2,1)S(1)}, u32[]{:S(2)}, u32[]{:S(2)}) async-start(bf16[16,72,256]{2,1,0:T(8,128)(2,1)} %pad_maximum_fusion), calls=%async_computation.3 | async-start | bytes 1179648 | tf_op jit(solution)/shard_map/all_to_all | solution.py:431
  128.0 6.8 %collective-permute-start.11 = (bf16[88,256]{1,0:T(8,128)(2,1)S(1)}, bf16[88,256]{1,0:T(8,128)(2,1)S(1)}, u32[]{:S(2)}, u32[]{:S(2)}) collective-permute-start(bf16[88,256]{1,0:T(8,128)(2,1)S(1)} %get-tuple-element.59), channel_id=1, source_target_pairs={{0,96},{32,0},{64,32},{96,64},{1,97},{33,1},{65,33},{97,65},{2,98}... | collective-permute-start | bytes 135176 | tf_op jit(solution)/shard_map/ppermute | solution.py:330
  132.6 5.7 %collective-permute-start.10 = (bf16[88,256]{1,0:T(8,128)(2,1)S(1)}, bf16[88,256]{1,0:T(8,128)(2,1)S(1)}, u32[]{:S(2)}, u32[]{:S(2)}) collective-permute-start(bf16[88,256]{1,0:T(8,128)(2,1)S(1)} %get-tuple-element.60), channel_id=1, source_target_pairs={{0,32},{32,64},{64,96},{96,0},{1,33},{33,65},{65,97},{97,1},{2,34}... | collective-permute-start | bytes 135176 | tf_op jit(solution)/shard_map/ppermute | solution.py:330
  132.6 5.7 %collective-permute-start.9 = (bf16[88,256]{1,0:T(8,128)(2,1)S(1)}, bf16[88,256]{1,0:T(8,128)(2,1)S(1)}, u32[]{:S(2)}, u32[]{:S(2)}) collective-permute-start(bf16[88,256]{1,0:T(8,128)(2,1)S(1)} %get-tuple-element.58), channel_id=1, source_target_pairs={{0,64},{32,96},{64,0},{96,32},{1,65},{33,97},{65,1},{97,33},{2,66}... | collective-permute-start | bytes 135176 | tf_op jit(solution)/shard_map/ppermute | solution.py:330
  (5 other events, 4.9 us)

commit v15 on v14

--- a/solution.py
+++ b/solution.py
@@ -9,7 +9,7 @@
 
 F32 = jnp.float32
 BF16 = jnp.bfloat16
-VMEM_LIMIT = 48 * 1024 * 1024
+VMEM_LIMIT = 56 * 1024 * 1024
 
 FR = 4
 ROWS = 16

time: 142 us -> 149 us (1.049)
  the two profiles are of different devices: /device:TPU:0 before, /device:TPU:1 now
where the time goes in v15:
time: 149 us; the launch traced here: 148 us
  Pallas kernels  54 us (36%)
  starting transfers between devices  45.7 us (31%)
  waiting for transfers between devices  34.1 us (23%)
  local copies, waits for them, and re-layouts  9.69 us (7%)
  other arithmetic  3.56 us (2%)
    pallas_call x7, Pallas kernels, call(): pl.pallas_call(kernel, out_shape=shapes[0] if single else shapes, grid=gr...  54 us
    ppermute x1, waiting for transfers between devices, shards(): lax.ppermute(hidden_head, ('y', 'core'), [(2 * i + 1, 2 * i - 1) for i in...  19.2 us
    ppermute x6, starting transfers between devices, over_y(): return lax.ppermute(value, 'y', [(i, (i + step) % 4) for i in range(4)])  9.98 us
    all_to_all x1, waiting for transfers between devices, shards(): block = lax.all_to_all(windows, ('z', 'x_hi', 'width'), 0, 0, tiled=True)  7.85 us
    all_to_all x1, starting transfers between devices, shards(): block = lax.all_to_all(windows, ('z', 'x_hi', 'width'), 0, 0, tiled=True)  7.6 us
    all_to_all x1, starting transfers between devices, shards(): late = lax.all_to_all(late, ('z', 'x_hi', 'width'), 0, 0, tiled=True)  6.65 us
    all_to_all x1, starting transfers between devices, shards(): early = lax.all_to_all(early, ('z', 'x_hi', 'width'), 0, 0, tiled=True)  5.62 us
    ppermute x2, starting transfers between devices, shift(): lax.ppermute(value, axis, [(i, i + step) for i in range(count) if 0 <= i...  5.5 us
  transfers between devices with their start and end apart: 16, of which 8 were waited for; matrix products, arithmetic and copies ran while one was open for 4% of the time, Pallas kernels for 32%

profile of v15, /device:TPU:1, one launch (start us, length us, event | category | flops | bytes accessed | tf_op | source)
XLA Modules:
  0.0 148.0 jit_solution(4765588832763490251)
XLA Ops:
  0.6 4.0 %collective-permute-start = (bf16[2,128,256]{2,1,0:T(8,128)(2,1)}, bf16[2,128,256]{2,1,0:T(8,128)(2,1)S(1)}, u32[]{:S(2)}, u32[]{:S(2)}) collective-permute-start(bf16[2,128,256]{2,1,0:T(8,128)(2,1)} %bitcast.52), channel_id=1, source_target_pairs={{0,32},{32,64},{64,96},{1,33},{33,65},{65,97},{2,34},{34,66},{66,9... | collective-permute-start | bytes 393224 | tf_op jit(solution)/shard_map/ppermute | solution.py:326
  5.9 1.3 collective-permute-start.1
  7.2 1.6 %collective-permute-done.1 = bf16[2,4,4,512]{3,2,1,0:T(4,128)(2,1)S(1)} collective-permute-done((bf16[2,4,4,512]{3,2,1,0:T(4,128)(2,1)S(1)}, bf16[2,4,4,512]{3,2,1,0:T(4,128)(2,1)S(1)}, u32[]{:S(2)}, u32[]{:S(2)}) %collective-permute-start.1) | collective-permute-done | bytes 32800 | tf_op jit(solution)/shard_map/ppermute | solution.py:353
  10.8 7.6 %all-to-all-start = ((bf16[16,4,16,256]{3,2,1,0:T(8,128)(2,1)}), bf16[16,4,16,256]{3,2,1,0:T(8,128)(2,1)S(1)}, u32[]{:S(2)}, u32[]{:S(2)}) async-start(bf16[16,4,16,256]{3,2,1,0:T(8,128)(2,1)} %bitcast.8), calls=%async_computation | async-start | bytes 1048576 | tf_op jit(solution)/shard_map/all_to_all | solution.py:360
  19.8 7.9 %all-to-all-done.mine = bf16[16,4,16,256]{3,2,1,0:T(8,128)(2,1)S(1)} async-done(((bf16[16,4,16,256]{3,2,1,0:T(8,128)(2,1)}), bf16[16,4,16,256]{3,2,1,0:T(8,128)(2,1)S(1)}, u32[]{:S(2)}, u32[]{:S(2)}) %all-to-all-start) | async-done | bytes 524320 | tf_op jit(solution)/shard_map/all_to_all | solution.py:360
  27.7 3.2 %collective-permute-start.2 = (bf16[16,4,16,256]{3,2,1,0:T(8,128)(2,1)S(1)}, bf16[16,4,16,256]{3,2,1,0:T(8,128)(2,1)S(1)}, u32[]{:S(2)}, u32[]{:S(2)}) collective-permute-start(bf16[16,4,16,256]{3,2,1,0:T(8,128)(2,1)S(1)} %all-to-all-done.mine), channel_id=1, source_target_pairs={{0,16},{16,0},{1,17},{17,1},{2,18},{18,2},{3,19},{19,3},{4,20},{20... | collective-permute-start | bytes 1572872 | tf_op jit(solution)/shard_map/ppermute | solution.py:368
  30.9 3.6 %all-to-all-start.1 = ((bf16[8,8,16,512]{3,2,1,0:T(8,128)(2,1)}), bf16[8,8,16,512]{3,2,1,0:T(8,128)(2,1)S(1)}, u32[]{:S(2)}, u32[]{:S(2)}) async-start(bf16[8,8,16,512]{3,2,1,0:T(8,128)(2,1)} %bitcast.9), calls=%async_computation.1 | async-start | bytes 2097152 | tf_op jit(solution)/shard_map/all_to_all | solution.py:369
  35.3 15.8 %shard_map.84 = (bf16[6,16,16,256]{3,2,1,0:T(8,128)(2,1)}, f32[4,16,16,256]{3,2,1,0:T(8,128)}, f32[4,16,16,256]{3,2,1,0:T(8,128)}, bf16[4,16,16,256]{3,2,1,0:T(8,128)(2,1)}) custom-call(s32[1]{0:T(128)} %bitcast.core_ref, bf16[16,4,16,256]{3,2,1,0:T(8,128)(2,1)} %copy-done.3, bf16[16,4,16,256]{3,2,1,0:T(8,128)(2,1)} %copy-done.6, ...), custom_call_target="tpu_custom_call" | custom-call | flops 8992587776 | bytes 11550724 | tf_op jit(solution)/shard_map/pallas_call | solution.py:312
  53.2 1.7 %collective-permute-done.3.other = bf16[8,2,2,2,16,512]{5,4,3,2,1,0:T(8,128)(2,1)S(1)} collective-permute-done((bf16[8,2,2,2,16,512]{5,4,3,2,1,0:T(8,128)(2,1)S(1)}, bf16[8,2,2,2,16,512]{5,4,3,2,1,0:T(8,128)(2,1)S(1)}, u32[]{:S(2)}, u32[]{:S(2)}) %collective-permute-start.3) | collective-permute-done | bytes 1048608 | tf_op jit(solution)/shard_map/ppermute | solution.py:379
  55.8 6.9 %shard_map.85 = (bf16[4,16,16,256]{3,2,1,0:T(8,128)(2,1)}, bf16[2,16,16,256]{3,2,1,0:T(8,128)(2,1)}) custom-call(s32[1]{0:T(128)} %bitcast.core_ref, bf16[8,2,2,2,16,512]{5,4,3,2,1,0:T(8,128)(2,1)} %bitcast.46, bf16[8,2,2,2,16,512]{5,4,3,2,1,0:T(8,128)(2,1)} %copy-done.1, bf16[4,4,256,256]{3,2,1,0:T(8,128)(2,1)} %weights.3, ...), custom_call_target="tpu_custom_call" | custom-call | flops 2147483648 | bytes 6045700 | tf_op jit(solution)/shard_map/pallas_call | solution.py:312
  62.7 1.5 collective-permute-start.4
  64.2 4.4 %shard_map.86.up = bf16[64,32,256]{2,1,0:T(8,128)(2,1)} custom-call(s32[1]{0:T(128)} %bitcast.core_ref, bf16[4,16,16,256]{3,2,1,0:T(8,128)(2,1)} %get-tuple-element.40.act, bf16[8,2,2,2,16,512]{5,4,3,2,1,0:T(8,128)(2,1)} %bitcast.47, bf16[8,2,2,2,16,512]{5,4,3,2,1,0:T(8,128)(2,1)} %copy-done.1), custom_call_target="tpu_custom_call" | custom-call | flops 536870912 | bytes 3670020 | tf_op jit(solution)/shard_map/pallas_call | solution.py:312
  68.6 7.5 %shard_map.87 = bf16[64,88,256]{2,1,0:T(8,128)(2,1)} custom-call(s32[2]{0:T(128)} %pad_add_fusion.place, bf16[6,16,16,256]{3,2,1,0:T(8,128)(2,1)} %get-tuple-element.39.act, bf16[4,16,16,256]{3,2,1,0:T(8,128)(2,1)} %get-tuple-element.38.block.grad_sum, bf16[64,32,256]{2,1,0:T(8,128)(2,1)} %shard_map.86.up), custom_call_target="tpu_custom_call" | custom-call | flops 3623878656 | bytes 5242888 | tf_op jit(solution)/shard_map/pallas_call | solution.py:312
  76.8 5.6 %all-to-all-start.2 = ((bf16[64,88,256]{2,1,0:T(8,128)(2,1)}), bf16[64,88,256]{2,1,0:T(8,128)(2,1)S(1)}, u32[]{:S(2)}, u32[]{:S(2)}) async-start(bf16[64,88,256]{2,1,0:T(8,128)(2,1)} %shard_map.87), calls=%async_computation.2 | async-start | bytes 5767168 | tf_op jit(solution)/shard_map/all_to_all | solution.py:401
  82.5 7.5 %shard_map.88 = (bf16[4,16,16,256]{3,2,1,0:T(8,128)(2,1)}, bf16[2,16,16,256]{3,2,1,0:T(8,128)(2,1)}) custom-call(bf16[4,16,16,256]{3,2,1,0:T(8,128)(2,1)} %get-tuple-element.38.block.grad_sum, bf16[2,16,16,256]{3,2,1,0:T(8,128)(2,1)} %copy-done.8, f32[4,16,16,256]{3,2,1,0:T(8,128)} %get-tuple-element.43.slope, bf16[3,3,3,256,256]{4,3,2,1,0:T(8,128)(2,1)} %weights.4, ...), custom_call_target="tpu_custom_call" | custom-call | flops 3623878656 | bytes 6176768 | tf_op jit(solution)/shard_map/pallas_call | solution.py:312
  90.0 6.9 %shard_map.89 = (bf16[16,56,256]{2,1,0:T(8,128)(2,1)}, bf16[16,56,256]{2,1,0:T(8,128)(2,1)}, bf16[16,56,256]{2,1,0:T(8,128)(2,1)}, bf16[16,56,256]{2,1,0:T(8,128)(2,1)}) custom-call(s32[2]{0:T(128)} %pad_add_fusion.place, bf16[16,4,16,256]{3,2,1,0:T(8,128)(2,1)} %copy-done.3, bf16[16,4,16,256]{3,2,1,0:T(8,128)(2,1)} %copy-done.6, ...), custom_call_target="tpu_custom_call" | custom-call | flops 3623878656 | bytes 3407880 | tf_op jit(solution)/shard_map/pallas_call | solution.py:312
  96.9 3.9 %collective-permute-start.8 = (bf16[16,56,256]{2,1,0:T(8,128)(2,1)}, bf16[16,56,256]{2,1,0:T(8,128)(2,1)S(1)}, u32[]{:S(2)}, u32[]{:S(2)}) collective-permute-start(bf16[16,56,256]{2,1,0:T(8,128)(2,1)} %get-tuple-element.52), channel_id=1, source_target_pairs={{0,96},{32,0},{64,32},{96,64},{1,97},{33,1},{65,33},{97,65},{2,98}... | collective-permute-start | bytes 1376264 | tf_op jit(solution)/shard_map/ppermute | solution.py:330
  100.8 1.6 %collective-permute-start.6 = (bf16[16,56,256]{2,1,0:T(8,128)(2,1)}, bf16[16,56,256]{2,1,0:T(8,128)(2,1)S(1)}, u32[]{:S(2)}, u32[]{:S(2)}) collective-permute-start(bf16[16,56,256]{2,1,0:T(8,128)(2,1)} %get-tuple-element.50), channel_id=1, source_target_pairs={{0,64},{32,96},{64,0},{96,32},{1,65},{33,97},{65,1},{97,33},{2,66}... | collective-permute-start | bytes 1376264 | tf_op jit(solution)/shard_map/ppermute | solution.py:330
  102.4 1.5 %collective-permute-start.5 = (bf16[2,16,16,256]{3,2,1,0:T(8,128)(2,1)S(1)}, bf16[2,16,16,256]{3,2,1,0:T(8,128)(2,1)S(1)}, u32[]{:S(2)}, u32[]{:S(2)}) collective-permute-start(bf16[2,16,16,256]{3,2,1,0:T(8,128)(2,1)S(1)} %copy-done.7), channel_id=1, source_target_pairs={{48,16},{80,48},{112,80},{49,17},{81,49},{113,81},{50,18},{82,50},... | collective-permute-start | bytes 786440 | tf_op jit(solution)/shard_map/ppermute | solution.py:408
  103.9 19.2 %collective-permute-done.5.later = bf16[2,16,16,256]{3,2,1,0:T(8,128)(2,1)S(1)} collective-permute-done((bf16[2,16,16,256]{3,2,1,0:T(8,128)(2,1)S(1)}, bf16[2,16,16,256]{3,2,1,0:T(8,128)(2,1)S(1)}, u32[]{:S(2)}, u32[]{:S(2)}) %collective-permute-start.5) | collective-permute-done | bytes 262176 | tf_op jit(solution)/shard_map/ppermute | solution.py:408
  123.8 5.0 %shard_map.90 = bf16[16,2,8,256]{3,2,1,0:T(8,128)(2,1)} custom-call(s32[1]{0:T(128)} %bitcast.core_ref, bf16[4,16,16,256]{3,2,1,0:T(8,128)(2,1)} %get-tuple-element.46.block, bf16[2,16,16,256]{3,2,1,0:T(8,128)(2,1)} %copy-done.5, bf16[4,16,16,256]{3,2,1,0:T(8,128)(2,1)} %get-tuple-element.38.block.grad_sum, bf16[3,3,3,256,256]{4,3,2,1,0:T(8,128)(2,1)} %weights.5), custom_call_target="tpu_custom_call" | custom-call | flops 939524096 | bytes 4980740 | tf_op jit(solution)/shard_map/pallas_call | solution.py:312
  130.6 6.7 %all-to-all-start.3 = ((bf16[16,72,256]{2,1,0:T(8,128)(2,1)}), bf16[16,72,256]{2,1,0:T(8,128)(2,1)S(1)}, u32[]{:S(2)}, u32[]{:S(2)}) async-start(bf16[16,72,256]{2,1,0:T(8,128)(2,1)} %pad_maximum_fusion), calls=%async_computation.3 | async-start | bytes 1179648 | tf_op jit(solution)/shard_map/all_to_all | solution.py:431
  137.7 1.4 collective-permute-start.11
  139.2 2.9 %collective-permute-start.9 = (bf16[88,256]{1,0:T(8,128)(2,1)S(1)}, bf16[88,256]{1,0:T(8,128)(2,1)S(1)}, u32[]{:S(2)}, u32[]{:S(2)}) collective-permute-start(bf16[88,256]{1,0:T(8,128)(2,1)S(1)} %get-tuple-element.58), channel_id=1, source_target_pairs={{0,64},{32,96},{64,0},{96,32},{1,65},{33,97},{65,1},{97,33},{2,66}... | collective-permute-start | bytes 135176 | tf_op jit(solution)/shard_map/ppermute | solution.py:330
  (62 shorter events, 18.0 us)
Async XLA Ops:
  0.6 8.2 %collective-permute-start = (bf16[2,128,256]{2,1,0:T(8,128)(2,1)}, bf16[2,128,256]{2,1,0:T(8,128)(2,1)S(1)}, u32[]{:S(2)}, u32[]{:S(2)}) collective-permute-start(bf16[2,128,256]{2,1,0:T(8,128)(2,1)} %bitcast.52), channel_id=1, source_target_pairs={{0,32},{32,64},{64,96},{1,33},{33,65},{65,97},{2,34},{34,66},{66,9... | collective-permute-start | bytes 393224 | tf_op jit(solution)/shard_map/ppermute | solution.py:326
  5.9 2.8 %collective-permute-start.1 = (bf16[2,4,4,512]{3,2,1,0:T(4,128)(2,1)S(1)}, bf16[2,4,4,512]{3,2,1,0:T(4,128)(2,1)S(1)}, u32[]{:S(2)}, u32[]{:S(2)}) collective-permute-start(bf16[2,4,4,512]{3,2,1,0:T(4,128)(2,1)S(1)} %slice_select_fusion), channel_id=1, source_target_pairs={{0,1},{1,0},{2,3},{3,2},{4,5},{5,4},{6,7},{7,6},{8,9},{9,8},{10,11... | collective-permute-start | bytes 98312 | tf_op jit(solution)/shard_map/ppermute | solution.py:353
  10.8 16.9 %all-to-all-start = ((bf16[16,4,16,256]{3,2,1,0:T(8,128)(2,1)}), bf16[16,4,16,256]{3,2,1,0:T(8,128)(2,1)S(1)}, u32[]{:S(2)}, u32[]{:S(2)}) async-start(bf16[16,4,16,256]{3,2,1,0:T(8,128)(2,1)} %bitcast.8), calls=%async_computation | async-start | bytes 1048576 | tf_op jit(solution)/shard_map/all_to_all | solution.py:360
  27.7 7.6 %copy-start.3 = (bf16[16,4,16,256]{3,2,1,0:T(8,128)(2,1)}, bf16[16,4,16,256]{3,2,1,0:T(8,128)(2,1)S(1)}, u32[]{:S(2)}) copy-start(bf16[16,4,16,256]{3,2,1,0:T(8,128)(2,1)S(1)} %all-to-all-done.mine) | copy-start | bytes 1572868
  27.7 6.8 %collective-permute-start.2 = (bf16[16,4,16,256]{3,2,1,0:T(8,128)(2,1)S(1)}, bf16[16,4,16,256]{3,2,1,0:T(8,128)(2,1)S(1)}, u32[]{:S(2)}, u32[]{:S(2)}) collective-permute-start(bf16[16,4,16,256]{3,2,1,0:T(8,128)(2,1)S(1)} %all-to-all-done.mine), channel_id=1, source_target_pairs={{0,16},{16,0},{1,17},{17,1},{2,18},{18,2},{3,19},{19,3},{4,20},{20... | collective-permute-start | bytes 1572872 | tf_op jit(solution)/shard_map/ppermute | solution.py:368
  30.9 20.9 %all-to-all-start.1 = ((bf16[8,8,16,512]{3,2,1,0:T(8,128)(2,1)}), bf16[8,8,16,512]{3,2,1,0:T(8,128)(2,1)S(1)}, u32[]{:S(2)}, u32[]{:S(2)}) async-start(bf16[8,8,16,512]{3,2,1,0:T(8,128)(2,1)} %bitcast.9), calls=%async_computation.1 | async-start | bytes 2097152 | tf_op jit(solution)/shard_map/all_to_all | solution.py:369
  34.5 0.8 copy-start.6
  51.7 3.1 %copy-start = (bf16[8,8,16,512]{3,2,1,0:T(8,128)(2,1)}, bf16[8,8,16,512]{3,2,1,0:T(8,128)(2,1)S(1)}, u32[]{:S(2)}) copy-start(bf16[8,8,16,512]{3,2,1,0:T(8,128)(2,1)S(1)} %all-to-all-done.1) | copy-start | bytes 3145732
  51.7 3.1 %collective-permute-start.3 = (bf16[8,2,2,2,16,512]{5,4,3,2,1,0:T(8,128)(2,1)S(1)}, bf16[8,2,2,2,16,512]{5,4,3,2,1,0:T(8,128)(2,1)S(1)}, u32[]{:S(2)}, u32[]{:S(2)}) collective-permute-start(bf16[8,2,2,2,16,512]{5,4,3,2,1,0:T(8,128)(2,1)S(1)} %bitcast.45), channel_id=1, source_target_pairs={{0,16},{16,0},{1,17},{17,1},{2,18},{18,2},{3,19},{19,3},{4,20},{20... | collective-permute-start | bytes 3145736 | tf_op jit(solution)/shard_map/ppermute | solution.py:379
  54.9 1.0 copy-start.1
  62.7 13.4 %collective-permute-start.4 = (bf16[2,16,16,256]{3,2,1,0:T(8,128)(2,1)}, bf16[2,16,16,256]{3,2,1,0:T(8,128)(2,1)S(1)}, u32[]{:S(2)}, u32[]{:S(2)}) collective-permute-start(bf16[2,16,16,256]{3,2,1,0:T(8,128)(2,1)} %get-tuple-element.41), channel_id=1, source_target_pairs={{32,0},{64,32},{96,64},{33,1},{65,33},{97,65},{34,2},{66,34},{98,6... | collective-permute-start | bytes 786440 | tf_op jit(solution)/shard_map/ppermute | solution.py:326
  76.1 0.7 copy-start.8
  76.8 52.3 %all-to-all-start.2 = ((bf16[64,88,256]{2,1,0:T(8,128)(2,1)}), bf16[64,88,256]{2,1,0:T(8,128)(2,1)S(1)}, u32[]{:S(2)}, u32[]{:S(2)}) async-start(bf16[64,88,256]{2,1,0:T(8,128)(2,1)} %shard_map.87), calls=%async_computation.2 | async-start | bytes 5767168 | tf_op jit(solution)/shard_map/all_to_all | solution.py:401
  90.0 12.4 %copy-start.7 = (bf16[2,16,16,256]{3,2,1,0:T(8,128)(2,1)S(1)}, bf16[2,16,16,256]{3,2,1,0:T(8,128)(2,1)}, u32[]{:S(2)}) copy-start(bf16[2,16,16,256]{3,2,1,0:T(8,128)(2,1)} %get-tuple-element.47) | copy-start | bytes 786436
  96.9 31.9 %collective-permute-start.8 = (bf16[16,56,256]{2,1,0:T(8,128)(2,1)}, bf16[16,56,256]{2,1,0:T(8,128)(2,1)S(1)}, u32[]{:S(2)}, u32[]{:S(2)}) collective-permute-start(bf16[16,56,256]{2,1,0:T(8,128)(2,1)} %get-tuple-element.52), channel_id=1, source_target_pairs={{0,96},{32,0},{64,32},{96,64},{1,97},{33,1},{65,33},{97,65},{2,98}... | collective-permute-start | bytes 1376264 | tf_op jit(solution)/shard_map/ppermute | solution.py:330
  100.8 28.0 %collective-permute-start.7 = (bf16[16,56,256]{2,1,0:T(8,128)(2,1)}, bf16[16,56,256]{2,1,0:T(8,128)(2,1)S(1)}, u32[]{:S(2)}, u32[]{:S(2)}) collective-permute-start(bf16[16,56,256]{2,1,0:T(8,128)(2,1)} %get-tuple-element.51), channel_id=1, source_target_pairs={{0,32},{32,64},{64,96},{96,0},{1,33},{33,65},{65,97},{97,1},{2,34}... | collective-permute-start | bytes 1376264 | tf_op jit(solution)/shard_map/ppermute | solution.py:330
  100.8 28.0 %collective-permute-start.6 = (bf16[16,56,256]{2,1,0:T(8,128)(2,1)}, bf16[16,56,256]{2,1,0:T(8,128)(2,1)S(1)}, u32[]{:S(2)}, u32[]{:S(2)}) collective-permute-start(bf16[16,56,256]{2,1,0:T(8,128)(2,1)} %get-tuple-element.50), channel_id=1, source_target_pairs={{0,64},{32,96},{64,0},{96,32},{1,65},{33,97},{65,1},{97,33},{2,66}... | collective-permute-start | bytes 1376264 | tf_op jit(solution)/shard_map/ppermute | solution.py:330
  102.4 20.7 %collective-permute-start.5 = (bf16[2,16,16,256]{3,2,1,0:T(8,128)(2,1)S(1)}, bf16[2,16,16,256]{3,2,1,0:T(8,128)(2,1)S(1)}, u32[]{:S(2)}, u32[]{:S(2)}) collective-permute-start(bf16[2,16,16,256]{3,2,1,0:T(8,128)(2,1)S(1)} %copy-done.7), channel_id=1, source_target_pairs={{48,16},{80,48},{112,80},{49,17},{81,49},{113,81},{50,18},{82,50},... | collective-permute-start | bytes 786440 | tf_op jit(solution)/shard_map/ppermute | solution.py:408
  103.9 24.9 %copy-start.4 = (bf16[16,56,256]{2,1,0:T(8,128)(2,1)S(1)}, bf16[16,56,256]{2,1,0:T(8,128)(2,1)}, u32[]{:S(2)}) copy-start(bf16[16,56,256]{2,1,0:T(8,128)(2,1)} %get-tuple-element.45) | copy-start | bytes 1376260
  128.8 0.9 copy-start.2
  130.6 16.0 %all-to-all-start.3 = ((bf16[16,72,256]{2,1,0:T(8,128)(2,1)}), bf16[16,72,256]{2,1,0:T(8,128)(2,1)S(1)}, u32[]{:S(2)}, u32[]{:S(2)}) async-start(bf16[16,72,256]{2,1,0:T(8,128)(2,1)} %pad_maximum_fusion), calls=%async_computation.3 | async-start | bytes 1179648 | tf_op jit(solution)/shard_map/all_to_all | solution.py:431
  137.7 4.5 %collective-permute-start.11 = (bf16[88,256]{1,0:T(8,128)(2,1)S(1)}, bf16[88,256]{1,0:T(8,128)(2,1)S(1)}, u32[]{:S(2)}, u32[]{:S(2)}) collective-permute-start(bf16[88,256]{1,0:T(8,128)(2,1)S(1)} %get-tuple-element.59), channel_id=1, source_target_pairs={{0,96},{32,0},{64,32},{96,64},{1,97},{33,1},{65,33},{97,65},{2,98}... | collective-permute-start | bytes 135176 | tf_op jit(solution)/shard_map/ppermute | solution.py:330
  139.1 4.1 %collective-permute-start.10 = (bf16[88,256]{1,0:T(8,128)(2,1)S(1)}, bf16[88,256]{1,0:T(8,128)(2,1)S(1)}, u32[]{:S(2)}, u32[]{:S(2)}) collective-permute-start(bf16[88,256]{1,0:T(8,128)(2,1)S(1)} %get-tuple-element.60), channel_id=1, source_target_pairs={{0,32},{32,64},{64,96},{96,0},{1,33},{33,65},{65,97},{97,1},{2,34}... | collective-permute-start | bytes 135176 | tf_op jit(solution)/shard_map/ppermute | solution.py:330
  139.2 4.9 %collective-permute-start.9 = (bf16[88,256]{1,0:T(8,128)(2,1)S(1)}, bf16[88,256]{1,0:T(8,128)(2,1)S(1)}, u32[]{:S(2)}, u32[]{:S(2)}) collective-permute-start(bf16[88,256]{1,0:T(8,128)(2,1)S(1)} %get-tuple-element.58), channel_id=1, source_target_pairs={{0,64},{32,96},{64,0},{96,32},{1,65},{33,97},{65,1},{97,33},{2,66}... | collective-permute-start | bytes 135176 | tf_op jit(solution)/shard_map/ppermute | solution.py:330
  (1 other events, 0.7 us)
